TPU v7x, 32 devices: a whole 2x2x4 slice. The times are simulated.
32 devices in a mesh: chan: 8 (over y, x, core), tm: 4 (over z).
Axes of the slice: x: 2, y: 2, z: 4, core: 2. Of those that a mesh axis runs over, the one named last changes fastest.
Arguments:
- spectra: bfloat16 [64, 8, 2, 768], P(None, 'tm', None, 'chan'), may hold values from -120 to 120
- bad_channels: int32 [768], P('chan'), may hold values 0 or 1
- tile_list: int32 [64, 2], P('chan'), may hold values from 0 to 5, as said below
Outputs:
- correlations: float32 [64, 32, 128, 128], P(('chan', 'tm'))
Inputs may be any that keep to these rules, and one draw needn't show every extreme that they name: `tile_list`: each row (a, b) has a <= b; a pair may appear more than once.
All inputs are finite; a program needn't handle non-finite values. No bound on the sum of `bad_channels` on one device may be relied on, other than what follows from the above.
Results may differ from a plain program's by a relative error of at most 0.004.
Values may be sent and summed in bfloat16 or wider, within the bound.
No kernel may reach another device: no remote copies, remote signals or barrier semaphores. Data moves between devices by JAX's collectives and lax.ppermute only.
A program may use at most 128 MiB of HBM per device.

v0:
```python
import math

import jax
import jax.numpy as jnp
from jax import lax
from jax.sharding import PartitionSpec as P

HR_DEV = 2
F = 64
LAGS = 32
TILE = 128


EPSILON = 1e-06


def whiten(spectra, bad_channels):
    values = spectra.astype(jnp.float32)
    power = jnp.mean(values * values, axis=(0, 2))
    keep_mask = (1 - bad_channels).astype(jnp.float32)
    white = values * lax.rsqrt(power + EPSILON)[None, :, None, :] * keep_mask[None, None, None, :]
    return white.astype(jnp.bfloat16)


def lag_table(hour_count):
    bin_number = jnp.arange(F, dtype=jnp.float32) + 1.0
    lag_steps = jnp.arange(LAGS, dtype=jnp.float32) - float(LAGS // 2)
    phases = math.pi / F * bin_number[:, None] * lag_steps[None, :]
    norm_scale = 1.0 / math.sqrt(F * hour_count)
    return jnp.stack([jnp.cos(phases) * norm_scale, -jnp.sin(phases) * norm_scale], axis=1)


def take_block(spectra_all, block_index):
    return lax.dynamic_slice_in_dim(spectra_all, block_index * TILE, TILE, axis=3)


def cross_spec(spectra_all, tile_pair):
    left_block = take_block(spectra_all, tile_pair[0])
    right_block = take_block(spectra_all, tile_pair[1])
    bin_total = left_block.shape[0]
    hour_count = left_block.shape[1]
    row_block = left_block.reshape(bin_total, 2 * hour_count, TILE)
    turned = jnp.stack([-right_block[:, :, 1], right_block[:, :, 0]], axis=2)
    col_block = jnp.concatenate([right_block, turned], axis=3).reshape(
        bin_total, 2 * hour_count, 2 * TILE
    )
    return jnp.einsum("fki,fkj->fij", row_block, col_block, preferred_element_type=jnp.float32)


def transform(cross, table):
    parted = cross.reshape(cross.shape[0], TILE, 2, TILE)
    return jnp.einsum("fixj,fxt->tij", parted, table, precision=lax.Precision.HIGHEST)


def tile_lags(spectra_all, table, pairs):
    return jax.vmap(lambda tile_pair: transform(cross_spec(spectra_all, tile_pair), table))(pairs)


def per_device(spectra, bad_channels, tile_list):
    white = whiten(spectra, bad_channels)
    tile_dev = tile_list.shape[0] // lax.axis_size("tm")
    table = lag_table(HR_DEV * lax.axis_size("tm"))
    hours_all = lax.all_gather(white, "tm", axis=1, tiled=True)
    spectra_all = lax.all_gather(hours_all, "chan", axis=3, tiled=True)
    own_pairs = lax.dynamic_slice_in_dim(
        tile_list, lax.axis_index("tm") * tile_dev, tile_dev, axis=0
    )
    return tile_lags(spectra_all, table, own_pairs)


def solution(mesh):
    placed = (P(None, "tm", None, "chan"), P("chan"), P("chan", None))
    return jax.shard_map(
        per_device,
        mesh=mesh,
        in_specs=placed,
        out_specs=P(("chan", "tm"), None, None, None),
        check_vma=False,
    )
```

profile of v0, /device:TPU:1, one launch (start us, length us, event | category | flops | bytes accessed | tf_op | source)
XLA Modules:
  0.0 124.5 jit_solution(5274875769018931717)
XLA Ops:
  6.5 0.0 copy-start
  6.5 0.0 all-gather.2.cloned.1.call-start
  6.5 0.9 fusion.7
  7.4 0.7 subtract_convert_fusion
  8.1 0.9 fusion.9
  9.0 13.3 %all_gather.6 = bf16[64,8,2,96]{3,0,2,1:T(8,128)(2,1)S(1)} all-gather(bf16[64,2,2,96]{3,0,2,1:T(8,128)(2,1)S(1)} %fusion.9), channel_id=1, replica_groups=mesh['chan'=8,'tm'=4] {'tm'}, dimensions={1}, use_global_device_ids=true | all-gather | bytes 245760 | tf_op jit(solution)/shard_map/all_gather | solution.py:63
  22.3 1.1 copy.15
  23.3 0.0 all-gather.2.cloned.1.call-update
  23.4 0.0 copy-done
  23.4 0.1 constant_dynamic-slice_fusion
  23.5 0.1 fusion.12
  23.6 35.9 %all-gather.2.cloned.1.call-done = bf16[64,8,2,768]{0,1,2,3:T(8,128)(2,1)} async-done(((bf16[64,8,2,96]{0,1,2,3:T(8,128)(2,1)}), bf16[64,8,2,768]{0,1,2,3:T(8,128)(2,1)}) %all-gather.2.cloned.1.call-update) | async-done | bytes 1572880 | tf_op jit(solution)/shard_map/all_gather | solution.py:64
  59.5 2.6 %gather_fusion.1 = bf16[2,64,8,2,128]{1,2,3,4,0:T(8,128)(2,1)S(1)} fusion(bf16[64,8,2,768]{0,1,2,3:T(8,128)(2,1)} %all-gather.2.cloned.1.call-done, s32[2]{0:T(128)S(1)} %get-tuple-element.10), kind=kCustom, calls=%fused_computation.1 | custom fusion | bytes 1048608 | tf_op jit(solution)/shard_map/vmap()/gather | solution.py:34
  62.1 0.1 slice_negate_fusion
  62.3 0.5 maximum_maximum_fusion
  62.8 3.1 %copy.17 = bf16[2,64,8,2,256]{4,3,2,1,0:T(2,128)(2,1)S(1)} copy(bf16[2,64,8,2,256]{1,2,3,4,0:T(8,128)(2,1)S(1)} %maximum_maximum_fusion) | data formatting | bytes 2097152 | tf_op jit(solution)/shard_map/vmap()/concatenate | solution.py:44
  65.9 0.4 reshape.116
  66.3 2.6 %gather_fusion = bf16[2,64,8,2,128]{1,2,3,4,0:T(8,128)(2,1)S(1)} fusion(bf16[64,8,2,768]{0,1,2,3:T(8,128)(2,1)} %all-gather.2.cloned.1.call-done, s32[2]{0:T(128)S(1)} %get-tuple-element.9), kind=kCustom, calls=%fused_computation | custom fusion | bytes 1048608 | tf_op jit(solution)/shard_map/vmap()/gather | solution.py:34
  69.0 0.9 copy.16
  69.9 8.1 %fusion.5 = f32[2,64,128,256]{3,2,1,0:T(8,128)} fusion(bf16[2,64,16,256]{3,2,1,0:T(8,128)(2,1)S(1)} %reshape.116, bf16[2,64,16,128]{3,1,2,0:T(8,128)(2,1)S(1)} %bitcast.18), kind=kOutput, calls=%fused_computation.7 | convolution fusion | flops 134217728 | bytes 18350080 | tf_op jit(solution)/shard_map/vmap(fki,fkj->fij)/dot_general | solution.py:47
  78.0 20.8 %reshape.117 = f32[2,64,128,2,128]{4,3,2,1,0:T(2,128)} reshape(f32[2,64,128,256]{3,2,1,0:T(8,128)} %fusion.5) | data formatting | bytes 33554432 | tf_op jit(solution)/shard_map/vmap()/reshape | solution.py:51
  98.8 14.5 %fusion.2 = f32[2,32,128,128]{3,1,2,0:T(8,128)S(1)} fusion(f32[2,64,128,2,128]{4,3,2,1,0:T(2,128)} %reshape.117, f32[64,1,32]{0,2,1:T(8,128)S(1)} %get-tuple-element.8, f32[64,1,32]{0,2,1:T(8,128)S(1)} %get-tuple-element.7), kind=kOutput, calls=%fused_computation.4 | convolution fusion | flops 1610616832 | bytes 20987904 | tf_op jit(solution)/shard_map/vmap(fixj,fxt->tij)/dot_general | solution.py:52
  113.2 4.4 %copy.20 = f32[2,32,128,128]{3,2,1,0:T(8,128)} copy(f32[2,32,128,128]{3,1,2,0:T(8,128)S(1)} %fusion.2) | data formatting | bytes 8388608 | tf_op jit(solution)/shard_map/vmap()/transpose | solution.py:56
  (4 shorter events, 0.0 us)
Async XLA Ops:
  6.5 16.9 %copy-start = (s32[8,2]{0,1:T(2,128)S(1)}, s32[8,2]{0,1:T(2,128)}, u32[]{:S(2)}) copy-start(s32[8,2]{0,1:T(2,128)} %param.5) | copy-start | bytes 196
  6.5 53.0 %all-gather.2.cloned.1.call-start = ((), (), s32[]{:S(2)}) async-start(), calls=%async_computation | async-start | bytes 3538944 | tf_op jit(solution)/shard_map/all_gather | solution.py:64
Sparse Core Ops, SparseCore 0:
  23.5 35.9 all-gather.1
where the time goes:
time: 125 us
  local copies, waits for them, and re-layouts  36.1 us (29%)
  waiting for transfers between devices  35.9 us (29%)
  matrix products  22.6 us (18%)
  between operations  13.5 us (11%)
  blocking collectives  13.3 us (11%)
  other arithmetic  3.19 us (3%)
    all_gather x1, waiting for transfers between devices, per_device(): spectra_all = lax.all_gather(hours_all, 'chan', axis=3, tiled=True)  35.9 us
    reshape x1, local copies, waits for them, and re-layouts, transform(): parted = cross.reshape(cross.shape[0], TILE, 2, TILE)  20.8 us
    dot_general x1, matrix products, transform(): jnp.einsum('fixj,fxt->tij', parted, table, precision=lax.Precision.HIGHEST)  14.5 us
    all_gather x1, blocking collectives, per_device(): hours_all = lax.all_gather(white, 'tm', axis=1, tiled=True)  13.3 us
    dot_general x1, matrix products, cross_spec(): jnp.einsum('fki,fkj->fij', row_block, col_block, preferred_element_type=j...  8.11 us
    gather x3, local copies, waits for them, and re-layouts, take_block(): lax.dynamic_slice_in_dim(spectra_all, block_index * TILE, TILE, axis=3)  6.16 us
    transpose x1, local copies, waits for them, and re-layouts, tile_lags(): jax.vmap(lambda tile_pair: transform(cross_spec(spectra_all, tile_pair),...  4.44 us
    concatenate x1, local copies, waits for them, and re-layouts, cross_spec(): jnp.concatenate([right_block, turned], axis=3)  3.11 us
  transfers between devices with their start and end apart: 1, of which 1 were waited for; matrix products, arithmetic and copies ran while one was open for 0% of the time, Pallas kernels for 0%

commit v1 on v0

v1 whole, which is shorter than its diff:
```python
import functools
import math

import jax
import jax.numpy as jnp
import numpy as np
from jax import lax
from jax.experimental import pallas as pl
from jax.experimental.pallas import tpu as pltpu
from jax.sharding import PartitionSpec as P

F = 64
LAGS = 32
TILE = 128
EPSILON = 1e-06
COARSE = 8
LEFT_TURNS = LAGS // COARSE
PAIR = 2


def turn_tables(hours, hours_dev):
    bins = np.repeat(np.arange(1, F + 1, dtype=np.float64), hours_dev)
    left = math.pi / F * bins[None] * (COARSE * np.arange(LEFT_TURNS) - LAGS // 2)[:, None]
    right = -math.pi / F * bins[None] * np.arange(COARSE)[:, None]
    norm = 1.0 / math.sqrt(F * hours)
    left_table = np.stack([np.cos(left) * norm, np.sin(left) * norm], axis=1)
    right_table = np.stack([np.cos(right), np.sin(right)], axis=1)
    return left_table.astype(np.float32), right_table.astype(np.float32)


def whiten_kernel(spectra_ref, bad_ref, out_ref):
    bins, hours, _, chans = spectra_ref.shape
    rows = bins * hours * 2
    values = spectra_ref[...].reshape(rows, chans).astype(jnp.float32)
    row = lax.broadcasted_iota(jnp.int32, (rows, chans), 0)
    hour = (row // 2) % hours
    squares = values * values
    keep = (1 - bad_ref[...]).astype(jnp.float32)
    scale = jnp.zeros((rows, chans), jnp.float32)
    for h in range(hours):
        power = jnp.sum(jnp.where(hour == h, squares, 0.0), axis=0, keepdims=True) * (1.0 / (2 * bins))
        scale = jnp.where(hour == h, lax.rsqrt(power + EPSILON) * keep, scale)
    white = (values * scale).astype(jnp.bfloat16)
    src = lax.broadcasted_iota(jnp.int32, (rows, rows), 0)
    dst = lax.broadcasted_iota(jnp.int32, (rows, rows), 1)
    move = jnp.where((src % 2) * (rows // 2) + src // 2 == dst, 1.0, 0.0).astype(jnp.bfloat16)
    out_ref[...] = lax.dot_general(
        white, move, (((0,), (0,)), ((), ())), preferred_element_type=jnp.float32
    ).astype(jnp.bfloat16)


def whiten(spectra, bad_channels):
    bins, hours, _, chans = spectra.shape
    return pl.pallas_call(
        whiten_kernel,
        out_shape=jax.ShapeDtypeStruct((chans, bins * hours * 2), jnp.bfloat16),
        name="whiten",
    )(spectra, bad_channels.reshape(1, chans))


def turned(block, cos, sin):
    half = block.shape[1] // 2
    re = block[:, :half].astype(jnp.float32)
    im = block[:, half:].astype(jnp.float32)
    return jnp.concatenate([re * cos - im * sin, re * sin + im * cos], axis=1).astype(jnp.bfloat16)


def correlate_kernel(pairs_ref, left_ref, right_ref, left_table_ref, right_table_ref, out_ref, left_turned, right_turned):
    groups = left_ref.shape[0]
    lanes = left_ref.shape[2]

    @pl.when(pl.program_id(1) == 0)
    def _():
        for g in range(groups):
            block = left_ref[g]
            for u in range(LEFT_TURNS):
                left_turned[u * TILE:(u + 1) * TILE, g * lanes:(g + 1) * lanes] = turned(
                    block, left_table_ref[u, 0:1, :], left_table_ref[u, 1:2, :]
                )

    for g in range(groups):
        block = right_ref[g]
        for s in range(PAIR):
            right_turned[s * TILE:(s + 1) * TILE, g * lanes:(g + 1) * lanes] = turned(
                block, right_table_ref[s, 0:1, :], right_table_ref[s, 1:2, :]
            )
    total = lax.dot_general(
        left_turned[...], right_turned[...], (((1,), (1,)), ((), ())), preferred_element_type=jnp.float32
    )
    for u in range(LEFT_TURNS):
        for s in range(PAIR):
            out_ref[0, u, s] = total[u * TILE:(u + 1) * TILE, s * TILE:(s + 1) * TILE]


def correlate(spectra_all, pairs, hours):
    groups, _, lanes = spectra_all.shape
    tiles = pairs.shape[0]
    half = lanes // 2
    left_table, right_table = turn_tables(hours, half // F)
    out = pl.pallas_call(
        correlate_kernel,
        out_shape=jax.ShapeDtypeStruct((tiles, LEFT_TURNS, COARSE, TILE, TILE), jnp.float32),
        grid_spec=pltpu.PrefetchScalarGridSpec(
            num_scalar_prefetch=1,
            grid=(tiles, COARSE // PAIR),
            in_specs=[
                pl.BlockSpec((groups, TILE, lanes), lambda t, j, pairs: (0, pairs[t, 0], 0)),
                pl.BlockSpec((groups, TILE, lanes), lambda t, j, pairs: (0, pairs[t, 1], 0)),
                pl.BlockSpec((LEFT_TURNS, 2, half), lambda t, j, pairs: (0, 0, 0)),
                pl.BlockSpec((PAIR, 2, half), lambda t, j, pairs: (j, 0, 0)),
            ],
            out_specs=pl.BlockSpec((1, LEFT_TURNS, PAIR, TILE, TILE), lambda t, j, pairs: (t, 0, j, 0, 0)),
            scratch_shapes=[
                pltpu.VMEM((LEFT_TURNS * TILE, groups * lanes), jnp.bfloat16),
                pltpu.VMEM((PAIR * TILE, groups * lanes), jnp.bfloat16),
            ],
        ),
        compiler_params=pltpu.CompilerParams(vmem_limit_bytes=32 * 1024 * 1024),
        name="correlate",
    )(pairs, spectra_all, spectra_all, jnp.asarray(left_table), jnp.asarray(right_table))
    return out.reshape(tiles, LAGS, TILE, TILE)


def per_device(spectra, bad_channels, tile_list):
    groups = lax.axis_size("tm")
    hours = spectra.shape[1] * groups
    tile_dev = tile_list.shape[0] // groups
    white = whiten(spectra, bad_channels)
    gathered = lax.all_gather(white, ("tm", "chan"), axis=0, tiled=True)
    spectra_all = gathered.reshape(groups, gathered.shape[0] // groups, gathered.shape[1])
    pairs = lax.dynamic_slice_in_dim(tile_list, lax.axis_index("tm") * tile_dev, tile_dev, axis=0)
    return correlate(spectra_all, pairs, hours)


def solution(mesh):
    placed = (P(None, "tm", None, "chan"), P("chan"), P("chan", None))
    return jax.shard_map(
        per_device,
        mesh=mesh,
        in_specs=placed,
        out_specs=P(("chan", "tm"), None, None, None),
        check_vma=False,
    )
```

time: 125 us -> 84.6 us (0.68)
  local copies, waits for them, and re-layouts: 36.1 us -> 2.96 us
  waiting for transfers between devices: 35.9 us -> 59.1 us
  matrix products: 22.6 us -> 0 us
  blocking collectives: 13.3 us -> 0 us
  Pallas kernels: 0 us -> 8.72 us
  other arithmetic: 3.19 us -> 0 us
    all_gather x1, waiting for transfers between devices: 35.9 us -> 59.1 us  [per_device(): gathered = lax.all_gather(white, ('tm', 'chan'), axis=0, tiled=True)]
    dot_general x2 -> x0, matrix products: 22.6 us -> none  [the longest x1 14.5 us: transform(): jnp.einsum('fixj,fxt->tij', parted, table, precision=lax.Precision.HIGHEST)]
    reshape x2 -> x0, local copies, waits for them, and re-layouts: 21.2 us -> none  [the longest x1 20.8 us: transform(): parted = cross.reshape(cross.shape[0], TILE, 2, TILE)]
    all_gather x1 -> x0, blocking collectives: 13.3 us -> none  [per_device(): hours_all = lax.all_gather(white, 'tm', axis=1, tiled=True)]
    pallas_call x0 -> x2, Pallas kernels: none -> 8.72 us  [the longest x1 6.82 us: correlate(): pl.pallas_call(correlate_kernel, out_shape=jax.ShapeDtypeStruct((tiles, L...]
    gather x3 -> x0, local copies, waits for them, and re-layouts: 6.16 us -> none  [take_block(): lax.dynamic_slice_in_dim(spectra_all, block_index * TILE, TILE, axis=3)]
    transpose x1 -> x0, local copies, waits for them, and re-layouts: 4.44 us -> none  [tile_lags(): jax.vmap(lambda tile_pair: transform(cross_spec(spectra_all, tile_pair),...]
    concatenate x1 -> x0, local copies, waits for them, and re-layouts: 3.11 us -> none  [cross_spec(): jnp.concatenate([right_block, turned], axis=3)]
where the time goes in v1:
time: 84.6 us; the launch traced here: 84.2 us
  waiting for transfers between devices  59.1 us (70%)
  between operations  13.4 us (16%)
  Pallas kernels  8.72 us (10%)
  local copies, waits for them, and re-layouts  2.96 us (3%)
    all_gather x1, waiting for transfers between devices, per_device(): gathered = lax.all_gather(white, ('tm', 'chan'), axis=0, tiled=True)  59.1 us
    pallas_call x1, Pallas kernels, correlate(): pl.pallas_call(correlate_kernel, out_shape=jax.ShapeDtypeStruct((tiles, L...  6.82 us
    unnamed x9, local copies, waits for them, and re-layouts  2.89 us
    pallas_call x1, Pallas kernels, whiten(): pl.pallas_call(whiten_kernel, out_shape=jax.ShapeDtypeStruct((chans, bins...  1.9 us
  transfers between devices with their start and end apart: 1, of which 1 were waited for; matrix products, arithmetic and copies ran while one was open for 0% of the time, Pallas kernels for 0%

profile of v1, /device:TPU:1, one launch (start us, length us, event | category | flops | bytes accessed | tf_op | source)
XLA Modules:
  0.0 84.2 jit_solution(9394471571052391516)
XLA Ops:
  6.5 0.0 copy-start
  6.5 0.0 all-gather.2.cloned.1.call-start
  6.5 1.9 %whiten.1 = bf16[96,256]{1,0:T(8,128)(2,1)} custom-call(bf16[64,2,2,96]{3,2,1,0:T(2,128)(2,1)} %spectra_ref.1, s32[1,96]{1,0:T(1,128)} %bitcast.5), custom_call_target="tpu_custom_call" | custom-call | tf_op jit(solution)/shard_map/whiten/pallas_call | solution.py:54
  8.4 0.0 all-gather.2.cloned.1.call-update
  8.5 0.0 copy-done
  8.5 0.1 constant_dynamic-slice_fusion
  8.5 0.1 copy.7.pairs_ref
  8.6 59.1 %all-gather.2.cloned.1.call-done = bf16[3072,256]{1,0:T(8,128)(2,1)} async-done(((bf16[96,256]{1,0:T(8,128)(2,1)}), bf16[3072,256]{1,0:T(8,128)(2,1)}) %all-gather.2.cloned.1.call-update) | async-done | bytes 1572880 | tf_op jit(solution)/shard_map/all_gather | solution.py:129
  67.7 0.0 copy-start.1
  67.7 1.4 %copy-done.1 = bf16[3072,256]{1,0:T(8,128)(2,1)S(1)} copy-done((bf16[3072,256]{1,0:T(8,128)(2,1)S(1)}, bf16[3072,256]{1,0:T(8,128)(2,1)}, u32[]{:S(2)}) %copy-start.1) | copy-done | bytes 1572888
  69.1 0.0 copy-start.2
  69.1 0.7 copy-done.2
  69.8 0.0 copy-start.3
  69.8 0.7 copy-done.3
  70.5 6.8 %correlate.1 = f32[2,4,8,128,128]{4,3,2,1,0:T(8,128)} custom-call(s32[2,2]{1,0:T(2,128)S(1)} %copy.7.pairs_ref, bf16[4,768,256]{2,1,0:T(8,128)(2,1)S(1)} %bitcast.3, bf16[4,768,256]{2,1,0:T(8,128)(2,1)S(1)} %bitcast.4, f32[4,2,128]{2,1,0:T(2,128)S(1)} %copy-done.3, f32[8,2,128]{2,1,0:T(2,128)S(1)} %copy-done.2), custom_call_target="tpu_custom_call" | custom-call | tf_op jit(solution)/shard_map/correlate/pallas_call | solution.py:100
Async XLA Ops:
  6.5 1.9 %copy-start = (s32[8,2]{0,1:T(2,128)S(1)}, s32[8,2]{0,1:T(2,128)}, u32[]{:S(2)}) copy-start(s32[8,2]{0,1:T(2,128)} %param.7) | copy-start | bytes 196
  6.5 61.2 %all-gather.2.cloned.1.call-start = ((), (), s32[]{:S(2)}) async-start(), calls=%async_computation | async-start | bytes 1622016 | tf_op jit(solution)/shard_map/all_gather | solution.py:129
  67.7 1.4 %copy-start.1 = (bf16[3072,256]{1,0:T(8,128)(2,1)S(1)}, bf16[3072,256]{1,0:T(8,128)(2,1)}, u32[]{:S(2)}) copy-start(bf16[3072,256]{1,0:T(8,128)(2,1)} %all-gather.2.cloned.1.call-done) | copy-start | bytes 4718596
  69.1 0.7 copy-start.2
  69.8 0.7 copy-start.3
Sparse Core Ops, SparseCore 0:
  10.2 57.4 all-gather.1

commit v2 on v1

--- a/solution.py
+++ b/solution.py
@@ -65,24 +65,45 @@
     return jnp.concatenate([re * cos - im * sin, re * sin + im * cos], axis=1).astype(jnp.bfloat16)
 
 
-def correlate_kernel(pairs_ref, left_ref, right_ref, left_table_ref, right_table_ref, out_ref, left_turned, right_turned):
-    groups = left_ref.shape[0]
-    lanes = left_ref.shape[2]
+def correlate_kernel(where_ref, *refs):
+    pieces = refs[:-9]
+    left_table_hbm, right_table_hbm, out_ref, spectra, left_table, right_table, left_turned, right_turned, sem = refs[-9:]
+    tile, step = pl.program_id(0), pl.program_id(1)
+    groups, _, lanes = spectra.shape
+    rows = pieces[0].shape[1]
 
-    @pl.when(pl.program_id(1) == 0)
+    @pl.when((tile == 0) & (step == 0))
     def _():
+        own = where_ref[0]
+        copies = [
+            pltpu.make_async_copy(left_table_hbm, left_table, sem),
+            pltpu.make_async_copy(right_table_hbm, right_table, sem),
+        ]
+        for k, piece in enumerate(pieces):
+            place = pl.multiple_of((own ^ k) * rows, 32)
+            copies.append(pltpu.make_async_copy(piece, spectra.at[:, pl.ds(place, rows), :], sem))
+        for copy in copies:
+            copy.start()
+        for copy in copies:
+            copy.wait()
+
+    @pl.when(step == 0)
+    def _():
+        place = pl.multiple_of(where_ref[1 + 2 * tile] * TILE, TILE)
         for g in range(groups):
-            block = left_ref[g]
+            block = spectra[g, pl.ds(place, TILE), :]
             for u in range(LEFT_TURNS):
                 left_turned[u * TILE:(u + 1) * TILE, g * lanes:(g + 1) * lanes] = turned(
-                    block, left_table_ref[u, 0:1, :], left_table_ref[u, 1:2, :]
+                    block, left_table[u, 0:1, :], left_table[u, 1:2, :]
                 )
 
+    place = pl.multiple_of(where_ref[2 + 2 * tile] * TILE, TILE)
     for g in range(groups):
-        block = right_ref[g]
+        block = spectra[g, pl.ds(place, TILE), :]
         for s in range(PAIR):
+            turn = step * PAIR + s
             right_turned[s * TILE:(s + 1) * TILE, g * lanes:(g + 1) * lanes] = turned(
-                block, right_table_ref[s, 0:1, :], right_table_ref[s, 1:2, :]
+                block, right_table[turn, 0:1, :], right_table[turn, 1:2, :]
             )
     total = lax.dot_general(
         left_turned[...], right_turned[...], (((1,), (1,)), ((), ())), preferred_element_type=jnp.float32
@@ -92,33 +113,47 @@
             out_ref[0, u, s] = total[u * TILE:(u + 1) * TILE, s * TILE:(s + 1) * TILE]
 
 
-def correlate(spectra_all, pairs, hours):
-    groups, _, lanes = spectra_all.shape
+def correlate(pieces, pairs, own, hours):
+    groups, rows, lanes = pieces[0].shape
     tiles = pairs.shape[0]
     half = lanes // 2
     left_table, right_table = turn_tables(hours, half // F)
+    where = jnp.concatenate([own.reshape(1), pairs.reshape(-1)]).astype(jnp.int32)
     out = pl.pallas_call(
         correlate_kernel,
         out_shape=jax.ShapeDtypeStruct((tiles, LEFT_TURNS, COARSE, TILE, TILE), jnp.float32),
         grid_spec=pltpu.PrefetchScalarGridSpec(
             num_scalar_prefetch=1,
             grid=(tiles, COARSE // PAIR),
-            in_specs=[
-                pl.BlockSpec((groups, TILE, lanes), lambda t, j, pairs: (0, pairs[t, 0], 0)),
-                pl.BlockSpec((groups, TILE, lanes), lambda t, j, pairs: (0, pairs[t, 1], 0)),
-                pl.BlockSpec((LEFT_TURNS, 2, half), lambda t, j, pairs: (0, 0, 0)),
-                pl.BlockSpec((PAIR, 2, half), lambda t, j, pairs: (j, 0, 0)),
-            ],
-            out_specs=pl.BlockSpec((1, LEFT_TURNS, PAIR, TILE, TILE), lambda t, j, pairs: (t, 0, j, 0, 0)),
+            in_specs=[pl.BlockSpec(memory_space=pl.ANY)] * (len(pieces) + 2),
+            out_specs=pl.BlockSpec((1, LEFT_TURNS, PAIR, TILE, TILE), lambda t, j, where: (t, 0, j, 0, 0)),
             scratch_shapes=[
+                pltpu.VMEM((groups, len(pieces) * rows, lanes), jnp.bfloat16),
+                pltpu.VMEM(left_table.shape, jnp.float32),
+                pltpu.VMEM(right_table.shape, jnp.float32),
                 pltpu.VMEM((LEFT_TURNS * TILE, groups * lanes), jnp.bfloat16),
                 pltpu.VMEM((PAIR * TILE, groups * lanes), jnp.bfloat16),
+                pltpu.SemaphoreType.DMA,
             ],
         ),
-        compiler_params=pltpu.CompilerParams(vmem_limit_bytes=32 * 1024 * 1024),
+        compiler_params=pltpu.CompilerParams(vmem_limit_bytes=40 * 1024 * 1024),
         name="correlate",
-    )(pairs, spectra_all, spectra_all, jnp.asarray(left_table), jnp.asarray(right_table))
+    )(where, *pieces, jnp.asarray(left_table), jnp.asarray(right_table))
     return out.reshape(tiles, LAGS, TILE, TILE)
+
+
+def swap(array, axis, k):
+    if k == 0:
+        return array
+    return lax.ppermute(array, axis, [(i, i ^ k) for i in range(lax.axis_size(axis))])
+
+
+def gather_pieces(white):
+    stack = jnp.stack([swap(white, "tm", k) for k in range(lax.axis_size("tm"))])
+    pieces = {k: swap(stack, "chan", k) for k in range(0, lax.axis_size("chan"), 2)}
+    for k in list(pieces):
+        pieces[k + 1] = swap(pieces[k], "chan", 1)
+    return [pieces[k] for k in sorted(pieces)]
 
 
 def per_device(spectra, bad_channels, tile_list):
@@ -126,10 +161,9 @@
     hours = spectra.shape[1] * groups
     tile_dev = tile_list.shape[0] // groups
     white = whiten(spectra, bad_channels)
-    gathered = lax.all_gather(white, ("tm", "chan"), axis=0, tiled=True)
-    spectra_all = gathered.reshape(groups, gathered.shape[0] // groups, gathered.shape[1])
+    pieces = gather_pieces(white)
     pairs = lax.dynamic_slice_in_dim(tile_list, lax.axis_index("tm") * tile_dev, tile_dev, axis=0)
-    return correlate(spectra_all, pairs, hours)
+    return correlate(pieces, pairs, lax.axis_index("chan"), hours)
 
 
 def solution(mesh):

time: 84.6 us -> 34.6 us (0.41)
  waiting for transfers between devices: 59.1 us -> 7.42 us
  starting transfers between devices: 0.01 us -> 14.9 us
  between operations: 13.4 us -> 0.02 us
  local copies, waits for them, and re-layouts: 2.96 us -> 1.64 us
  other arithmetic: 0 us -> 0.9 us
    all_gather x1 -> x0, waiting for transfers between devices: 59.1 us -> none  [per_device(): gathered = lax.all_gather(white, ('tm', 'chan'), axis=0, tiled=True)]
    ppermute x0 -> x10, starting transfers between devices: none -> 14.9 us  [swap(): lax.ppermute(array, axis, [(i, i ^ k) for i in range(lax.axis_size(axis))])]
    ppermute x0 -> x10, waiting for transfers between devices: none -> 7.42 us  [swap(): lax.ppermute(array, axis, [(i, i ^ k) for i in range(lax.axis_size(axis))])]
    unnamed x9 -> x6, local copies, waits for them, and re-layouts: 2.89 us -> 1.39 us
  transfers between devices with their start and end apart: 1 -> 10, of which waited for: 1 -> 6; matrix products, arithmetic and copies ran while one was open for 0% -> 1% of each run, Pallas kernels for 0% -> 0%
where the time goes in v2:
time: 34.6 us; the launch traced here: 34.1 us
  starting transfers between devices  14.9 us (43%)
  Pallas kernels  9.23 us (27%)
  waiting for transfers between devices  7.42 us (21%)
  local copies, waits for them, and re-layouts  1.64 us (5%)
  other arithmetic  0.9 us (3%)
    ppermute x10, starting transfers between devices, swap(): lax.ppermute(array, axis, [(i, i ^ k) for i in range(lax.axis_size(axis))])  14.9 us
    ppermute x10, waiting for transfers between devices, swap(): lax.ppermute(array, axis, [(i, i ^ k) for i in range(lax.axis_size(axis))])  7.42 us
    pallas_call x1, Pallas kernels, correlate(): pl.pallas_call(correlate_kernel, out_shape=jax.ShapeDtypeStruct((tiles, L...  7.33 us
    pallas_call x1, Pallas kernels, whiten(): pl.pallas_call(whiten_kernel, out_shape=jax.ShapeDtypeStruct((chans, bins...  1.9 us
    unnamed x6, local copies, waits for them, and re-layouts  1.39 us
    another operation x1, other arithmetic, gather_pieces(): jnp.stack([swap(white, 'tm', k) for k in range(lax.axis_size('tm'))])  0.83 us
  transfers between devices with their start and end apart: 10, of which 6 were waited for; matrix products, arithmetic and copies ran while one was open for 1% of the time, Pallas kernels for 0%

profile of v2, /device:TPU:1, one launch (start us, length us, event | category | flops | bytes accessed | tf_op | source)
XLA Modules:
  0.0 34.1 jit_solution(9391620657372703166)
XLA Ops:
  0.0 0.0 copy-start
  0.0 1.9 %whiten.1 = bf16[96,256]{1,0:T(8,128)(2,1)} custom-call(bf16[64,2,2,96]{3,2,1,0:T(2,128)(2,1)} %spectra_ref.1, s32[1,96]{1,0:T(1,128)} %bitcast.11), custom_call_target="tpu_custom_call" | custom-call | tf_op jit(solution)/shard_map/whiten/pallas_call | solution.py:54
  1.9 4.2 %collective-permute-start.2 = (bf16[96,256]{1,0:T(8,128)(2,1)}, bf16[96,256]{1,0:T(8,128)(2,1)S(1)}, u32[]{:S(2)}, u32[]{:S(2)}) collective-permute-start(bf16[96,256]{1,0:T(8,128)(2,1)} %whiten.1), channel_id=1, source_target_pairs={{0,3},{1,2},{2,1},{3,0},{4,7},{5,6},{6,5},{7,4},{8,11},{9,10},{10,... | collective-permute-start | bytes 147464 | tf_op jit(solution)/shard_map/ppermute | solution.py:148
  6.1 0.0 collective-permute-start.1
  6.1 0.3 collective-permute-start
  6.3 1.4 %collective-permute-done.2 = bf16[96,256]{1,0:T(8,128)(2,1)S(1)} collective-permute-done((bf16[96,256]{1,0:T(8,128)(2,1)}, bf16[96,256]{1,0:T(8,128)(2,1)S(1)}, u32[]{:S(2)}, u32[]{:S(2)}) %collective-permute-start.2) | collective-permute-done | bytes 49184 | tf_op jit(solution)/shard_map/ppermute | solution.py:148
  7.8 2.9 %collective-permute-done.1 = bf16[96,256]{1,0:T(8,128)(2,1)S(1)} collective-permute-done((bf16[96,256]{1,0:T(8,128)(2,1)}, bf16[96,256]{1,0:T(8,128)(2,1)S(1)}, u32[]{:S(2)}, u32[]{:S(2)}) %collective-permute-start.1) | collective-permute-done | bytes 49184 | tf_op jit(solution)/shard_map/ppermute | solution.py:148
  10.6 0.0 collective-permute-done
  10.6 0.8 %pad_maximum_fusion.refs_0_ = bf16[4,96,256]{2,1,0:T(8,128)(2,1)S(1)} fusion(bf16[1,96,256]{2,1,0:T(8,128)(2,1)S(1)} %bitcast.8, bf16[1,96,256]{2,1,0:T(8,128)(2,1)S(1)} %bitcast.9, bf16[1,96,256]{2,1,0:T(8,128)(2,1)S(1)} %bitcast.10, bf16[1,96,256]{2,1,0:T(8,128)(2,1)} %bitcast.7), kind=kLoop, calls=%fused_computation | loop fusion | flops 294912 | bytes 393216 | tf_op jit(solution)/shard_map/stack | solution.py:152
  11.5 2.2 %collective-permute-start.8 = (bf16[4,96,256]{2,1,0:T(8,128)(2,1)S(1)}, bf16[4,96,256]{2,1,0:T(8,128)(2,1)S(1)}, u32[]{:S(2)}, u32[]{:S(2)}) collective-permute-start(bf16[4,96,256]{2,1,0:T(8,128)(2,1)S(1)} %pad_maximum_fusion.refs_0_), channel_id=1, source_target_pairs={{0,24},{4,28},{8,16},{12,20},{16,8},{20,12},{24,0},{28,4},{1,25},{... | collective-permute-start | bytes 589832 | tf_op jit(solution)/shard_map/ppermute | solution.py:148
  13.7 0.2 collective-permute-start.6
  13.9 0.3 collective-permute-start.4
  14.2 2.4 %collective-permute-start.3 = (bf16[4,96,256]{2,1,0:T(8,128)(2,1)S(1)}, bf16[4,96,256]{2,1,0:T(8,128)(2,1)S(1)}, u32[]{:S(2)}, u32[]{:S(2)}) collective-permute-start(bf16[4,96,256]{2,1,0:T(8,128)(2,1)S(1)} %pad_maximum_fusion.refs_0_), channel_id=1, source_target_pairs={{0,4},{4,0},{8,12},{12,8},{16,20},{20,16},{24,28},{28,24},{1,5},{5... | collective-permute-start | bytes 589832 | tf_op jit(solution)/shard_map/ppermute | solution.py:148
  16.6 0.7 %collective-permute-done.8.refs_6_ = bf16[4,96,256]{2,1,0:T(8,128)(2,1)S(1)} collective-permute-done((bf16[4,96,256]{2,1,0:T(8,128)(2,1)S(1)}, bf16[4,96,256]{2,1,0:T(8,128)(2,1)S(1)}, u32[]{:S(2)}, u32[]{:S(2)}) %collective-permute-start.8) | collective-permute-done | bytes 196640 | tf_op jit(solution)/shard_map/ppermute | solution.py:148
  17.3 4.2 %collective-permute-start.9 = (bf16[4,96,256]{2,1,0:T(8,128)(2,1)S(1)}, bf16[4,96,256]{2,1,0:T(8,128)(2,1)S(1)}, u32[]{:S(2)}, u32[]{:S(2)}) collective-permute-start(bf16[4,96,256]{2,1,0:T(8,128)(2,1)S(1)} %collective-permute-done.8.refs_6_), channel_id=1, source_target_pairs={{0,4},{4,0},{8,12},{12,8},{16,20},{20,16},{24,28},{28,24},{1,5},{5... | collective-permute-start | bytes 589832 | tf_op jit(solution)/shard_map/ppermute | solution.py:148
  21.5 1.4 %collective-permute-done.6.refs_4_ = bf16[4,96,256]{2,1,0:T(8,128)(2,1)S(1)} collective-permute-done((bf16[4,96,256]{2,1,0:T(8,128)(2,1)S(1)}, bf16[4,96,256]{2,1,0:T(8,128)(2,1)S(1)}, u32[]{:S(2)}, u32[]{:S(2)}) %collective-permute-start.6) | collective-permute-done | bytes 196640 | tf_op jit(solution)/shard_map/ppermute | solution.py:148
  22.9 1.0 %collective-permute-start.7 = (bf16[4,96,256]{2,1,0:T(8,128)(2,1)S(1)}, bf16[4,96,256]{2,1,0:T(8,128)(2,1)S(1)}, u32[]{:S(2)}, u32[]{:S(2)}) collective-permute-start(bf16[4,96,256]{2,1,0:T(8,128)(2,1)S(1)} %collective-permute-done.6.refs_4_), channel_id=1, source_target_pairs={{0,4},{4,0},{8,12},{12,8},{16,20},{20,16},{24,28},{28,24},{1,5},{5... | collective-permute-start | bytes 589832 | tf_op jit(solution)/shard_map/ppermute | solution.py:148
  24.0 0.0 collective-permute-done.4.refs_2_
  24.0 0.1 collective-permute-start.5
  24.1 0.0 copy-done
  24.1 0.1 constant_dynamic-slice_fusion
  24.1 0.1 copy.6
  24.2 0.1 reshape.13
  24.3 0.1 pad_add_fusion.where_ref
  24.4 0.0 collective-permute-done.3.refs_1_
  24.4 0.0 collective-permute-done.9.refs_7_
  24.4 0.6 %collective-permute-done.7.refs_5_ = bf16[4,96,256]{2,1,0:T(8,128)(2,1)S(1)} collective-permute-done((bf16[4,96,256]{2,1,0:T(8,128)(2,1)S(1)}, bf16[4,96,256]{2,1,0:T(8,128)(2,1)S(1)}, u32[]{:S(2)}, u32[]{:S(2)}) %collective-permute-start.7) | collective-permute-done | bytes 196640 | tf_op jit(solution)/shard_map/ppermute | solution.py:148
  25.0 0.4 %collective-permute-done.5.refs_3_ = bf16[4,96,256]{2,1,0:T(8,128)(2,1)S(1)} collective-permute-done((bf16[4,96,256]{2,1,0:T(8,128)(2,1)S(1)}, bf16[4,96,256]{2,1,0:T(8,128)(2,1)S(1)}, u32[]{:S(2)}, u32[]{:S(2)}) %collective-permute-start.5) | collective-permute-done | bytes 196640 | tf_op jit(solution)/shard_map/ppermute | solution.py:148
  25.4 0.0 copy-start.1
  25.4 0.7 %copy-done.1 = f32[8,2,128]{2,1,0:T(2,128)S(1)} copy-done((f32[8,2,128]{2,1,0:T(2,128)S(1)}, f32[8,2,128]{2,1,0:T(2,128)}, u32[]{:S(2)}) %copy-start.1) | copy-done | bytes 8216
  26.1 0.0 copy-start.2
  26.1 0.7 %copy-done.2 = f32[4,2,128]{2,1,0:T(2,128)S(1)} copy-done((f32[4,2,128]{2,1,0:T(2,128)S(1)}, f32[4,2,128]{2,1,0:T(2,128)}, u32[]{:S(2)}) %copy-start.2) | copy-done | bytes 4120
  26.8 7.3 %correlate.1 = f32[2,4,8,128,128]{4,3,2,1,0:T(8,128)} custom-call(s32[5]{0:T(128)S(1)} %pad_add_fusion.where_ref, bf16[4,96,256]{2,1,0:T(8,128)(2,1)S(1)} %pad_maximum_fusion.refs_0_, bf16[4,96,256]{2,1,0:T(8,128)(2,1)S(1)} %collective-permute-done.3.refs_1_, bf16[4,96,256]{2,1,0:T(8,128)(2,1)S(1)} %collective-permute-done.4.refs_2_, ...), custom_call_target="tpu_custom_call" | custom-call | tf_op jit(solution)/shard_map/correlate/pallas_call | solution.py:122
Async XLA Ops:
  0.0 24.1 %copy-start = (s32[8,2]{0,1:T(2,128)S(1)}, s32[8,2]{0,1:T(2,128)}, u32[]{:S(2)}) copy-start(s32[8,2]{0,1:T(2,128)} %param.7) | copy-start | bytes 196
  1.9 5.9 %collective-permute-start.2 = (bf16[96,256]{1,0:T(8,128)(2,1)}, bf16[96,256]{1,0:T(8,128)(2,1)S(1)}, u32[]{:S(2)}, u32[]{:S(2)}) collective-permute-start(bf16[96,256]{1,0:T(8,128)(2,1)} %whiten.1), channel_id=1, source_target_pairs={{0,3},{1,2},{2,1},{3,0},{4,7},{5,6},{6,5},{7,4},{8,11},{9,10},{10,... | collective-permute-start | bytes 147464 | tf_op jit(solution)/shard_map/ppermute | solution.py:148
  6.1 4.6 %collective-permute-start.1 = (bf16[96,256]{1,0:T(8,128)(2,1)}, bf16[96,256]{1,0:T(8,128)(2,1)S(1)}, u32[]{:S(2)}, u32[]{:S(2)}) collective-permute-start(bf16[96,256]{1,0:T(8,128)(2,1)} %whiten.1), channel_id=1, source_target_pairs={{0,2},{1,3},{2,0},{3,1},{4,6},{5,7},{6,4},{7,5},{8,10},{9,11},{10,... | collective-permute-start | bytes 147464 | tf_op jit(solution)/shard_map/ppermute | solution.py:148
  6.1 4.6 %collective-permute-start = (bf16[96,256]{1,0:T(8,128)(2,1)}, bf16[96,256]{1,0:T(8,128)(2,1)S(1)}, u32[]{:S(2)}, u32[]{:S(2)}) collective-permute-start(bf16[96,256]{1,0:T(8,128)(2,1)} %whiten.1), channel_id=1, source_target_pairs={{0,1},{1,0},{2,3},{3,2},{4,5},{5,4},{6,7},{7,6},{8,9},{9,8},{10,11... | collective-permute-start | bytes 147464 | tf_op jit(solution)/shard_map/ppermute | solution.py:148
  11.5 5.8 %collective-permute-start.8 = (bf16[4,96,256]{2,1,0:T(8,128)(2,1)S(1)}, bf16[4,96,256]{2,1,0:T(8,128)(2,1)S(1)}, u32[]{:S(2)}, u32[]{:S(2)}) collective-permute-start(bf16[4,96,256]{2,1,0:T(8,128)(2,1)S(1)} %pad_maximum_fusion.refs_0_), channel_id=1, source_target_pairs={{0,24},{4,28},{8,16},{12,20},{16,8},{20,12},{24,0},{28,4},{1,25},{... | collective-permute-start | bytes 589832 | tf_op jit(solution)/shard_map/ppermute | solution.py:148
  13.7 9.2 %collective-permute-start.6 = (bf16[4,96,256]{2,1,0:T(8,128)(2,1)S(1)}, bf16[4,96,256]{2,1,0:T(8,128)(2,1)S(1)}, u32[]{:S(2)}, u32[]{:S(2)}) collective-permute-start(bf16[4,96,256]{2,1,0:T(8,128)(2,1)S(1)} %pad_maximum_fusion.refs_0_), channel_id=1, source_target_pairs={{0,16},{4,20},{8,24},{12,28},{16,0},{20,4},{24,8},{28,12},{1,17},{... | collective-permute-start | bytes 589832 | tf_op jit(solution)/shard_map/ppermute | solution.py:148
  13.9 10.0 %collective-permute-start.4 = (bf16[4,96,256]{2,1,0:T(8,128)(2,1)S(1)}, bf16[4,96,256]{2,1,0:T(8,128)(2,1)S(1)}, u32[]{:S(2)}, u32[]{:S(2)}) collective-permute-start(bf16[4,96,256]{2,1,0:T(8,128)(2,1)S(1)} %pad_maximum_fusion.refs_0_), channel_id=1, source_target_pairs={{0,8},{4,12},{8,0},{12,4},{16,24},{20,28},{24,16},{28,20},{1,9},{5... | collective-permute-start | bytes 589832 | tf_op jit(solution)/shard_map/ppermute | solution.py:148
  14.2 10.2 %collective-permute-start.3 = (bf16[4,96,256]{2,1,0:T(8,128)(2,1)S(1)}, bf16[4,96,256]{2,1,0:T(8,128)(2,1)S(1)}, u32[]{:S(2)}, u32[]{:S(2)}) collective-permute-start(bf16[4,96,256]{2,1,0:T(8,128)(2,1)S(1)} %pad_maximum_fusion.refs_0_), channel_id=1, source_target_pairs={{0,4},{4,0},{8,12},{12,8},{16,20},{20,16},{24,28},{28,24},{1,5},{5... | collective-permute-start | bytes 589832 | tf_op jit(solution)/shard_map/ppermute | solution.py:148
  17.3 7.1 %collective-permute-start.9 = (bf16[4,96,256]{2,1,0:T(8,128)(2,1)S(1)}, bf16[4,96,256]{2,1,0:T(8,128)(2,1)S(1)}, u32[]{:S(2)}, u32[]{:S(2)}) collective-permute-start(bf16[4,96,256]{2,1,0:T(8,128)(2,1)S(1)} %collective-permute-done.8.refs_6_), channel_id=1, source_target_pairs={{0,4},{4,0},{8,12},{12,8},{16,20},{20,16},{24,28},{28,24},{1,5},{5... | collective-permute-start | bytes 589832 | tf_op jit(solution)/shard_map/ppermute | solution.py:148
  22.9 2.1 %collective-permute-start.7 = (bf16[4,96,256]{2,1,0:T(8,128)(2,1)S(1)}, bf16[4,96,256]{2,1,0:T(8,128)(2,1)S(1)}, u32[]{:S(2)}, u32[]{:S(2)}) collective-permute-start(bf16[4,96,256]{2,1,0:T(8,128)(2,1)S(1)} %collective-permute-done.6.refs_4_), channel_id=1, source_target_pairs={{0,4},{4,0},{8,12},{12,8},{16,20},{20,16},{24,28},{28,24},{1,5},{5... | collective-permute-start | bytes 589832 | tf_op jit(solution)/shard_map/ppermute | solution.py:148
  24.0 1.4 %collective-permute-start.5 = (bf16[4,96,256]{2,1,0:T(8,128)(2,1)S(1)}, bf16[4,96,256]{2,1,0:T(8,128)(2,1)S(1)}, u32[]{:S(2)}, u32[]{:S(2)}) collective-permute-start(bf16[4,96,256]{2,1,0:T(8,128)(2,1)S(1)} %collective-permute-done.4.refs_2_), channel_id=1, source_target_pairs={{0,4},{4,0},{8,12},{12,8},{16,20},{20,16},{24,28},{28,24},{1,5},{5... | collective-permute-start | bytes 589832 | tf_op jit(solution)/shard_map/ppermute | solution.py:148
  25.4 0.7 %copy-start.1 = (f32[8,2,128]{2,1,0:T(2,128)S(1)}, f32[8,2,128]{2,1,0:T(2,128)}, u32[]{:S(2)}) copy-start(f32[8,2,128]{2,1,0:T(2,128)} %constant.20.clone.refs_9_) | copy-start | bytes 24580
  26.1 0.7 %copy-start.2 = (f32[4,2,128]{2,1,0:T(2,128)S(1)}, f32[4,2,128]{2,1,0:T(2,128)}, u32[]{:S(2)}) copy-start(f32[4,2,128]{2,1,0:T(2,128)} %constant.19.clone.refs_8_) | copy-start | bytes 12292

commit v3 on v1

v3 whole, which is shorter than its diff:
```python
import math

import jax
import jax.numpy as jnp
from jax import lax
from jax.experimental import pallas as pl
from jax.experimental.pallas import tpu as pltpu
from jax.sharding import PartitionSpec as P

F = 64
LAGS = 32
TILE = 128
EPSILON = 1e-06
CORES = 2
COARSE = (-12, -4, 4, 12)
FINE = (-4, -3, -2, -1, 0, 1, 2, 3)
SEGMENT = 32


def whiten_kernel(spectra_ref, bad_ref, out_ref):
    bins, hours, _, chans = spectra_ref.shape
    rows = bins * hours * 2
    values = spectra_ref[...].reshape(rows, chans).astype(jnp.float32)
    row = lax.broadcasted_iota(jnp.int32, (rows, chans), 0)
    hour = (row // 2) % hours
    squares = values * values
    keep = (1 - bad_ref[...]).astype(jnp.float32)
    scale = jnp.zeros((rows, chans), jnp.float32)
    for h in range(hours):
        power = jnp.sum(jnp.where(hour == h, squares, 0.0), axis=0, keepdims=True) * (1.0 / (2 * bins))
        scale = jnp.where(hour == h, lax.rsqrt(power + EPSILON) * keep, scale)
    white = (values * scale).astype(jnp.bfloat16)
    src = lax.broadcasted_iota(jnp.int32, (rows, rows), 0)
    dst = lax.broadcasted_iota(jnp.int32, (rows, rows), 1)
    move = jnp.where((src % 2) * (rows // 2) + src // 2 == dst, 1.0, 0.0).astype(jnp.bfloat16)
    turned = lax.dot_general(
        white, move, (((0,), (0,)), ((), ())), preferred_element_type=jnp.float32
    ).astype(jnp.bfloat16)
    for copy in range(out_ref.shape[0]):
        out_ref[copy] = turned


def whiten(spectra, bad_channels, copies):
    bins, hours, _, chans = spectra.shape
    return pl.pallas_call(
        whiten_kernel,
        out_shape=jax.ShapeDtypeStruct((copies, chans, bins * hours * 2), jnp.bfloat16),
        name="whiten",
    )(spectra, bad_channels.reshape(1, chans))


def turn_by(re, im, cos, sin, both):
    rc, rs, ic, is_ = re * cos, re * sin, im * cos, im * sin
    forward = (rc - is_, rs + ic)
    return (forward, (rc + is_, ic - rs)) if both else (forward,)


def correlate_kernel(norm, where_ref, own_ref, sib_ref, out_ref, left_turned, right_turned, staging, sem):
    tiles = staging.shape[0]
    _, groups, rows, lanes = own_ref.shape
    half = lanes // 2
    hours_dev = half // F
    core = where_ref[0]
    bin_number = lax.broadcasted_iota(jnp.int32, (8, half), 1) // hours_dev + 1
    step = lax.broadcasted_iota(jnp.int32, (8, half), 0)
    step = jnp.where(step == 6, 12, step)
    turn = (step * bin_number) % (2 * F)
    angle = jnp.where(turn >= F, turn - 2 * F, turn).astype(jnp.float32) * (math.pi / F)
    cos, sin = jnp.cos(angle), jnp.sin(angle)
    table = {k: (cos[i:i + 1], sin[i:i + 1]) for k, i in ((1, 1), (2, 2), (3, 3), (4, 4), (12, 6))}

    def load(block, g):
        parts = []
        for i in range(TILE // SEGMENT):
            first = block * TILE + i * SEGMENT
            chan = first // rows
            place = pl.multiple_of(first % rows, SEGMENT)
            own = own_ref[chan // CORES, g, pl.ds(place, SEGMENT), :]
            sib = sib_ref[chan // CORES, g, pl.ds(place, SEGMENT), :]
            parts.append(jnp.where(chan % CORES == core, own, sib))
        whole = jnp.concatenate(parts, axis=0).astype(jnp.float32)
        return whole[:, :half], whole[:, half:]

    def store(ref, slot, index, g, value):
        rows_at = pl.ds(index * TILE, TILE)
        ref[slot, rows_at, g * lanes:g * lanes + half] = value[0].astype(jnp.bfloat16)
        ref[slot, rows_at, g * lanes + half:(g + 1) * lanes] = value[1].astype(jnp.bfloat16)

    copies = []
    pair = 2
    for t in range(tiles):
        slot = t % left_turned.shape[0]
        for g in range(groups):
            re, im = load(where_ref[1 + 2 * t], g)
            re, im = re * norm, im * norm
            for k in (4, 12):
                forward, backward = turn_by(re, im, *table[k], True)
                store(left_turned, slot, COARSE.index(k), g, forward)
                store(left_turned, slot, COARSE.index(-k), g, backward)
            re, im = load(where_ref[2 + 2 * t], g)
            store(right_turned, slot, FINE.index(0), g, (re, im))
            for k in (1, 2, 3):
                forward, backward = turn_by(re, im, *table[k], True)
                store(right_turned, slot, FINE.index(-k), g, forward)
                store(right_turned, slot, FINE.index(k), g, backward)
            store(right_turned, slot, FINE.index(-4), g, turn_by(re, im, *table[4], False)[0])
        for j in range(len(FINE) // pair):
            total = lax.dot_general(
                left_turned[slot],
                right_turned[slot, j * pair * TILE:(j + 1) * pair * TILE, :],
                (((1,), (1,)), ((), ())),
                preferred_element_type=jnp.float32,
            )
            for u in range(len(COARSE)):
                for s in range(pair):
                    staging[t, u, j * pair + s] = total[u * TILE:(u + 1) * TILE, s * TILE:(s + 1) * TILE]
            fine = pl.ds(j * pair, pair)
            copy = pltpu.make_async_copy(staging.at[t, :, fine], out_ref.at[t, :, fine], sem)
            copy.start()
            copies.append(copy)
    for copy in copies:
        copy.wait()


def correlate(own, sib, where, tiles, hours):
    _, groups, _, lanes = own.shape
    shape = (tiles, len(COARSE), len(FINE), TILE, TILE)
    norm = 1.0 / math.sqrt(F * hours)
    slots = min(tiles, 2)
    vmem = pl.BlockSpec(memory_space=pltpu.VMEM)
    out = pl.pallas_call(
        lambda *refs: correlate_kernel(norm, *refs),
        out_shape=jax.ShapeDtypeStruct(shape, jnp.float32),
        in_specs=[pl.BlockSpec(memory_space=pltpu.SMEM), vmem, vmem],
        out_specs=pl.BlockSpec(memory_space=pl.ANY),
        scratch_shapes=[
            pltpu.VMEM((slots, len(COARSE) * TILE, groups * lanes), jnp.bfloat16),
            pltpu.VMEM((slots, len(FINE) * TILE, groups * lanes), jnp.bfloat16),
            pltpu.VMEM(shape, jnp.float32),
            pltpu.SemaphoreType.DMA,
        ],
        compiler_params=pltpu.CompilerParams(vmem_limit_bytes=44 * 1024 * 1024),
        name="correlate",
    )(where, own, sib)
    return out.reshape(tiles, LAGS, TILE, TILE)


def gather(white):
    stack = lax.all_to_all(white, "tm", split_axis=0, concat_axis=0)
    chips = lax.axis_size("chan") // CORES
    same_core = [[chip * CORES + core for chip in range(chips)] for core in range(CORES)]
    own = lax.all_to_all(
        jnp.broadcast_to(stack[None], (chips, *stack.shape)),
        "chan", split_axis=0, concat_axis=0, axis_index_groups=same_core,
    )
    sib = lax.ppermute(own, "chan", [(i, i ^ 1) for i in range(chips * CORES)])
    return own, sib


def per_device(spectra, bad_channels, tile_list):
    groups = lax.axis_size("tm")
    hours = spectra.shape[1] * groups
    tiles = tile_list.shape[0] // groups
    white = whiten(spectra, bad_channels, groups)
    own, sib = gather(white)
    pairs = lax.dynamic_slice_in_dim(tile_list, lax.axis_index("tm") * tiles, tiles, axis=0)
    core = lax.axis_index("chan") % CORES
    where = jnp.concatenate([core.reshape(1), pairs.reshape(-1)]).astype(jnp.int32)
    return correlate(own, sib, where, tiles, hours)


def solution(mesh):
    placed = (P(None, "tm", None, "chan"), P("chan"), P("chan", None))
    return jax.shard_map(
        per_device,
        mesh=mesh,
        in_specs=placed,
        out_specs=P(("chan", "tm"), None, None, None),
        check_vma=False,
    )
```

time: 84.6 us -> 36.5 us (0.43)
  waiting for transfers between devices: 59.1 us -> 1.58 us
  blocking collectives: 0 us -> 22.4 us
  between operations: 13.4 us -> 0.01 us
  starting transfers between devices: 0.01 us -> 4.28 us
  local copies, waits for them, and re-layouts: 2.96 us -> 0.32 us
  Pallas kernels: 8.72 us -> 7.22 us
    all_gather x1 -> x0, waiting for transfers between devices: 59.1 us -> none  [per_device(): gathered = lax.all_gather(white, ('tm', 'chan'), axis=0, tiled=True)]
    all_to_all x0 -> x2, blocking collectives: none -> 22.4 us  [the longest x1 11.2 us: gather(): lax.all_to_all(jnp.broadcast_to(stack[None], (chips, *stack.shape)), 'cha...]
    ppermute x0 -> x1, starting transfers between devices: none -> 4.28 us  [gather(): sib = lax.ppermute(own, 'chan', [(i, i ^ 1) for i in range(chips * CORES)])]
    unnamed x9 -> x2, local copies, waits for them, and re-layouts: 2.89 us -> 0.01 us
    ppermute x0 -> x1, waiting for transfers between devices: none -> 1.58 us  [gather(): sib = lax.ppermute(own, 'chan', [(i, i ^ 1) for i in range(chips * CORES)])]
    pallas_call x2, Pallas kernels: 8.72 us -> 7.22 us  [the longest x1 5.27 us: correlate(): pl.pallas_call(lambda *refs: correlate_kernel(norm, *refs), out_shape=jax...]
  transfers between devices with their start and end apart: 1 -> 1, of which waited for: 1 -> 1; matrix products, arithmetic and copies ran while one was open for 0% -> 1% of each run, Pallas kernels for 0% -> 0%
where the time goes in v3:
time: 36.5 us; the launch traced here: 35.9 us
  blocking collectives  22.4 us (61%)
  Pallas kernels  7.22 us (20%)
  starting transfers between devices  4.28 us (12%)
  waiting for transfers between devices  1.58 us (4%)
    all_to_all x1, blocking collectives, gather(): lax.all_to_all(jnp.broadcast_to(stack[None], (chips, *stack.shape)), 'cha...  11.2 us
    all_to_all x1, blocking collectives, gather(): stack = lax.all_to_all(white, 'tm', split_axis=0, concat_axis=0)  11.1 us
    pallas_call x1, Pallas kernels, correlate(): pl.pallas_call(lambda *refs: correlate_kernel(norm, *refs), out_shape=jax...  5.27 us
    ppermute x1, starting transfers between devices, gather(): sib = lax.ppermute(own, 'chan', [(i, i ^ 1) for i in range(chips * CORES)])  4.28 us
    pallas_call x1, Pallas kernels, whiten(): pl.pallas_call(whiten_kernel, out_shape=jax.ShapeDtypeStruct((copies, cha...  1.96 us
    ppermute x1, waiting for transfers between devices, gather(): sib = lax.ppermute(own, 'chan', [(i, i ^ 1) for i in range(chips * CORES)])  1.58 us
  transfers between devices with their start and end apart: 1, of which 1 were waited for; matrix products, arithmetic and copies ran while one was open for 1% of the time, Pallas kernels for 0%

profile of v3, /device:TPU:1, one launch (start us, length us, event | category | flops | bytes accessed | tf_op | source)
XLA Modules:
  0.0 35.9 jit_solution(1445332240602154614)
XLA Ops:
  0.0 0.0 copy-start
  0.0 2.0 %whiten.1 = bf16[4,96,256]{2,1,0:T(8,128)(2,1)} custom-call(bf16[64,2,2,96]{3,2,1,0:T(2,128)(2,1)} %spectra_ref.1, s32[1,96]{1,0:T(1,128)} %bitcast.3), custom_call_target="tpu_custom_call" | custom-call | tf_op jit(solution)/shard_map/whiten/pallas_call | solution.py:45
  2.0 11.1 %all_to_all.10 = bf16[4,96,256]{2,1,0:T(8,128)(2,1)S(1)} all-to-all(bf16[4,96,256]{2,1,0:T(8,128)(2,1)} %whiten.1), channel_id=1, replica_groups=mesh['chan'=8,'tm'=4] {'tm'}, dimensions={0} | all-to-all | bytes 393216 | tf_op jit(solution)/shard_map/all_to_all | solution.py:149
  13.1 0.1 broadcast_in_dim.2
  13.2 11.2 %all_to_all.11.refs_1_ = bf16[4,4,96,256]{3,2,1,0:T(8,128)(2,1)S(1)} all-to-all(bf16[4,4,96,256]{3,2,1,0:T(8,128)(2,1)S(1)} %broadcast_in_dim.2), channel_id=1, replica_groups={{0,8,16,24},{4,12,20,28},{1,9,17,25},{5,13,21,29},{2,10,18,26},{6,14,22..., dimensions={0} | all-to-all | bytes 1572864 | tf_op jit(solution)/shard_map/all_to_all | solution.py:152
  24.4 4.3 %collective-permute-start = (bf16[4,4,96,256]{3,2,1,0:T(8,128)(2,1)S(1)}, bf16[4,4,96,256]{3,2,1,0:T(8,128)(2,1)S(1)}, u32[]{:S(2)}, u32[]{:S(2)}) collective-permute-start(bf16[4,4,96,256]{3,2,1,0:T(8,128)(2,1)S(1)} %all_to_all.11.refs_1_), channel_id=1, source_target_pairs={{0,4},{4,0},{8,12},{12,8},{16,20},{20,16},{24,28},{28,24},{1,5},{5... | collective-permute-start | bytes 2359304 | tf_op jit(solution)/shard_map/ppermute | solution.py:156
  28.7 0.0 copy-done
  28.7 0.1 constant_dynamic-slice_fusion
  28.8 0.1 copy.4
  28.9 0.1 reshape.14
  28.9 0.1 pad_add_fusion.refs_0_
  29.0 1.6 %collective-permute-done.refs_2_ = bf16[4,4,96,256]{3,2,1,0:T(8,128)(2,1)S(1)} collective-permute-done((bf16[4,4,96,256]{3,2,1,0:T(8,128)(2,1)S(1)}, bf16[4,4,96,256]{3,2,1,0:T(8,128)(2,1)S(1)}, u32[]{:S(2)}, u32[]{:S(2)}) %collective-permute-start) | collective-permute-done | bytes 786464 | tf_op jit(solution)/shard_map/ppermute | solution.py:156
  30.6 5.3 %correlate.1 = f32[2,4,8,128,128]{4,3,2,1,0:T(8,128)} custom-call(s32[5]{0:T(128)S(1)} %pad_add_fusion.refs_0_, bf16[4,4,96,256]{3,2,1,0:T(8,128)(2,1)S(1)} %all_to_all.11.refs_1_, bf16[4,4,96,256]{3,2,1,0:T(8,128)(2,1)S(1)} %collective-permute-done.refs_2_), custom_call_target="tpu_custom_call" | custom-call | tf_op jit(solution)/shard_map/correlate/pallas_call | solution.py:131
Async XLA Ops:
  0.0 28.7 %copy-start = (s32[8,2]{0,1:T(2,128)S(1)}, s32[8,2]{0,1:T(2,128)}, u32[]{:S(2)}) copy-start(s32[8,2]{0,1:T(2,128)} %param.5) | copy-start | bytes 196
  24.4 6.2 %collective-permute-start = (bf16[4,4,96,256]{3,2,1,0:T(8,128)(2,1)S(1)}, bf16[4,4,96,256]{3,2,1,0:T(8,128)(2,1)S(1)}, u32[]{:S(2)}, u32[]{:S(2)}) collective-permute-start(bf16[4,4,96,256]{3,2,1,0:T(8,128)(2,1)S(1)} %all_to_all.11.refs_1_), channel_id=1, source_target_pairs={{0,4},{4,0},{8,12},{12,8},{16,20},{20,16},{24,28},{28,24},{1,5},{5... | collective-permute-start | bytes 2359304 | tf_op jit(solution)/shard_map/ppermute | solution.py:156

commit v4 on v3

v4 whole, which is shorter than its diff:
```python
import math

import jax
import jax.numpy as jnp
from jax import lax
from jax.experimental import pallas as pl
from jax.experimental.pallas import tpu as pltpu
from jax.sharding import PartitionSpec as P

F = 64
LAGS = 32
TILE = 128
EPSILON = 1e-06
COARSE = (-12, -4, 4, 12)
FINE_PAIRS = ((-4, 0), (-1, 1), (-2, 2), (-3, 3))


def whiten_kernel(spectra_ref, bad_ref, out_ref):
    bins, hours, _, chans = spectra_ref.shape
    rows = bins * hours * 2
    values = spectra_ref[...].reshape(rows, chans).astype(jnp.float32)
    row = lax.broadcasted_iota(jnp.int32, (rows, chans), 0)
    hour = (row // 2) % hours
    squares = values * values
    keep = (1 - bad_ref[...]).astype(jnp.float32)
    scale = jnp.zeros((rows, chans), jnp.float32)
    for h in range(hours):
        power = jnp.sum(jnp.where(hour == h, squares, 0.0), axis=0, keepdims=True) * (1.0 / (2 * bins))
        scale = jnp.where(hour == h, lax.rsqrt(power + EPSILON) * keep, scale)
    white = (values * scale).astype(jnp.bfloat16)
    src = lax.broadcasted_iota(jnp.int32, (rows, rows), 0)
    dst = lax.broadcasted_iota(jnp.int32, (rows, rows), 1)
    move = jnp.where((src % 2) * (rows // 2) + src // 2 == dst, 1.0, 0.0).astype(jnp.bfloat16)
    out_ref[...] = lax.dot_general(
        white, move, (((0,), (0,)), ((), ())), preferred_element_type=jnp.float32
    ).astype(jnp.bfloat16)


def whiten(spectra, bad_channels):
    bins, hours, _, chans = spectra.shape
    return pl.pallas_call(
        whiten_kernel,
        out_shape=jax.ShapeDtypeStruct((chans, bins * hours * 2), jnp.bfloat16),
        name="whiten",
    )(spectra, bad_channels.reshape(1, chans))


def turn_by(re, im, cos, sin, both):
    rc, rs, ic, is_ = re * cos, re * sin, im * cos, im * sin
    forward = (rc - is_, rs + ic)
    return (forward, (rc + is_, ic - rs)) if both else (forward,)


def correlate_kernel(norm, where_ref, *refs):
    pieces = refs[:-6]
    out_ref, spectra, left_turned, right_turned, staging, sem = refs[-6:]
    tiles = staging.shape[0]
    groups, _, lanes = spectra.shape
    half = lanes // 2
    hours_dev = half // F
    bin_number = lax.broadcasted_iota(jnp.int32, (8, half), 1) // hours_dev + 1
    step = lax.broadcasted_iota(jnp.int32, (8, half), 0)
    step = jnp.where(step == 6, 12, step)
    turn = (step * bin_number) % (2 * F)
    angle = jnp.where(turn >= F, turn - 2 * F, turn).astype(jnp.float32) * (math.pi / F)
    cos, sin = jnp.cos(angle), jnp.sin(angle)
    table = {k: (cos[i:i + 1], sin[i:i + 1]) for k, i in ((1, 1), (2, 2), (3, 3), (4, 4), (12, 6))}

    chans = spectra.shape[1] // pieces[0].shape[1]
    first = 0
    for start in range(0, len(pieces), chans):
        depth, rows, _ = pieces[start].shape
        for k in range(chans):
            place = pl.multiple_of((where_ref[0] ^ k) * rows, 32)
            spectra[first:first + depth, pl.ds(place, rows), :] = pieces[start + k][...]
        first += depth

    def load(block, g):
        whole = spectra[g, pl.ds(pl.multiple_of(block * TILE, TILE), TILE), :].astype(jnp.float32)
        return whole[:, :half], whole[:, half:]

    def store(ref, slot, index, g, value):
        rows_at = pl.ds(index * TILE, TILE)
        ref[slot, rows_at, g * lanes:g * lanes + half] = value[0].astype(jnp.bfloat16)
        ref[slot, rows_at, g * lanes + half:(g + 1) * lanes] = value[1].astype(jnp.bfloat16)

    copies = []
    for t in range(tiles):
        slot = t % left_turned.shape[0]
        for g in range(groups):
            re, im = load(where_ref[1 + 2 * t], g)
            re, im = re * norm, im * norm
            for k in (4, 12):
                forward, backward = turn_by(re, im, *table[k], True)
                store(left_turned, slot, COARSE.index(k), g, forward)
                store(left_turned, slot, COARSE.index(-k), g, backward)
        for j in range(len(FINE_PAIRS)):
            for g in range(groups):
                re, im = load(where_ref[2 + 2 * t], g)
                if j == 0:
                    store(right_turned, slot, 0, g, turn_by(re, im, *table[4], False)[0])
                    store(right_turned, slot, 1, g, (re, im))
                else:
                    forward, backward = turn_by(re, im, *table[j], True)
                    store(right_turned, slot, 2 * j, g, forward)
                    store(right_turned, slot, 2 * j + 1, g, backward)
            total = lax.dot_general(
                left_turned[slot],
                right_turned[slot, 2 * j * TILE:2 * (j + 1) * TILE, :],
                (((1,), (1,)), ((), ())),
                preferred_element_type=jnp.float32,
            )
            for u in range(len(COARSE)):
                for s in range(2):
                    staging[t, u, 2 * j + s] = total[u * TILE:(u + 1) * TILE, s * TILE:(s + 1) * TILE]
            for s in range(2):
                fine = FINE_PAIRS[j][s] + 4
                copy = pltpu.make_async_copy(staging.at[t, :, 2 * j + s], out_ref.at[t, :, fine], sem)
                copy.start()
                copies.append(copy)
    for copy in copies:
        copy.wait()


def correlate(pieces, where, tiles, hours):
    groups = lax.axis_size("tm")
    _, rows, lanes = pieces[0].shape
    fine = 2 * len(FINE_PAIRS)
    shape = (tiles, len(COARSE), fine, TILE, TILE)
    norm = 1.0 / math.sqrt(F * hours)
    slots = min(tiles, 2)
    vmem = pl.BlockSpec(memory_space=pltpu.VMEM)
    out = pl.pallas_call(
        lambda *refs: correlate_kernel(norm, *refs),
        out_shape=jax.ShapeDtypeStruct(shape, jnp.float32),
        in_specs=[pl.BlockSpec(memory_space=pltpu.SMEM)] + [vmem] * len(pieces),
        out_specs=pl.BlockSpec(memory_space=pl.ANY),
        scratch_shapes=[
            pltpu.VMEM((groups, lax.axis_size("chan") * rows, lanes), jnp.bfloat16),
            pltpu.VMEM((slots, len(COARSE) * TILE, groups * lanes), jnp.bfloat16),
            pltpu.VMEM((slots, fine * TILE, groups * lanes), jnp.bfloat16),
            pltpu.VMEM(shape, jnp.float32),
            pltpu.SemaphoreType.DMA,
        ],
        compiler_params=pltpu.CompilerParams(vmem_limit_bytes=40 * 1024 * 1024),
        name="correlate",
    )(where, *pieces)
    return out.reshape(tiles, LAGS, TILE, TILE)


def swap(array, axis, k):
    return lax.ppermute(array, axis, [(i, i ^ k) for i in range(lax.axis_size(axis))])


def between_chips(half):
    pieces = {0: half}
    for k in range(2, lax.axis_size("chan"), 2):
        pieces[k] = swap(half, "chan", k)
    for k in list(pieces):
        pieces[k + 1] = swap(pieces[k], "chan", 1)
    return [pieces[k] for k in sorted(pieces)]


def gather(white):
    near = [white] + [swap(white, "tm", k) for k in (1,)]
    far = [swap(white, "tm", k) for k in range(2, lax.axis_size("tm"))]
    return between_chips(jnp.stack(near)) + between_chips(jnp.stack(far))


def per_device(spectra, bad_channels, tile_list):
    groups = lax.axis_size("tm")
    hours = spectra.shape[1] * groups
    tiles = tile_list.shape[0] // groups
    white = whiten(spectra, bad_channels)
    pieces = gather(white)
    pairs = lax.dynamic_slice_in_dim(tile_list, lax.axis_index("tm") * tiles, tiles, axis=0)
    where = jnp.concatenate([lax.axis_index("chan").reshape(1), pairs.reshape(-1)]).astype(jnp.int32)
    return correlate(pieces, where, tiles, hours)


def solution(mesh):
    placed = (P(None, "tm", None, "chan"), P("chan"), P("chan", None))
    return jax.shard_map(
        per_device,
        mesh=mesh,
        in_specs=placed,
        out_specs=P(("chan", "tm"), None, None, None),
        check_vma=False,
    )
```

time: 36.5 us -> 28.1 us (0.77)
  blocking collectives: 22.4 us -> 0 us
  starting transfers between devices: 4.28 us -> 18.4 us
  other arithmetic: 0.08 us -> 0.92 us
    all_to_all x2 -> x0, blocking collectives: 22.4 us -> none  [the longest x1 11.2 us: gather(): lax.all_to_all(jnp.broadcast_to(stack[None], (chips, *stack.shape)), 'cha...]
    ppermute x1 -> x17, starting transfers between devices: 4.28 us -> 18.4 us  [swap(): lax.ppermute(array, axis, [(i, i ^ k) for i in range(lax.axis_size(axis))])]
    another operation x0 -> x2, other arithmetic: none -> 0.85 us  [gather(): return between_chips(jnp.stack(near)) + between_chips(jnp.stack(far))]
    ppermute x1 -> x17, waiting for transfers between devices: 1.58 us -> 1.28 us  [swap(): lax.ppermute(array, axis, [(i, i ^ k) for i in range(lax.axis_size(axis))])]
  transfers between devices with their start and end apart: 1 -> 17, of which waited for: 1 -> 5; matrix products, arithmetic and copies ran while one was open for 1% -> 4% of each run, Pallas kernels for 0% -> 0%
where the time goes in v4:
time: 28.1 us; the launch traced here: 27.8 us
  starting transfers between devices  18.4 us (65%)
  Pallas kernels  6.87 us (24%)
  waiting for transfers between devices  1.28 us (5%)
  other arithmetic  0.92 us (3%)
    ppermute x17, starting transfers between devices, swap(): lax.ppermute(array, axis, [(i, i ^ k) for i in range(lax.axis_size(axis))])  18.4 us
    pallas_call x1, Pallas kernels, correlate(): pl.pallas_call(lambda *refs: correlate_kernel(norm, *refs), out_shape=jax...  4.97 us
    pallas_call x1, Pallas kernels, whiten(): pl.pallas_call(whiten_kernel, out_shape=jax.ShapeDtypeStruct((chans, bins...  1.9 us
    ppermute x17, waiting for transfers between devices, swap(): lax.ppermute(array, axis, [(i, i ^ k) for i in range(lax.axis_size(axis))])  1.28 us
    another operation x2, other arithmetic, gather(): return between_chips(jnp.stack(near)) + between_chips(jnp.stack(far))  0.85 us
  transfers between devices with their start and end apart: 17, of which 5 were waited for; matrix products, arithmetic and copies ran while one was open for 4% of the time, Pallas kernels for 0%

profile of v4, /device:TPU:1, one launch (start us, length us, event | category | flops | bytes accessed | tf_op | source)
XLA Modules:
  0.0 27.8 jit_solution(14339247137836536048)
XLA Ops:
  0.0 0.0 copy-start
  0.0 1.9 %whiten.1 = bf16[96,256]{1,0:T(8,128)(2,1)} custom-call(bf16[64,2,2,96]{3,2,1,0:T(2,128)(2,1)} %spectra_ref.1, s32[1,96]{1,0:T(1,128)} %bitcast.11), custom_call_target="tpu_custom_call" | custom-call | tf_op jit(solution)/shard_map/whiten/pallas_call | solution.py:41
  1.9 2.1 %collective-permute-start = (bf16[96,256]{1,0:T(8,128)(2,1)}, bf16[96,256]{1,0:T(8,128)(2,1)S(1)}, u32[]{:S(2)}, u32[]{:S(2)}) collective-permute-start(bf16[96,256]{1,0:T(8,128)(2,1)} %whiten.1), channel_id=1, source_target_pairs={{0,1},{1,0},{2,3},{3,2},{4,5},{5,4},{6,7},{7,6},{8,9},{9,8},{10,11... | collective-permute-start | bytes 147464 | tf_op jit(solution)/shard_map/ppermute | solution.py:152
  4.0 2.2 %collective-permute-start.9 = (bf16[96,256]{1,0:T(8,128)(2,1)}, bf16[96,256]{1,0:T(8,128)(2,1)S(1)}, u32[]{:S(2)}, u32[]{:S(2)}) collective-permute-start(bf16[96,256]{1,0:T(8,128)(2,1)} %whiten.1), channel_id=1, source_target_pairs={{0,3},{1,2},{2,1},{3,0},{4,7},{5,6},{6,5},{7,4},{8,11},{9,10},{10,... | collective-permute-start | bytes 147464 | tf_op jit(solution)/shard_map/ppermute | solution.py:152
  6.2 0.1 collective-permute-start.8
  6.3 0.0 collective-permute-done
  6.3 0.8 %pad_maximum_fusion.refs_1_ = bf16[2,96,256]{2,1,0:T(8,128)(2,1)S(1)} fusion(bf16[1,96,256]{2,1,0:T(8,128)(2,1)S(1)} %bitcast.10, bf16[1,96,256]{2,1,0:T(8,128)(2,1)} %bitcast.7), kind=kLoop, calls=%fused_computation | loop fusion | flops 49152 | bytes 196608 | tf_op jit(solution)/shard_map/stack | solution.py:167
  7.2 2.2 %collective-permute-start.6 = (bf16[2,96,256]{2,1,0:T(8,128)(2,1)S(1)}, bf16[2,96,256]{2,1,0:T(8,128)(2,1)S(1)}, u32[]{:S(2)}, u32[]{:S(2)}) collective-permute-start(bf16[2,96,256]{2,1,0:T(8,128)(2,1)S(1)} %pad_maximum_fusion.refs_1_), channel_id=1, source_target_pairs={{0,24},{4,28},{8,16},{12,20},{16,8},{20,12},{24,0},{28,4},{1,25},{... | collective-permute-start | bytes 294920 | tf_op jit(solution)/shard_map/ppermute | solution.py:152
  9.4 0.2 collective-permute-start.4
  9.6 0.3 collective-permute-start.2
  9.9 0.0 collective-permute-done.9
  9.9 2.1 %collective-permute-start.1 = (bf16[2,96,256]{2,1,0:T(8,128)(2,1)S(1)}, bf16[2,96,256]{2,1,0:T(8,128)(2,1)S(1)}, u32[]{:S(2)}, u32[]{:S(2)}) collective-permute-start(bf16[2,96,256]{2,1,0:T(8,128)(2,1)S(1)} %pad_maximum_fusion.refs_1_), channel_id=1, source_target_pairs={{0,4},{4,0},{8,12},{12,8},{16,20},{20,16},{24,28},{28,24},{1,5},{5... | collective-permute-start | bytes 294920 | tf_op jit(solution)/shard_map/ppermute | solution.py:152
  12.0 0.0 collective-permute-done.8
  12.0 2.3 %collective-permute-start.15 = (bf16[2,96,256]{2,1,0:T(8,128)(2,1)S(1)}, bf16[2,96,256]{2,1,0:T(8,128)(2,1)S(1)}, u32[]{:S(2)}, u32[]{:S(2)}) collective-permute-start(bf16[2,96,256]{2,1,0:T(8,128)(2,1)S(1)} %pad_maximum_fusion.1.refs_9_), channel_id=1, source_target_pairs={{0,24},{4,28},{8,16},{12,20},{16,8},{20,12},{24,0},{28,4},{1,25},{... | collective-permute-start | bytes 294920 | tf_op jit(solution)/shard_map/ppermute | solution.py:152
  14.3 0.0 collective-permute-done.6.refs_7_
  14.3 0.2 collective-permute-start.13
  14.6 0.0 collective-permute-done.4.refs_5_
  14.6 0.2 collective-permute-start.11
  14.7 0.0 collective-permute-done.2.refs_3_
  14.7 2.9 %collective-permute-start.10 = (bf16[2,96,256]{2,1,0:T(8,128)(2,1)S(1)}, bf16[2,96,256]{2,1,0:T(8,128)(2,1)S(1)}, u32[]{:S(2)}, u32[]{:S(2)}) collective-permute-start(bf16[2,96,256]{2,1,0:T(8,128)(2,1)S(1)} %pad_maximum_fusion.1.refs_9_), channel_id=1, source_target_pairs={{0,4},{4,0},{8,12},{12,8},{16,20},{20,16},{24,28},{28,24},{1,5},{5... | collective-permute-start | bytes 294920 | tf_op jit(solution)/shard_map/ppermute | solution.py:152
  17.6 0.0 collective-permute-done.1.refs_2_
  17.6 0.1 collective-permute-start.7
  17.7 0.0 copy-done
  17.7 0.1 constant_dynamic-slice_fusion
  17.7 0.1 copy.4
  17.8 0.1 reshape.13
  17.9 0.0 collective-permute-done.15.refs_15_
  17.9 1.8 %collective-permute-start.5 = (bf16[2,96,256]{2,1,0:T(8,128)(2,1)S(1)}, bf16[2,96,256]{2,1,0:T(8,128)(2,1)S(1)}, u32[]{:S(2)}, u32[]{:S(2)}) collective-permute-start(bf16[2,96,256]{2,1,0:T(8,128)(2,1)S(1)} %collective-permute-done.4.refs_5_), channel_id=1, source_target_pairs={{0,4},{4,0},{8,12},{12,8},{16,20},{20,16},{24,28},{28,24},{1,5},{5... | collective-permute-start | bytes 294920 | tf_op jit(solution)/shard_map/ppermute | solution.py:152
  19.7 0.1 collective-permute-done.13.refs_13_
  19.8 1.1 %collective-permute-start.3 = (bf16[2,96,256]{2,1,0:T(8,128)(2,1)S(1)}, bf16[2,96,256]{2,1,0:T(8,128)(2,1)S(1)}, u32[]{:S(2)}, u32[]{:S(2)}) collective-permute-start(bf16[2,96,256]{2,1,0:T(8,128)(2,1)S(1)} %collective-permute-done.2.refs_3_), channel_id=1, source_target_pairs={{0,4},{4,0},{8,12},{12,8},{16,20},{20,16},{24,28},{28,24},{1,5},{5... | collective-permute-start | bytes 294920 | tf_op jit(solution)/shard_map/ppermute | solution.py:152
  21.0 0.0 collective-permute-done.11.refs_11_
  21.0 0.0 collective-permute-start.16
  21.0 0.0 collective-permute-done.10.refs_10_
  21.0 0.5 %collective-permute-start.14 = (bf16[2,96,256]{2,1,0:T(8,128)(2,1)S(1)}, bf16[2,96,256]{2,1,0:T(8,128)(2,1)S(1)}, u32[]{:S(2)}, u32[]{:S(2)}) collective-permute-start(bf16[2,96,256]{2,1,0:T(8,128)(2,1)S(1)} %collective-permute-done.13.refs_13_), channel_id=1, source_target_pairs={{0,4},{4,0},{8,12},{12,8},{16,20},{20,16},{24,28},{28,24},{1,5},{5... | collective-permute-start | bytes 294920 | tf_op jit(solution)/shard_map/ppermute | solution.py:152
  21.5 0.0 collective-permute-done.7.refs_8_
  21.5 0.1 collective-permute-start.12
  21.6 0.1 pad_add_fusion.refs_0_
  21.6 0.0 collective-permute-done.5.refs_6_
  21.6 0.3 collective-permute-done.3.refs_4_
  21.9 0.4 %collective-permute-done.16.refs_16_ = bf16[2,96,256]{2,1,0:T(8,128)(2,1)S(1)} collective-permute-done((bf16[2,96,256]{2,1,0:T(8,128)(2,1)S(1)}, bf16[2,96,256]{2,1,0:T(8,128)(2,1)S(1)}, u32[]{:S(2)}, u32[]{:S(2)}) %collective-permute-start.16) | collective-permute-done | bytes 98336 | tf_op jit(solution)/shard_map/ppermute | solution.py:152
  22.3 0.2 collective-permute-done.14.refs_14_
  22.4 0.4 %collective-permute-done.12.refs_12_ = bf16[2,96,256]{2,1,0:T(8,128)(2,1)S(1)} collective-permute-done((bf16[2,96,256]{2,1,0:T(8,128)(2,1)S(1)}, bf16[2,96,256]{2,1,0:T(8,128)(2,1)S(1)}, u32[]{:S(2)}, u32[]{:S(2)}) %collective-permute-start.12) | collective-permute-done | bytes 98336 | tf_op jit(solution)/shard_map/ppermute | solution.py:152
  22.8 5.0 %correlate.1 = f32[2,4,8,128,128]{4,3,2,1,0:T(8,128)} custom-call(s32[5]{0:T(128)S(1)} %pad_add_fusion.refs_0_, bf16[2,96,256]{2,1,0:T(8,128)(2,1)S(1)} %pad_maximum_fusion.refs_1_, bf16[2,96,256]{2,1,0:T(8,128)(2,1)S(1)} %collective-permute-done.1.refs_2_, bf16[2,96,256]{2,1,0:T(8,128)(2,1)S(1)} %collective-permute-done.2.refs_3_, ...), custom_call_target="tpu_custom_call" | custom-call | tf_op jit(solution)/shard_map/correlate/pallas_call | solution.py:133
  (1 shorter events, 0.0 us)
Async XLA Ops:
  0.0 17.7 %copy-start = (s32[8,2]{0,1:T(2,128)S(1)}, s32[8,2]{0,1:T(2,128)}, u32[]{:S(2)}) copy-start(s32[8,2]{0,1:T(2,128)} %param.5) | copy-start | bytes 196
  1.9 4.4 %collective-permute-start = (bf16[96,256]{1,0:T(8,128)(2,1)}, bf16[96,256]{1,0:T(8,128)(2,1)S(1)}, u32[]{:S(2)}, u32[]{:S(2)}) collective-permute-start(bf16[96,256]{1,0:T(8,128)(2,1)} %whiten.1), channel_id=1, source_target_pairs={{0,1},{1,0},{2,3},{3,2},{4,5},{5,4},{6,7},{7,6},{8,9},{9,8},{10,11... | collective-permute-start | bytes 147464 | tf_op jit(solution)/shard_map/ppermute | solution.py:152
  4.0 5.9 %collective-permute-start.9 = (bf16[96,256]{1,0:T(8,128)(2,1)}, bf16[96,256]{1,0:T(8,128)(2,1)S(1)}, u32[]{:S(2)}, u32[]{:S(2)}) collective-permute-start(bf16[96,256]{1,0:T(8,128)(2,1)} %whiten.1), channel_id=1, source_target_pairs={{0,3},{1,2},{2,1},{3,0},{4,7},{5,6},{6,5},{7,4},{8,11},{9,10},{10,... | collective-permute-start | bytes 147464 | tf_op jit(solution)/shard_map/ppermute | solution.py:152
  6.2 5.8 %collective-permute-start.8 = (bf16[96,256]{1,0:T(8,128)(2,1)}, bf16[96,256]{1,0:T(8,128)(2,1)S(1)}, u32[]{:S(2)}, u32[]{:S(2)}) collective-permute-start(bf16[96,256]{1,0:T(8,128)(2,1)} %whiten.1), channel_id=1, source_target_pairs={{0,2},{1,3},{2,0},{3,1},{4,6},{5,7},{6,4},{7,5},{8,10},{9,11},{10,... | collective-permute-start | bytes 147464 | tf_op jit(solution)/shard_map/ppermute | solution.py:152
  7.2 7.1 %collective-permute-start.6 = (bf16[2,96,256]{2,1,0:T(8,128)(2,1)S(1)}, bf16[2,96,256]{2,1,0:T(8,128)(2,1)S(1)}, u32[]{:S(2)}, u32[]{:S(2)}) collective-permute-start(bf16[2,96,256]{2,1,0:T(8,128)(2,1)S(1)} %pad_maximum_fusion.refs_1_), channel_id=1, source_target_pairs={{0,24},{4,28},{8,16},{12,20},{16,8},{20,12},{24,0},{28,4},{1,25},{... | collective-permute-start | bytes 294920 | tf_op jit(solution)/shard_map/ppermute | solution.py:152
  9.4 5.1 %collective-permute-start.4 = (bf16[2,96,256]{2,1,0:T(8,128)(2,1)S(1)}, bf16[2,96,256]{2,1,0:T(8,128)(2,1)S(1)}, u32[]{:S(2)}, u32[]{:S(2)}) collective-permute-start(bf16[2,96,256]{2,1,0:T(8,128)(2,1)S(1)} %pad_maximum_fusion.refs_1_), channel_id=1, source_target_pairs={{0,16},{4,20},{8,24},{12,28},{16,0},{20,4},{24,8},{28,12},{1,17},{... | collective-permute-start | bytes 294920 | tf_op jit(solution)/shard_map/ppermute | solution.py:152
  9.6 5.1 %collective-permute-start.2 = (bf16[2,96,256]{2,1,0:T(8,128)(2,1)S(1)}, bf16[2,96,256]{2,1,0:T(8,128)(2,1)S(1)}, u32[]{:S(2)}, u32[]{:S(2)}) collective-permute-start(bf16[2,96,256]{2,1,0:T(8,128)(2,1)S(1)} %pad_maximum_fusion.refs_1_), channel_id=1, source_target_pairs={{0,8},{4,12},{8,0},{12,4},{16,24},{20,28},{24,16},{28,20},{1,9},{5... | collective-permute-start | bytes 294920 | tf_op jit(solution)/shard_map/ppermute | solution.py:152
  9.9 7.7 %collective-permute-start.1 = (bf16[2,96,256]{2,1,0:T(8,128)(2,1)S(1)}, bf16[2,96,256]{2,1,0:T(8,128)(2,1)S(1)}, u32[]{:S(2)}, u32[]{:S(2)}) collective-permute-start(bf16[2,96,256]{2,1,0:T(8,128)(2,1)S(1)} %pad_maximum_fusion.refs_1_), channel_id=1, source_target_pairs={{0,4},{4,0},{8,12},{12,8},{16,20},{20,16},{24,28},{28,24},{1,5},{5... | collective-permute-start | bytes 294920 | tf_op jit(solution)/shard_map/ppermute | solution.py:152
  12.0 5.9 %collective-permute-start.15 = (bf16[2,96,256]{2,1,0:T(8,128)(2,1)S(1)}, bf16[2,96,256]{2,1,0:T(8,128)(2,1)S(1)}, u32[]{:S(2)}, u32[]{:S(2)}) collective-permute-start(bf16[2,96,256]{2,1,0:T(8,128)(2,1)S(1)} %pad_maximum_fusion.1.refs_9_), channel_id=1, source_target_pairs={{0,24},{4,28},{8,16},{12,20},{16,8},{20,12},{24,0},{28,4},{1,25},{... | collective-permute-start | bytes 294920 | tf_op jit(solution)/shard_map/ppermute | solution.py:152
  14.3 5.5 %collective-permute-start.13 = (bf16[2,96,256]{2,1,0:T(8,128)(2,1)S(1)}, bf16[2,96,256]{2,1,0:T(8,128)(2,1)S(1)}, u32[]{:S(2)}, u32[]{:S(2)}) collective-permute-start(bf16[2,96,256]{2,1,0:T(8,128)(2,1)S(1)} %pad_maximum_fusion.1.refs_9_), channel_id=1, source_target_pairs={{0,16},{4,20},{8,24},{12,28},{16,0},{20,4},{24,8},{28,12},{1,17},{... | collective-permute-start | bytes 294920 | tf_op jit(solution)/shard_map/ppermute | solution.py:152
  14.6 6.4 %collective-permute-start.11 = (bf16[2,96,256]{2,1,0:T(8,128)(2,1)S(1)}, bf16[2,96,256]{2,1,0:T(8,128)(2,1)S(1)}, u32[]{:S(2)}, u32[]{:S(2)}) collective-permute-start(bf16[2,96,256]{2,1,0:T(8,128)(2,1)S(1)} %pad_maximum_fusion.1.refs_9_), channel_id=1, source_target_pairs={{0,8},{4,12},{8,0},{12,4},{16,24},{20,28},{24,16},{28,20},{1,9},{5... | collective-permute-start | bytes 294920 | tf_op jit(solution)/shard_map/ppermute | solution.py:152
  14.7 6.3 %collective-permute-start.10 = (bf16[2,96,256]{2,1,0:T(8,128)(2,1)S(1)}, bf16[2,96,256]{2,1,0:T(8,128)(2,1)S(1)}, u32[]{:S(2)}, u32[]{:S(2)}) collective-permute-start(bf16[2,96,256]{2,1,0:T(8,128)(2,1)S(1)} %pad_maximum_fusion.1.refs_9_), channel_id=1, source_target_pairs={{0,4},{4,0},{8,12},{12,8},{16,20},{20,16},{24,28},{28,24},{1,5},{5... | collective-permute-start | bytes 294920 | tf_op jit(solution)/shard_map/ppermute | solution.py:152
  17.6 3.9 %collective-permute-start.7 = (bf16[2,96,256]{2,1,0:T(8,128)(2,1)S(1)}, bf16[2,96,256]{2,1,0:T(8,128)(2,1)S(1)}, u32[]{:S(2)}, u32[]{:S(2)}) collective-permute-start(bf16[2,96,256]{2,1,0:T(8,128)(2,1)S(1)} %collective-permute-done.6.refs_7_), channel_id=1, source_target_pairs={{0,4},{4,0},{8,12},{12,8},{16,20},{20,16},{24,28},{28,24},{1,5},{5... | collective-permute-start | bytes 294920 | tf_op jit(solution)/shard_map/ppermute | solution.py:152
  17.9 3.7 %collective-permute-start.5 = (bf16[2,96,256]{2,1,0:T(8,128)(2,1)S(1)}, bf16[2,96,256]{2,1,0:T(8,128)(2,1)S(1)}, u32[]{:S(2)}, u32[]{:S(2)}) collective-permute-start(bf16[2,96,256]{2,1,0:T(8,128)(2,1)S(1)} %collective-permute-done.4.refs_5_), channel_id=1, source_target_pairs={{0,4},{4,0},{8,12},{12,8},{16,20},{20,16},{24,28},{28,24},{1,5},{5... | collective-permute-start | bytes 294920 | tf_op jit(solution)/shard_map/ppermute | solution.py:152
  19.8 2.1 %collective-permute-start.3 = (bf16[2,96,256]{2,1,0:T(8,128)(2,1)S(1)}, bf16[2,96,256]{2,1,0:T(8,128)(2,1)S(1)}, u32[]{:S(2)}, u32[]{:S(2)}) collective-permute-start(bf16[2,96,256]{2,1,0:T(8,128)(2,1)S(1)} %collective-permute-done.2.refs_3_), channel_id=1, source_target_pairs={{0,4},{4,0},{8,12},{12,8},{16,20},{20,16},{24,28},{28,24},{1,5},{5... | collective-permute-start | bytes 294920 | tf_op jit(solution)/shard_map/ppermute | solution.py:152
  21.0 1.3 %collective-permute-start.16 = (bf16[2,96,256]{2,1,0:T(8,128)(2,1)S(1)}, bf16[2,96,256]{2,1,0:T(8,128)(2,1)S(1)}, u32[]{:S(2)}, u32[]{:S(2)}) collective-permute-start(bf16[2,96,256]{2,1,0:T(8,128)(2,1)S(1)} %collective-permute-done.15.refs_15_), channel_id=1, source_target_pairs={{0,4},{4,0},{8,12},{12,8},{16,20},{20,16},{24,28},{28,24},{1,5},{5... | collective-permute-start | bytes 294920 | tf_op jit(solution)/shard_map/ppermute | solution.py:152
  21.0 1.5 %collective-permute-start.14 = (bf16[2,96,256]{2,1,0:T(8,128)(2,1)S(1)}, bf16[2,96,256]{2,1,0:T(8,128)(2,1)S(1)}, u32[]{:S(2)}, u32[]{:S(2)}) collective-permute-start(bf16[2,96,256]{2,1,0:T(8,128)(2,1)S(1)} %collective-permute-done.13.refs_13_), channel_id=1, source_target_pairs={{0,4},{4,0},{8,12},{12,8},{16,20},{20,16},{24,28},{28,24},{1,5},{5... | collective-permute-start | bytes 294920 | tf_op jit(solution)/shard_map/ppermute | solution.py:152
  21.5 1.3 %collective-permute-start.12 = (bf16[2,96,256]{2,1,0:T(8,128)(2,1)S(1)}, bf16[2,96,256]{2,1,0:T(8,128)(2,1)S(1)}, u32[]{:S(2)}, u32[]{:S(2)}) collective-permute-start(bf16[2,96,256]{2,1,0:T(8,128)(2,1)S(1)} %collective-permute-done.11.refs_11_), channel_id=1, source_target_pairs={{0,4},{4,0},{8,12},{12,8},{16,20},{20,16},{24,28},{28,24},{1,5},{5... | collective-permute-start | bytes 294920 | tf_op jit(solution)/shard_map/ppermute | solution.py:152

commit v5 on v4

--- a/solution.py
+++ b/solution.py
@@ -11,6 +11,7 @@
 LAGS = 32
 TILE = 128
 EPSILON = 1e-06
+CORES = 2
 COARSE = (-12, -4, 4, 12)
 FINE_PAIRS = ((-4, 0), (-1, 1), (-2, 2), (-3, 3))
 
@@ -51,10 +52,8 @@
     return (forward, (rc + is_, ic - rs)) if both else (forward,)
 
 
-def correlate_kernel(norm, where_ref, *refs):
-    pieces = refs[:-6]
-    out_ref, spectra, left_turned, right_turned, staging, sem = refs[-6:]
-    tiles = staging.shape[0]
+def correlate_kernel(norm, add, tiles, where_ref, spectra, *refs):
+    out_ref, left_turned, right_turned, sem = refs[-4:]
     groups, _, lanes = spectra.shape
     half = lanes // 2
     hours_dev = half // F
@@ -66,15 +65,6 @@
     cos, sin = jnp.cos(angle), jnp.sin(angle)
     table = {k: (cos[i:i + 1], sin[i:i + 1]) for k, i in ((1, 1), (2, 2), (3, 3), (4, 4), (12, 6))}
 
-    chans = spectra.shape[1] // pieces[0].shape[1]
-    first = 0
-    for start in range(0, len(pieces), chans):
-        depth, rows, _ = pieces[start].shape
-        for k in range(chans):
-            place = pl.multiple_of((where_ref[0] ^ k) * rows, 32)
-            spectra[first:first + depth, pl.ds(place, rows), :] = pieces[start + k][...]
-        first += depth
-
     def load(block, g):
         whole = spectra[g, pl.ds(pl.multiple_of(block * TILE, TILE), TILE), :].astype(jnp.float32)
         return whole[:, :half], whole[:, half:]
@@ -88,7 +78,7 @@
     for t in range(tiles):
         slot = t % left_turned.shape[0]
         for g in range(groups):
-            re, im = load(where_ref[1 + 2 * t], g)
+            re, im = load(where_ref[2 + 2 * t], g)
             re, im = re * norm, im * norm
             for k in (4, 12):
                 forward, backward = turn_by(re, im, *table[k], True)
@@ -96,7 +86,7 @@
                 store(left_turned, slot, COARSE.index(-k), g, backward)
         for j in range(len(FINE_PAIRS)):
             for g in range(groups):
-                re, im = load(where_ref[2 + 2 * t], g)
+                re, im = load(where_ref[3 + 2 * t], g)
                 if j == 0:
                     store(right_turned, slot, 0, g, turn_by(re, im, *table[4], False)[0])
                     store(right_turned, slot, 1, g, (re, im))
@@ -110,72 +100,143 @@
                 (((1,), (1,)), ((), ())),
                 preferred_element_type=jnp.float32,
             )
+            partial = refs[0] if add else out_ref
             for u in range(len(COARSE)):
                 for s in range(2):
-                    staging[t, u, 2 * j + s] = total[u * TILE:(u + 1) * TILE, s * TILE:(s + 1) * TILE]
-            for s in range(2):
-                fine = FINE_PAIRS[j][s] + 4
-                copy = pltpu.make_async_copy(staging.at[t, :, 2 * j + s], out_ref.at[t, :, fine], sem)
-                copy.start()
-                copies.append(copy)
+                    fine = FINE_PAIRS[j][s] + 4
+                    value = total[u * TILE:(u + 1) * TILE, s * TILE:(s + 1) * TILE]
+                    partial[t, u, fine] = partial[t, u, fine] + value if add else value
+            if add:
+                for s in range(2):
+                    fine = FINE_PAIRS[j][s] + 4
+                    copy = pltpu.make_async_copy(partial.at[t, :, fine], out_ref.at[t, :, fine], sem)
+                    copy.start()
+                    copies.append(copy)
     for copy in copies:
         copy.wait()
 
 
-def correlate(pieces, where, tiles, hours):
-    groups = lax.axis_size("tm")
-    _, rows, lanes = pieces[0].shape
+VMEM = pl.BlockSpec(memory_space=pltpu.VMEM)
+SMEM = pl.BlockSpec(memory_space=pltpu.SMEM)
+
+
+def correlate(spectra, where, tiles, hours, partial=None):
+    groups, _, lanes = spectra.shape
     fine = 2 * len(FINE_PAIRS)
     shape = (tiles, len(COARSE), fine, TILE, TILE)
     norm = 1.0 / math.sqrt(F * hours)
     slots = min(tiles, 2)
-    vmem = pl.BlockSpec(memory_space=pltpu.VMEM)
-    out = pl.pallas_call(
-        lambda *refs: correlate_kernel(norm, *refs),
+    add = partial is not None
+    more = (partial,) if add else ()
+    return pl.pallas_call(
+        lambda *refs: correlate_kernel(norm, add, tiles, *refs),
         out_shape=jax.ShapeDtypeStruct(shape, jnp.float32),
-        in_specs=[pl.BlockSpec(memory_space=pltpu.SMEM)] + [vmem] * len(pieces),
-        out_specs=pl.BlockSpec(memory_space=pl.ANY),
+        in_specs=[SMEM, VMEM] + [VMEM] * add,
+        out_specs=pl.BlockSpec(memory_space=pl.ANY) if add else VMEM,
         scratch_shapes=[
-            pltpu.VMEM((groups, lax.axis_size("chan") * rows, lanes), jnp.bfloat16),
             pltpu.VMEM((slots, len(COARSE) * TILE, groups * lanes), jnp.bfloat16),
             pltpu.VMEM((slots, fine * TILE, groups * lanes), jnp.bfloat16),
-            pltpu.VMEM(shape, jnp.float32),
             pltpu.SemaphoreType.DMA,
         ],
-        compiler_params=pltpu.CompilerParams(vmem_limit_bytes=40 * 1024 * 1024),
-        name="correlate",
+        compiler_params=pltpu.CompilerParams(vmem_limit_bytes=24 * 1024 * 1024),
+        cost_estimate=pl.CostEstimate(
+            flops=2 * tiles * TILE * TILE * LAGS * groups * lanes, bytes_accessed=0, transcendentals=0
+        ),
+        name="correlate_add" if add else "correlate",
+    )(where, spectra, *more)
+
+
+def pack_kernel(windows, sources, where_ref, *refs):
+    out_ref = refs[-1]
+    first = where_ref[1] == 0
+    for w in range(windows):
+        for core in range(CORES):
+            one, two = sources[0][w, core], sources[1][w, core]
+            out_ref[w, core] = jnp.where(first, refs[one][...], refs[two][...])
+
+
+def pack(where, windows, sources, blocks):
+    return pl.pallas_call(
+        lambda *refs: pack_kernel(windows, sources, *refs),
+        out_shape=jax.ShapeDtypeStruct((windows, CORES, *blocks[0].shape), jnp.bfloat16),
+        in_specs=[SMEM] + [VMEM] * len(blocks),
+        out_specs=VMEM,
+        name="pack",
+    )(where, *blocks)
+
+
+def collect_kernel(where_ref, *refs):
+    out_ref = refs[-1]
+    _, cores, rows, _ = refs[0].shape
+    for k, piece in enumerate(refs[:-1]):
+        for core in range(cores):
+            place = pl.multiple_of(((where_ref[0] ^ k) * cores + core) * rows, 32)
+            out_ref[:, pl.ds(place, rows), :] = piece[:, core]
+
+
+def collect(where, pieces):
+    windows, cores, rows, lanes = pieces[0].shape
+    return pl.pallas_call(
+        collect_kernel,
+        out_shape=jax.ShapeDtypeStruct((windows, len(pieces) * cores * rows, lanes), jnp.bfloat16),
+        in_specs=[SMEM] + [VMEM] * len(pieces),
+        out_specs=VMEM,
+        name="collect",
     )(where, *pieces)
-    return out.reshape(tiles, LAGS, TILE, TILE)
-
-
-def swap(array, axis, k):
-    return lax.ppermute(array, axis, [(i, i ^ k) for i in range(lax.axis_size(axis))])
-
-
-def between_chips(half):
-    pieces = {0: half}
-    for k in range(2, lax.axis_size("chan"), 2):
-        pieces[k] = swap(half, "chan", k)
-    for k in list(pieces):
-        pieces[k + 1] = swap(pieces[k], "chan", 1)
-    return [pieces[k] for k in sorted(pieces)]
-
-
-def gather(white):
-    near = [white] + [swap(white, "tm", k) for k in (1,)]
-    far = [swap(white, "tm", k) for k in range(2, lax.axis_size("tm"))]
-    return between_chips(jnp.stack(near)) + between_chips(jnp.stack(far))
+
+
+def swap(array, k):
+    return lax.ppermute(array, "chan", [(i, i ^ k) for i in range(lax.axis_size("chan"))])
+
+
+def fetch(block, sources):
+    chans, groups = lax.axis_size("chan"), lax.axis_size("tm")
+    pairs = []
+    for chan in range(chans):
+        for tm in range(groups):
+            if chan % CORES in sources:
+                k, core = sources[chan % CORES]
+                source = chan // CORES * CORES + core
+                pairs.append((source * groups + (tm ^ k), chan * groups + tm))
+    return lax.ppermute(block, ("chan", "tm"), pairs)
+
+
+def own_windows(white, where):
+    groups = lax.axis_size("tm")
+    windows = groups // 2
+    near, far = list(range(1, windows)), list(range(windows, groups))
+    steps = [((k, 0), (far[i], 1)) for i, k in enumerate(near)]
+    steps += [((k, 1), (far[i], 0)) for i, k in enumerate(near + [0])]
+    steps += [(None, (far[-1], 1))]
+    blocks = [white]
+    at = ({(0, 0): 0}, {})
+    for step in steps:
+        sources = {core: source for core, source in enumerate(step) if source}
+        for core, source in sources.items():
+            at[core][source] = len(blocks)
+        blocks.append(fetch(white, sources))
+    sources = tuple(
+        {(w, core): at[own][(first + w, core)] for w in range(windows) for core in range(CORES)}
+        for own, first in enumerate((0, windows))
+    )
+    return pack(where, windows, sources, blocks)
 
 
 def per_device(spectra, bad_channels, tile_list):
     groups = lax.axis_size("tm")
     hours = spectra.shape[1] * groups
     tiles = tile_list.shape[0] // groups
-    white = whiten(spectra, bad_channels)
-    pieces = gather(white)
+    chan = lax.axis_index("chan")
     pairs = lax.dynamic_slice_in_dim(tile_list, lax.axis_index("tm") * tiles, tiles, axis=0)
-    where = jnp.concatenate([lax.axis_index("chan").reshape(1), pairs.reshape(-1)]).astype(jnp.int32)
-    return correlate(pieces, where, tiles, hours)
+    place = jnp.stack([chan // CORES, chan % CORES])
+    where = jnp.concatenate([place, pairs.reshape(-1)]).astype(jnp.int32)
+    packed = own_windows(whiten(spectra, bad_channels), where)
+    pieces = [packed] + [swap(packed, k) for k in range(CORES, lax.axis_size("chan"), CORES)]
+    one = collect(where, pieces)
+    two = swap(one, 1)
+    partial = correlate(one, where, tiles, hours)
+    out = correlate(two, where, tiles, hours, partial)
+    return out.reshape(tiles, LAGS, TILE, TILE)
 
 
 def solution(mesh):

time: 28.1 us -> 39.2 us (1.40)
  waiting for transfers between devices: 1.28 us -> 9.99 us
  starting transfers between devices: 18.4 us -> 13 us
  Pallas kernels: 6.87 us -> 11.2 us
  local copies, waits for them, and re-layouts: 0.26 us -> 3.97 us
    ppermute x17 -> x8, waiting for transfers between devices: 1.28 us -> 9.99 us  [the longest x4 7.59 us: swap(): lax.ppermute(array, 'chan', [(i, i ^ k) for i in range(lax.axis_size('cha...]
    ppermute x17 -> x8, starting transfers between devices: 18.4 us -> 13 us  [the longest x4 9.91 us: fetch(): return lax.ppermute(block, ('chan', 'tm'), pairs)]
    pallas_call x1 -> x4, Pallas kernels: 4.97 us -> 9.31 us  [the longest x2 5.56 us: correlate(): pl.pallas_call(lambda *refs: correlate_kernel(norm, add, tiles, *refs), o...]
    unnamed x2 -> x20, local copies, waits for them, and re-layouts: 0.01 us -> 3.72 us
    another operation x2 -> x0, other arithmetic: 0.85 us -> none  [gather(): return between_chips(jnp.stack(near)) + between_chips(jnp.stack(far))]
    concatenate x1, other arithmetic: 0.07 us -> 0.62 us  [per_device(): where = jnp.concatenate([place, pairs.reshape(-1)]).astype(jnp.int32)]
  transfers between devices with their start and end apart: 17 -> 8, of which waited for: 5 -> 4; matrix products, arithmetic and copies ran while one was open for 4% -> 2% of each run, Pallas kernels for 0% -> 6%
where the time goes in v5:
time: 39.2 us; the launch traced here: 38.8 us
  starting transfers between devices  13 us (33%)
  Pallas kernels  11.2 us (29%)
  waiting for transfers between devices  9.99 us (25%)
  local copies, waits for them, and re-layouts  3.97 us (10%)
  other arithmetic  0.62 us (2%)
    ppermute x4, starting transfers between devices, fetch(): return lax.ppermute(block, ('chan', 'tm'), pairs)  9.91 us
    ppermute x4, waiting for transfers between devices, swap(): lax.ppermute(array, 'chan', [(i, i ^ k) for i in range(lax.axis_size('cha...  7.59 us
    pallas_call x2, Pallas kernels, correlate(): pl.pallas_call(lambda *refs: correlate_kernel(norm, add, tiles, *refs), o...  5.56 us
    unnamed x20, local copies, waits for them, and re-layouts  3.72 us
    ppermute x4, starting transfers between devices, swap(): lax.ppermute(array, 'chan', [(i, i ^ k) for i in range(lax.axis_size('cha...  3.04 us
    ppermute x4, waiting for transfers between devices, fetch(): return lax.ppermute(block, ('chan', 'tm'), pairs)  2.39 us
    pallas_call x1, Pallas kernels, collect(): pl.pallas_call(collect_kernel, out_shape=jax.ShapeDtypeStruct((windows, l...  2.16 us
    pallas_call x1, Pallas kernels, whiten(): pl.pallas_call(whiten_kernel, out_shape=jax.ShapeDtypeStruct((chans, bins...  1.9 us
  transfers between devices with their start and end apart: 8, of which 4 were waited for; matrix products, arithmetic and copies ran while one was open for 2% of the time, Pallas kernels for 6%

profile of v5, /device:TPU:1, one launch (start us, length us, event | category | flops | bytes accessed | tf_op | source)
XLA Modules:
  0.0 38.8 jit_solution(10532279360348345267)
XLA Ops:
  0.0 0.0 copy-start
  0.0 1.9 %whiten.1.refs_1_ = bf16[96,256]{1,0:T(8,128)(2,1)} custom-call(bf16[64,2,2,96]{3,2,1,0:T(2,128)(2,1)} %spectra_ref.1, s32[1,96]{1,0:T(1,128)} %bitcast.4), custom_call_target="tpu_custom_call" | custom-call | tf_op jit(solution)/shard_map/whiten/pallas_call | solution.py:42
  1.9 6.0 %collective-permute-start.3 = (bf16[96,256]{1,0:T(8,128)(2,1)}, bf16[96,256]{1,0:T(8,128)(2,1)S(1)}, u32[]{:S(2)}, u32[]{:S(2)}) collective-permute-start(bf16[96,256]{1,0:T(8,128)(2,1)} %whiten.1.refs_1_), channel_id=1, source_target_pairs={{7,4},{6,5},{5,6},{4,7},{15,12},{14,13},{13,14},{12,15},{23,20},{2... | collective-permute-start | bytes 147464 | tf_op jit(solution)/shard_map/ppermute | solution.py:201
  8.0 0.1 collective-permute-start.2
  8.0 0.1 collective-permute-start.1
  8.1 3.7 %collective-permute-start = (bf16[96,256]{1,0:T(8,128)(2,1)}, bf16[96,256]{1,0:T(8,128)(2,1)S(1)}, u32[]{:S(2)}, u32[]{:S(2)}) collective-permute-start(bf16[96,256]{1,0:T(8,128)(2,1)} %whiten.1.refs_1_), channel_id=1, source_target_pairs={{1,0},{0,1},{3,2},{2,3},{6,4},{7,5},{4,6},{5,7},{9,8},{8,9},{11,10... | collective-permute-start | bytes 147464 | tf_op jit(solution)/shard_map/ppermute | solution.py:201
  11.8 0.0 copy-done
  11.8 0.1 constant_dynamic-slice_fusion
  11.9 0.1 copy.4
  12.0 0.1 reshape.9
  12.1 0.6 %pad_add_fusion.refs_0_.where_ref = s32[6]{0:T(128)} fusion(s32[4]{0:T(128)S(1)} %reshape.9, s32[1]{0:T(128)} %bitcast.1, s32[1]{0:T(128)} %bitcast), kind=kLoop, calls=%fused_computation | loop fusion | flops 12 | bytes 48 | tf_op jit(solution)/shard_map/concatenate | solution.py:232
  12.7 0.0 collective-permute-done.3.refs_5_
  12.7 0.0 copy-start.6
  12.7 1.4 %collective-permute-done.2.refs_4_ = bf16[96,256]{1,0:T(8,128)(2,1)S(1)} collective-permute-done((bf16[96,256]{1,0:T(8,128)(2,1)}, bf16[96,256]{1,0:T(8,128)(2,1)S(1)}, u32[]{:S(2)}, u32[]{:S(2)}) %collective-permute-start.2) | collective-permute-done | bytes 49184 | tf_op jit(solution)/shard_map/ppermute | solution.py:201
  14.2 0.0 copy-start.7
  14.2 0.0 collective-permute-done.1.refs_3_
  14.2 0.0 copy-start.8
  14.2 1.0 %collective-permute-done.refs_2_ = bf16[96,256]{1,0:T(8,128)(2,1)S(1)} collective-permute-done((bf16[96,256]{1,0:T(8,128)(2,1)}, bf16[96,256]{1,0:T(8,128)(2,1)S(1)}, u32[]{:S(2)}, u32[]{:S(2)}) %collective-permute-start) | collective-permute-done | bytes 49184 | tf_op jit(solution)/shard_map/ppermute | solution.py:201
  15.1 0.0 copy-done.6
  15.1 0.0 copy-done.7
  15.1 0.0 copy-done.8
  15.1 0.0 copy-start.9
  15.1 0.6 %copy-done.9 = bf16[96,256]{1,0:T(8,128)(2,1)} copy-done((bf16[96,256]{1,0:T(8,128)(2,1)}, bf16[96,256]{1,0:T(8,128)(2,1)S(1)}, u32[]{:S(2)}) %copy-start.9) | copy-done | bytes 49176
  15.7 1.6 %pack.1.refs_0_ = bf16[2,2,96,256]{3,2,1,0:T(8,128)(2,1)} custom-call(s32[6]{0:T(128)} %pad_add_fusion.refs_0_.where_ref, bf16[96,256]{1,0:T(8,128)(2,1)} %whiten.1.refs_1_, bf16[96,256]{1,0:T(8,128)(2,1)} %copy-done.9, bf16[96,256]{1,0:T(8,128)(2,1)} %copy-done.8, bf16[96,256]{1,0:T(8,128)(2,1)} %copy-done.7, bf16[96,256]{1,0:T(8,128)(2,1)} %copy-done.6), custom_call_target="tpu_custom_call" | custom-call | tf_op jit(solution)/shard_map/pack/pallas_call | solution.py:159
  17.3 2.2 %collective-permute-start.6 = (bf16[2,2,96,256]{3,2,1,0:T(8,128)(2,1)}, bf16[2,2,96,256]{3,2,1,0:T(8,128)(2,1)S(1)}, u32[]{:S(2)}, u32[]{:S(2)}) collective-permute-start(bf16[2,2,96,256]{3,2,1,0:T(8,128)(2,1)} %pack.1.refs_0_), channel_id=1, source_target_pairs={{0,24},{4,28},{8,16},{12,20},{16,8},{20,12},{24,0},{28,4},{1,25},{... | collective-permute-start | bytes 589832 | tf_op jit(solution)/shard_map/ppermute | solution.py:189
  19.5 0.2 collective-permute-start.5
  19.7 0.3 collective-permute-start.4
  20.0 4.6 %collective-permute-done.6.refs_3_ = bf16[2,2,96,256]{3,2,1,0:T(8,128)(2,1)S(1)} collective-permute-done((bf16[2,2,96,256]{3,2,1,0:T(8,128)(2,1)}, bf16[2,2,96,256]{3,2,1,0:T(8,128)(2,1)S(1)}, u32[]{:S(2)}, u32[]{:S(2)}) %collective-permute-start.6) | collective-permute-done | bytes 196640 | tf_op jit(solution)/shard_map/ppermute | solution.py:189
  24.6 0.0 copy-start.3
  24.6 3.0 %collective-permute-done.5.refs_2_ = bf16[2,2,96,256]{3,2,1,0:T(8,128)(2,1)S(1)} collective-permute-done((bf16[2,2,96,256]{3,2,1,0:T(8,128)(2,1)}, bf16[2,2,96,256]{3,2,1,0:T(8,128)(2,1)S(1)}, u32[]{:S(2)}, u32[]{:S(2)}) %collective-permute-start.5) | collective-permute-done | bytes 196640 | tf_op jit(solution)/shard_map/ppermute | solution.py:189
  27.6 0.0 copy-start.4
  27.6 0.0 collective-permute-done.4.refs_1_
  27.6 0.0 copy-done.3
  27.6 0.7 %copy-done.4 = bf16[2,2,96,256]{3,2,1,0:T(8,128)(2,1)} copy-done((bf16[2,2,96,256]{3,2,1,0:T(8,128)(2,1)}, bf16[2,2,96,256]{3,2,1,0:T(8,128)(2,1)S(1)}, u32[]{:S(2)}) %copy-start.4) | copy-done | bytes 196632
  28.2 0.0 copy-start.5
  28.2 0.7 %copy-done.5 = bf16[2,2,96,256]{3,2,1,0:T(8,128)(2,1)} copy-done((bf16[2,2,96,256]{3,2,1,0:T(8,128)(2,1)}, bf16[2,2,96,256]{3,2,1,0:T(8,128)(2,1)S(1)}, u32[]{:S(2)}) %copy-start.5) | copy-done | bytes 196632
  28.9 2.2 %collect.1.refs_1_ = bf16[2,768,256]{2,1,0:T(8,128)(2,1)} custom-call(s32[6]{0:T(128)} %pad_add_fusion.refs_0_.where_ref, bf16[2,2,96,256]{3,2,1,0:T(8,128)(2,1)} %pack.1.refs_0_, bf16[2,2,96,256]{3,2,1,0:T(8,128)(2,1)} %copy-done.5, bf16[2,2,96,256]{3,2,1,0:T(8,128)(2,1)} %copy-done.4, bf16[2,2,96,256]{3,2,1,0:T(8,128)(2,1)} %copy-done.3), custom_call_target="tpu_custom_call" | custom-call | tf_op jit(solution)/shard_map/collect/pallas_call | solution.py:179
  31.1 0.4 %collective-permute-start.7 = (bf16[2,768,256]{2,1,0:T(8,128)(2,1)}, bf16[2,768,256]{2,1,0:T(8,128)(2,1)S(1)}, u32[]{:S(2)}, u32[]{:S(2)}) collective-permute-start(bf16[2,768,256]{2,1,0:T(8,128)(2,1)} %collect.1.refs_1_), channel_id=1, source_target_pairs={{0,4},{4,0},{8,12},{12,8},{16,20},{20,16},{24,28},{28,24},{1,5},{5... | collective-permute-start | bytes 2359304 | tf_op jit(solution)/shard_map/ppermute | solution.py:189
  31.5 0.0 copy-start.1
  31.5 1.1 %copy-done.1 = bf16[2,768,256]{2,1,0:T(8,128)(2,1)S(1)} copy-done((bf16[2,768,256]{2,1,0:T(8,128)(2,1)S(1)}, bf16[2,768,256]{2,1,0:T(8,128)(2,1)}, u32[]{:S(2)}) %copy-start.1) | copy-done | bytes 786456
  32.6 0.0 copy-start.2
  32.6 0.6 %copy-done.2 = s32[6]{0:T(128)S(1)} copy-done((s32[6]{0:T(128)S(1)}, s32[6]{0:T(128)}, u32[]{:S(2)}) %copy-start.2) | copy-done | bytes 48
  33.2 2.1 %correlate.1.refs_2_ = f32[2,4,8,128,128]{4,3,2,1,0:T(8,128)S(1)} custom-call(s32[6]{0:T(128)S(1)} %copy-done.2, bf16[2,768,256]{2,1,0:T(8,128)(2,1)S(1)} %copy-done.1), custom_call_target="tpu_custom_call" | custom-call | flops 1073741824 | tf_op jit(solution)/shard_map/correlate/pallas_call | solution.py:131
  35.4 0.0 collective-permute-done.7.refs_1_
  35.4 3.4 %correlate_add.1 = f32[2,4,8,128,128]{4,3,2,1,0:T(8,128)} custom-call(s32[6]{0:T(128)S(1)} %copy-done.2, bf16[2,768,256]{2,1,0:T(8,128)(2,1)S(1)} %collective-permute-done.7.refs_1_, f32[2,4,8,128,128]{4,3,2,1,0:T(8,128)S(1)} %correlate.1.refs_2_), custom_call_target="tpu_custom_call" | custom-call | flops 1073741824 | tf_op jit(solution)/shard_map/correlate_add/pallas_call | solution.py:131
Async XLA Ops:
  0.0 11.8 %copy-start = (s32[8,2]{0,1:T(2,128)S(1)}, s32[8,2]{0,1:T(2,128)}, u32[]{:S(2)}) copy-start(s32[8,2]{0,1:T(2,128)} %param.5) | copy-start | bytes 196
  1.9 10.8 %collective-permute-start.3 = (bf16[96,256]{1,0:T(8,128)(2,1)}, bf16[96,256]{1,0:T(8,128)(2,1)S(1)}, u32[]{:S(2)}, u32[]{:S(2)}) collective-permute-start(bf16[96,256]{1,0:T(8,128)(2,1)} %whiten.1.refs_1_), channel_id=1, source_target_pairs={{7,4},{6,5},{5,6},{4,7},{15,12},{14,13},{13,14},{12,15},{23,20},{2... | collective-permute-start | bytes 147464 | tf_op jit(solution)/shard_map/ppermute | solution.py:201
  8.0 6.2 %collective-permute-start.2 = (bf16[96,256]{1,0:T(8,128)(2,1)}, bf16[96,256]{1,0:T(8,128)(2,1)S(1)}, u32[]{:S(2)}, u32[]{:S(2)}) collective-permute-start(bf16[96,256]{1,0:T(8,128)(2,1)} %whiten.1.refs_1_), channel_id=1, source_target_pairs={{4,0},{5,1},{6,2},{7,3},{3,4},{2,5},{1,6},{0,7},{12,8},{13,9},{14,... | collective-permute-start | bytes 147464 | tf_op jit(solution)/shard_map/ppermute | solution.py:201
  8.0 6.1 %collective-permute-start.1 = (bf16[96,256]{1,0:T(8,128)(2,1)}, bf16[96,256]{1,0:T(8,128)(2,1)S(1)}, u32[]{:S(2)}, u32[]{:S(2)}) collective-permute-start(bf16[96,256]{1,0:T(8,128)(2,1)} %whiten.1.refs_1_), channel_id=1, source_target_pairs={{5,0},{4,1},{7,2},{6,3},{2,4},{3,5},{0,6},{1,7},{13,8},{12,9},{15,... | collective-permute-start | bytes 147464 | tf_op jit(solution)/shard_map/ppermute | solution.py:201
  8.1 7.0 %collective-permute-start = (bf16[96,256]{1,0:T(8,128)(2,1)}, bf16[96,256]{1,0:T(8,128)(2,1)S(1)}, u32[]{:S(2)}, u32[]{:S(2)}) collective-permute-start(bf16[96,256]{1,0:T(8,128)(2,1)} %whiten.1.refs_1_), channel_id=1, source_target_pairs={{1,0},{0,1},{3,2},{2,3},{6,4},{7,5},{4,6},{5,7},{9,8},{8,9},{11,10... | collective-permute-start | bytes 147464 | tf_op jit(solution)/shard_map/ppermute | solution.py:201
  12.7 2.4 %copy-start.6 = (bf16[96,256]{1,0:T(8,128)(2,1)}, bf16[96,256]{1,0:T(8,128)(2,1)S(1)}, u32[]{:S(2)}) copy-start(bf16[96,256]{1,0:T(8,128)(2,1)S(1)} %collective-permute-done.3.refs_5_) | copy-start | bytes 147460
  14.2 1.0 %copy-start.7 = (bf16[96,256]{1,0:T(8,128)(2,1)}, bf16[96,256]{1,0:T(8,128)(2,1)S(1)}, u32[]{:S(2)}) copy-start(bf16[96,256]{1,0:T(8,128)(2,1)S(1)} %collective-permute-done.2.refs_4_) | copy-start | bytes 147460
  14.2 1.0 %copy-start.8 = (bf16[96,256]{1,0:T(8,128)(2,1)}, bf16[96,256]{1,0:T(8,128)(2,1)S(1)}, u32[]{:S(2)}) copy-start(bf16[96,256]{1,0:T(8,128)(2,1)S(1)} %collective-permute-done.1.refs_3_) | copy-start | bytes 147460
  15.1 0.6 %copy-start.9 = (bf16[96,256]{1,0:T(8,128)(2,1)}, bf16[96,256]{1,0:T(8,128)(2,1)S(1)}, u32[]{:S(2)}) copy-start(bf16[96,256]{1,0:T(8,128)(2,1)S(1)} %collective-permute-done.refs_2_) | copy-start | bytes 147460
  17.3 7.3 %collective-permute-start.6 = (bf16[2,2,96,256]{3,2,1,0:T(8,128)(2,1)}, bf16[2,2,96,256]{3,2,1,0:T(8,128)(2,1)S(1)}, u32[]{:S(2)}, u32[]{:S(2)}) collective-permute-start(bf16[2,2,96,256]{3,2,1,0:T(8,128)(2,1)} %pack.1.refs_0_), channel_id=1, source_target_pairs={{0,24},{4,28},{8,16},{12,20},{16,8},{20,12},{24,0},{28,4},{1,25},{... | collective-permute-start | bytes 589832 | tf_op jit(solution)/shard_map/ppermute | solution.py:189
  19.5 8.1 %collective-permute-start.5 = (bf16[2,2,96,256]{3,2,1,0:T(8,128)(2,1)}, bf16[2,2,96,256]{3,2,1,0:T(8,128)(2,1)S(1)}, u32[]{:S(2)}, u32[]{:S(2)}) collective-permute-start(bf16[2,2,96,256]{3,2,1,0:T(8,128)(2,1)} %pack.1.refs_0_), channel_id=1, source_target_pairs={{0,16},{4,20},{8,24},{12,28},{16,0},{20,4},{24,8},{28,12},{1,17},{... | collective-permute-start | bytes 589832 | tf_op jit(solution)/shard_map/ppermute | solution.py:189
  19.7 7.8 %collective-permute-start.4 = (bf16[2,2,96,256]{3,2,1,0:T(8,128)(2,1)}, bf16[2,2,96,256]{3,2,1,0:T(8,128)(2,1)S(1)}, u32[]{:S(2)}, u32[]{:S(2)}) collective-permute-start(bf16[2,2,96,256]{3,2,1,0:T(8,128)(2,1)} %pack.1.refs_0_), channel_id=1, source_target_pairs={{0,8},{4,12},{8,0},{12,4},{16,24},{20,28},{24,16},{28,20},{1,9},{5... | collective-permute-start | bytes 589832 | tf_op jit(solution)/shard_map/ppermute | solution.py:189
  24.6 3.0 %copy-start.3 = (bf16[2,2,96,256]{3,2,1,0:T(8,128)(2,1)}, bf16[2,2,96,256]{3,2,1,0:T(8,128)(2,1)S(1)}, u32[]{:S(2)}) copy-start(bf16[2,2,96,256]{3,2,1,0:T(8,128)(2,1)S(1)} %collective-permute-done.6.refs_3_) | copy-start | bytes 589828
  27.6 0.7 %copy-start.4 = (bf16[2,2,96,256]{3,2,1,0:T(8,128)(2,1)}, bf16[2,2,96,256]{3,2,1,0:T(8,128)(2,1)S(1)}, u32[]{:S(2)}) copy-start(bf16[2,2,96,256]{3,2,1,0:T(8,128)(2,1)S(1)} %collective-permute-done.5.refs_2_) | copy-start | bytes 589828
  28.2 0.7 %copy-start.5 = (bf16[2,2,96,256]{3,2,1,0:T(8,128)(2,1)}, bf16[2,2,96,256]{3,2,1,0:T(8,128)(2,1)S(1)}, u32[]{:S(2)}) copy-start(bf16[2,2,96,256]{3,2,1,0:T(8,128)(2,1)S(1)} %collective-permute-done.4.refs_1_) | copy-start | bytes 589828
  31.1 4.3 %collective-permute-start.7 = (bf16[2,768,256]{2,1,0:T(8,128)(2,1)}, bf16[2,768,256]{2,1,0:T(8,128)(2,1)S(1)}, u32[]{:S(2)}, u32[]{:S(2)}) collective-permute-start(bf16[2,768,256]{2,1,0:T(8,128)(2,1)} %collect.1.refs_1_), channel_id=1, source_target_pairs={{0,4},{4,0},{8,12},{12,8},{16,20},{20,16},{24,28},{28,24},{1,5},{5... | collective-permute-start | bytes 2359304 | tf_op jit(solution)/shard_map/ppermute | solution.py:189
  31.5 1.1 %copy-start.1 = (bf16[2,768,256]{2,1,0:T(8,128)(2,1)S(1)}, bf16[2,768,256]{2,1,0:T(8,128)(2,1)}, u32[]{:S(2)}) copy-start(bf16[2,768,256]{2,1,0:T(8,128)(2,1)} %collect.1.refs_1_) | copy-start | bytes 2359300
  32.6 0.6 %copy-start.2 = (s32[6]{0:T(128)S(1)}, s32[6]{0:T(128)}, u32[]{:S(2)}) copy-start(s32[6]{0:T(128)} %pad_add_fusion.refs_0_.where_ref) | copy-start | bytes 76

commit v6 on v5

--- a/solution.py
+++ b/solution.py
@@ -12,6 +12,7 @@
 TILE = 128
 EPSILON = 1e-06
 CORES = 2
+SMALL = 4 * 1024 * 1024
 COARSE = (-12, -4, 4, 12)
 FINE_PAIRS = ((-4, 0), (-1, 1), (-2, 2), (-3, 3))
 
@@ -42,6 +43,7 @@
     return pl.pallas_call(
         whiten_kernel,
         out_shape=jax.ShapeDtypeStruct((chans, bins * hours * 2), jnp.bfloat16),
+        compiler_params=pltpu.CompilerParams(vmem_limit_bytes=SMALL),
         name="whiten",
     )(spectra, bad_channels.reshape(1, chans))
 
@@ -138,7 +140,7 @@
             pltpu.VMEM((slots, fine * TILE, groups * lanes), jnp.bfloat16),
             pltpu.SemaphoreType.DMA,
         ],
-        compiler_params=pltpu.CompilerParams(vmem_limit_bytes=24 * 1024 * 1024),
+        compiler_params=pltpu.CompilerParams(vmem_limit_bytes=12 * 1024 * 1024),
         cost_estimate=pl.CostEstimate(
             flops=2 * tiles * TILE * TILE * LAGS * groups * lanes, bytes_accessed=0, transcendentals=0
         ),
@@ -161,6 +163,7 @@
         out_shape=jax.ShapeDtypeStruct((windows, CORES, *blocks[0].shape), jnp.bfloat16),
         in_specs=[SMEM] + [VMEM] * len(blocks),
         out_specs=VMEM,
+        compiler_params=pltpu.CompilerParams(vmem_limit_bytes=SMALL),
         name="pack",
     )(where, *blocks)
 
@@ -181,6 +184,7 @@
         out_shape=jax.ShapeDtypeStruct((windows, len(pieces) * cores * rows, lanes), jnp.bfloat16),
         in_specs=[SMEM] + [VMEM] * len(pieces),
         out_specs=VMEM,
+        compiler_params=pltpu.CompilerParams(vmem_limit_bytes=SMALL),
         name="collect",
     )(where, *pieces)
 

time: 39.2 us -> 32.5 us (0.83)
  Pallas kernels: 11.2 us -> 7.16 us
  local copies, waits for them, and re-layouts: 3.97 us -> 1.76 us
  other arithmetic: 0.62 us -> 0.08 us
    unnamed x20 -> x6, local copies, waits for them, and re-layouts: 3.72 us -> 1.51 us
    pallas_call x1, Pallas kernels: 2.16 us -> 0.6 us  [collect(): pl.pallas_call(collect_kernel, out_shape=jax.ShapeDtypeStruct((windows, l...]
    pallas_call x1, Pallas kernels: 1.9 us -> 0.42 us  [whiten(): pl.pallas_call(whiten_kernel, out_shape=jax.ShapeDtypeStruct((chans, bins...]
    pallas_call x1, Pallas kernels: 1.59 us -> 0.56 us  [pack(): pl.pallas_call(lambda *refs: pack_kernel(windows, sources, *refs), out_sh...]
    concatenate x1, other arithmetic: 0.62 us -> 0.08 us  [per_device(): where = jnp.concatenate([place, pairs.reshape(-1)]).astype(jnp.int32)]
  transfers between devices with their start and end apart: 8 -> 8, of which waited for: 4 -> 4; matrix products, arithmetic and copies ran while one was open for 2% -> 1% of each run, Pallas kernels for 6% -> 7%
where the time goes in v6:
time: 32.5 us; the launch traced here: 32.3 us
  starting transfers between devices  13.1 us (40%)
  waiting for transfers between devices  10.1 us (31%)
  Pallas kernels  7.16 us (22%)
  local copies, waits for them, and re-layouts  1.76 us (5%)
    ppermute x4, starting transfers between devices, fetch(): return lax.ppermute(block, ('chan', 'tm'), pairs)  9.92 us
    ppermute x4, waiting for transfers between devices, swap(): lax.ppermute(array, 'chan', [(i, i ^ k) for i in range(lax.axis_size('cha...  7.4 us
    pallas_call x2, Pallas kernels, correlate(): pl.pallas_call(lambda *refs: correlate_kernel(norm, add, tiles, *refs), o...  5.58 us
    ppermute x4, starting transfers between devices, swap(): lax.ppermute(array, 'chan', [(i, i ^ k) for i in range(lax.axis_size('cha...  3.17 us
    ppermute x4, waiting for transfers between devices, fetch(): return lax.ppermute(block, ('chan', 'tm'), pairs)  2.72 us
    unnamed x6, local copies, waits for them, and re-layouts  1.51 us
  transfers between devices with their start and end apart: 8, of which 4 were waited for; matrix products, arithmetic and copies ran while one was open for 1% of the time, Pallas kernels for 7%

profile of v6, /device:TPU:1, one launch (start us, length us, event | category | flops | bytes accessed | tf_op | source)
XLA Modules:
  0.0 32.3 jit_solution(6394233235873074746)
XLA Ops:
  0.0 0.0 copy-start
  0.0 0.0 copy-start.1
  0.0 0.9 %copy-done.1 = bf16[64,2,2,96]{3,2,1,0:T(2,128)(2,1)S(1)} copy-done((bf16[64,2,2,96]{3,2,1,0:T(2,128)(2,1)S(1)}, bf16[64,2,2,96]{3,2,1,0:T(2,128)(2,1)}, u32[]{:S(2)}) %copy-start.1) | copy-done | bytes 49176
  0.9 0.0 copy-start.2
  0.9 0.7 %copy-done.2 = s32[96]{0:T(128)S(1)} copy-done((s32[96]{0:T(128)S(1)}, s32[96]{0:T(128)}, u32[]{:S(2)}) %copy-start.2) | copy-done | bytes 408
  1.5 0.4 %whiten.1.refs_1_ = bf16[96,256]{1,0:T(8,128)(2,1)S(1)} custom-call(bf16[64,2,2,96]{3,2,1,0:T(2,128)(2,1)S(1)} %copy-done.1, s32[1,96]{1,0:T(1,128)S(1)} %bitcast.4), custom_call_target="tpu_custom_call" | custom-call | tf_op jit(solution)/shard_map/whiten/pallas_call | solution.py:43
  1.9 6.1 %collective-permute-start.3 = (bf16[96,256]{1,0:T(8,128)(2,1)S(1)}, bf16[96,256]{1,0:T(8,128)(2,1)S(1)}, u32[]{:S(2)}, u32[]{:S(2)}) collective-permute-start(bf16[96,256]{1,0:T(8,128)(2,1)S(1)} %whiten.1.refs_1_), channel_id=1, source_target_pairs={{7,4},{6,5},{5,6},{4,7},{15,12},{14,13},{13,14},{12,15},{23,20},{2... | collective-permute-start | bytes 147464 | tf_op jit(solution)/shard_map/ppermute | solution.py:205
  8.0 0.1 collective-permute-start.2
  8.1 0.1 collective-permute-start.1
  8.1 3.7 %collective-permute-start = (bf16[96,256]{1,0:T(8,128)(2,1)S(1)}, bf16[96,256]{1,0:T(8,128)(2,1)S(1)}, u32[]{:S(2)}, u32[]{:S(2)}) collective-permute-start(bf16[96,256]{1,0:T(8,128)(2,1)S(1)} %whiten.1.refs_1_), channel_id=1, source_target_pairs={{1,0},{0,1},{3,2},{2,3},{6,4},{7,5},{4,6},{5,7},{9,8},{8,9},{11,10... | collective-permute-start | bytes 147464 | tf_op jit(solution)/shard_map/ppermute | solution.py:205
  11.9 0.0 copy-done
  11.9 0.1 constant_dynamic-slice_fusion
  12.0 0.1 copy.4
  12.1 0.1 reshape.9
  12.1 0.1 pad_add_fusion.refs_0_.where_ref
  12.2 0.0 collective-permute-done.3.refs_5_
  12.2 1.8 %collective-permute-done.2.refs_4_ = bf16[96,256]{1,0:T(8,128)(2,1)S(1)} collective-permute-done((bf16[96,256]{1,0:T(8,128)(2,1)S(1)}, bf16[96,256]{1,0:T(8,128)(2,1)S(1)}, u32[]{:S(2)}, u32[]{:S(2)}) %collective-permute-start.2) | collective-permute-done | bytes 49184 | tf_op jit(solution)/shard_map/ppermute | solution.py:205
  14.0 0.0 collective-permute-done.1.refs_3_
  14.0 0.9 %collective-permute-done.refs_2_ = bf16[96,256]{1,0:T(8,128)(2,1)S(1)} collective-permute-done((bf16[96,256]{1,0:T(8,128)(2,1)S(1)}, bf16[96,256]{1,0:T(8,128)(2,1)S(1)}, u32[]{:S(2)}, u32[]{:S(2)}) %collective-permute-start) | collective-permute-done | bytes 49184 | tf_op jit(solution)/shard_map/ppermute | solution.py:205
  14.9 0.6 %pack.1.refs_0_ = bf16[2,2,96,256]{3,2,1,0:T(8,128)(2,1)S(1)} custom-call(s32[6]{0:T(128)S(1)} %pad_add_fusion.refs_0_.where_ref, bf16[96,256]{1,0:T(8,128)(2,1)S(1)} %whiten.1.refs_1_, bf16[96,256]{1,0:T(8,128)(2,1)S(1)} %collective-permute-done.refs_2_, bf16[96,256]{1,0:T(8,128)(2,1)S(1)} %collective-permute-done.1.refs_3_, ...), custom_call_target="tpu_custom_call" | custom-call | tf_op jit(solution)/shard_map/pack/pallas_call | solution.py:161
  15.5 2.2 %collective-permute-start.6 = (bf16[2,2,96,256]{3,2,1,0:T(8,128)(2,1)S(1)}, bf16[2,2,96,256]{3,2,1,0:T(8,128)(2,1)S(1)}, u32[]{:S(2)}, u32[]{:S(2)}) collective-permute-start(bf16[2,2,96,256]{3,2,1,0:T(8,128)(2,1)S(1)} %pack.1.refs_0_), channel_id=1, source_target_pairs={{0,24},{4,28},{8,16},{12,20},{16,8},{20,12},{24,0},{28,4},{1,25},{... | collective-permute-start | bytes 589832 | tf_op jit(solution)/shard_map/ppermute | solution.py:193
  17.7 0.2 collective-permute-start.5
  18.0 0.3 collective-permute-start.4
  18.2 4.3 %collective-permute-done.6.refs_3_ = bf16[2,2,96,256]{3,2,1,0:T(8,128)(2,1)S(1)} collective-permute-done((bf16[2,2,96,256]{3,2,1,0:T(8,128)(2,1)S(1)}, bf16[2,2,96,256]{3,2,1,0:T(8,128)(2,1)S(1)}, u32[]{:S(2)}, u32[]{:S(2)}) %collective-permute-start.6) | collective-permute-done | bytes 196640 | tf_op jit(solution)/shard_map/ppermute | solution.py:193
  22.5 3.1 %collective-permute-done.5.refs_2_ = bf16[2,2,96,256]{3,2,1,0:T(8,128)(2,1)S(1)} collective-permute-done((bf16[2,2,96,256]{3,2,1,0:T(8,128)(2,1)S(1)}, bf16[2,2,96,256]{3,2,1,0:T(8,128)(2,1)S(1)}, u32[]{:S(2)}, u32[]{:S(2)}) %collective-permute-start.5) | collective-permute-done | bytes 196640 | tf_op jit(solution)/shard_map/ppermute | solution.py:193
  25.6 0.0 collective-permute-done.4.refs_1_
  25.6 0.6 %collect.1.refs_1_ = bf16[2,768,256]{2,1,0:T(8,128)(2,1)S(1)} custom-call(s32[6]{0:T(128)S(1)} %pad_add_fusion.refs_0_.where_ref, bf16[2,2,96,256]{3,2,1,0:T(8,128)(2,1)S(1)} %pack.1.refs_0_, bf16[2,2,96,256]{3,2,1,0:T(8,128)(2,1)S(1)} %collective-permute-done.4.refs_1_, bf16[2,2,96,256]{3,2,1,0:T(8,128)(2,1)S(1)} %collective-permute-done.5.refs_2_, ...), custom_call_target="tpu_custom_call" | custom-call | tf_op jit(solution)/shard_map/collect/pallas_call | solution.py:182
  26.2 0.5 %collective-permute-start.7 = (bf16[2,768,256]{2,1,0:T(8,128)(2,1)S(1)}, bf16[2,768,256]{2,1,0:T(8,128)(2,1)S(1)}, u32[]{:S(2)}, u32[]{:S(2)}) collective-permute-start(bf16[2,768,256]{2,1,0:T(8,128)(2,1)S(1)} %collect.1.refs_1_), channel_id=1, source_target_pairs={{0,4},{4,0},{8,12},{12,8},{16,20},{20,16},{24,28},{28,24},{1,5},{5... | collective-permute-start | bytes 2359304 | tf_op jit(solution)/shard_map/ppermute | solution.py:193
  26.7 2.2 %correlate.1.refs_2_ = f32[2,4,8,128,128]{4,3,2,1,0:T(8,128)S(1)} custom-call(s32[6]{0:T(128)S(1)} %pad_add_fusion.refs_0_.where_ref, bf16[2,768,256]{2,1,0:T(8,128)(2,1)S(1)} %collect.1.refs_1_), custom_call_target="tpu_custom_call" | custom-call | flops 1073741824 | tf_op jit(solution)/shard_map/correlate/pallas_call | solution.py:133
  28.9 0.0 collective-permute-done.7.refs_1_
  28.9 3.4 %correlate_add.1 = f32[2,4,8,128,128]{4,3,2,1,0:T(8,128)} custom-call(s32[6]{0:T(128)S(1)} %pad_add_fusion.refs_0_.where_ref, bf16[2,768,256]{2,1,0:T(8,128)(2,1)S(1)} %collective-permute-done.7.refs_1_, f32[2,4,8,128,128]{4,3,2,1,0:T(8,128)S(1)} %correlate.1.refs_2_), custom_call_target="tpu_custom_call" | custom-call | flops 1073741824 | tf_op jit(solution)/shard_map/correlate_add/pallas_call | solution.py:133
Async XLA Ops:
  0.0 11.9 %copy-start = (s32[8,2]{0,1:T(2,128)S(1)}, s32[8,2]{0,1:T(2,128)}, u32[]{:S(2)}) copy-start(s32[8,2]{0,1:T(2,128)} %param.5) | copy-start | bytes 196
  0.0 0.9 %copy-start.1 = (bf16[64,2,2,96]{3,2,1,0:T(2,128)(2,1)S(1)}, bf16[64,2,2,96]{3,2,1,0:T(2,128)(2,1)}, u32[]{:S(2)}) copy-start(bf16[64,2,2,96]{3,2,1,0:T(2,128)(2,1)} %spectra_ref.1) | copy-start | bytes 147460
  0.9 0.7 %copy-start.2 = (s32[96]{0:T(128)S(1)}, s32[96]{0:T(128)}, u32[]{:S(2)}) copy-start(s32[96]{0:T(128)} %param.4) | copy-start | bytes 1156
  1.9 10.3 %collective-permute-start.3 = (bf16[96,256]{1,0:T(8,128)(2,1)S(1)}, bf16[96,256]{1,0:T(8,128)(2,1)S(1)}, u32[]{:S(2)}, u32[]{:S(2)}) collective-permute-start(bf16[96,256]{1,0:T(8,128)(2,1)S(1)} %whiten.1.refs_1_), channel_id=1, source_target_pairs={{7,4},{6,5},{5,6},{4,7},{15,12},{14,13},{13,14},{12,15},{23,20},{2... | collective-permute-start | bytes 147464 | tf_op jit(solution)/shard_map/ppermute | solution.py:205
  8.0 6.0 %collective-permute-start.2 = (bf16[96,256]{1,0:T(8,128)(2,1)S(1)}, bf16[96,256]{1,0:T(8,128)(2,1)S(1)}, u32[]{:S(2)}, u32[]{:S(2)}) collective-permute-start(bf16[96,256]{1,0:T(8,128)(2,1)S(1)} %whiten.1.refs_1_), channel_id=1, source_target_pairs={{4,0},{5,1},{6,2},{7,3},{3,4},{2,5},{1,6},{0,7},{12,8},{13,9},{14,... | collective-permute-start | bytes 147464 | tf_op jit(solution)/shard_map/ppermute | solution.py:205
  8.1 5.9 %collective-permute-start.1 = (bf16[96,256]{1,0:T(8,128)(2,1)S(1)}, bf16[96,256]{1,0:T(8,128)(2,1)S(1)}, u32[]{:S(2)}, u32[]{:S(2)}) collective-permute-start(bf16[96,256]{1,0:T(8,128)(2,1)S(1)} %whiten.1.refs_1_), channel_id=1, source_target_pairs={{5,0},{4,1},{7,2},{6,3},{2,4},{3,5},{0,6},{1,7},{13,8},{12,9},{15,... | collective-permute-start | bytes 147464 | tf_op jit(solution)/shard_map/ppermute | solution.py:205
  8.1 6.8 %collective-permute-start = (bf16[96,256]{1,0:T(8,128)(2,1)S(1)}, bf16[96,256]{1,0:T(8,128)(2,1)S(1)}, u32[]{:S(2)}, u32[]{:S(2)}) collective-permute-start(bf16[96,256]{1,0:T(8,128)(2,1)S(1)} %whiten.1.refs_1_), channel_id=1, source_target_pairs={{1,0},{0,1},{3,2},{2,3},{6,4},{7,5},{4,6},{5,7},{9,8},{8,9},{11,10... | collective-permute-start | bytes 147464 | tf_op jit(solution)/shard_map/ppermute | solution.py:205
  15.5 7.0 %collective-permute-start.6 = (bf16[2,2,96,256]{3,2,1,0:T(8,128)(2,1)S(1)}, bf16[2,2,96,256]{3,2,1,0:T(8,128)(2,1)S(1)}, u32[]{:S(2)}, u32[]{:S(2)}) collective-permute-start(bf16[2,2,96,256]{3,2,1,0:T(8,128)(2,1)S(1)} %pack.1.refs_0_), channel_id=1, source_target_pairs={{0,24},{4,28},{8,16},{12,20},{16,8},{20,12},{24,0},{28,4},{1,25},{... | collective-permute-start | bytes 589832 | tf_op jit(solution)/shard_map/ppermute | solution.py:193
  17.7 7.9 %collective-permute-start.5 = (bf16[2,2,96,256]{3,2,1,0:T(8,128)(2,1)S(1)}, bf16[2,2,96,256]{3,2,1,0:T(8,128)(2,1)S(1)}, u32[]{:S(2)}, u32[]{:S(2)}) collective-permute-start(bf16[2,2,96,256]{3,2,1,0:T(8,128)(2,1)S(1)} %pack.1.refs_0_), channel_id=1, source_target_pairs={{0,16},{4,20},{8,24},{12,28},{16,0},{20,4},{24,8},{28,12},{1,17},{... | collective-permute-start | bytes 589832 | tf_op jit(solution)/shard_map/ppermute | solution.py:193
  18.0 7.6 %collective-permute-start.4 = (bf16[2,2,96,256]{3,2,1,0:T(8,128)(2,1)S(1)}, bf16[2,2,96,256]{3,2,1,0:T(8,128)(2,1)S(1)}, u32[]{:S(2)}, u32[]{:S(2)}) collective-permute-start(bf16[2,2,96,256]{3,2,1,0:T(8,128)(2,1)S(1)} %pack.1.refs_0_), channel_id=1, source_target_pairs={{0,8},{4,12},{8,0},{12,4},{16,24},{20,28},{24,16},{28,20},{1,9},{5... | collective-permute-start | bytes 589832 | tf_op jit(solution)/shard_map/ppermute | solution.py:193
  26.2 2.6 %collective-permute-start.7 = (bf16[2,768,256]{2,1,0:T(8,128)(2,1)S(1)}, bf16[2,768,256]{2,1,0:T(8,128)(2,1)S(1)}, u32[]{:S(2)}, u32[]{:S(2)}) collective-permute-start(bf16[2,768,256]{2,1,0:T(8,128)(2,1)S(1)} %collect.1.refs_1_), channel_id=1, source_target_pairs={{0,4},{4,0},{8,12},{12,8},{16,20},{20,16},{24,28},{28,24},{1,5},{5... | collective-permute-start | bytes 2359304 | tf_op jit(solution)/shard_map/ppermute | solution.py:193

commit v7 on v6

--- a/solution.py
+++ b/solution.py
@@ -13,22 +13,23 @@
 EPSILON = 1e-06
 CORES = 2
 SMALL = 4 * 1024 * 1024
+VMEM = pl.BlockSpec(memory_space=pltpu.VMEM)
+SMEM = pl.BlockSpec(memory_space=pltpu.SMEM)
 COARSE = (-12, -4, 4, 12)
 FINE_PAIRS = ((-4, 0), (-1, 1), (-2, 2), (-3, 3))
 
 
-def whiten_kernel(spectra_ref, bad_ref, out_ref):
+def whiten_kernel(spectra_ref, keep_ref, out_ref):
     bins, hours, _, chans = spectra_ref.shape
     rows = bins * hours * 2
     values = spectra_ref[...].reshape(rows, chans).astype(jnp.float32)
     row = lax.broadcasted_iota(jnp.int32, (rows, chans), 0)
     hour = (row // 2) % hours
     squares = values * values
-    keep = (1 - bad_ref[...]).astype(jnp.float32)
     scale = jnp.zeros((rows, chans), jnp.float32)
     for h in range(hours):
         power = jnp.sum(jnp.where(hour == h, squares, 0.0), axis=0, keepdims=True) * (1.0 / (2 * bins))
-        scale = jnp.where(hour == h, lax.rsqrt(power + EPSILON) * keep, scale)
+        scale = jnp.where(hour == h, lax.rsqrt(power + EPSILON) * keep_ref[...], scale)
     white = (values * scale).astype(jnp.bfloat16)
     src = lax.broadcasted_iota(jnp.int32, (rows, rows), 0)
     dst = lax.broadcasted_iota(jnp.int32, (rows, rows), 1)
@@ -40,12 +41,15 @@
 
 def whiten(spectra, bad_channels):
     bins, hours, _, chans = spectra.shape
+    keep = (1 - bad_channels).astype(jnp.float32).reshape(1, chans)
     return pl.pallas_call(
         whiten_kernel,
         out_shape=jax.ShapeDtypeStruct((chans, bins * hours * 2), jnp.bfloat16),
+        in_specs=[VMEM, VMEM],
+        out_specs=VMEM,
         compiler_params=pltpu.CompilerParams(vmem_limit_bytes=SMALL),
         name="whiten",
-    )(spectra, bad_channels.reshape(1, chans))
+    )(spectra, keep)
 
 
 def turn_by(re, im, cos, sin, both):
@@ -118,10 +122,6 @@
         copy.wait()
 
 
-VMEM = pl.BlockSpec(memory_space=pltpu.VMEM)
-SMEM = pl.BlockSpec(memory_space=pltpu.SMEM)
-
-
 def correlate(spectra, where, tiles, hours, partial=None):
     groups, _, lanes = spectra.shape
     fine = 2 * len(FINE_PAIRS)
@@ -148,19 +148,17 @@
     )(where, spectra, *more)
 
 
-def pack_kernel(windows, sources, where_ref, *refs):
+def pack_kernel(choices, where_ref, *refs):
     out_ref = refs[-1]
     first = where_ref[1] == 0
-    for w in range(windows):
-        for core in range(CORES):
-            one, two = sources[0][w, core], sources[1][w, core]
-            out_ref[w, core] = jnp.where(first, refs[one][...], refs[two][...])
-
-
-def pack(where, windows, sources, blocks):
-    return pl.pallas_call(
-        lambda *refs: pack_kernel(windows, sources, *refs),
-        out_shape=jax.ShapeDtypeStruct((windows, CORES, *blocks[0].shape), jnp.bfloat16),
+    for slot, (one, two) in enumerate(choices):
+        out_ref[slot] = jnp.where(first, refs[one][...], refs[two][...])
+
+
+def pack(where, choices, blocks):
+    return pl.pallas_call(
+        lambda *refs: pack_kernel(choices, *refs),
+        out_shape=jax.ShapeDtypeStruct((len(choices), *blocks[0].shape), jnp.bfloat16),
         in_specs=[SMEM] + [VMEM] * len(blocks),
         out_specs=VMEM,
         compiler_params=pltpu.CompilerParams(vmem_limit_bytes=SMALL),
@@ -193,37 +191,26 @@
     return lax.ppermute(array, "chan", [(i, i ^ k) for i in range(lax.axis_size("chan"))])
 
 
-def fetch(block, sources):
+def fetch(block, offsets):
     chans, groups = lax.axis_size("chan"), lax.axis_size("tm")
-    pairs = []
-    for chan in range(chans):
-        for tm in range(groups):
-            if chan % CORES in sources:
-                k, core = sources[chan % CORES]
-                source = chan // CORES * CORES + core
-                pairs.append((source * groups + (tm ^ k), chan * groups + tm))
+    pairs = [
+        (chan * groups + (tm ^ offsets[chan % CORES]), chan * groups + tm)
+        for chan in range(chans)
+        for tm in range(groups)
+        if chan % CORES in offsets
+    ]
     return lax.ppermute(block, ("chan", "tm"), pairs)
 
 
 def own_windows(white, where):
     groups = lax.axis_size("tm")
     windows = groups // 2
-    near, far = list(range(1, windows)), list(range(windows, groups))
-    steps = [((k, 0), (far[i], 1)) for i, k in enumerate(near)]
-    steps += [((k, 1), (far[i], 0)) for i, k in enumerate(near + [0])]
-    steps += [(None, (far[-1], 1))]
-    blocks = [white]
-    at = ({(0, 0): 0}, {})
-    for step in steps:
-        sources = {core: source for core, source in enumerate(step) if source}
-        for core, source in sources.items():
-            at[core][source] = len(blocks)
-        blocks.append(fetch(white, sources))
-    sources = tuple(
-        {(w, core): at[own][(first + w, core)] for w in range(windows) for core in range(CORES)}
-        for own, first in enumerate((0, windows))
-    )
-    return pack(where, windows, sources, blocks)
+    both = pack(where, [(0, 1), (1, 0)], [white, swap(white, 1)])
+    blocks = [both]
+    for k in range(windows):
+        offsets = {1: windows + k} if k + 1 == windows else {0: k + 1, 1: windows + k}
+        blocks.append(fetch(both, offsets))
+    return pack(where, [(w, w + 1) for w in range(windows)], blocks)
 
 
 def per_device(spectra, bad_channels, tile_list):

time: 32.5 us -> 31.2 us (0.960); the launches traced: 32.3 us -> 30.7 us
  starting transfers between devices: 13.1 us -> 9.36 us
  waiting for transfers between devices: 10.1 us -> 11.7 us
  other arithmetic: 0.08 us -> 0.75 us
  local copies, waits for them, and re-layouts: 1.76 us -> 1.09 us
  Pallas kernels: 7.16 us -> 7.72 us
    ppermute x4 -> x2, starting transfers between devices: 9.92 us -> 6.46 us  [fetch(): return lax.ppermute(block, ('chan', 'tm'), pairs)]
    ppermute x4 -> x2, waiting for transfers between devices: 2.72 us -> 5.18 us  [fetch(): return lax.ppermute(block, ('chan', 'tm'), pairs)]
    ppermute x4 -> x5, waiting for transfers between devices: 7.4 us -> 6.48 us  [swap(): lax.ppermute(array, 'chan', [(i, i ^ k) for i in range(lax.axis_size('cha...]
    reshape x0 -> x1, other arithmetic: none -> 0.67 us  [whiten(): keep = (1 - bad_channels).astype(jnp.float32).reshape(1, chans)]
    unnamed x6 -> x4, local copies, waits for them, and re-layouts: 1.51 us -> 0.84 us
    pallas_call x1 -> x2, Pallas kernels: 0.56 us -> 1.11 us  [pack(): pl.pallas_call(lambda *refs: pack_kernel(choices, *refs), out_shape=jax.S...]
    ppermute x4 -> x5, starting transfers between devices: 3.17 us -> 2.91 us  [swap(): lax.ppermute(array, 'chan', [(i, i ^ k) for i in range(lax.axis_size('cha...]
  transfers between devices with their start and end apart: 8 -> 7, of which waited for: 4 -> 6; matrix products, arithmetic and copies ran while one was open for 1% -> 1% of each run, Pallas kernels for 7% -> 7%
where the time goes in v7:
time: 31.2 us; the launch traced here: 30.7 us
  waiting for transfers between devices  11.7 us (38%)
  starting transfers between devices  9.36 us (30%)
  Pallas kernels  7.72 us (25%)
  local copies, waits for them, and re-layouts  1.09 us (3%)
  other arithmetic  0.75 us (2%)
    ppermute x5, waiting for transfers between devices, swap(): lax.ppermute(array, 'chan', [(i, i ^ k) for i in range(lax.axis_size('cha...  6.48 us
    ppermute x2, starting transfers between devices, fetch(): return lax.ppermute(block, ('chan', 'tm'), pairs)  6.46 us
    pallas_call x2, Pallas kernels, correlate(): pl.pallas_call(lambda *refs: correlate_kernel(norm, add, tiles, *refs), o...  5.59 us
    ppermute x2, waiting for transfers between devices, fetch(): return lax.ppermute(block, ('chan', 'tm'), pairs)  5.18 us
    ppermute x5, starting transfers between devices, swap(): lax.ppermute(array, 'chan', [(i, i ^ k) for i in range(lax.axis_size('cha...  2.91 us
    pallas_call x2, Pallas kernels, pack(): pl.pallas_call(lambda *refs: pack_kernel(choices, *refs), out_shape=jax.S...  1.11 us
    unnamed x4, local copies, waits for them, and re-layouts  0.84 us
    reshape x1, other arithmetic, whiten(): keep = (1 - bad_channels).astype(jnp.float32).reshape(1, chans)  0.67 us
  transfers between devices with their start and end apart: 7, of which 6 were waited for; matrix products, arithmetic and copies ran while one was open for 1% of the time, Pallas kernels for 7%

profile of v7, /device:TPU:1, one launch (start us, length us, event | category | flops | bytes accessed | tf_op | source)
XLA Modules:
  0.0 30.7 jit_solution(7362166399343916058)
XLA Ops:
  0.0 0.0 copy-start
  0.0 0.7 %convert_bitcast_fusion.keep_ref = f32[1,96]{1,0:T(1,128)S(1)} fusion(s32[96]{0:T(128)} %param.4), kind=kLoop, calls=%fused_computation.1 | loop fusion | flops 192 | bytes 768 | tf_op jit(solution)/shard_map/reshape | solution.py:44
  0.7 0.0 copy-start.1
  0.7 0.8 %copy-done.1 = bf16[64,2,2,96]{3,2,1,0:T(2,128)(2,1)S(1)} copy-done((bf16[64,2,2,96]{3,2,1,0:T(2,128)(2,1)S(1)}, bf16[64,2,2,96]{3,2,1,0:T(2,128)(2,1)}, u32[]{:S(2)}) %copy-start.1) | copy-done | bytes 49176
  1.5 0.4 %whiten.1.refs_1_ = bf16[96,256]{1,0:T(8,128)(2,1)S(1)} custom-call(bf16[64,2,2,96]{3,2,1,0:T(2,128)(2,1)S(1)} %copy-done.1, f32[1,96]{1,0:T(1,128)S(1)} %convert_bitcast_fusion.keep_ref), custom_call_target="tpu_custom_call" | custom-call | tf_op jit(solution)/shard_map/whiten/pallas_call | solution.py:45
  1.9 0.1 collective-permute-start
  2.1 0.0 copy-done
  2.1 0.1 constant_dynamic-slice_fusion
  2.1 0.1 copy.4
  2.2 0.1 reshape.9
  2.3 0.1 pad_add_fusion.refs_0_.where_ref
  2.4 0.8 %collective-permute-done.refs_2_ = bf16[96,256]{1,0:T(8,128)(2,1)S(1)} collective-permute-done((bf16[96,256]{1,0:T(8,128)(2,1)S(1)}, bf16[96,256]{1,0:T(8,128)(2,1)S(1)}, u32[]{:S(2)}, u32[]{:S(2)}) %collective-permute-start) | collective-permute-done | bytes 49184 | tf_op jit(solution)/shard_map/ppermute | solution.py:191
  3.2 0.6 %pack.2.refs_1_ = bf16[2,96,256]{2,1,0:T(8,128)(2,1)S(1)} custom-call(s32[6]{0:T(128)S(1)} %pad_add_fusion.refs_0_.where_ref, bf16[96,256]{1,0:T(8,128)(2,1)S(1)} %whiten.1.refs_1_, bf16[96,256]{1,0:T(8,128)(2,1)S(1)} %collective-permute-done.refs_2_), custom_call_target="tpu_custom_call" | custom-call | tf_op jit(solution)/shard_map/pack/pallas_call | solution.py:159
  3.8 6.4 %collective-permute-start.2 = (bf16[2,96,256]{2,1,0:T(8,128)(2,1)S(1)}, bf16[2,96,256]{2,1,0:T(8,128)(2,1)S(1)}, u32[]{:S(2)}, u32[]{:S(2)}) collective-permute-start(bf16[2,96,256]{2,1,0:T(8,128)(2,1)S(1)} %pack.2.refs_1_), channel_id=1, source_target_pairs={{7,4},{6,5},{5,6},{4,7},{15,12},{14,13},{13,14},{12,15},{23,20},{2... | collective-permute-start | bytes 294920 | tf_op jit(solution)/shard_map/ppermute | solution.py:202
  10.2 0.1 collective-permute-start.1
  10.3 2.8 %collective-permute-done.2.refs_3_ = bf16[2,96,256]{2,1,0:T(8,128)(2,1)S(1)} collective-permute-done((bf16[2,96,256]{2,1,0:T(8,128)(2,1)S(1)}, bf16[2,96,256]{2,1,0:T(8,128)(2,1)S(1)}, u32[]{:S(2)}, u32[]{:S(2)}) %collective-permute-start.2) | collective-permute-done | bytes 98336 | tf_op jit(solution)/shard_map/ppermute | solution.py:202
  13.1 2.4 %collective-permute-done.1.refs_2_ = bf16[2,96,256]{2,1,0:T(8,128)(2,1)S(1)} collective-permute-done((bf16[2,96,256]{2,1,0:T(8,128)(2,1)S(1)}, bf16[2,96,256]{2,1,0:T(8,128)(2,1)S(1)}, u32[]{:S(2)}, u32[]{:S(2)}) %collective-permute-start.1) | collective-permute-done | bytes 98336 | tf_op jit(solution)/shard_map/ppermute | solution.py:202
  15.5 0.6 %pack.3.refs_0_ = bf16[2,2,96,256]{3,2,1,0:T(8,128)(2,1)S(1)} custom-call(s32[6]{0:T(128)S(1)} %pad_add_fusion.refs_0_.where_ref, bf16[2,96,256]{2,1,0:T(8,128)(2,1)S(1)} %pack.2.refs_1_, bf16[2,96,256]{2,1,0:T(8,128)(2,1)S(1)} %collective-permute-done.1.refs_2_, bf16[2,96,256]{2,1,0:T(8,128)(2,1)S(1)} %collective-permute-done.2.refs_3_), custom_call_target="tpu_custom_call" | custom-call | tf_op jit(solution)/shard_map/pack/pallas_call | solution.py:159
  16.0 2.2 %collective-permute-start.5 = (bf16[2,2,96,256]{3,2,1,0:T(8,128)(2,1)S(1)}, bf16[2,2,96,256]{3,2,1,0:T(8,128)(2,1)S(1)}, u32[]{:S(2)}, u32[]{:S(2)}) collective-permute-start(bf16[2,2,96,256]{3,2,1,0:T(8,128)(2,1)S(1)} %pack.3.refs_0_), channel_id=1, source_target_pairs={{0,24},{4,28},{8,16},{12,20},{16,8},{20,12},{24,0},{28,4},{1,25},{... | collective-permute-start | bytes 589832 | tf_op jit(solution)/shard_map/ppermute | solution.py:191
  18.3 0.2 collective-permute-start.4
  18.5 0.3 collective-permute-start.3
  18.7 3.7 %collective-permute-done.5.refs_3_ = bf16[2,2,96,256]{3,2,1,0:T(8,128)(2,1)S(1)} collective-permute-done((bf16[2,2,96,256]{3,2,1,0:T(8,128)(2,1)S(1)}, bf16[2,2,96,256]{3,2,1,0:T(8,128)(2,1)S(1)}, u32[]{:S(2)}, u32[]{:S(2)}) %collective-permute-start.5) | collective-permute-done | bytes 196640 | tf_op jit(solution)/shard_map/ppermute | solution.py:191
  22.4 1.9 %collective-permute-done.4.refs_2_ = bf16[2,2,96,256]{3,2,1,0:T(8,128)(2,1)S(1)} collective-permute-done((bf16[2,2,96,256]{3,2,1,0:T(8,128)(2,1)S(1)}, bf16[2,2,96,256]{3,2,1,0:T(8,128)(2,1)S(1)}, u32[]{:S(2)}, u32[]{:S(2)}) %collective-permute-start.4) | collective-permute-done | bytes 196640 | tf_op jit(solution)/shard_map/ppermute | solution.py:191
  24.3 0.0 collective-permute-done.3.refs_1_
  24.3 0.6 %collect.1.refs_1_ = bf16[2,768,256]{2,1,0:T(8,128)(2,1)S(1)} custom-call(s32[6]{0:T(128)S(1)} %pad_add_fusion.refs_0_.where_ref, bf16[2,2,96,256]{3,2,1,0:T(8,128)(2,1)S(1)} %pack.3.refs_0_, bf16[2,2,96,256]{3,2,1,0:T(8,128)(2,1)S(1)} %collective-permute-done.3.refs_1_, bf16[2,2,96,256]{3,2,1,0:T(8,128)(2,1)S(1)} %collective-permute-done.4.refs_2_, ...), custom_call_target="tpu_custom_call" | custom-call | tf_op jit(solution)/shard_map/collect/pallas_call | solution.py:180
  24.9 0.1 collective-permute-start.6
  25.0 2.2 %correlate.1.refs_2_ = f32[2,4,8,128,128]{4,3,2,1,0:T(8,128)S(1)} custom-call(s32[6]{0:T(128)S(1)} %pad_add_fusion.refs_0_.where_ref, bf16[2,768,256]{2,1,0:T(8,128)(2,1)S(1)} %collect.1.refs_1_), custom_call_target="tpu_custom_call" | custom-call | flops 1073741824 | tf_op jit(solution)/shard_map/correlate/pallas_call | solution.py:133
  27.1 0.1 collective-permute-done.6.refs_1_
  27.2 3.4 %correlate_add.1 = f32[2,4,8,128,128]{4,3,2,1,0:T(8,128)} custom-call(s32[6]{0:T(128)S(1)} %pad_add_fusion.refs_0_.where_ref, bf16[2,768,256]{2,1,0:T(8,128)(2,1)S(1)} %collective-permute-done.6.refs_1_, f32[2,4,8,128,128]{4,3,2,1,0:T(8,128)S(1)} %correlate.1.refs_2_), custom_call_target="tpu_custom_call" | custom-call | flops 1073741824 | tf_op jit(solution)/shard_map/correlate_add/pallas_call | solution.py:133
Async XLA Ops:
  0.0 2.1 %copy-start = (s32[8,2]{0,1:T(2,128)S(1)}, s32[8,2]{0,1:T(2,128)}, u32[]{:S(2)}) copy-start(s32[8,2]{0,1:T(2,128)} %param.5) | copy-start | bytes 196
  0.7 0.8 %copy-start.1 = (bf16[64,2,2,96]{3,2,1,0:T(2,128)(2,1)S(1)}, bf16[64,2,2,96]{3,2,1,0:T(2,128)(2,1)}, u32[]{:S(2)}) copy-start(bf16[64,2,2,96]{3,2,1,0:T(2,128)(2,1)} %spectra_ref.1) | copy-start | bytes 147460
  1.9 1.3 %collective-permute-start = (bf16[96,256]{1,0:T(8,128)(2,1)S(1)}, bf16[96,256]{1,0:T(8,128)(2,1)S(1)}, u32[]{:S(2)}, u32[]{:S(2)}) collective-permute-start(bf16[96,256]{1,0:T(8,128)(2,1)S(1)} %whiten.1.refs_1_), channel_id=1, source_target_pairs={{0,4},{4,0},{8,12},{12,8},{16,20},{20,16},{24,28},{28,24},{1,5},{5... | collective-permute-start | bytes 147464 | tf_op jit(solution)/shard_map/ppermute | solution.py:191
  3.8 9.3 %collective-permute-start.2 = (bf16[2,96,256]{2,1,0:T(8,128)(2,1)S(1)}, bf16[2,96,256]{2,1,0:T(8,128)(2,1)S(1)}, u32[]{:S(2)}, u32[]{:S(2)}) collective-permute-start(bf16[2,96,256]{2,1,0:T(8,128)(2,1)S(1)} %pack.2.refs_1_), channel_id=1, source_target_pairs={{7,4},{6,5},{5,6},{4,7},{15,12},{14,13},{13,14},{12,15},{23,20},{2... | collective-permute-start | bytes 294920 | tf_op jit(solution)/shard_map/ppermute | solution.py:202
  10.2 5.3 %collective-permute-start.1 = (bf16[2,96,256]{2,1,0:T(8,128)(2,1)S(1)}, bf16[2,96,256]{2,1,0:T(8,128)(2,1)S(1)}, u32[]{:S(2)}, u32[]{:S(2)}) collective-permute-start(bf16[2,96,256]{2,1,0:T(8,128)(2,1)S(1)} %pack.2.refs_1_), channel_id=1, source_target_pairs={{1,0},{0,1},{3,2},{2,3},{6,4},{7,5},{4,6},{5,7},{9,8},{8,9},{11,10... | collective-permute-start | bytes 294920 | tf_op jit(solution)/shard_map/ppermute | solution.py:202
  16.0 6.4 %collective-permute-start.5 = (bf16[2,2,96,256]{3,2,1,0:T(8,128)(2,1)S(1)}, bf16[2,2,96,256]{3,2,1,0:T(8,128)(2,1)S(1)}, u32[]{:S(2)}, u32[]{:S(2)}) collective-permute-start(bf16[2,2,96,256]{3,2,1,0:T(8,128)(2,1)S(1)} %pack.3.refs_0_), channel_id=1, source_target_pairs={{0,24},{4,28},{8,16},{12,20},{16,8},{20,12},{24,0},{28,4},{1,25},{... | collective-permute-start | bytes 589832 | tf_op jit(solution)/shard_map/ppermute | solution.py:191
  18.3 6.0 %collective-permute-start.4 = (bf16[2,2,96,256]{3,2,1,0:T(8,128)(2,1)S(1)}, bf16[2,2,96,256]{3,2,1,0:T(8,128)(2,1)S(1)}, u32[]{:S(2)}, u32[]{:S(2)}) collective-permute-start(bf16[2,2,96,256]{3,2,1,0:T(8,128)(2,1)S(1)} %pack.3.refs_0_), channel_id=1, source_target_pairs={{0,16},{4,20},{8,24},{12,28},{16,0},{20,4},{24,8},{28,12},{1,17},{... | collective-permute-start | bytes 589832 | tf_op jit(solution)/shard_map/ppermute | solution.py:191
  18.5 5.8 %collective-permute-start.3 = (bf16[2,2,96,256]{3,2,1,0:T(8,128)(2,1)S(1)}, bf16[2,2,96,256]{3,2,1,0:T(8,128)(2,1)S(1)}, u32[]{:S(2)}, u32[]{:S(2)}) collective-permute-start(bf16[2,2,96,256]{3,2,1,0:T(8,128)(2,1)S(1)} %pack.3.refs_0_), channel_id=1, source_target_pairs={{0,8},{4,12},{8,0},{12,4},{16,24},{20,28},{24,16},{28,20},{1,9},{5... | collective-permute-start | bytes 589832 | tf_op jit(solution)/shard_map/ppermute | solution.py:191
  24.9 2.4 %collective-permute-start.6 = (bf16[2,768,256]{2,1,0:T(8,128)(2,1)S(1)}, bf16[2,768,256]{2,1,0:T(8,128)(2,1)S(1)}, u32[]{:S(2)}, u32[]{:S(2)}) collective-permute-start(bf16[2,768,256]{2,1,0:T(8,128)(2,1)S(1)} %collect.1.refs_1_), channel_id=1, source_target_pairs={{0,4},{4,0},{8,12},{12,8},{16,20},{20,16},{24,28},{28,24},{1,5},{5... | collective-permute-start | bytes 2359304 | tf_op jit(solution)/shard_map/ppermute | solution.py:191

commit v8 on v4

--- a/solution.py
+++ b/solution.py
@@ -11,26 +11,37 @@
 LAGS = 32
 TILE = 128
 EPSILON = 1e-06
+SMALL = 4 * 1024 * 1024
+VMEM = pl.BlockSpec(memory_space=pltpu.VMEM)
+SMEM = pl.BlockSpec(memory_space=pltpu.SMEM)
 COARSE = (-12, -4, 4, 12)
 FINE_PAIRS = ((-4, 0), (-1, 1), (-2, 2), (-3, 3))
 
 
-def whiten_kernel(spectra_ref, bad_ref, out_ref):
+def whiten_kernel(spectra_hbm, bad_hbm, out_ref, spectra_ref, bad_ref, sems):
+    copies = [
+        pltpu.make_async_copy(spectra_hbm, spectra_ref, sems.at[0]),
+        pltpu.make_async_copy(bad_hbm, bad_ref, sems.at[1]),
+    ]
+    for copy in copies:
+        copy.start()
     bins, hours, _, chans = spectra_ref.shape
     rows = bins * hours * 2
-    values = spectra_ref[...].reshape(rows, chans).astype(jnp.float32)
     row = lax.broadcasted_iota(jnp.int32, (rows, chans), 0)
     hour = (row // 2) % hours
+    src = lax.broadcasted_iota(jnp.int32, (rows, rows), 0)
+    dst = lax.broadcasted_iota(jnp.int32, (rows, rows), 1)
+    move = jnp.where((src % 2) * (rows // 2) + src // 2 == dst, 1.0, 0.0).astype(jnp.bfloat16)
+    for copy in copies:
+        copy.wait()
+    values = spectra_ref[...].reshape(rows, chans).astype(jnp.float32)
+    keep = (1 - bad_ref[...]).astype(jnp.float32)
     squares = values * values
-    keep = (1 - bad_ref[...]).astype(jnp.float32)
     scale = jnp.zeros((rows, chans), jnp.float32)
     for h in range(hours):
         power = jnp.sum(jnp.where(hour == h, squares, 0.0), axis=0, keepdims=True) * (1.0 / (2 * bins))
         scale = jnp.where(hour == h, lax.rsqrt(power + EPSILON) * keep, scale)
     white = (values * scale).astype(jnp.bfloat16)
-    src = lax.broadcasted_iota(jnp.int32, (rows, rows), 0)
-    dst = lax.broadcasted_iota(jnp.int32, (rows, rows), 1)
-    move = jnp.where((src % 2) * (rows // 2) + src // 2 == dst, 1.0, 0.0).astype(jnp.bfloat16)
     out_ref[...] = lax.dot_general(
         white, move, (((0,), (0,)), ((), ())), preferred_element_type=jnp.float32
     ).astype(jnp.bfloat16)
@@ -38,11 +49,21 @@
 
 def whiten(spectra, bad_channels):
     bins, hours, _, chans = spectra.shape
+    spectra = pltpu.with_memory_space_constraint(spectra, pltpu.HBM)
+    bad_channels = pltpu.with_memory_space_constraint(bad_channels.reshape(1, chans), pltpu.HBM)
     return pl.pallas_call(
         whiten_kernel,
         out_shape=jax.ShapeDtypeStruct((chans, bins * hours * 2), jnp.bfloat16),
+        in_specs=[pl.BlockSpec(memory_space=pltpu.HBM)] * 2,
+        out_specs=VMEM,
+        scratch_shapes=[
+            pltpu.VMEM(spectra.shape, spectra.dtype),
+            pltpu.VMEM((1, chans), bad_channels.dtype),
+            pltpu.SemaphoreType.DMA((2,)),
+        ],
+        compiler_params=pltpu.CompilerParams(vmem_limit_bytes=SMALL),
         name="whiten",
-    )(spectra, bad_channels.reshape(1, chans))
+    )(spectra, bad_channels)
 
 
 def turn_by(re, im, cos, sin, both):
@@ -129,20 +150,22 @@
     shape = (tiles, len(COARSE), fine, TILE, TILE)
     norm = 1.0 / math.sqrt(F * hours)
     slots = min(tiles, 2)
-    vmem = pl.BlockSpec(memory_space=pltpu.VMEM)
+    chans = lax.axis_size("chan") * rows
+    turned = slots * (len(COARSE) + fine) * TILE * groups * lanes
+    scratch = 2 * (groups * chans * lanes + turned) + 4 * math.prod(shape)
     out = pl.pallas_call(
         lambda *refs: correlate_kernel(norm, *refs),
         out_shape=jax.ShapeDtypeStruct(shape, jnp.float32),
-        in_specs=[pl.BlockSpec(memory_space=pltpu.SMEM)] + [vmem] * len(pieces),
+        in_specs=[SMEM] + [VMEM] * len(pieces),
         out_specs=pl.BlockSpec(memory_space=pl.ANY),
         scratch_shapes=[
-            pltpu.VMEM((groups, lax.axis_size("chan") * rows, lanes), jnp.bfloat16),
+            pltpu.VMEM((groups, chans, lanes), jnp.bfloat16),
             pltpu.VMEM((slots, len(COARSE) * TILE, groups * lanes), jnp.bfloat16),
             pltpu.VMEM((slots, fine * TILE, groups * lanes), jnp.bfloat16),
             pltpu.VMEM(shape, jnp.float32),
             pltpu.SemaphoreType.DMA,
         ],
-        compiler_params=pltpu.CompilerParams(vmem_limit_bytes=40 * 1024 * 1024),
+        compiler_params=pltpu.CompilerParams(vmem_limit_bytes=scratch + SMALL),
         name="correlate",
     )(where, *pieces)
     return out.reshape(tiles, LAGS, TILE, TILE)
@@ -161,10 +184,30 @@
     return [pieces[k] for k in sorted(pieces)]
 
 
+def stack_kernel(one_ref, two_ref, out_ref):
+    depth = one_ref.shape[0]
+    out_ref[:depth] = one_ref[...]
+    out_ref[depth:] = two_ref[...]
+
+
+def stack(one, two):
+    return pl.pallas_call(
+        stack_kernel,
+        out_shape=jax.ShapeDtypeStruct((2 * one.shape[0], *one.shape[1:]), one.dtype),
+        in_specs=[VMEM, VMEM],
+        out_specs=VMEM,
+        compiler_params=pltpu.CompilerParams(vmem_limit_bytes=SMALL),
+        name="stack",
+    )(one, two)
+
+
 def gather(white):
-    near = [white] + [swap(white, "tm", k) for k in (1,)]
-    far = [swap(white, "tm", k) for k in range(2, lax.axis_size("tm"))]
-    return between_chips(jnp.stack(near)) + between_chips(jnp.stack(far))
+    half = white[None]
+    k = lax.axis_size("tm") // 2
+    while k > 1:
+        half = stack(half, swap(half, "tm", k))
+        k //= 2
+    return between_chips(half) + between_chips(swap(half, "tm", 1))
 
 
 def per_device(spectra, bad_channels, tile_list):

time: 28.1 us -> 28.9 us (1.028)
  waiting for transfers between devices: 1.28 us -> 3.04 us
  other arithmetic: 0.92 us -> 0.07 us
  Pallas kernels: 6.87 us -> 6.25 us
  starting transfers between devices: 18.4 us -> 19 us
    ppermute x17 -> x16, waiting for transfers between devices: 1.28 us -> 3.04 us  [swap(): lax.ppermute(array, axis, [(i, i ^ k) for i in range(lax.axis_size(axis))])]
    another operation x2 -> x0, other arithmetic: 0.85 us -> none  [gather(): return between_chips(jnp.stack(near)) + between_chips(jnp.stack(far))]
    pallas_call x1, Pallas kernels: 1.9 us -> 1.29 us  [whiten(): pl.pallas_call(whiten_kernel, out_shape=jax.ShapeDtypeStruct((chans, bins...]
    ppermute x17 -> x16, starting transfers between devices: 18.4 us -> 19 us  [swap(): lax.ppermute(array, axis, [(i, i ^ k) for i in range(lax.axis_size(axis))])]
  transfers between devices with their start and end apart: 17 -> 16, of which waited for: 5 -> 7; matrix products, arithmetic and copies ran while one was open for 4% -> 1% of each run, Pallas kernels for 0% -> 0%
where the time goes in v8:
time: 28.9 us; the launch traced here: 28.6 us
  starting transfers between devices  19 us (66%)
  Pallas kernels  6.25 us (22%)
  waiting for transfers between devices  3.04 us (11%)
    ppermute x16, starting transfers between devices, swap(): lax.ppermute(array, axis, [(i, i ^ k) for i in range(lax.axis_size(axis))])  19 us
    pallas_call x1, Pallas kernels, correlate(): pl.pallas_call(lambda *refs: correlate_kernel(norm, *refs), out_shape=jax...  4.95 us
    ppermute x16, waiting for transfers between devices, swap(): lax.ppermute(array, axis, [(i, i ^ k) for i in range(lax.axis_size(axis))])  3.04 us
    pallas_call x1, Pallas kernels, whiten(): pl.pallas_call(whiten_kernel, out_shape=jax.ShapeDtypeStruct((chans, bins...  1.29 us
  transfers between devices with their start and end apart: 16, of which 7 were waited for; matrix products, arithmetic and copies ran while one was open for 1% of the time, Pallas kernels for 0%

profile of v8, /device:TPU:1, one launch (start us, length us, event | category | flops | bytes accessed | tf_op | source)
XLA Modules:
  0.0 28.6 jit_solution(17560225287802957673)
XLA Ops:
  0.0 0.0 copy-start
  0.0 1.3 %whiten.1 = bf16[96,256]{1,0:T(8,128)(2,1)S(1)} custom-call(bf16[64,2,2,96]{3,2,1,0:T(2,128)(2,1)} %spectra_hbm.1, s32[1,96]{1,0:T(1,128)} %bitcast.6), custom_call_target="tpu_custom_call" | custom-call | tf_op jit(solution)/shard_map/whiten/pallas_call | solution.py:54
  1.3 3.2 %collective-permute-start = (bf16[1,96,256]{2,1,0:T(8,128)(2,1)S(1)}, bf16[1,96,256]{2,1,0:T(8,128)(2,1)S(1)}, u32[]{:S(2)}, u32[]{:S(2)}) collective-permute-start(bf16[1,96,256]{2,1,0:T(8,128)(2,1)S(1)} %bitcast.4), channel_id=1, source_target_pairs={{0,2},{1,3},{2,0},{3,1},{4,6},{5,7},{6,4},{7,5},{8,10},{9,11},{10,... | collective-permute-start | bytes 147464 | tf_op jit(solution)/shard_map/ppermute | solution.py:175
  4.5 1.5 %collective-permute-done.two_ref = bf16[1,96,256]{2,1,0:T(8,128)(2,1)S(1)} collective-permute-done((bf16[1,96,256]{2,1,0:T(8,128)(2,1)S(1)}, bf16[1,96,256]{2,1,0:T(8,128)(2,1)S(1)}, u32[]{:S(2)}, u32[]{:S(2)}) %collective-permute-start) | collective-permute-done | bytes 49184 | tf_op jit(solution)/shard_map/ppermute | solution.py:175
  6.0 1.5 %collective-permute-start.8 = (bf16[2,96,256]{2,1,0:T(8,128)(2,1)S(1)}, bf16[2,96,256]{2,1,0:T(8,128)(2,1)S(1)}, u32[]{:S(2)}, u32[]{:S(2)}) collective-permute-start(bf16[2,96,256]{2,1,0:T(8,128)(2,1)S(1)} %stack.1.refs_1_), channel_id=1, source_target_pairs={{0,1},{1,0},{2,3},{3,2},{4,5},{5,4},{6,7},{7,6},{8,9},{9,8},{10,11... | collective-permute-start | bytes 294920 | tf_op jit(solution)/shard_map/ppermute | solution.py:175
  7.5 2.1 %collective-permute-start.6 = (bf16[2,96,256]{2,1,0:T(8,128)(2,1)S(1)}, bf16[2,96,256]{2,1,0:T(8,128)(2,1)S(1)}, u32[]{:S(2)}, u32[]{:S(2)}) collective-permute-start(bf16[2,96,256]{2,1,0:T(8,128)(2,1)S(1)} %stack.1.refs_1_), channel_id=1, source_target_pairs={{0,24},{4,28},{8,16},{12,20},{16,8},{20,12},{24,0},{28,4},{1,25},{... | collective-permute-start | bytes 294920 | tf_op jit(solution)/shard_map/ppermute | solution.py:175
  9.6 0.2 collective-permute-start.4
  9.8 0.3 %collective-permute-start.2 = (bf16[2,96,256]{2,1,0:T(8,128)(2,1)S(1)}, bf16[2,96,256]{2,1,0:T(8,128)(2,1)S(1)}, u32[]{:S(2)}, u32[]{:S(2)}) collective-permute-start(bf16[2,96,256]{2,1,0:T(8,128)(2,1)S(1)} %stack.1.refs_1_), channel_id=1, source_target_pairs={{0,8},{4,12},{8,0},{12,4},{16,24},{20,28},{24,16},{28,20},{1,9},{5... | collective-permute-start | bytes 294920 | tf_op jit(solution)/shard_map/ppermute | solution.py:175
  10.2 2.8 %collective-permute-start.1 = (bf16[2,96,256]{2,1,0:T(8,128)(2,1)S(1)}, bf16[2,96,256]{2,1,0:T(8,128)(2,1)S(1)}, u32[]{:S(2)}, u32[]{:S(2)}) collective-permute-start(bf16[2,96,256]{2,1,0:T(8,128)(2,1)S(1)} %stack.1.refs_1_), channel_id=1, source_target_pairs={{0,4},{4,0},{8,12},{12,8},{16,20},{20,16},{24,28},{28,24},{1,5},{5... | collective-permute-start | bytes 294920 | tf_op jit(solution)/shard_map/ppermute | solution.py:175
  13.0 0.0 collective-permute-done.8.refs_9_
  13.0 2.2 %collective-permute-start.14 = (bf16[2,96,256]{2,1,0:T(8,128)(2,1)S(1)}, bf16[2,96,256]{2,1,0:T(8,128)(2,1)S(1)}, u32[]{:S(2)}, u32[]{:S(2)}) collective-permute-start(bf16[2,96,256]{2,1,0:T(8,128)(2,1)S(1)} %collective-permute-done.8.refs_9_), channel_id=1, source_target_pairs={{0,24},{4,28},{8,16},{12,20},{16,8},{20,12},{24,0},{28,4},{1,25},{... | collective-permute-start | bytes 294920 | tf_op jit(solution)/shard_map/ppermute | solution.py:175
  15.2 0.0 collective-permute-done.6.refs_7_
  15.2 0.2 collective-permute-start.12
  15.4 0.0 collective-permute-done.4.refs_5_
  15.4 0.3 collective-permute-start.10
  15.7 0.0 collective-permute-done.2.refs_3_
  15.7 2.5 %collective-permute-start.9 = (bf16[2,96,256]{2,1,0:T(8,128)(2,1)S(1)}, bf16[2,96,256]{2,1,0:T(8,128)(2,1)S(1)}, u32[]{:S(2)}, u32[]{:S(2)}) collective-permute-start(bf16[2,96,256]{2,1,0:T(8,128)(2,1)S(1)} %collective-permute-done.8.refs_9_), channel_id=1, source_target_pairs={{0,4},{4,0},{8,12},{12,8},{16,20},{20,16},{24,28},{28,24},{1,5},{5... | collective-permute-start | bytes 294920 | tf_op jit(solution)/shard_map/ppermute | solution.py:175
  18.2 0.0 collective-permute-done.1.refs_2_
  18.2 0.1 collective-permute-start.7
  18.2 0.0 copy-done
  18.2 0.1 constant_dynamic-slice_fusion
  18.3 0.1 copy.4
  18.4 0.1 reshape.13
  18.5 0.2 collective-permute-done.14.refs_15_
  18.7 2.0 %collective-permute-start.5 = (bf16[2,96,256]{2,1,0:T(8,128)(2,1)S(1)}, bf16[2,96,256]{2,1,0:T(8,128)(2,1)S(1)}, u32[]{:S(2)}, u32[]{:S(2)}) collective-permute-start(bf16[2,96,256]{2,1,0:T(8,128)(2,1)S(1)} %collective-permute-done.4.refs_5_), channel_id=1, source_target_pairs={{0,4},{4,0},{8,12},{12,8},{16,20},{20,16},{24,28},{28,24},{1,5},{5... | collective-permute-start | bytes 294920 | tf_op jit(solution)/shard_map/ppermute | solution.py:175
  20.8 0.2 collective-permute-done.12.refs_13_
  20.9 0.9 %collective-permute-start.3 = (bf16[2,96,256]{2,1,0:T(8,128)(2,1)S(1)}, bf16[2,96,256]{2,1,0:T(8,128)(2,1)S(1)}, u32[]{:S(2)}, u32[]{:S(2)}) collective-permute-start(bf16[2,96,256]{2,1,0:T(8,128)(2,1)S(1)} %collective-permute-done.2.refs_3_), channel_id=1, source_target_pairs={{0,4},{4,0},{8,12},{12,8},{16,20},{20,16},{24,28},{28,24},{1,5},{5... | collective-permute-start | bytes 294920 | tf_op jit(solution)/shard_map/ppermute | solution.py:175
  21.9 0.0 collective-permute-done.10.refs_11_
  21.9 0.0 collective-permute-start.15
  21.9 0.0 collective-permute-done.9.refs_10_
  21.9 0.5 %collective-permute-start.13 = (bf16[2,96,256]{2,1,0:T(8,128)(2,1)S(1)}, bf16[2,96,256]{2,1,0:T(8,128)(2,1)S(1)}, u32[]{:S(2)}, u32[]{:S(2)}) collective-permute-start(bf16[2,96,256]{2,1,0:T(8,128)(2,1)S(1)} %collective-permute-done.12.refs_13_), channel_id=1, source_target_pairs={{0,4},{4,0},{8,12},{12,8},{16,20},{20,16},{24,28},{28,24},{1,5},{5... | collective-permute-start | bytes 294920 | tf_op jit(solution)/shard_map/ppermute | solution.py:175
  22.4 0.0 collective-permute-done.7.refs_8_
  22.4 0.1 collective-permute-start.11
  22.4 0.1 pad_add_fusion.refs_0_
  22.5 0.0 collective-permute-done.5.refs_6_
  22.5 0.3 collective-permute-done.3.refs_4_
  22.8 0.4 %collective-permute-done.15.refs_16_ = bf16[2,96,256]{2,1,0:T(8,128)(2,1)S(1)} collective-permute-done((bf16[2,96,256]{2,1,0:T(8,128)(2,1)S(1)}, bf16[2,96,256]{2,1,0:T(8,128)(2,1)S(1)}, u32[]{:S(2)}, u32[]{:S(2)}) %collective-permute-start.15) | collective-permute-done | bytes 98336 | tf_op jit(solution)/shard_map/ppermute | solution.py:175
  23.2 0.2 collective-permute-done.13.refs_14_
  23.3 0.4 %collective-permute-done.11.refs_12_ = bf16[2,96,256]{2,1,0:T(8,128)(2,1)S(1)} collective-permute-done((bf16[2,96,256]{2,1,0:T(8,128)(2,1)S(1)}, bf16[2,96,256]{2,1,0:T(8,128)(2,1)S(1)}, u32[]{:S(2)}, u32[]{:S(2)}) %collective-permute-start.11) | collective-permute-done | bytes 98336 | tf_op jit(solution)/shard_map/ppermute | solution.py:175
  23.7 5.0 %correlate.1 = f32[2,4,8,128,128]{4,3,2,1,0:T(8,128)} custom-call(s32[5]{0:T(128)S(1)} %pad_add_fusion.refs_0_, bf16[2,96,256]{2,1,0:T(8,128)(2,1)S(1)} %stack.1.refs_1_, bf16[2,96,256]{2,1,0:T(8,128)(2,1)S(1)} %collective-permute-done.1.refs_2_, bf16[2,96,256]{2,1,0:T(8,128)(2,1)S(1)} %collective-permute-done.2.refs_3_, ...), custom_call_target="tpu_custom_call" | custom-call | tf_op jit(solution)/shard_map/correlate/pallas_call | solution.py:156
  (1 shorter events, 0.0 us)
Async XLA Ops:
  0.0 18.2 %copy-start = (s32[8,2]{0,1:T(2,128)S(1)}, s32[8,2]{0,1:T(2,128)}, u32[]{:S(2)}) copy-start(s32[8,2]{0,1:T(2,128)} %param.5) | copy-start | bytes 196
  1.3 4.7 %collective-permute-start = (bf16[1,96,256]{2,1,0:T(8,128)(2,1)S(1)}, bf16[1,96,256]{2,1,0:T(8,128)(2,1)S(1)}, u32[]{:S(2)}, u32[]{:S(2)}) collective-permute-start(bf16[1,96,256]{2,1,0:T(8,128)(2,1)S(1)} %bitcast.4), channel_id=1, source_target_pairs={{0,2},{1,3},{2,0},{3,1},{4,6},{5,7},{6,4},{7,5},{8,10},{9,11},{10,... | collective-permute-start | bytes 147464 | tf_op jit(solution)/shard_map/ppermute | solution.py:175
  6.0 7.0 %collective-permute-start.8 = (bf16[2,96,256]{2,1,0:T(8,128)(2,1)S(1)}, bf16[2,96,256]{2,1,0:T(8,128)(2,1)S(1)}, u32[]{:S(2)}, u32[]{:S(2)}) collective-permute-start(bf16[2,96,256]{2,1,0:T(8,128)(2,1)S(1)} %stack.1.refs_1_), channel_id=1, source_target_pairs={{0,1},{1,0},{2,3},{3,2},{4,5},{5,4},{6,7},{7,6},{8,9},{9,8},{10,11... | collective-permute-start | bytes 294920 | tf_op jit(solution)/shard_map/ppermute | solution.py:175
  7.5 7.7 %collective-permute-start.6 = (bf16[2,96,256]{2,1,0:T(8,128)(2,1)S(1)}, bf16[2,96,256]{2,1,0:T(8,128)(2,1)S(1)}, u32[]{:S(2)}, u32[]{:S(2)}) collective-permute-start(bf16[2,96,256]{2,1,0:T(8,128)(2,1)S(1)} %stack.1.refs_1_), channel_id=1, source_target_pairs={{0,24},{4,28},{8,16},{12,20},{16,8},{20,12},{24,0},{28,4},{1,25},{... | collective-permute-start | bytes 294920 | tf_op jit(solution)/shard_map/ppermute | solution.py:175
  9.6 5.8 %collective-permute-start.4 = (bf16[2,96,256]{2,1,0:T(8,128)(2,1)S(1)}, bf16[2,96,256]{2,1,0:T(8,128)(2,1)S(1)}, u32[]{:S(2)}, u32[]{:S(2)}) collective-permute-start(bf16[2,96,256]{2,1,0:T(8,128)(2,1)S(1)} %stack.1.refs_1_), channel_id=1, source_target_pairs={{0,16},{4,20},{8,24},{12,28},{16,0},{20,4},{24,8},{28,12},{1,17},{... | collective-permute-start | bytes 294920 | tf_op jit(solution)/shard_map/ppermute | solution.py:175
  9.8 5.8 %collective-permute-start.2 = (bf16[2,96,256]{2,1,0:T(8,128)(2,1)S(1)}, bf16[2,96,256]{2,1,0:T(8,128)(2,1)S(1)}, u32[]{:S(2)}, u32[]{:S(2)}) collective-permute-start(bf16[2,96,256]{2,1,0:T(8,128)(2,1)S(1)} %stack.1.refs_1_), channel_id=1, source_target_pairs={{0,8},{4,12},{8,0},{12,4},{16,24},{20,28},{24,16},{28,20},{1,9},{5... | collective-permute-start | bytes 294920 | tf_op jit(solution)/shard_map/ppermute | solution.py:175
  10.2 8.0 %collective-permute-start.1 = (bf16[2,96,256]{2,1,0:T(8,128)(2,1)S(1)}, bf16[2,96,256]{2,1,0:T(8,128)(2,1)S(1)}, u32[]{:S(2)}, u32[]{:S(2)}) collective-permute-start(bf16[2,96,256]{2,1,0:T(8,128)(2,1)S(1)} %stack.1.refs_1_), channel_id=1, source_target_pairs={{0,4},{4,0},{8,12},{12,8},{16,20},{20,16},{24,28},{28,24},{1,5},{5... | collective-permute-start | bytes 294920 | tf_op jit(solution)/shard_map/ppermute | solution.py:175
  13.0 5.7 %collective-permute-start.14 = (bf16[2,96,256]{2,1,0:T(8,128)(2,1)S(1)}, bf16[2,96,256]{2,1,0:T(8,128)(2,1)S(1)}, u32[]{:S(2)}, u32[]{:S(2)}) collective-permute-start(bf16[2,96,256]{2,1,0:T(8,128)(2,1)S(1)} %collective-permute-done.8.refs_9_), channel_id=1, source_target_pairs={{0,24},{4,28},{8,16},{12,20},{16,8},{20,12},{24,0},{28,4},{1,25},{... | collective-permute-start | bytes 294920 | tf_op jit(solution)/shard_map/ppermute | solution.py:175
  15.2 5.7 %collective-permute-start.12 = (bf16[2,96,256]{2,1,0:T(8,128)(2,1)S(1)}, bf16[2,96,256]{2,1,0:T(8,128)(2,1)S(1)}, u32[]{:S(2)}, u32[]{:S(2)}) collective-permute-start(bf16[2,96,256]{2,1,0:T(8,128)(2,1)S(1)} %collective-permute-done.8.refs_9_), channel_id=1, source_target_pairs={{0,16},{4,20},{8,24},{12,28},{16,0},{20,4},{24,8},{28,12},{1,17},{... | collective-permute-start | bytes 294920 | tf_op jit(solution)/shard_map/ppermute | solution.py:175
  15.4 6.5 %collective-permute-start.10 = (bf16[2,96,256]{2,1,0:T(8,128)(2,1)S(1)}, bf16[2,96,256]{2,1,0:T(8,128)(2,1)S(1)}, u32[]{:S(2)}, u32[]{:S(2)}) collective-permute-start(bf16[2,96,256]{2,1,0:T(8,128)(2,1)S(1)} %collective-permute-done.8.refs_9_), channel_id=1, source_target_pairs={{0,8},{4,12},{8,0},{12,4},{16,24},{20,28},{24,16},{28,20},{1,9},{5... | collective-permute-start | bytes 294920 | tf_op jit(solution)/shard_map/ppermute | solution.py:175
  15.7 6.2 %collective-permute-start.9 = (bf16[2,96,256]{2,1,0:T(8,128)(2,1)S(1)}, bf16[2,96,256]{2,1,0:T(8,128)(2,1)S(1)}, u32[]{:S(2)}, u32[]{:S(2)}) collective-permute-start(bf16[2,96,256]{2,1,0:T(8,128)(2,1)S(1)} %collective-permute-done.8.refs_9_), channel_id=1, source_target_pairs={{0,4},{4,0},{8,12},{12,8},{16,20},{20,16},{24,28},{28,24},{1,5},{5... | collective-permute-start | bytes 294920 | tf_op jit(solution)/shard_map/ppermute | solution.py:175
  18.2 4.2 %collective-permute-start.7 = (bf16[2,96,256]{2,1,0:T(8,128)(2,1)S(1)}, bf16[2,96,256]{2,1,0:T(8,128)(2,1)S(1)}, u32[]{:S(2)}, u32[]{:S(2)}) collective-permute-start(bf16[2,96,256]{2,1,0:T(8,128)(2,1)S(1)} %collective-permute-done.6.refs_7_), channel_id=1, source_target_pairs={{0,4},{4,0},{8,12},{12,8},{16,20},{20,16},{24,28},{28,24},{1,5},{5... | collective-permute-start | bytes 294920 | tf_op jit(solution)/shard_map/ppermute | solution.py:175
  18.7 3.8 %collective-permute-start.5 = (bf16[2,96,256]{2,1,0:T(8,128)(2,1)S(1)}, bf16[2,96,256]{2,1,0:T(8,128)(2,1)S(1)}, u32[]{:S(2)}, u32[]{:S(2)}) collective-permute-start(bf16[2,96,256]{2,1,0:T(8,128)(2,1)S(1)} %collective-permute-done.4.refs_5_), channel_id=1, source_target_pairs={{0,4},{4,0},{8,12},{12,8},{16,20},{20,16},{24,28},{28,24},{1,5},{5... | collective-permute-start | bytes 294920 | tf_op jit(solution)/shard_map/ppermute | solution.py:175
  20.9 1.9 %collective-permute-start.3 = (bf16[2,96,256]{2,1,0:T(8,128)(2,1)S(1)}, bf16[2,96,256]{2,1,0:T(8,128)(2,1)S(1)}, u32[]{:S(2)}, u32[]{:S(2)}) collective-permute-start(bf16[2,96,256]{2,1,0:T(8,128)(2,1)S(1)} %collective-permute-done.2.refs_3_), channel_id=1, source_target_pairs={{0,4},{4,0},{8,12},{12,8},{16,20},{20,16},{24,28},{28,24},{1,5},{5... | collective-permute-start | bytes 294920 | tf_op jit(solution)/shard_map/ppermute | solution.py:175
  21.9 1.3 %collective-permute-start.15 = (bf16[2,96,256]{2,1,0:T(8,128)(2,1)S(1)}, bf16[2,96,256]{2,1,0:T(8,128)(2,1)S(1)}, u32[]{:S(2)}, u32[]{:S(2)}) collective-permute-start(bf16[2,96,256]{2,1,0:T(8,128)(2,1)S(1)} %collective-permute-done.14.refs_15_), channel_id=1, source_target_pairs={{0,4},{4,0},{8,12},{12,8},{16,20},{20,16},{24,28},{28,24},{1,5},{5... | collective-permute-start | bytes 294920 | tf_op jit(solution)/shard_map/ppermute | solution.py:175
  21.9 1.5 %collective-permute-start.13 = (bf16[2,96,256]{2,1,0:T(8,128)(2,1)S(1)}, bf16[2,96,256]{2,1,0:T(8,128)(2,1)S(1)}, u32[]{:S(2)}, u32[]{:S(2)}) collective-permute-start(bf16[2,96,256]{2,1,0:T(8,128)(2,1)S(1)} %collective-permute-done.12.refs_13_), channel_id=1, source_target_pairs={{0,4},{4,0},{8,12},{12,8},{16,20},{20,16},{24,28},{28,24},{1,5},{5... | collective-permute-start | bytes 294920 | tf_op jit(solution)/shard_map/ppermute | solution.py:175
  22.4 1.3 %collective-permute-start.11 = (bf16[2,96,256]{2,1,0:T(8,128)(2,1)S(1)}, bf16[2,96,256]{2,1,0:T(8,128)(2,1)S(1)}, u32[]{:S(2)}, u32[]{:S(2)}) collective-permute-start(bf16[2,96,256]{2,1,0:T(8,128)(2,1)S(1)} %collective-permute-done.10.refs_11_), channel_id=1, source_target_pairs={{0,4},{4,0},{8,12},{12,8},{16,20},{20,16},{24,28},{28,24},{1,5},{5... | collective-permute-start | bytes 294920 | tf_op jit(solution)/shard_map/ppermute | solution.py:175

commit v9 on v8

--- a/solution.py
+++ b/solution.py
@@ -11,6 +11,7 @@
 LAGS = 32
 TILE = 128
 EPSILON = 1e-06
+CORES = 2
 SMALL = 4 * 1024 * 1024
 VMEM = pl.BlockSpec(memory_space=pltpu.VMEM)
 SMEM = pl.BlockSpec(memory_space=pltpu.SMEM)
@@ -72,10 +73,9 @@
     return (forward, (rc + is_, ic - rs)) if both else (forward,)
 
 
-def correlate_kernel(norm, where_ref, *refs):
-    pieces = refs[:-6]
-    out_ref, spectra, left_turned, right_turned, staging, sem = refs[-6:]
-    tiles = staging.shape[0]
+def correlate_kernel(norm, add, tiles, where_ref, *refs):
+    pieces = refs[:-5 - add]
+    out_ref, spectra, left_turned, right_turned, sem = refs[-5:]
     groups, _, lanes = spectra.shape
     half = lanes // 2
     hours_dev = half // F
@@ -87,14 +87,11 @@
     cos, sin = jnp.cos(angle), jnp.sin(angle)
     table = {k: (cos[i:i + 1], sin[i:i + 1]) for k, i in ((1, 1), (2, 2), (3, 3), (4, 4), (12, 6))}
 
-    chans = spectra.shape[1] // pieces[0].shape[1]
-    first = 0
-    for start in range(0, len(pieces), chans):
-        depth, rows, _ = pieces[start].shape
-        for k in range(chans):
-            place = pl.multiple_of((where_ref[0] ^ k) * rows, 32)
-            spectra[first:first + depth, pl.ds(place, rows), :] = pieces[start + k][...]
-        first += depth
+    rows = pieces[0].shape[1]
+    for core, piece in enumerate(pieces):
+        for k in range(piece.shape[0] // groups):
+            place = pl.multiple_of((where_ref[0] ^ (CORES * k + core)) * rows, 32)
+            spectra[:, pl.ds(place, rows), :] = piece[k * groups:(k + 1) * groups]
 
     def load(block, g):
         whole = spectra[g, pl.ds(pl.multiple_of(block * TILE, TILE), TILE), :].astype(jnp.float32)
@@ -131,83 +128,84 @@
                 (((1,), (1,)), ((), ())),
                 preferred_element_type=jnp.float32,
             )
+            partial = refs[-6] if add else out_ref
             for u in range(len(COARSE)):
                 for s in range(2):
-                    staging[t, u, 2 * j + s] = total[u * TILE:(u + 1) * TILE, s * TILE:(s + 1) * TILE]
-            for s in range(2):
-                fine = FINE_PAIRS[j][s] + 4
-                copy = pltpu.make_async_copy(staging.at[t, :, 2 * j + s], out_ref.at[t, :, fine], sem)
-                copy.start()
-                copies.append(copy)
+                    fine = FINE_PAIRS[j][s] + 4
+                    value = total[u * TILE:(u + 1) * TILE, s * TILE:(s + 1) * TILE]
+                    partial[t, u, fine] = partial[t, u, fine] + value if add else value
+            if add:
+                for s in range(2):
+                    fine = FINE_PAIRS[j][s] + 4
+                    copy = pltpu.make_async_copy(partial.at[t, :, fine], out_ref.at[t, :, fine], sem)
+                    copy.start()
+                    copies.append(copy)
     for copy in copies:
         copy.wait()
 
 
-def correlate(pieces, where, tiles, hours):
-    groups = lax.axis_size("tm")
-    _, rows, lanes = pieces[0].shape
+def correlate(pieces, groups, where, tiles, hours, partial=None):
+    depth, rows, lanes = pieces[0].shape
     fine = 2 * len(FINE_PAIRS)
     shape = (tiles, len(COARSE), fine, TILE, TILE)
     norm = 1.0 / math.sqrt(F * hours)
     slots = min(tiles, 2)
-    chans = lax.axis_size("chan") * rows
-    turned = slots * (len(COARSE) + fine) * TILE * groups * lanes
-    scratch = 2 * (groups * chans * lanes + turned) + 4 * math.prod(shape)
-    out = pl.pallas_call(
-        lambda *refs: correlate_kernel(norm, *refs),
+    chans = len(pieces) * depth // groups * rows
+    scratch = 2 * (groups * chans * lanes + slots * (len(COARSE) + fine) * TILE * groups * lanes)
+    add = partial is not None
+    more = (partial,) if add else ()
+    return pl.pallas_call(
+        lambda *refs: correlate_kernel(norm, add, tiles, *refs),
         out_shape=jax.ShapeDtypeStruct(shape, jnp.float32),
-        in_specs=[SMEM] + [VMEM] * len(pieces),
-        out_specs=pl.BlockSpec(memory_space=pl.ANY),
+        in_specs=[SMEM] + [VMEM] * (len(pieces) + add),
+        out_specs=pl.BlockSpec(memory_space=pl.ANY) if add else VMEM,
         scratch_shapes=[
             pltpu.VMEM((groups, chans, lanes), jnp.bfloat16),
             pltpu.VMEM((slots, len(COARSE) * TILE, groups * lanes), jnp.bfloat16),
             pltpu.VMEM((slots, fine * TILE, groups * lanes), jnp.bfloat16),
-            pltpu.VMEM(shape, jnp.float32),
             pltpu.SemaphoreType.DMA,
         ],
         compiler_params=pltpu.CompilerParams(vmem_limit_bytes=scratch + SMALL),
-        name="correlate",
-    )(where, *pieces)
-    return out.reshape(tiles, LAGS, TILE, TILE)
+        cost_estimate=pl.CostEstimate(
+            flops=0, bytes_accessed=0, transcendentals=0
+        ),
+        name="correlate_add" if add else "correlate",
+    )(where, *pieces, *more)
 
 
 def swap(array, axis, k):
     return lax.ppermute(array, axis, [(i, i ^ k) for i in range(lax.axis_size(axis))])
 
 
-def between_chips(half):
-    pieces = {0: half}
-    for k in range(2, lax.axis_size("chan"), 2):
-        pieces[k] = swap(half, "chan", k)
-    for k in list(pieces):
-        pieces[k + 1] = swap(pieces[k], "chan", 1)
-    return [pieces[k] for k in sorted(pieces)]
-
-
-def stack_kernel(one_ref, two_ref, out_ref):
-    depth = one_ref.shape[0]
-    out_ref[:depth] = one_ref[...]
-    out_ref[depth:] = two_ref[...]
-
-
-def stack(one, two):
+def stack_kernel(*refs):
+    out_ref = refs[-1]
+    first = 0
+    for block in refs[:-1]:
+        out_ref[first:first + block.shape[0]] = block[...]
+        first += block.shape[0]
+
+
+def stack(blocks):
+    depth = sum(block.shape[0] for block in blocks)
     return pl.pallas_call(
         stack_kernel,
-        out_shape=jax.ShapeDtypeStruct((2 * one.shape[0], *one.shape[1:]), one.dtype),
-        in_specs=[VMEM, VMEM],
+        out_shape=jax.ShapeDtypeStruct((depth, *blocks[0].shape[1:]), blocks[0].dtype),
+        in_specs=[VMEM] * len(blocks),
         out_specs=VMEM,
         compiler_params=pltpu.CompilerParams(vmem_limit_bytes=SMALL),
         name="stack",
-    )(one, two)
-
-
-def gather(white):
-    half = white[None]
-    k = lax.axis_size("tm") // 2
-    while k > 1:
-        half = stack(half, swap(half, "tm", k))
-        k //= 2
-    return between_chips(half) + between_chips(swap(half, "tm", 1))
+    )(*blocks)
+
+
+def halves(white):
+    groups = lax.axis_size("tm")
+    blocks = [white[None]] + [swap(white[None], "tm", k) for k in range(1, groups)]
+    return [stack(blocks[first:first + groups // 2]) for first in (0, groups // 2)]
+
+
+def between_devices(half):
+    own = stack([half] + [swap(half, "chan", k) for k in range(CORES, lax.axis_size("chan"), CORES)])
+    return own, swap(own, "chan", 1)
 
 
 def per_device(spectra, bad_channels, tile_list):
@@ -215,10 +213,12 @@
     hours = spectra.shape[1] * groups
     tiles = tile_list.shape[0] // groups
     white = whiten(spectra, bad_channels)
-    pieces = gather(white)
     pairs = lax.dynamic_slice_in_dim(tile_list, lax.axis_index("tm") * tiles, tiles, axis=0)
     where = jnp.concatenate([lax.axis_index("chan").reshape(1), pairs.reshape(-1)]).astype(jnp.int32)
-    return correlate(pieces, where, tiles, hours)
+    near, far = [between_devices(half) for half in halves(white)]
+    partial = correlate(near, groups // 2, where, tiles, hours)
+    out = correlate(far, groups // 2, where, tiles, hours, partial)
+    return out.reshape(tiles, LAGS, TILE, TILE)
 
 
 def solution(mesh):

time: 28.9 us -> 31 us (1.073)
  waiting for transfers between devices: 3.04 us -> 5.42 us
  starting transfers between devices: 19 us -> 18 us
  Pallas kernels: 6.25 us -> 6.97 us
    ppermute x16 -> x11, waiting for transfers between devices: 3.04 us -> 5.42 us  [swap(): lax.ppermute(array, axis, [(i, i ^ k) for i in range(lax.axis_size(axis))])]
    ppermute x16 -> x11, starting transfers between devices: 19 us -> 18 us  [swap(): lax.ppermute(array, axis, [(i, i ^ k) for i in range(lax.axis_size(axis))])]
    pallas_call x2 -> x6, Pallas kernels: 4.96 us -> 5.68 us  [the longest x2 5.61 us: correlate(): pl.pallas_call(lambda *refs: correlate_kernel(norm, add, tiles, *refs), o...]
  transfers between devices with their start and end apart: 16 -> 11, of which waited for: 7 -> 3; matrix products, arithmetic and copies ran while one was open for 1% -> 1% of each run, Pallas kernels for 0% -> 7%
where the time goes in v9:
time: 31 us; the launch traced here: 30.8 us
  starting transfers between devices  18 us (58%)
  Pallas kernels  6.97 us (22%)
  waiting for transfers between devices  5.42 us (17%)
    ppermute x11, starting transfers between devices, swap(): lax.ppermute(array, axis, [(i, i ^ k) for i in range(lax.axis_size(axis))])  18 us
    pallas_call x2, Pallas kernels, correlate(): pl.pallas_call(lambda *refs: correlate_kernel(norm, add, tiles, *refs), o...  5.61 us
    ppermute x11, waiting for transfers between devices, swap(): lax.ppermute(array, axis, [(i, i ^ k) for i in range(lax.axis_size(axis))])  5.42 us
    pallas_call x1, Pallas kernels, whiten(): pl.pallas_call(whiten_kernel, out_shape=jax.ShapeDtypeStruct((chans, bins...  1.29 us
  transfers between devices with their start and end apart: 11, of which 3 were waited for; matrix products, arithmetic and copies ran while one was open for 1% of the time, Pallas kernels for 7%

profile of v9, /device:TPU:1, one launch (start us, length us, event | category | flops | bytes accessed | tf_op | source)
XLA Modules:
  0.0 30.8 jit_solution(10677579186791010060)
XLA Ops:
  0.0 0.0 copy-start
  0.0 1.3 %whiten.1 = bf16[96,256]{1,0:T(8,128)(2,1)S(1)} custom-call(bf16[64,2,2,96]{3,2,1,0:T(2,128)(2,1)} %spectra_hbm.1, s32[1,96]{1,0:T(1,128)} %bitcast.8), custom_call_target="tpu_custom_call" | custom-call | tf_op jit(solution)/shard_map/whiten/pallas_call | solution.py:55
  1.3 2.2 %collective-permute-start.6 = (bf16[1,96,256]{2,1,0:T(8,128)(2,1)S(1)}, bf16[1,96,256]{2,1,0:T(8,128)(2,1)S(1)}, u32[]{:S(2)}, u32[]{:S(2)}) collective-permute-start(bf16[1,96,256]{2,1,0:T(8,128)(2,1)S(1)} %bitcast.4), channel_id=1, source_target_pairs={{0,1},{1,0},{2,3},{3,2},{4,5},{5,4},{6,7},{7,6},{8,9},{9,8},{10,11... | collective-permute-start | bytes 147464 | tf_op jit(solution)/shard_map/ppermute | solution.py:177
  3.5 1.5 %collective-permute-done.6.refs_1_ = bf16[1,96,256]{2,1,0:T(8,128)(2,1)S(1)} collective-permute-done((bf16[1,96,256]{2,1,0:T(8,128)(2,1)S(1)}, bf16[1,96,256]{2,1,0:T(8,128)(2,1)S(1)}, u32[]{:S(2)}, u32[]{:S(2)}) %collective-permute-start.6) | collective-permute-done | bytes 49184 | tf_op jit(solution)/shard_map/ppermute | solution.py:177
  5.0 2.4 %collective-permute-start.9 = (bf16[2,96,256]{2,1,0:T(8,128)(2,1)S(1)}, bf16[2,96,256]{2,1,0:T(8,128)(2,1)S(1)}, u32[]{:S(2)}, u32[]{:S(2)}) collective-permute-start(bf16[2,96,256]{2,1,0:T(8,128)(2,1)S(1)} %stack.6.refs_0_), channel_id=1, source_target_pairs={{0,24},{4,28},{8,16},{12,20},{16,8},{20,12},{24,0},{28,4},{1,25},{... | collective-permute-start | bytes 294920 | tf_op jit(solution)/shard_map/ppermute | solution.py:177
  7.4 3.3 %collective-permute-start.1 = (bf16[1,96,256]{2,1,0:T(8,128)(2,1)S(1)}, bf16[1,96,256]{2,1,0:T(8,128)(2,1)S(1)}, u32[]{:S(2)}, u32[]{:S(2)}) collective-permute-start(bf16[1,96,256]{2,1,0:T(8,128)(2,1)S(1)} %bitcast.6), channel_id=1, source_target_pairs={{0,3},{1,2},{2,1},{3,0},{4,7},{5,6},{6,5},{7,4},{8,11},{9,10},{10,... | collective-permute-start | bytes 147464 | tf_op jit(solution)/shard_map/ppermute | solution.py:177
  10.7 0.0 collective-permute-start
  10.7 0.2 collective-permute-start.8
  10.9 0.3 collective-permute-start.7
  11.2 1.0 %collective-permute-done.1.refs_1_ = bf16[1,96,256]{2,1,0:T(8,128)(2,1)S(1)} collective-permute-done((bf16[1,96,256]{2,1,0:T(8,128)(2,1)S(1)}, bf16[1,96,256]{2,1,0:T(8,128)(2,1)S(1)}, u32[]{:S(2)}, u32[]{:S(2)}) %collective-permute-start.1) | collective-permute-done | bytes 49184 | tf_op jit(solution)/shard_map/ppermute | solution.py:177
  12.2 2.9 %collective-permute-done.refs_0_ = bf16[1,96,256]{2,1,0:T(8,128)(2,1)S(1)} collective-permute-done((bf16[1,96,256]{2,1,0:T(8,128)(2,1)S(1)}, bf16[1,96,256]{2,1,0:T(8,128)(2,1)S(1)}, u32[]{:S(2)}, u32[]{:S(2)}) %collective-permute-start) | collective-permute-done | bytes 49184 | tf_op jit(solution)/shard_map/ppermute | solution.py:177
  15.1 0.3 collective-permute-start.4
  15.4 1.2 %collective-permute-start.3 = (bf16[2,96,256]{2,1,0:T(8,128)(2,1)S(1)}, bf16[2,96,256]{2,1,0:T(8,128)(2,1)S(1)}, u32[]{:S(2)}, u32[]{:S(2)}) collective-permute-start(bf16[2,96,256]{2,1,0:T(8,128)(2,1)S(1)} %stack.4.refs_0_), channel_id=1, source_target_pairs={{0,16},{4,20},{8,24},{12,28},{16,0},{20,4},{24,8},{28,12},{1,17},{... | collective-permute-start | bytes 294920 | tf_op jit(solution)/shard_map/ppermute | solution.py:177
  16.6 0.0 collective-permute-done.9.refs_3_
  16.6 1.2 %collective-permute-start.2 = (bf16[2,96,256]{2,1,0:T(8,128)(2,1)S(1)}, bf16[2,96,256]{2,1,0:T(8,128)(2,1)S(1)}, u32[]{:S(2)}, u32[]{:S(2)}) collective-permute-start(bf16[2,96,256]{2,1,0:T(8,128)(2,1)S(1)} %stack.4.refs_0_), channel_id=1, source_target_pairs={{0,8},{4,12},{8,0},{12,4},{16,24},{20,28},{24,16},{28,20},{1,9},{5... | collective-permute-start | bytes 294920 | tf_op jit(solution)/shard_map/ppermute | solution.py:177
  17.8 0.0 collective-permute-done.8.refs_2_
  17.8 0.0 collective-permute-done.7.refs_1_
  17.9 3.9 %collective-permute-start.10 = (bf16[8,96,256]{2,1,0:T(8,128)(2,1)S(1)}, bf16[8,96,256]{2,1,0:T(8,128)(2,1)S(1)}, u32[]{:S(2)}, u32[]{:S(2)}) collective-permute-start(bf16[8,96,256]{2,1,0:T(8,128)(2,1)S(1)} %stack.7.refs_1_), channel_id=1, source_target_pairs={{0,4},{4,0},{8,12},{12,8},{16,20},{20,16},{24,28},{28,24},{1,5},{5... | collective-permute-start | bytes 1179656 | tf_op jit(solution)/shard_map/ppermute | solution.py:177
  21.7 0.0 collective-permute-done.4.refs_3_
  21.8 0.0 collective-permute-done.3.refs_2_
  21.8 0.0 collective-permute-done.2.refs_1_
  21.8 3.1 %collective-permute-start.5 = (bf16[8,96,256]{2,1,0:T(8,128)(2,1)S(1)}, bf16[8,96,256]{2,1,0:T(8,128)(2,1)S(1)}, u32[]{:S(2)}, u32[]{:S(2)}) collective-permute-start(bf16[8,96,256]{2,1,0:T(8,128)(2,1)S(1)} %stack.5.refs_1_), channel_id=1, source_target_pairs={{0,4},{4,0},{8,12},{12,8},{16,20},{20,16},{24,28},{28,24},{1,5},{5... | collective-permute-start | bytes 1179656 | tf_op jit(solution)/shard_map/ppermute | solution.py:177
  24.9 0.0 copy-done
  24.9 0.1 constant_dynamic-slice_fusion
  24.9 0.1 copy.4
  25.0 0.1 reshape.13
  25.1 0.1 pad_add_fusion.refs_0_
  25.2 0.0 collective-permute-done.10.refs_2_
  25.2 2.2 %correlate.1.refs_3_ = f32[2,4,8,128,128]{4,3,2,1,0:T(8,128)S(1)} custom-call(s32[5]{0:T(128)S(1)} %pad_add_fusion.refs_0_, bf16[8,96,256]{2,1,0:T(8,128)(2,1)S(1)} %stack.7.refs_1_, bf16[8,96,256]{2,1,0:T(8,128)(2,1)S(1)} %collective-permute-done.10.refs_2_), custom_call_target="tpu_custom_call" | custom-call | tf_op jit(solution)/shard_map/correlate/pallas_call | solution.py:157
  27.4 0.0 collective-permute-done.5.refs_2_
  27.4 3.5 %correlate_add.1 = f32[2,4,8,128,128]{4,3,2,1,0:T(8,128)} custom-call(s32[5]{0:T(128)S(1)} %pad_add_fusion.refs_0_, bf16[8,96,256]{2,1,0:T(8,128)(2,1)S(1)} %stack.5.refs_1_, bf16[8,96,256]{2,1,0:T(8,128)(2,1)S(1)} %collective-permute-done.5.refs_2_, f32[2,4,8,128,128]{4,3,2,1,0:T(8,128)S(1)} %correlate.1.refs_3_), custom_call_target="tpu_custom_call" | custom-call | tf_op jit(solution)/shard_map/correlate_add/pallas_call | solution.py:157
  (4 shorter events, 0.1 us)
Async XLA Ops:
  0.0 24.9 %copy-start = (s32[8,2]{0,1:T(2,128)S(1)}, s32[8,2]{0,1:T(2,128)}, u32[]{:S(2)}) copy-start(s32[8,2]{0,1:T(2,128)} %param.5) | copy-start | bytes 196
  1.3 3.7 %collective-permute-start.6 = (bf16[1,96,256]{2,1,0:T(8,128)(2,1)S(1)}, bf16[1,96,256]{2,1,0:T(8,128)(2,1)S(1)}, u32[]{:S(2)}, u32[]{:S(2)}) collective-permute-start(bf16[1,96,256]{2,1,0:T(8,128)(2,1)S(1)} %bitcast.4), channel_id=1, source_target_pairs={{0,1},{1,0},{2,3},{3,2},{4,5},{5,4},{6,7},{7,6},{8,9},{9,8},{10,11... | collective-permute-start | bytes 147464 | tf_op jit(solution)/shard_map/ppermute | solution.py:177
  5.0 11.6 %collective-permute-start.9 = (bf16[2,96,256]{2,1,0:T(8,128)(2,1)S(1)}, bf16[2,96,256]{2,1,0:T(8,128)(2,1)S(1)}, u32[]{:S(2)}, u32[]{:S(2)}) collective-permute-start(bf16[2,96,256]{2,1,0:T(8,128)(2,1)S(1)} %stack.6.refs_0_), channel_id=1, source_target_pairs={{0,24},{4,28},{8,16},{12,20},{16,8},{20,12},{24,0},{28,4},{1,25},{... | collective-permute-start | bytes 294920 | tf_op jit(solution)/shard_map/ppermute | solution.py:177
  7.4 4.8 %collective-permute-start.1 = (bf16[1,96,256]{2,1,0:T(8,128)(2,1)S(1)}, bf16[1,96,256]{2,1,0:T(8,128)(2,1)S(1)}, u32[]{:S(2)}, u32[]{:S(2)}) collective-permute-start(bf16[1,96,256]{2,1,0:T(8,128)(2,1)S(1)} %bitcast.6), channel_id=1, source_target_pairs={{0,3},{1,2},{2,1},{3,0},{4,7},{5,6},{6,5},{7,4},{8,11},{9,10},{10,... | collective-permute-start | bytes 147464 | tf_op jit(solution)/shard_map/ppermute | solution.py:177
  10.7 4.4 %collective-permute-start = (bf16[1,96,256]{2,1,0:T(8,128)(2,1)S(1)}, bf16[1,96,256]{2,1,0:T(8,128)(2,1)S(1)}, u32[]{:S(2)}, u32[]{:S(2)}) collective-permute-start(bf16[1,96,256]{2,1,0:T(8,128)(2,1)S(1)} %bitcast.7), channel_id=1, source_target_pairs={{0,2},{1,3},{2,0},{3,1},{4,6},{5,7},{6,4},{7,5},{8,10},{9,11},{10,... | collective-permute-start | bytes 147464 | tf_op jit(solution)/shard_map/ppermute | solution.py:177
  10.7 7.1 %collective-permute-start.8 = (bf16[2,96,256]{2,1,0:T(8,128)(2,1)S(1)}, bf16[2,96,256]{2,1,0:T(8,128)(2,1)S(1)}, u32[]{:S(2)}, u32[]{:S(2)}) collective-permute-start(bf16[2,96,256]{2,1,0:T(8,128)(2,1)S(1)} %stack.6.refs_0_), channel_id=1, source_target_pairs={{0,16},{4,20},{8,24},{12,28},{16,0},{20,4},{24,8},{28,12},{1,17},{... | collective-permute-start | bytes 294920 | tf_op jit(solution)/shard_map/ppermute | solution.py:177
  10.9 6.9 %collective-permute-start.7 = (bf16[2,96,256]{2,1,0:T(8,128)(2,1)S(1)}, bf16[2,96,256]{2,1,0:T(8,128)(2,1)S(1)}, u32[]{:S(2)}, u32[]{:S(2)}) collective-permute-start(bf16[2,96,256]{2,1,0:T(8,128)(2,1)S(1)} %stack.6.refs_0_), channel_id=1, source_target_pairs={{0,8},{4,12},{8,0},{12,4},{16,24},{20,28},{24,16},{28,20},{1,9},{5... | collective-permute-start | bytes 294920 | tf_op jit(solution)/shard_map/ppermute | solution.py:177
  15.1 6.6 %collective-permute-start.4 = (bf16[2,96,256]{2,1,0:T(8,128)(2,1)S(1)}, bf16[2,96,256]{2,1,0:T(8,128)(2,1)S(1)}, u32[]{:S(2)}, u32[]{:S(2)}) collective-permute-start(bf16[2,96,256]{2,1,0:T(8,128)(2,1)S(1)} %stack.4.refs_0_), channel_id=1, source_target_pairs={{0,24},{4,28},{8,16},{12,20},{16,8},{20,12},{24,0},{28,4},{1,25},{... | collective-permute-start | bytes 294920 | tf_op jit(solution)/shard_map/ppermute | solution.py:177
  15.4 6.4 %collective-permute-start.3 = (bf16[2,96,256]{2,1,0:T(8,128)(2,1)S(1)}, bf16[2,96,256]{2,1,0:T(8,128)(2,1)S(1)}, u32[]{:S(2)}, u32[]{:S(2)}) collective-permute-start(bf16[2,96,256]{2,1,0:T(8,128)(2,1)S(1)} %stack.4.refs_0_), channel_id=1, source_target_pairs={{0,16},{4,20},{8,24},{12,28},{16,0},{20,4},{24,8},{28,12},{1,17},{... | collective-permute-start | bytes 294920 | tf_op jit(solution)/shard_map/ppermute | solution.py:177
  16.6 5.1 %collective-permute-start.2 = (bf16[2,96,256]{2,1,0:T(8,128)(2,1)S(1)}, bf16[2,96,256]{2,1,0:T(8,128)(2,1)S(1)}, u32[]{:S(2)}, u32[]{:S(2)}) collective-permute-start(bf16[2,96,256]{2,1,0:T(8,128)(2,1)S(1)} %stack.4.refs_0_), channel_id=1, source_target_pairs={{0,8},{4,12},{8,0},{12,4},{16,24},{20,28},{24,16},{28,20},{1,9},{5... | collective-permute-start | bytes 294920 | tf_op jit(solution)/shard_map/ppermute | solution.py:177
  17.9 7.3 %collective-permute-start.10 = (bf16[8,96,256]{2,1,0:T(8,128)(2,1)S(1)}, bf16[8,96,256]{2,1,0:T(8,128)(2,1)S(1)}, u32[]{:S(2)}, u32[]{:S(2)}) collective-permute-start(bf16[8,96,256]{2,1,0:T(8,128)(2,1)S(1)} %stack.7.refs_1_), channel_id=1, source_target_pairs={{0,4},{4,0},{8,12},{12,8},{16,20},{20,16},{24,28},{28,24},{1,5},{5... | collective-permute-start | bytes 1179656 | tf_op jit(solution)/shard_map/ppermute | solution.py:177
  21.8 5.6 %collective-permute-start.5 = (bf16[8,96,256]{2,1,0:T(8,128)(2,1)S(1)}, bf16[8,96,256]{2,1,0:T(8,128)(2,1)S(1)}, u32[]{:S(2)}, u32[]{:S(2)}) collective-permute-start(bf16[8,96,256]{2,1,0:T(8,128)(2,1)S(1)} %stack.5.refs_1_), channel_id=1, source_target_pairs={{0,4},{4,0},{8,12},{12,8},{16,20},{20,16},{24,28},{28,24},{1,5},{5... | collective-permute-start | bytes 1179656 | tf_op jit(solution)/shard_map/ppermute | solution.py:177

commit v10 on v9

--- a/solution.py
+++ b/solution.py
@@ -102,44 +102,51 @@
         ref[slot, rows_at, g * lanes:g * lanes + half] = value[0].astype(jnp.bfloat16)
         ref[slot, rows_at, g * lanes + half:(g + 1) * lanes] = value[1].astype(jnp.bfloat16)
 
-    copies = []
-    for t in range(tiles):
-        slot = t % left_turned.shape[0]
+    def turn_left(t):
         for g in range(groups):
             re, im = load(where_ref[1 + 2 * t], g)
-            re, im = re * norm, im * norm
             for k in (4, 12):
-                forward, backward = turn_by(re, im, *table[k], True)
-                store(left_turned, slot, COARSE.index(k), g, forward)
-                store(left_turned, slot, COARSE.index(-k), g, backward)
-        for j in range(len(FINE_PAIRS)):
-            for g in range(groups):
-                re, im = load(where_ref[2 + 2 * t], g)
-                if j == 0:
-                    store(right_turned, slot, 0, g, turn_by(re, im, *table[4], False)[0])
-                    store(right_turned, slot, 1, g, (re, im))
-                else:
-                    forward, backward = turn_by(re, im, *table[j], True)
-                    store(right_turned, slot, 2 * j, g, forward)
-                    store(right_turned, slot, 2 * j + 1, g, backward)
-            total = lax.dot_general(
-                left_turned[slot],
-                right_turned[slot, 2 * j * TILE:2 * (j + 1) * TILE, :],
-                (((1,), (1,)), ((), ())),
-                preferred_element_type=jnp.float32,
-            )
-            partial = refs[-6] if add else out_ref
+                forward, backward = turn_by(re, im, *(norm * part for part in table[k]), True)
+                store(left_turned, t % slots, COARSE.index(k), g, forward)
+                store(left_turned, t % slots, COARSE.index(-k), g, backward)
+
+    def turn_right(t, j):
+        for g in range(groups):
+            re, im = load(where_ref[2 + 2 * t], g)
+            if j == 0:
+                store(right_turned, t % slots, 0, g, turn_by(re, im, *table[4], False)[0])
+                store(right_turned, t % slots, 1, g, (re, im))
+            else:
+                forward, backward = turn_by(re, im, *table[j], True)
+                store(right_turned, t % slots, 2 * j, g, forward)
+                store(right_turned, t % slots, 2 * j + 1, g, backward)
+
+    slots = left_turned.shape[0]
+    partial = refs[-6] if add else out_ref
+    copies = []
+    steps = [(t, j) for t in range(tiles) for j in range(len(FINE_PAIRS))]
+    turn_left(0)
+    turn_right(0, 0)
+    for (t, j), after in zip(steps, steps[1:] + [None]):
+        if after:
+            if after[1] == 0:
+                turn_left(after[0])
+            turn_right(*after)
+        total = lax.dot_general(
+            left_turned[t % slots],
+            right_turned[t % slots, 2 * j * TILE:2 * (j + 1) * TILE, :],
+            (((1,), (1,)), ((), ())),
+            preferred_element_type=jnp.float32,
+        )
+        for s in range(2):
+            fine = FINE_PAIRS[j][s] + 4
             for u in range(len(COARSE)):
-                for s in range(2):
-                    fine = FINE_PAIRS[j][s] + 4
-                    value = total[u * TILE:(u + 1) * TILE, s * TILE:(s + 1) * TILE]
-                    partial[t, u, fine] = partial[t, u, fine] + value if add else value
+                value = total[u * TILE:(u + 1) * TILE, s * TILE:(s + 1) * TILE]
+                partial[t, u, fine] = partial[t, u, fine] + value if add else value
             if add:
-                for s in range(2):
-                    fine = FINE_PAIRS[j][s] + 4
-                    copy = pltpu.make_async_copy(partial.at[t, :, fine], out_ref.at[t, :, fine], sem)
-                    copy.start()
-                    copies.append(copy)
+                copy = pltpu.make_async_copy(partial.at[t, :, fine], out_ref.at[t, :, fine], sem)
+                copy.start()
+                copies.append(copy)
     for copy in copies:
         copy.wait()
 
@@ -185,7 +192,7 @@
         first += block.shape[0]
 
 
-def stack(blocks):
+def stack(blocks, flops=0):
     depth = sum(block.shape[0] for block in blocks)
     return pl.pallas_call(
         stack_kernel,
@@ -193,6 +200,7 @@
         in_specs=[VMEM] * len(blocks),
         out_specs=VMEM,
         compiler_params=pltpu.CompilerParams(vmem_limit_bytes=SMALL),
+        cost_estimate=pl.CostEstimate(flops=flops, bytes_accessed=0, transcendentals=0),
         name="stack",
     )(*blocks)
 
@@ -200,7 +208,7 @@
 def halves(white):
     groups = lax.axis_size("tm")
     blocks = [white[None]] + [swap(white[None], "tm", k) for k in range(1, groups)]
-    return [stack(blocks[first:first + groups // 2]) for first in (0, groups // 2)]
+    return stack(blocks[:groups // 2]), stack(blocks[groups // 2:], flops=10**9)
 
 
 def between_devices(half):

time: 31 us -> 26.4 us (0.85)
  starting transfers between devices: 18 us -> 15.3 us
  waiting for transfers between devices: 5.42 us -> 3.5 us
    ppermute x11, starting transfers between devices: 18 us -> 15.3 us  [swap(): lax.ppermute(array, axis, [(i, i ^ k) for i in range(lax.axis_size(axis))])]
    ppermute x11, waiting for transfers between devices: 5.42 us -> 3.5 us  [swap(): lax.ppermute(array, axis, [(i, i ^ k) for i in range(lax.axis_size(axis))])]
  transfers between devices with their start and end apart: 11 -> 11, of which waited for: 3 -> 3; matrix products, arithmetic and copies ran while one was open for 1% -> 1% of each run, Pallas kernels for 7% -> 8%
where the time goes in v10:
time: 26.4 us; the launch traced here: 26.2 us
  starting transfers between devices  15.3 us (58%)
  Pallas kernels  7.01 us (27%)
  waiting for transfers between devices  3.5 us (13%)
    ppermute x11, starting transfers between devices, swap(): lax.ppermute(array, axis, [(i, i ^ k) for i in range(lax.axis_size(axis))])  15.3 us
    pallas_call x2, Pallas kernels, correlate(): pl.pallas_call(lambda *refs: correlate_kernel(norm, add, tiles, *refs), o...  5.66 us
    ppermute x11, waiting for transfers between devices, swap(): lax.ppermute(array, axis, [(i, i ^ k) for i in range(lax.axis_size(axis))])  3.5 us
    pallas_call x1, Pallas kernels, whiten(): pl.pallas_call(whiten_kernel, out_shape=jax.ShapeDtypeStruct((chans, bins...  1.29 us
  transfers between devices with their start and end apart: 11, of which 3 were waited for; matrix products, arithmetic and copies ran while one was open for 1% of the time, Pallas kernels for 8%

profile of v10, /device:TPU:1, one launch (start us, length us, event | category | flops | bytes accessed | tf_op | source)
XLA Modules:
  0.0 26.2 jit_solution(12166837565930006136)
XLA Ops:
  0.0 0.0 copy-start
  0.0 1.3 %whiten.1 = bf16[96,256]{1,0:T(8,128)(2,1)S(1)} custom-call(bf16[64,2,2,96]{3,2,1,0:T(2,128)(2,1)} %spectra_hbm.1, s32[1,96]{1,0:T(1,128)} %bitcast.8), custom_call_target="tpu_custom_call" | custom-call | tf_op jit(solution)/shard_map/whiten/pallas_call | solution.py:55
  1.3 2.2 %collective-permute-start.6 = (bf16[1,96,256]{2,1,0:T(8,128)(2,1)S(1)}, bf16[1,96,256]{2,1,0:T(8,128)(2,1)S(1)}, u32[]{:S(2)}, u32[]{:S(2)}) collective-permute-start(bf16[1,96,256]{2,1,0:T(8,128)(2,1)S(1)} %bitcast.4), channel_id=1, source_target_pairs={{0,1},{1,0},{2,3},{3,2},{4,5},{5,4},{6,7},{7,6},{8,9},{9,8},{10,11... | collective-permute-start | bytes 147464 | tf_op jit(solution)/shard_map/ppermute | solution.py:184
  3.5 2.2 %collective-permute-start.1 = (bf16[1,96,256]{2,1,0:T(8,128)(2,1)S(1)}, bf16[1,96,256]{2,1,0:T(8,128)(2,1)S(1)}, u32[]{:S(2)}, u32[]{:S(2)}) collective-permute-start(bf16[1,96,256]{2,1,0:T(8,128)(2,1)S(1)} %bitcast.5), channel_id=1, source_target_pairs={{0,3},{1,2},{2,1},{3,0},{4,7},{5,6},{6,5},{7,4},{8,11},{9,10},{10,... | collective-permute-start | bytes 147464 | tf_op jit(solution)/shard_map/ppermute | solution.py:184
  5.7 0.1 collective-permute-start
  5.8 0.0 collective-permute-done.6.refs_1_
  5.8 2.2 %collective-permute-start.9 = (bf16[2,96,256]{2,1,0:T(8,128)(2,1)S(1)}, bf16[2,96,256]{2,1,0:T(8,128)(2,1)S(1)}, u32[]{:S(2)}, u32[]{:S(2)}) collective-permute-start(bf16[2,96,256]{2,1,0:T(8,128)(2,1)S(1)} %stack.6.refs_0_), channel_id=1, source_target_pairs={{0,24},{4,28},{8,16},{12,20},{16,8},{20,12},{24,0},{28,4},{1,25},{... | collective-permute-start | bytes 294920 | tf_op jit(solution)/shard_map/ppermute | solution.py:184
  8.1 0.2 collective-permute-start.8
  8.3 0.3 collective-permute-start.7
  8.5 0.2 collective-permute-done.1.refs_1_
  8.7 1.9 %collective-permute-done.refs_0_ = bf16[1,96,256]{2,1,0:T(8,128)(2,1)S(1)} collective-permute-done((bf16[1,96,256]{2,1,0:T(8,128)(2,1)S(1)}, bf16[1,96,256]{2,1,0:T(8,128)(2,1)S(1)}, u32[]{:S(2)}, u32[]{:S(2)}) %collective-permute-start) | collective-permute-done | bytes 49184 | tf_op jit(solution)/shard_map/ppermute | solution.py:184
  10.6 2.2 %collective-permute-start.4 = (bf16[2,96,256]{2,1,0:T(8,128)(2,1)S(1)}, bf16[2,96,256]{2,1,0:T(8,128)(2,1)S(1)}, u32[]{:S(2)}, u32[]{:S(2)}) collective-permute-start(bf16[2,96,256]{2,1,0:T(8,128)(2,1)S(1)} %stack.4.refs_0_), channel_id=1, source_target_pairs={{0,24},{4,28},{8,16},{12,20},{16,8},{20,12},{24,0},{28,4},{1,25},{... | collective-permute-start | bytes 294920 | tf_op jit(solution)/shard_map/ppermute | solution.py:184
  12.8 0.2 collective-permute-start.3
  13.0 0.0 collective-permute-done.9.refs_3_
  13.1 0.3 collective-permute-start.2
  13.3 0.0 collective-permute-done.8.refs_2_
  13.3 0.0 collective-permute-done.7.refs_1_
  13.3 2.8 %collective-permute-start.10 = (bf16[8,96,256]{2,1,0:T(8,128)(2,1)S(1)}, bf16[8,96,256]{2,1,0:T(8,128)(2,1)S(1)}, u32[]{:S(2)}, u32[]{:S(2)}) collective-permute-start(bf16[8,96,256]{2,1,0:T(8,128)(2,1)S(1)} %stack.7.refs_1_), channel_id=1, source_target_pairs={{0,4},{4,0},{8,12},{12,8},{16,20},{20,16},{24,28},{28,24},{1,5},{5... | collective-permute-start | bytes 1179656 | tf_op jit(solution)/shard_map/ppermute | solution.py:184
  16.1 0.0 collective-permute-done.4.refs_3_
  16.1 1.4 %collective-permute-done.3.refs_2_ = bf16[2,96,256]{2,1,0:T(8,128)(2,1)S(1)} collective-permute-done((bf16[2,96,256]{2,1,0:T(8,128)(2,1)S(1)}, bf16[2,96,256]{2,1,0:T(8,128)(2,1)S(1)}, u32[]{:S(2)}, u32[]{:S(2)}) %collective-permute-start.3) | collective-permute-done | bytes 98336 | tf_op jit(solution)/shard_map/ppermute | solution.py:184
  17.6 0.0 collective-permute-done.2.refs_1_
  17.6 2.6 %collective-permute-start.5 = (bf16[8,96,256]{2,1,0:T(8,128)(2,1)S(1)}, bf16[8,96,256]{2,1,0:T(8,128)(2,1)S(1)}, u32[]{:S(2)}, u32[]{:S(2)}) collective-permute-start(bf16[8,96,256]{2,1,0:T(8,128)(2,1)S(1)} %stack.5.refs_1_), channel_id=1, source_target_pairs={{0,4},{4,0},{8,12},{12,8},{16,20},{20,16},{24,28},{28,24},{1,5},{5... | collective-permute-start | bytes 1179656 | tf_op jit(solution)/shard_map/ppermute | solution.py:184
  20.2 0.0 copy-done
  20.2 0.1 constant_dynamic-slice_fusion
  20.3 0.1 copy.4
  20.4 0.1 reshape.13
  20.4 0.1 pad_add_fusion.refs_0_
  20.5 0.0 collective-permute-done.10.refs_2_
  20.5 2.2 %correlate.1.refs_3_ = f32[2,4,8,128,128]{4,3,2,1,0:T(8,128)S(1)} custom-call(s32[5]{0:T(128)S(1)} %pad_add_fusion.refs_0_, bf16[8,96,256]{2,1,0:T(8,128)(2,1)S(1)} %stack.7.refs_1_, bf16[8,96,256]{2,1,0:T(8,128)(2,1)S(1)} %collective-permute-done.10.refs_2_), custom_call_target="tpu_custom_call" | custom-call | tf_op jit(solution)/shard_map/correlate/pallas_call | solution.py:164
  22.7 0.0 collective-permute-done.5.refs_2_
  22.7 3.5 %correlate_add.1 = f32[2,4,8,128,128]{4,3,2,1,0:T(8,128)} custom-call(s32[5]{0:T(128)S(1)} %pad_add_fusion.refs_0_, bf16[8,96,256]{2,1,0:T(8,128)(2,1)S(1)} %stack.5.refs_1_, bf16[8,96,256]{2,1,0:T(8,128)(2,1)S(1)} %collective-permute-done.5.refs_2_, f32[2,4,8,128,128]{4,3,2,1,0:T(8,128)S(1)} %correlate.1.refs_3_), custom_call_target="tpu_custom_call" | custom-call | tf_op jit(solution)/shard_map/correlate_add/pallas_call | solution.py:164
  (4 shorter events, 0.1 us)
Async XLA Ops:
  0.0 20.2 %copy-start = (s32[8,2]{0,1:T(2,128)S(1)}, s32[8,2]{0,1:T(2,128)}, u32[]{:S(2)}) copy-start(s32[8,2]{0,1:T(2,128)} %param.5) | copy-start | bytes 196
  1.3 4.5 %collective-permute-start.6 = (bf16[1,96,256]{2,1,0:T(8,128)(2,1)S(1)}, bf16[1,96,256]{2,1,0:T(8,128)(2,1)S(1)}, u32[]{:S(2)}, u32[]{:S(2)}) collective-permute-start(bf16[1,96,256]{2,1,0:T(8,128)(2,1)S(1)} %bitcast.4), channel_id=1, source_target_pairs={{0,1},{1,0},{2,3},{3,2},{4,5},{5,4},{6,7},{7,6},{8,9},{9,8},{10,11... | collective-permute-start | bytes 147464 | tf_op jit(solution)/shard_map/ppermute | solution.py:184
  3.5 5.2 %collective-permute-start.1 = (bf16[1,96,256]{2,1,0:T(8,128)(2,1)S(1)}, bf16[1,96,256]{2,1,0:T(8,128)(2,1)S(1)}, u32[]{:S(2)}, u32[]{:S(2)}) collective-permute-start(bf16[1,96,256]{2,1,0:T(8,128)(2,1)S(1)} %bitcast.5), channel_id=1, source_target_pairs={{0,3},{1,2},{2,1},{3,0},{4,7},{5,6},{6,5},{7,4},{8,11},{9,10},{10,... | collective-permute-start | bytes 147464 | tf_op jit(solution)/shard_map/ppermute | solution.py:184
  5.7 4.9 %collective-permute-start = (bf16[1,96,256]{2,1,0:T(8,128)(2,1)S(1)}, bf16[1,96,256]{2,1,0:T(8,128)(2,1)S(1)}, u32[]{:S(2)}, u32[]{:S(2)}) collective-permute-start(bf16[1,96,256]{2,1,0:T(8,128)(2,1)S(1)} %bitcast.6), channel_id=1, source_target_pairs={{0,2},{1,3},{2,0},{3,1},{4,6},{5,7},{6,4},{7,5},{8,10},{9,11},{10,... | collective-permute-start | bytes 147464 | tf_op jit(solution)/shard_map/ppermute | solution.py:184
  5.8 7.2 %collective-permute-start.9 = (bf16[2,96,256]{2,1,0:T(8,128)(2,1)S(1)}, bf16[2,96,256]{2,1,0:T(8,128)(2,1)S(1)}, u32[]{:S(2)}, u32[]{:S(2)}) collective-permute-start(bf16[2,96,256]{2,1,0:T(8,128)(2,1)S(1)} %stack.6.refs_0_), channel_id=1, source_target_pairs={{0,24},{4,28},{8,16},{12,20},{16,8},{20,12},{24,0},{28,4},{1,25},{... | collective-permute-start | bytes 294920 | tf_op jit(solution)/shard_map/ppermute | solution.py:184
  8.1 5.3 %collective-permute-start.8 = (bf16[2,96,256]{2,1,0:T(8,128)(2,1)S(1)}, bf16[2,96,256]{2,1,0:T(8,128)(2,1)S(1)}, u32[]{:S(2)}, u32[]{:S(2)}) collective-permute-start(bf16[2,96,256]{2,1,0:T(8,128)(2,1)S(1)} %stack.6.refs_0_), channel_id=1, source_target_pairs={{0,16},{4,20},{8,24},{12,28},{16,0},{20,4},{24,8},{28,12},{1,17},{... | collective-permute-start | bytes 294920 | tf_op jit(solution)/shard_map/ppermute | solution.py:184
  8.3 5.0 %collective-permute-start.7 = (bf16[2,96,256]{2,1,0:T(8,128)(2,1)S(1)}, bf16[2,96,256]{2,1,0:T(8,128)(2,1)S(1)}, u32[]{:S(2)}, u32[]{:S(2)}) collective-permute-start(bf16[2,96,256]{2,1,0:T(8,128)(2,1)S(1)} %stack.6.refs_0_), channel_id=1, source_target_pairs={{0,8},{4,12},{8,0},{12,4},{16,24},{20,28},{24,16},{28,20},{1,9},{5... | collective-permute-start | bytes 294920 | tf_op jit(solution)/shard_map/ppermute | solution.py:184
  10.6 5.5 %collective-permute-start.4 = (bf16[2,96,256]{2,1,0:T(8,128)(2,1)S(1)}, bf16[2,96,256]{2,1,0:T(8,128)(2,1)S(1)}, u32[]{:S(2)}, u32[]{:S(2)}) collective-permute-start(bf16[2,96,256]{2,1,0:T(8,128)(2,1)S(1)} %stack.4.refs_0_), channel_id=1, source_target_pairs={{0,24},{4,28},{8,16},{12,20},{16,8},{20,12},{24,0},{28,4},{1,25},{... | collective-permute-start | bytes 294920 | tf_op jit(solution)/shard_map/ppermute | solution.py:184
  12.8 4.7 %collective-permute-start.3 = (bf16[2,96,256]{2,1,0:T(8,128)(2,1)S(1)}, bf16[2,96,256]{2,1,0:T(8,128)(2,1)S(1)}, u32[]{:S(2)}, u32[]{:S(2)}) collective-permute-start(bf16[2,96,256]{2,1,0:T(8,128)(2,1)S(1)} %stack.4.refs_0_), channel_id=1, source_target_pairs={{0,16},{4,20},{8,24},{12,28},{16,0},{20,4},{24,8},{28,12},{1,17},{... | collective-permute-start | bytes 294920 | tf_op jit(solution)/shard_map/ppermute | solution.py:184
  13.1 4.5 %collective-permute-start.2 = (bf16[2,96,256]{2,1,0:T(8,128)(2,1)S(1)}, bf16[2,96,256]{2,1,0:T(8,128)(2,1)S(1)}, u32[]{:S(2)}, u32[]{:S(2)}) collective-permute-start(bf16[2,96,256]{2,1,0:T(8,128)(2,1)S(1)} %stack.4.refs_0_), channel_id=1, source_target_pairs={{0,8},{4,12},{8,0},{12,4},{16,24},{20,28},{24,16},{28,20},{1,9},{5... | collective-permute-start | bytes 294920 | tf_op jit(solution)/shard_map/ppermute | solution.py:184
  13.3 7.2 %collective-permute-start.10 = (bf16[8,96,256]{2,1,0:T(8,128)(2,1)S(1)}, bf16[8,96,256]{2,1,0:T(8,128)(2,1)S(1)}, u32[]{:S(2)}, u32[]{:S(2)}) collective-permute-start(bf16[8,96,256]{2,1,0:T(8,128)(2,1)S(1)} %stack.7.refs_1_), channel_id=1, source_target_pairs={{0,4},{4,0},{8,12},{12,8},{16,20},{20,16},{24,28},{28,24},{1,5},{5... | collective-permute-start | bytes 1179656 | tf_op jit(solution)/shard_map/ppermute | solution.py:184
  17.6 5.1 %collective-permute-start.5 = (bf16[8,96,256]{2,1,0:T(8,128)(2,1)S(1)}, bf16[8,96,256]{2,1,0:T(8,128)(2,1)S(1)}, u32[]{:S(2)}, u32[]{:S(2)}) collective-permute-start(bf16[8,96,256]{2,1,0:T(8,128)(2,1)S(1)} %stack.5.refs_1_), channel_id=1, source_target_pairs={{0,4},{4,0},{8,12},{12,8},{16,20},{20,16},{24,28},{28,24},{1,5},{5... | collective-permute-start | bytes 1179656 | tf_op jit(solution)/shard_map/ppermute | solution.py:184

commit v11 on v9

--- a/solution.py
+++ b/solution.py
@@ -14,7 +14,6 @@
 CORES = 2
 SMALL = 4 * 1024 * 1024
 VMEM = pl.BlockSpec(memory_space=pltpu.VMEM)
-SMEM = pl.BlockSpec(memory_space=pltpu.SMEM)
 COARSE = (-12, -4, 4, 12)
 FINE_PAIRS = ((-4, 0), (-1, 1), (-2, 2), (-3, 3))
 
@@ -73,9 +72,10 @@
     return (forward, (rc + is_, ic - rs)) if both else (forward,)
 
 
-def correlate_kernel(norm, add, tiles, where_ref, *refs):
-    pieces = refs[:-5 - add]
-    out_ref, spectra, left_turned, right_turned, sem = refs[-5:]
+def correlate_kernel(norm, picked, adds, where_ref, own_ref, sib_ref, *refs):
+    partials = refs[:adds]
+    out_ref = refs[adds]
+    spectra, left_turned, right_turned, *more = refs[adds + 1:]
     groups, _, lanes = spectra.shape
     half = lanes // 2
     hours_dev = half // F
@@ -87,10 +87,11 @@
     cos, sin = jnp.cos(angle), jnp.sin(angle)
     table = {k: (cos[i:i + 1], sin[i:i + 1]) for k, i in ((1, 1), (2, 2), (3, 3), (4, 4), (12, 6))}
 
-    rows = pieces[0].shape[1]
-    for core, piece in enumerate(pieces):
+    chan = where_ref[0, 0]
+    rows = own_ref.shape[1]
+    for core, piece in enumerate((own_ref, sib_ref)):
         for k in range(piece.shape[0] // groups):
-            place = pl.multiple_of((where_ref[0] ^ (CORES * k + core)) * rows, 32)
+            place = pl.multiple_of((chan ^ (CORES * k + core)) * rows, 32)
             spectra[:, pl.ds(place, rows), :] = piece[k * groups:(k + 1) * groups]
 
     def load(block, g):
@@ -103,18 +104,18 @@
         ref[slot, rows_at, g * lanes + half:(g + 1) * lanes] = value[1].astype(jnp.bfloat16)
 
     copies = []
-    for t in range(tiles):
-        slot = t % left_turned.shape[0]
+    for i, t in enumerate(picked):
+        slot = i % left_turned.shape[0]
+        left_block, right_block = where_ref[0, 1 + 2 * t], where_ref[0, 2 + 2 * t]
         for g in range(groups):
-            re, im = load(where_ref[1 + 2 * t], g)
-            re, im = re * norm, im * norm
+            re, im = load(left_block, g)
             for k in (4, 12):
-                forward, backward = turn_by(re, im, *table[k], True)
+                forward, backward = turn_by(re, im, *(norm * part for part in table[k]), True)
                 store(left_turned, slot, COARSE.index(k), g, forward)
                 store(left_turned, slot, COARSE.index(-k), g, backward)
         for j in range(len(FINE_PAIRS)):
             for g in range(groups):
-                re, im = load(where_ref[2 + 2 * t], g)
+                re, im = load(right_block, g)
                 if j == 0:
                     store(right_turned, slot, 0, g, turn_by(re, im, *table[4], False)[0])
                     store(right_turned, slot, 1, g, (re, im))
@@ -128,84 +129,86 @@
                 (((1,), (1,)), ((), ())),
                 preferred_element_type=jnp.float32,
             )
-            partial = refs[-6] if add else out_ref
-            for u in range(len(COARSE)):
-                for s in range(2):
-                    fine = FINE_PAIRS[j][s] + 4
+            for s in range(2):
+                fine = FINE_PAIRS[j][s] + 4
+                for u in range(len(COARSE)):
                     value = total[u * TILE:(u + 1) * TILE, s * TILE:(s + 1) * TILE]
-                    partial[t, u, fine] = partial[t, u, fine] + value if add else value
-            if add:
-                for s in range(2):
-                    fine = FINE_PAIRS[j][s] + 4
-                    copy = pltpu.make_async_copy(partial.at[t, :, fine], out_ref.at[t, :, fine], sem)
+                    if adds:
+                        each = len(picked) // adds
+                        more[0][i, u, fine] = partials[i // each][i % each, u, fine] + value
+                    else:
+                        out_ref[i, u, fine] = value
+                if adds:
+                    copy = pltpu.make_async_copy(more[0].at[i, :, fine], out_ref.at[i, :, fine], more[1])
                     copy.start()
                     copies.append(copy)
     for copy in copies:
         copy.wait()
 
 
-def correlate(pieces, groups, where, tiles, hours, partial=None):
+def correlate(pieces, groups, where, picked, hours, partials=()):
     depth, rows, lanes = pieces[0].shape
     fine = 2 * len(FINE_PAIRS)
-    shape = (tiles, len(COARSE), fine, TILE, TILE)
+    shape = (len(picked), len(COARSE), fine, TILE, TILE)
     norm = 1.0 / math.sqrt(F * hours)
-    slots = min(tiles, 2)
+    slots = min(len(picked), 2)
     chans = len(pieces) * depth // groups * rows
     scratch = 2 * (groups * chans * lanes + slots * (len(COARSE) + fine) * TILE * groups * lanes)
-    add = partial is not None
-    more = (partial,) if add else ()
+    adds = len(partials)
+    more = []
+    if adds:
+        more = [pltpu.VMEM(shape, jnp.float32), pltpu.SemaphoreType.DMA]
+        scratch += 4 * math.prod(shape)
     return pl.pallas_call(
-        lambda *refs: correlate_kernel(norm, add, tiles, *refs),
+        lambda *refs: correlate_kernel(norm, picked, adds, *refs),
         out_shape=jax.ShapeDtypeStruct(shape, jnp.float32),
-        in_specs=[SMEM] + [VMEM] * (len(pieces) + add),
-        out_specs=pl.BlockSpec(memory_space=pl.ANY) if add else VMEM,
+        in_specs=[VMEM] * (1 + len(pieces) + adds),
+        out_specs=pl.BlockSpec(memory_space=pl.ANY) if adds else VMEM,
         scratch_shapes=[
             pltpu.VMEM((groups, chans, lanes), jnp.bfloat16),
             pltpu.VMEM((slots, len(COARSE) * TILE, groups * lanes), jnp.bfloat16),
             pltpu.VMEM((slots, fine * TILE, groups * lanes), jnp.bfloat16),
-            pltpu.SemaphoreType.DMA,
+            *more,
         ],
         compiler_params=pltpu.CompilerParams(vmem_limit_bytes=scratch + SMALL),
-        cost_estimate=pl.CostEstimate(
-            flops=0, bytes_accessed=0, transcendentals=0
-        ),
-        name="correlate_add" if add else "correlate",
-    )(where, *pieces, *more)
+        cost_estimate=pl.CostEstimate(flops=0, bytes_accessed=0, transcendentals=0),
+        name="correlate_add" if adds else "correlate",
+    )(where, *pieces, *partials)
 
 
 def swap(array, axis, k):
     return lax.ppermute(array, axis, [(i, i ^ k) for i in range(lax.axis_size(axis))])
 
 
-def stack_kernel(*refs):
+def stack_kernel(blocks, *refs):
     out_ref = refs[-1]
     first = 0
-    for block in refs[:-1]:
+    for block in refs[:blocks]:
         out_ref[first:first + block.shape[0]] = block[...]
         first += block.shape[0]
 
 
-def stack(blocks):
+def stack(blocks, after=(), flops=0):
     depth = sum(block.shape[0] for block in blocks)
     return pl.pallas_call(
-        stack_kernel,
+        lambda *refs: stack_kernel(len(blocks), *refs),
         out_shape=jax.ShapeDtypeStruct((depth, *blocks[0].shape[1:]), blocks[0].dtype),
-        in_specs=[VMEM] * len(blocks),
+        in_specs=[VMEM] * len(blocks) + [pl.BlockSpec(memory_space=pl.ANY)] * len(after),
         out_specs=VMEM,
         compiler_params=pltpu.CompilerParams(vmem_limit_bytes=SMALL),
+        cost_estimate=pl.CostEstimate(flops=flops, bytes_accessed=0, transcendentals=0),
         name="stack",
-    )(*blocks)
-
-
-def halves(white):
+    )(*blocks, *after)
+
+
+def halves(white, where):
     groups = lax.axis_size("tm")
     blocks = [white[None]] + [swap(white[None], "tm", k) for k in range(1, groups)]
-    return [stack(blocks[first:first + groups // 2]) for first in (0, groups // 2)]
-
-
-def between_devices(half):
-    own = stack([half] + [swap(half, "chan", k) for k in range(CORES, lax.axis_size("chan"), CORES)])
-    return own, swap(own, "chan", 1)
+    return stack(blocks[:groups // 2], after=(where,)), stack(blocks[groups // 2:], flops=10**9)
+
+
+def between_chips(half):
+    return [half] + [swap(half, "chan", k) for k in range(CORES, lax.axis_size("chan"), CORES)]
 
 
 def per_device(spectra, bad_channels, tile_list):
@@ -214,10 +217,14 @@
     tiles = tile_list.shape[0] // groups
     white = whiten(spectra, bad_channels)
     pairs = lax.dynamic_slice_in_dim(tile_list, lax.axis_index("tm") * tiles, tiles, axis=0)
-    where = jnp.concatenate([lax.axis_index("chan").reshape(1), pairs.reshape(-1)]).astype(jnp.int32)
-    near, far = [between_devices(half) for half in halves(white)]
-    partial = correlate(near, groups // 2, where, tiles, hours)
-    out = correlate(far, groups // 2, where, tiles, hours, partial)
+    where = jnp.concatenate([lax.axis_index("chan").reshape(1), pairs.reshape(-1)]).astype(jnp.int32).reshape(1, -1)
+    near, far = [between_chips(half) for half in halves(white, where)]
+    near = stack(near)
+    near = (near, swap(near, "chan", 1))
+    far = stack(far)
+    far = (far, swap(far, "chan", 1))
+    partial = correlate(near, groups // 2, where, range(tiles), hours)
+    out = correlate(far, groups // 2, where, range(tiles), hours, [partial])
     return out.reshape(tiles, LAGS, TILE, TILE)
 
 

time: 31 us -> 25.1 us (0.81)
  waiting for transfers between devices: 5.42 us -> 2.9 us
  starting transfers between devices: 18 us -> 15.6 us
  Pallas kernels: 6.97 us -> 6.11 us
    ppermute x11, waiting for transfers between devices: 5.42 us -> 2.9 us  [swap(): lax.ppermute(array, axis, [(i, i ^ k) for i in range(lax.axis_size(axis))])]
    ppermute x11, starting transfers between devices: 18 us -> 15.6 us  [swap(): lax.ppermute(array, axis, [(i, i ^ k) for i in range(lax.axis_size(axis))])]
    pallas_call x6, Pallas kernels: 5.68 us -> 4.82 us  [the longest x2 4.75 us: correlate(): pl.pallas_call(lambda *refs: correlate_kernel(norm, picked, adds, *refs),...]
  transfers between devices with their start and end apart: 11 -> 11, of which waited for: 3 -> 2; matrix products, arithmetic and copies ran while one was open for 1% -> 1% of each run, Pallas kernels for 7% -> 7%
where the time goes in v11:
time: 25.1 us; the launch traced here: 25 us
  starting transfers between devices  15.6 us (62%)
  Pallas kernels  6.11 us (24%)
  waiting for transfers between devices  2.9 us (12%)
  local copies, waits for them, and re-layouts  0.26 us (1%)
    ppermute x11, starting transfers between devices, swap(): lax.ppermute(array, axis, [(i, i ^ k) for i in range(lax.axis_size(axis))])  15.6 us
    pallas_call x2, Pallas kernels, correlate(): pl.pallas_call(lambda *refs: correlate_kernel(norm, picked, adds, *refs),...  4.75 us
    ppermute x11, waiting for transfers between devices, swap(): lax.ppermute(array, axis, [(i, i ^ k) for i in range(lax.axis_size(axis))])  2.9 us
    pallas_call x1, Pallas kernels, whiten(): pl.pallas_call(whiten_kernel, out_shape=jax.ShapeDtypeStruct((chans, bins...  1.29 us
  transfers between devices with their start and end apart: 11, of which 2 were waited for; matrix products, arithmetic and copies ran while one was open for 1% of the time, Pallas kernels for 7%

profile of v11, /device:TPU:1, one launch (start us, length us, event | category | flops | bytes accessed | tf_op | source)
XLA Modules:
  0.0 25.0 jit_solution(17153226307064151554)
XLA Ops:
  0.0 0.0 copy-start
  0.0 1.3 %whiten.1 = bf16[96,256]{1,0:T(8,128)(2,1)S(1)} custom-call(bf16[64,2,2,96]{3,2,1,0:T(2,128)(2,1)} %spectra_hbm.1, s32[1,96]{1,0:T(1,128)} %bitcast.10), custom_call_target="tpu_custom_call" | custom-call | tf_op jit(solution)/shard_map/whiten/pallas_call | solution.py:54
  1.3 2.2 %collective-permute-start.6 = (bf16[1,96,256]{2,1,0:T(8,128)(2,1)S(1)}, bf16[1,96,256]{2,1,0:T(8,128)(2,1)S(1)}, u32[]{:S(2)}, u32[]{:S(2)}) collective-permute-start(bf16[1,96,256]{2,1,0:T(8,128)(2,1)S(1)} %bitcast.6), channel_id=1, source_target_pairs={{0,1},{1,0},{2,3},{3,2},{4,5},{5,4},{6,7},{7,6},{8,9},{9,8},{10,11... | collective-permute-start | bytes 147464 | tf_op jit(solution)/shard_map/ppermute | solution.py:180
  3.5 2.2 %collective-permute-start.1 = (bf16[1,96,256]{2,1,0:T(8,128)(2,1)S(1)}, bf16[1,96,256]{2,1,0:T(8,128)(2,1)S(1)}, u32[]{:S(2)}, u32[]{:S(2)}) collective-permute-start(bf16[1,96,256]{2,1,0:T(8,128)(2,1)S(1)} %bitcast.7), channel_id=1, source_target_pairs={{0,3},{1,2},{2,1},{3,0},{4,7},{5,6},{6,5},{7,4},{8,11},{9,10},{10,... | collective-permute-start | bytes 147464 | tf_op jit(solution)/shard_map/ppermute | solution.py:180
  5.7 0.1 collective-permute-start
  5.8 0.0 copy-done
  5.8 0.1 constant_dynamic-slice_fusion
  5.9 0.1 copy.4
  6.0 0.1 reshape.16
  6.1 0.1 add_bitcast_fusion.refs_2_.refs_0_
  6.1 0.0 collective-permute-done.6.refs_1_
  6.2 2.2 %collective-permute-start.9 = (bf16[2,96,256]{2,1,0:T(8,128)(2,1)S(1)}, bf16[2,96,256]{2,1,0:T(8,128)(2,1)S(1)}, u32[]{:S(2)}, u32[]{:S(2)}) collective-permute-start(bf16[2,96,256]{2,1,0:T(8,128)(2,1)S(1)} %stack.6.refs_0_), channel_id=1, source_target_pairs={{0,24},{4,28},{8,16},{12,20},{16,8},{20,12},{24,0},{28,4},{1,25},{... | collective-permute-start | bytes 294920 | tf_op jit(solution)/shard_map/ppermute | solution.py:180
  8.4 0.2 collective-permute-start.8
  8.6 0.3 %collective-permute-start.7 = (bf16[2,96,256]{2,1,0:T(8,128)(2,1)S(1)}, bf16[2,96,256]{2,1,0:T(8,128)(2,1)S(1)}, u32[]{:S(2)}, u32[]{:S(2)}) collective-permute-start(bf16[2,96,256]{2,1,0:T(8,128)(2,1)S(1)} %stack.6.refs_0_), channel_id=1, source_target_pairs={{0,8},{4,12},{8,0},{12,4},{16,24},{20,28},{24,16},{28,20},{1,9},{5... | collective-permute-start | bytes 294920 | tf_op jit(solution)/shard_map/ppermute | solution.py:180
  8.9 0.0 collective-permute-done.1.refs_1_
  8.9 1.7 %collective-permute-done.refs_0_ = bf16[1,96,256]{2,1,0:T(8,128)(2,1)S(1)} collective-permute-done((bf16[1,96,256]{2,1,0:T(8,128)(2,1)S(1)}, bf16[1,96,256]{2,1,0:T(8,128)(2,1)S(1)}, u32[]{:S(2)}, u32[]{:S(2)}) %collective-permute-start) | collective-permute-done | bytes 49184 | tf_op jit(solution)/shard_map/ppermute | solution.py:180
  10.6 2.2 %collective-permute-start.4 = (bf16[2,96,256]{2,1,0:T(8,128)(2,1)S(1)}, bf16[2,96,256]{2,1,0:T(8,128)(2,1)S(1)}, u32[]{:S(2)}, u32[]{:S(2)}) collective-permute-start(bf16[2,96,256]{2,1,0:T(8,128)(2,1)S(1)} %stack.4.refs_0_), channel_id=1, source_target_pairs={{0,24},{4,28},{8,16},{12,20},{16,8},{20,12},{24,0},{28,4},{1,25},{... | collective-permute-start | bytes 294920 | tf_op jit(solution)/shard_map/ppermute | solution.py:180
  12.8 0.2 collective-permute-start.3
  13.0 0.0 collective-permute-done.9.refs_3_
  13.1 0.3 %collective-permute-start.2 = (bf16[2,96,256]{2,1,0:T(8,128)(2,1)S(1)}, bf16[2,96,256]{2,1,0:T(8,128)(2,1)S(1)}, u32[]{:S(2)}, u32[]{:S(2)}) collective-permute-start(bf16[2,96,256]{2,1,0:T(8,128)(2,1)S(1)} %stack.4.refs_0_), channel_id=1, source_target_pairs={{0,8},{4,12},{8,0},{12,4},{16,24},{20,28},{24,16},{28,20},{1,9},{5... | collective-permute-start | bytes 294920 | tf_op jit(solution)/shard_map/ppermute | solution.py:180
  13.3 0.0 collective-permute-done.8.refs_2_
  13.3 0.0 collective-permute-done.7.refs_1_
  13.3 2.8 %collective-permute-start.10 = (bf16[8,96,256]{2,1,0:T(8,128)(2,1)S(1)}, bf16[8,96,256]{2,1,0:T(8,128)(2,1)S(1)}, u32[]{:S(2)}, u32[]{:S(2)}) collective-permute-start(bf16[8,96,256]{2,1,0:T(8,128)(2,1)S(1)} %stack.7.refs_1_), channel_id=1, source_target_pairs={{0,4},{4,0},{8,12},{12,8},{16,20},{20,16},{24,28},{28,24},{1,5},{5... | collective-permute-start | bytes 1179656 | tf_op jit(solution)/shard_map/ppermute | solution.py:180
  16.1 0.0 collective-permute-done.4.refs_3_
  16.1 1.2 %collective-permute-done.3.refs_2_ = bf16[2,96,256]{2,1,0:T(8,128)(2,1)S(1)} collective-permute-done((bf16[2,96,256]{2,1,0:T(8,128)(2,1)S(1)}, bf16[2,96,256]{2,1,0:T(8,128)(2,1)S(1)}, u32[]{:S(2)}, u32[]{:S(2)}) %collective-permute-start.3) | collective-permute-done | bytes 98336 | tf_op jit(solution)/shard_map/ppermute | solution.py:180
  17.3 0.0 collective-permute-done.2.refs_1_
  17.3 2.9 %collective-permute-start.5 = (bf16[8,96,256]{2,1,0:T(8,128)(2,1)S(1)}, bf16[8,96,256]{2,1,0:T(8,128)(2,1)S(1)}, u32[]{:S(2)}, u32[]{:S(2)}) collective-permute-start(bf16[8,96,256]{2,1,0:T(8,128)(2,1)S(1)} %stack.5.refs_1_), channel_id=1, source_target_pairs={{0,4},{4,0},{8,12},{12,8},{16,20},{20,16},{24,28},{28,24},{1,5},{5... | collective-permute-start | bytes 1179656 | tf_op jit(solution)/shard_map/ppermute | solution.py:180
  20.2 0.0 collective-permute-done.10.refs_2_
  20.2 1.7 %correlate.1.refs_3_ = f32[2,4,8,128,128]{4,3,2,1,0:T(8,128)S(1)} custom-call(s32[1,5]{1,0:T(1,128)S(1)} %add_bitcast_fusion.refs_2_.refs_0_, bf16[8,96,256]{2,1,0:T(8,128)(2,1)S(1)} %stack.7.refs_1_, bf16[8,96,256]{2,1,0:T(8,128)(2,1)S(1)} %collective-permute-done.10.refs_2_), custom_call_target="tpu_custom_call" | custom-call | tf_op jit(solution)/shard_map/correlate/pallas_call | solution.py:162
  21.9 0.0 collective-permute-done.5.refs_2_
  21.9 3.0 %correlate_add.1 = f32[2,4,8,128,128]{4,3,2,1,0:T(8,128)} custom-call(s32[1,5]{1,0:T(1,128)S(1)} %add_bitcast_fusion.refs_2_.refs_0_, bf16[8,96,256]{2,1,0:T(8,128)(2,1)S(1)} %stack.5.refs_1_, bf16[8,96,256]{2,1,0:T(8,128)(2,1)S(1)} %collective-permute-done.5.refs_2_, f32[2,4,8,128,128]{4,3,2,1,0:T(8,128)S(1)} %correlate.1.refs_3_), custom_call_target="tpu_custom_call" | custom-call | tf_op jit(solution)/shard_map/correlate_add/pallas_call | solution.py:162
  (4 shorter events, 0.1 us)
Async XLA Ops:
  0.0 5.8 %copy-start = (s32[8,2]{0,1:T(2,128)S(1)}, s32[8,2]{0,1:T(2,128)}, u32[]{:S(2)}) copy-start(s32[8,2]{0,1:T(2,128)} %param.5) | copy-start | bytes 196
  1.3 4.8 %collective-permute-start.6 = (bf16[1,96,256]{2,1,0:T(8,128)(2,1)S(1)}, bf16[1,96,256]{2,1,0:T(8,128)(2,1)S(1)}, u32[]{:S(2)}, u32[]{:S(2)}) collective-permute-start(bf16[1,96,256]{2,1,0:T(8,128)(2,1)S(1)} %bitcast.6), channel_id=1, source_target_pairs={{0,1},{1,0},{2,3},{3,2},{4,5},{5,4},{6,7},{7,6},{8,9},{9,8},{10,11... | collective-permute-start | bytes 147464 | tf_op jit(solution)/shard_map/ppermute | solution.py:180
  3.5 5.4 %collective-permute-start.1 = (bf16[1,96,256]{2,1,0:T(8,128)(2,1)S(1)}, bf16[1,96,256]{2,1,0:T(8,128)(2,1)S(1)}, u32[]{:S(2)}, u32[]{:S(2)}) collective-permute-start(bf16[1,96,256]{2,1,0:T(8,128)(2,1)S(1)} %bitcast.7), channel_id=1, source_target_pairs={{0,3},{1,2},{2,1},{3,0},{4,7},{5,6},{6,5},{7,4},{8,11},{9,10},{10,... | collective-permute-start | bytes 147464 | tf_op jit(solution)/shard_map/ppermute | solution.py:180
  5.7 4.9 %collective-permute-start = (bf16[1,96,256]{2,1,0:T(8,128)(2,1)S(1)}, bf16[1,96,256]{2,1,0:T(8,128)(2,1)S(1)}, u32[]{:S(2)}, u32[]{:S(2)}) collective-permute-start(bf16[1,96,256]{2,1,0:T(8,128)(2,1)S(1)} %bitcast.8), channel_id=1, source_target_pairs={{0,2},{1,3},{2,0},{3,1},{4,6},{5,7},{6,4},{7,5},{8,10},{9,11},{10,... | collective-permute-start | bytes 147464 | tf_op jit(solution)/shard_map/ppermute | solution.py:180
  6.2 6.9 %collective-permute-start.9 = (bf16[2,96,256]{2,1,0:T(8,128)(2,1)S(1)}, bf16[2,96,256]{2,1,0:T(8,128)(2,1)S(1)}, u32[]{:S(2)}, u32[]{:S(2)}) collective-permute-start(bf16[2,96,256]{2,1,0:T(8,128)(2,1)S(1)} %stack.6.refs_0_), channel_id=1, source_target_pairs={{0,24},{4,28},{8,16},{12,20},{16,8},{20,12},{24,0},{28,4},{1,25},{... | collective-permute-start | bytes 294920 | tf_op jit(solution)/shard_map/ppermute | solution.py:180
  8.4 4.9 %collective-permute-start.8 = (bf16[2,96,256]{2,1,0:T(8,128)(2,1)S(1)}, bf16[2,96,256]{2,1,0:T(8,128)(2,1)S(1)}, u32[]{:S(2)}, u32[]{:S(2)}) collective-permute-start(bf16[2,96,256]{2,1,0:T(8,128)(2,1)S(1)} %stack.6.refs_0_), channel_id=1, source_target_pairs={{0,16},{4,20},{8,24},{12,28},{16,0},{20,4},{24,8},{28,12},{1,17},{... | collective-permute-start | bytes 294920 | tf_op jit(solution)/shard_map/ppermute | solution.py:180
  8.6 4.7 %collective-permute-start.7 = (bf16[2,96,256]{2,1,0:T(8,128)(2,1)S(1)}, bf16[2,96,256]{2,1,0:T(8,128)(2,1)S(1)}, u32[]{:S(2)}, u32[]{:S(2)}) collective-permute-start(bf16[2,96,256]{2,1,0:T(8,128)(2,1)S(1)} %stack.6.refs_0_), channel_id=1, source_target_pairs={{0,8},{4,12},{8,0},{12,4},{16,24},{20,28},{24,16},{28,20},{1,9},{5... | collective-permute-start | bytes 294920 | tf_op jit(solution)/shard_map/ppermute | solution.py:180
  10.6 5.5 %collective-permute-start.4 = (bf16[2,96,256]{2,1,0:T(8,128)(2,1)S(1)}, bf16[2,96,256]{2,1,0:T(8,128)(2,1)S(1)}, u32[]{:S(2)}, u32[]{:S(2)}) collective-permute-start(bf16[2,96,256]{2,1,0:T(8,128)(2,1)S(1)} %stack.4.refs_0_), channel_id=1, source_target_pairs={{0,24},{4,28},{8,16},{12,20},{16,8},{20,12},{24,0},{28,4},{1,25},{... | collective-permute-start | bytes 294920 | tf_op jit(solution)/shard_map/ppermute | solution.py:180
  12.8 4.5 %collective-permute-start.3 = (bf16[2,96,256]{2,1,0:T(8,128)(2,1)S(1)}, bf16[2,96,256]{2,1,0:T(8,128)(2,1)S(1)}, u32[]{:S(2)}, u32[]{:S(2)}) collective-permute-start(bf16[2,96,256]{2,1,0:T(8,128)(2,1)S(1)} %stack.4.refs_0_), channel_id=1, source_target_pairs={{0,16},{4,20},{8,24},{12,28},{16,0},{20,4},{24,8},{28,12},{1,17},{... | collective-permute-start | bytes 294920 | tf_op jit(solution)/shard_map/ppermute | solution.py:180
  13.1 4.2 %collective-permute-start.2 = (bf16[2,96,256]{2,1,0:T(8,128)(2,1)S(1)}, bf16[2,96,256]{2,1,0:T(8,128)(2,1)S(1)}, u32[]{:S(2)}, u32[]{:S(2)}) collective-permute-start(bf16[2,96,256]{2,1,0:T(8,128)(2,1)S(1)} %stack.4.refs_0_), channel_id=1, source_target_pairs={{0,8},{4,12},{8,0},{12,4},{16,24},{20,28},{24,16},{28,20},{1,9},{5... | collective-permute-start | bytes 294920 | tf_op jit(solution)/shard_map/ppermute | solution.py:180
  13.3 6.8 %collective-permute-start.10 = (bf16[8,96,256]{2,1,0:T(8,128)(2,1)S(1)}, bf16[8,96,256]{2,1,0:T(8,128)(2,1)S(1)}, u32[]{:S(2)}, u32[]{:S(2)}) collective-permute-start(bf16[8,96,256]{2,1,0:T(8,128)(2,1)S(1)} %stack.7.refs_1_), channel_id=1, source_target_pairs={{0,4},{4,0},{8,12},{12,8},{16,20},{20,16},{24,28},{28,24},{1,5},{5... | collective-permute-start | bytes 1179656 | tf_op jit(solution)/shard_map/ppermute | solution.py:180
  17.3 4.6 %collective-permute-start.5 = (bf16[8,96,256]{2,1,0:T(8,128)(2,1)S(1)}, bf16[8,96,256]{2,1,0:T(8,128)(2,1)S(1)}, u32[]{:S(2)}, u32[]{:S(2)}) collective-permute-start(bf16[8,96,256]{2,1,0:T(8,128)(2,1)S(1)} %stack.5.refs_1_), channel_id=1, source_target_pairs={{0,4},{4,0},{8,12},{12,8},{16,20},{20,16},{24,28},{28,24},{1,5},{5... | collective-permute-start | bytes 1179656 | tf_op jit(solution)/shard_map/ppermute | solution.py:180

commit v12 on v11

--- a/solution.py
+++ b/solution.py
@@ -66,6 +66,19 @@
     )(spectra, bad_channels)
 
 
+def cos_sin(turn):
+    quarter = F // 2
+    shifted = turn + quarter // 2
+    x = (shifted % quarter - quarter // 2).astype(jnp.float32) * (math.pi / F)
+    y = x * x
+    cos = 1 - y * (1 / 2 - y * (1 / 24 - y * (1 / 720 - y * (1 / 40320 - y / 3628800))))
+    sin = x * (1 - y * (1 / 6 - y * (1 / 120 - y * (1 / 5040 - y / 362880))))
+    quadrant = shifted // quarter % 4
+    odd = quadrant % 2 == 1
+    cos, sin = jnp.where(odd, sin, cos), jnp.where(odd, cos, sin)
+    return jnp.where((quadrant == 1) | (quadrant == 2), -cos, cos), jnp.where(quadrant >= 2, -sin, sin)
+
+
 def turn_by(re, im, cos, sin, both):
     rc, rs, ic, is_ = re * cos, re * sin, im * cos, im * sin
     forward = (rc - is_, rs + ic)
@@ -81,10 +94,7 @@
     hours_dev = half // F
     bin_number = lax.broadcasted_iota(jnp.int32, (8, half), 1) // hours_dev + 1
     step = lax.broadcasted_iota(jnp.int32, (8, half), 0)
-    step = jnp.where(step == 6, 12, step)
-    turn = (step * bin_number) % (2 * F)
-    angle = jnp.where(turn >= F, turn - 2 * F, turn).astype(jnp.float32) * (math.pi / F)
-    cos, sin = jnp.cos(angle), jnp.sin(angle)
+    cos, sin = cos_sin(jnp.where(step == 6, 12, step) * bin_number)
     table = {k: (cos[i:i + 1], sin[i:i + 1]) for k, i in ((1, 1), (2, 2), (3, 3), (4, 4), (12, 6))}
 
     chan = where_ref[0, 0]
@@ -140,7 +150,7 @@
                         out_ref[i, u, fine] = value
                 if adds:
                     copy = pltpu.make_async_copy(more[0].at[i, :, fine], out_ref.at[i, :, fine], more[1])
-                    copy.start()
+                    copy.start(priority=s)
                     copies.append(copy)
     for copy in copies:
         copy.wait()

time: 25.1 us -> 25.1 us (level)
  no operation moved by 1% of the time
where the time goes in v12:
time: 25.1 us; the launch traced here: 25 us
  starting transfers between devices  15.6 us (62%)
  Pallas kernels  6.11 us (24%)
  waiting for transfers between devices  2.9 us (12%)
  local copies, waits for them, and re-layouts  0.26 us (1%)
    ppermute x11, starting transfers between devices, swap(): lax.ppermute(array, axis, [(i, i ^ k) for i in range(lax.axis_size(axis))])  15.6 us
    pallas_call x2, Pallas kernels, correlate(): pl.pallas_call(lambda *refs: correlate_kernel(norm, picked, adds, *refs),...  4.75 us
    ppermute x11, waiting for transfers between devices, swap(): lax.ppermute(array, axis, [(i, i ^ k) for i in range(lax.axis_size(axis))])  2.9 us
    pallas_call x1, Pallas kernels, whiten(): pl.pallas_call(whiten_kernel, out_shape=jax.ShapeDtypeStruct((chans, bins...  1.29 us
  transfers between devices with their start and end apart: 11, of which 2 were waited for; matrix products, arithmetic and copies ran while one was open for 1% of the time, Pallas kernels for 7%

profile of v12, /device:TPU:1, one launch (start us, length us, event | category | flops | bytes accessed | tf_op | source)
XLA Modules:
  0.0 25.0 jit_solution(4908714448229510486)
XLA Ops:
  0.0 0.0 copy-start
  0.0 1.3 %whiten.1 = bf16[96,256]{1,0:T(8,128)(2,1)S(1)} custom-call(bf16[64,2,2,96]{3,2,1,0:T(2,128)(2,1)} %spectra_hbm.1, s32[1,96]{1,0:T(1,128)} %bitcast.10), custom_call_target="tpu_custom_call" | custom-call | tf_op jit(solution)/shard_map/whiten/pallas_call | solution.py:54
  1.3 2.2 %collective-permute-start.6 = (bf16[1,96,256]{2,1,0:T(8,128)(2,1)S(1)}, bf16[1,96,256]{2,1,0:T(8,128)(2,1)S(1)}, u32[]{:S(2)}, u32[]{:S(2)}) collective-permute-start(bf16[1,96,256]{2,1,0:T(8,128)(2,1)S(1)} %bitcast.6), channel_id=1, source_target_pairs={{0,1},{1,0},{2,3},{3,2},{4,5},{5,4},{6,7},{7,6},{8,9},{9,8},{10,11... | collective-permute-start | bytes 147464 | tf_op jit(solution)/shard_map/ppermute | solution.py:190
  3.5 2.2 %collective-permute-start.1 = (bf16[1,96,256]{2,1,0:T(8,128)(2,1)S(1)}, bf16[1,96,256]{2,1,0:T(8,128)(2,1)S(1)}, u32[]{:S(2)}, u32[]{:S(2)}) collective-permute-start(bf16[1,96,256]{2,1,0:T(8,128)(2,1)S(1)} %bitcast.7), channel_id=1, source_target_pairs={{0,3},{1,2},{2,1},{3,0},{4,7},{5,6},{6,5},{7,4},{8,11},{9,10},{10,... | collective-permute-start | bytes 147464 | tf_op jit(solution)/shard_map/ppermute | solution.py:190
  5.7 0.1 collective-permute-start
  5.8 0.0 copy-done
  5.8 0.1 constant_dynamic-slice_fusion
  5.9 0.1 copy.4
  6.0 0.1 reshape.16
  6.1 0.1 add_bitcast_fusion.refs_2_.refs_0_
  6.1 0.0 collective-permute-done.6.refs_1_
  6.2 2.2 %collective-permute-start.9 = (bf16[2,96,256]{2,1,0:T(8,128)(2,1)S(1)}, bf16[2,96,256]{2,1,0:T(8,128)(2,1)S(1)}, u32[]{:S(2)}, u32[]{:S(2)}) collective-permute-start(bf16[2,96,256]{2,1,0:T(8,128)(2,1)S(1)} %stack.6.refs_0_), channel_id=1, source_target_pairs={{0,24},{4,28},{8,16},{12,20},{16,8},{20,12},{24,0},{28,4},{1,25},{... | collective-permute-start | bytes 294920 | tf_op jit(solution)/shard_map/ppermute | solution.py:190
  8.4 0.2 collective-permute-start.8
  8.6 0.3 %collective-permute-start.7 = (bf16[2,96,256]{2,1,0:T(8,128)(2,1)S(1)}, bf16[2,96,256]{2,1,0:T(8,128)(2,1)S(1)}, u32[]{:S(2)}, u32[]{:S(2)}) collective-permute-start(bf16[2,96,256]{2,1,0:T(8,128)(2,1)S(1)} %stack.6.refs_0_), channel_id=1, source_target_pairs={{0,8},{4,12},{8,0},{12,4},{16,24},{20,28},{24,16},{28,20},{1,9},{5... | collective-permute-start | bytes 294920 | tf_op jit(solution)/shard_map/ppermute | solution.py:190
  8.9 0.0 collective-permute-done.1.refs_1_
  8.9 1.7 %collective-permute-done.refs_0_ = bf16[1,96,256]{2,1,0:T(8,128)(2,1)S(1)} collective-permute-done((bf16[1,96,256]{2,1,0:T(8,128)(2,1)S(1)}, bf16[1,96,256]{2,1,0:T(8,128)(2,1)S(1)}, u32[]{:S(2)}, u32[]{:S(2)}) %collective-permute-start) | collective-permute-done | bytes 49184 | tf_op jit(solution)/shard_map/ppermute | solution.py:190
  10.6 2.2 %collective-permute-start.4 = (bf16[2,96,256]{2,1,0:T(8,128)(2,1)S(1)}, bf16[2,96,256]{2,1,0:T(8,128)(2,1)S(1)}, u32[]{:S(2)}, u32[]{:S(2)}) collective-permute-start(bf16[2,96,256]{2,1,0:T(8,128)(2,1)S(1)} %stack.4.refs_0_), channel_id=1, source_target_pairs={{0,24},{4,28},{8,16},{12,20},{16,8},{20,12},{24,0},{28,4},{1,25},{... | collective-permute-start | bytes 294920 | tf_op jit(solution)/shard_map/ppermute | solution.py:190
  12.8 0.2 collective-permute-start.3
  13.0 0.0 collective-permute-done.9.refs_3_
  13.1 0.3 %collective-permute-start.2 = (bf16[2,96,256]{2,1,0:T(8,128)(2,1)S(1)}, bf16[2,96,256]{2,1,0:T(8,128)(2,1)S(1)}, u32[]{:S(2)}, u32[]{:S(2)}) collective-permute-start(bf16[2,96,256]{2,1,0:T(8,128)(2,1)S(1)} %stack.4.refs_0_), channel_id=1, source_target_pairs={{0,8},{4,12},{8,0},{12,4},{16,24},{20,28},{24,16},{28,20},{1,9},{5... | collective-permute-start | bytes 294920 | tf_op jit(solution)/shard_map/ppermute | solution.py:190
  13.3 0.0 collective-permute-done.8.refs_2_
  13.3 0.0 collective-permute-done.7.refs_1_
  13.3 2.8 %collective-permute-start.10 = (bf16[8,96,256]{2,1,0:T(8,128)(2,1)S(1)}, bf16[8,96,256]{2,1,0:T(8,128)(2,1)S(1)}, u32[]{:S(2)}, u32[]{:S(2)}) collective-permute-start(bf16[8,96,256]{2,1,0:T(8,128)(2,1)S(1)} %stack.7.refs_1_), channel_id=1, source_target_pairs={{0,4},{4,0},{8,12},{12,8},{16,20},{20,16},{24,28},{28,24},{1,5},{5... | collective-permute-start | bytes 1179656 | tf_op jit(solution)/shard_map/ppermute | solution.py:190
  16.1 0.0 collective-permute-done.4.refs_3_
  16.1 1.2 %collective-permute-done.3.refs_2_ = bf16[2,96,256]{2,1,0:T(8,128)(2,1)S(1)} collective-permute-done((bf16[2,96,256]{2,1,0:T(8,128)(2,1)S(1)}, bf16[2,96,256]{2,1,0:T(8,128)(2,1)S(1)}, u32[]{:S(2)}, u32[]{:S(2)}) %collective-permute-start.3) | collective-permute-done | bytes 98336 | tf_op jit(solution)/shard_map/ppermute | solution.py:190
  17.3 0.0 collective-permute-done.2.refs_1_
  17.3 2.9 %collective-permute-start.5 = (bf16[8,96,256]{2,1,0:T(8,128)(2,1)S(1)}, bf16[8,96,256]{2,1,0:T(8,128)(2,1)S(1)}, u32[]{:S(2)}, u32[]{:S(2)}) collective-permute-start(bf16[8,96,256]{2,1,0:T(8,128)(2,1)S(1)} %stack.5.refs_1_), channel_id=1, source_target_pairs={{0,4},{4,0},{8,12},{12,8},{16,20},{20,16},{24,28},{28,24},{1,5},{5... | collective-permute-start | bytes 1179656 | tf_op jit(solution)/shard_map/ppermute | solution.py:190
  20.2 0.0 collective-permute-done.10.refs_2_
  20.2 1.7 %correlate.1.refs_3_ = f32[2,4,8,128,128]{4,3,2,1,0:T(8,128)S(1)} custom-call(s32[1,5]{1,0:T(1,128)S(1)} %add_bitcast_fusion.refs_2_.refs_0_, bf16[8,96,256]{2,1,0:T(8,128)(2,1)S(1)} %stack.7.refs_1_, bf16[8,96,256]{2,1,0:T(8,128)(2,1)S(1)} %collective-permute-done.10.refs_2_), custom_call_target="tpu_custom_call" | custom-call | tf_op jit(solution)/shard_map/correlate/pallas_call | solution.py:172
  21.9 0.0 collective-permute-done.5.refs_2_
  21.9 3.1 %correlate_add.1 = f32[2,4,8,128,128]{4,3,2,1,0:T(8,128)} custom-call(s32[1,5]{1,0:T(1,128)S(1)} %add_bitcast_fusion.refs_2_.refs_0_, bf16[8,96,256]{2,1,0:T(8,128)(2,1)S(1)} %stack.5.refs_1_, bf16[8,96,256]{2,1,0:T(8,128)(2,1)S(1)} %collective-permute-done.5.refs_2_, f32[2,4,8,128,128]{4,3,2,1,0:T(8,128)S(1)} %correlate.1.refs_3_), custom_call_target="tpu_custom_call" | custom-call | tf_op jit(solution)/shard_map/correlate_add/pallas_call | solution.py:172
  (4 shorter events, 0.1 us)
Async XLA Ops:
  0.0 5.8 %copy-start = (s32[8,2]{0,1:T(2,128)S(1)}, s32[8,2]{0,1:T(2,128)}, u32[]{:S(2)}) copy-start(s32[8,2]{0,1:T(2,128)} %param.5) | copy-start | bytes 196
  1.3 4.8 %collective-permute-start.6 = (bf16[1,96,256]{2,1,0:T(8,128)(2,1)S(1)}, bf16[1,96,256]{2,1,0:T(8,128)(2,1)S(1)}, u32[]{:S(2)}, u32[]{:S(2)}) collective-permute-start(bf16[1,96,256]{2,1,0:T(8,128)(2,1)S(1)} %bitcast.6), channel_id=1, source_target_pairs={{0,1},{1,0},{2,3},{3,2},{4,5},{5,4},{6,7},{7,6},{8,9},{9,8},{10,11... | collective-permute-start | bytes 147464 | tf_op jit(solution)/shard_map/ppermute | solution.py:190
  3.5 5.4 %collective-permute-start.1 = (bf16[1,96,256]{2,1,0:T(8,128)(2,1)S(1)}, bf16[1,96,256]{2,1,0:T(8,128)(2,1)S(1)}, u32[]{:S(2)}, u32[]{:S(2)}) collective-permute-start(bf16[1,96,256]{2,1,0:T(8,128)(2,1)S(1)} %bitcast.7), channel_id=1, source_target_pairs={{0,3},{1,2},{2,1},{3,0},{4,7},{5,6},{6,5},{7,4},{8,11},{9,10},{10,... | collective-permute-start | bytes 147464 | tf_op jit(solution)/shard_map/ppermute | solution.py:190
  5.7 4.9 %collective-permute-start = (bf16[1,96,256]{2,1,0:T(8,128)(2,1)S(1)}, bf16[1,96,256]{2,1,0:T(8,128)(2,1)S(1)}, u32[]{:S(2)}, u32[]{:S(2)}) collective-permute-start(bf16[1,96,256]{2,1,0:T(8,128)(2,1)S(1)} %bitcast.8), channel_id=1, source_target_pairs={{0,2},{1,3},{2,0},{3,1},{4,6},{5,7},{6,4},{7,5},{8,10},{9,11},{10,... | collective-permute-start | bytes 147464 | tf_op jit(solution)/shard_map/ppermute | solution.py:190
  6.2 6.9 %collective-permute-start.9 = (bf16[2,96,256]{2,1,0:T(8,128)(2,1)S(1)}, bf16[2,96,256]{2,1,0:T(8,128)(2,1)S(1)}, u32[]{:S(2)}, u32[]{:S(2)}) collective-permute-start(bf16[2,96,256]{2,1,0:T(8,128)(2,1)S(1)} %stack.6.refs_0_), channel_id=1, source_target_pairs={{0,24},{4,28},{8,16},{12,20},{16,8},{20,12},{24,0},{28,4},{1,25},{... | collective-permute-start | bytes 294920 | tf_op jit(solution)/shard_map/ppermute | solution.py:190
  8.4 4.9 %collective-permute-start.8 = (bf16[2,96,256]{2,1,0:T(8,128)(2,1)S(1)}, bf16[2,96,256]{2,1,0:T(8,128)(2,1)S(1)}, u32[]{:S(2)}, u32[]{:S(2)}) collective-permute-start(bf16[2,96,256]{2,1,0:T(8,128)(2,1)S(1)} %stack.6.refs_0_), channel_id=1, source_target_pairs={{0,16},{4,20},{8,24},{12,28},{16,0},{20,4},{24,8},{28,12},{1,17},{... | collective-permute-start | bytes 294920 | tf_op jit(solution)/shard_map/ppermute | solution.py:190
  8.6 4.7 %collective-permute-start.7 = (bf16[2,96,256]{2,1,0:T(8,128)(2,1)S(1)}, bf16[2,96,256]{2,1,0:T(8,128)(2,1)S(1)}, u32[]{:S(2)}, u32[]{:S(2)}) collective-permute-start(bf16[2,96,256]{2,1,0:T(8,128)(2,1)S(1)} %stack.6.refs_0_), channel_id=1, source_target_pairs={{0,8},{4,12},{8,0},{12,4},{16,24},{20,28},{24,16},{28,20},{1,9},{5... | collective-permute-start | bytes 294920 | tf_op jit(solution)/shard_map/ppermute | solution.py:190
  10.6 5.5 %collective-permute-start.4 = (bf16[2,96,256]{2,1,0:T(8,128)(2,1)S(1)}, bf16[2,96,256]{2,1,0:T(8,128)(2,1)S(1)}, u32[]{:S(2)}, u32[]{:S(2)}) collective-permute-start(bf16[2,96,256]{2,1,0:T(8,128)(2,1)S(1)} %stack.4.refs_0_), channel_id=1, source_target_pairs={{0,24},{4,28},{8,16},{12,20},{16,8},{20,12},{24,0},{28,4},{1,25},{... | collective-permute-start | bytes 294920 | tf_op jit(solution)/shard_map/ppermute | solution.py:190
  12.8 4.5 %collective-permute-start.3 = (bf16[2,96,256]{2,1,0:T(8,128)(2,1)S(1)}, bf16[2,96,256]{2,1,0:T(8,128)(2,1)S(1)}, u32[]{:S(2)}, u32[]{:S(2)}) collective-permute-start(bf16[2,96,256]{2,1,0:T(8,128)(2,1)S(1)} %stack.4.refs_0_), channel_id=1, source_target_pairs={{0,16},{4,20},{8,24},{12,28},{16,0},{20,4},{24,8},{28,12},{1,17},{... | collective-permute-start | bytes 294920 | tf_op jit(solution)/shard_map/ppermute | solution.py:190
  13.1 4.2 %collective-permute-start.2 = (bf16[2,96,256]{2,1,0:T(8,128)(2,1)S(1)}, bf16[2,96,256]{2,1,0:T(8,128)(2,1)S(1)}, u32[]{:S(2)}, u32[]{:S(2)}) collective-permute-start(bf16[2,96,256]{2,1,0:T(8,128)(2,1)S(1)} %stack.4.refs_0_), channel_id=1, source_target_pairs={{0,8},{4,12},{8,0},{12,4},{16,24},{20,28},{24,16},{28,20},{1,9},{5... | collective-permute-start | bytes 294920 | tf_op jit(solution)/shard_map/ppermute | solution.py:190
  13.3 6.8 %collective-permute-start.10 = (bf16[8,96,256]{2,1,0:T(8,128)(2,1)S(1)}, bf16[8,96,256]{2,1,0:T(8,128)(2,1)S(1)}, u32[]{:S(2)}, u32[]{:S(2)}) collective-permute-start(bf16[8,96,256]{2,1,0:T(8,128)(2,1)S(1)} %stack.7.refs_1_), channel_id=1, source_target_pairs={{0,4},{4,0},{8,12},{12,8},{16,20},{20,16},{24,28},{28,24},{1,5},{5... | collective-permute-start | bytes 1179656 | tf_op jit(solution)/shard_map/ppermute | solution.py:190
  17.3 4.6 %collective-permute-start.5 = (bf16[8,96,256]{2,1,0:T(8,128)(2,1)S(1)}, bf16[8,96,256]{2,1,0:T(8,128)(2,1)S(1)}, u32[]{:S(2)}, u32[]{:S(2)}) collective-permute-start(bf16[8,96,256]{2,1,0:T(8,128)(2,1)S(1)} %stack.5.refs_1_), channel_id=1, source_target_pairs={{0,4},{4,0},{8,12},{12,8},{16,20},{20,16},{24,28},{28,24},{1,5},{5... | collective-permute-start | bytes 1179656 | tf_op jit(solution)/shard_map/ppermute | solution.py:190

commit v13 on v12

--- a/solution.py
+++ b/solution.py
@@ -85,7 +85,7 @@
     return (forward, (rc + is_, ic - rs)) if both else (forward,)
 
 
-def correlate_kernel(norm, picked, adds, where_ref, own_ref, sib_ref, *refs):
+def correlate_kernel(norm, picked, adds, crossings, where_ref, own_ref, sib_ref, *refs):
     partials = refs[:adds]
     out_ref = refs[adds]
     spectra, left_turned, right_turned, *more = refs[adds + 1:]
@@ -100,9 +100,11 @@
     chan = where_ref[0, 0]
     rows = own_ref.shape[1]
     for core, piece in enumerate((own_ref, sib_ref)):
-        for k in range(piece.shape[0] // groups):
-            place = pl.multiple_of((chan ^ (CORES * k + core)) * rows, 32)
-            spectra[:, pl.ds(place, rows), :] = piece[k * groups:(k + 1) * groups]
+        for slot in range(piece.shape[0]):
+            k, g = slot // groups, slot % groups
+            crossed = core ^ (k > 0) ^ crossings[g]
+            place = pl.multiple_of((chan ^ (CORES * k + crossed)) * rows, 32)
+            spectra[g, pl.ds(place, rows), :] = piece[slot]
 
     def load(block, g):
         whole = spectra[g, pl.ds(pl.multiple_of(block * TILE, TILE), TILE), :].astype(jnp.float32)
@@ -156,8 +158,9 @@
         copy.wait()
 
 
-def correlate(pieces, groups, where, picked, hours, partials=()):
+def correlate(pieces, crossings, where, picked, hours, partials=()):
     depth, rows, lanes = pieces[0].shape
+    groups = len(crossings)
     fine = 2 * len(FINE_PAIRS)
     shape = (len(picked), len(COARSE), fine, TILE, TILE)
     norm = 1.0 / math.sqrt(F * hours)
@@ -170,7 +173,7 @@
         more = [pltpu.VMEM(shape, jnp.float32), pltpu.SemaphoreType.DMA]
         scratch += 4 * math.prod(shape)
     return pl.pallas_call(
-        lambda *refs: correlate_kernel(norm, picked, adds, *refs),
+        lambda *refs: correlate_kernel(norm, picked, adds, crossings, *refs),
         out_shape=jax.ShapeDtypeStruct(shape, jnp.float32),
         in_specs=[VMEM] * (1 + len(pieces) + adds),
         out_specs=pl.BlockSpec(memory_space=pl.ANY) if adds else VMEM,
@@ -186,8 +189,12 @@
     )(where, *pieces, *partials)
 
 
-def swap(array, axis, k):
-    return lax.ppermute(array, axis, [(i, i ^ k) for i in range(lax.axis_size(axis))])
+def swap(array, chan_k, tm_k):
+    chans, groups = lax.axis_size("chan"), lax.axis_size("tm")
+    pairs = [
+        (chan * groups + tm, (chan ^ chan_k) * groups + (tm ^ tm_k)) for chan in range(chans) for tm in range(groups)
+    ]
+    return lax.ppermute(array, ("chan", "tm"), pairs)
 
 
 def stack_kernel(blocks, *refs):
@@ -213,12 +220,12 @@
 
 def halves(white, where):
     groups = lax.axis_size("tm")
-    blocks = [white[None]] + [swap(white[None], "tm", k) for k in range(1, groups)]
+    blocks = [white[None]] + [swap(white[None], 1, k) for k in range(1, groups)]
     return stack(blocks[:groups // 2], after=(where,)), stack(blocks[groups // 2:], flops=10**9)
 
 
 def between_chips(half):
-    return [half] + [swap(half, "chan", k) for k in range(CORES, lax.axis_size("chan"), CORES)]
+    return [half] + [swap(half, k + 1, 0) for k in range(CORES, lax.axis_size("chan"), CORES)]
 
 
 def per_device(spectra, bad_channels, tile_list):
@@ -228,13 +235,14 @@
     white = whiten(spectra, bad_channels)
     pairs = lax.dynamic_slice_in_dim(tile_list, lax.axis_index("tm") * tiles, tiles, axis=0)
     where = jnp.concatenate([lax.axis_index("chan").reshape(1), pairs.reshape(-1)]).astype(jnp.int32).reshape(1, -1)
+    crossings = [0] + [1] * (groups - 1)
     near, far = [between_chips(half) for half in halves(white, where)]
     near = stack(near)
-    near = (near, swap(near, "chan", 1))
+    near = (near, swap(near, 1, 0))
     far = stack(far)
-    far = (far, swap(far, "chan", 1))
-    partial = correlate(near, groups // 2, where, range(tiles), hours)
-    out = correlate(far, groups // 2, where, range(tiles), hours, [partial])
+    far = (far, swap(far, 1, 0))
+    partial = correlate(near, crossings[:groups // 2], where, range(tiles), hours)
+    out = correlate(far, crossings[groups // 2:], where, range(tiles), hours, [partial])
     return out.reshape(tiles, LAGS, TILE, TILE)
 
 

time: 25.1 us -> 25.7 us (1.024)
  waiting for transfers between devices: 2.9 us -> 6.71 us
  starting transfers between devices: 15.6 us -> 12.3 us
    ppermute x11, waiting for transfers between devices: 2.9 us -> 6.71 us  [swap(): return lax.ppermute(array, ('chan', 'tm'), pairs)]
    ppermute x11, starting transfers between devices: 15.6 us -> 12.3 us  [swap(): return lax.ppermute(array, ('chan', 'tm'), pairs)]
  transfers between devices with their start and end apart: 11 -> 11, of which waited for: 2 -> 3; matrix products, arithmetic and copies ran while one was open for 1% -> 1% of each run, Pallas kernels for 7% -> 7%
where the time goes in v13:
time: 25.7 us; the launch traced here: 25.4 us
  starting transfers between devices  12.3 us (48%)
  waiting for transfers between devices  6.71 us (26%)
  Pallas kernels  6.1 us (24%)
  local copies, waits for them, and re-layouts  0.26 us (1%)
    ppermute x11, starting transfers between devices, swap(): return lax.ppermute(array, ('chan', 'tm'), pairs)  12.3 us
    ppermute x11, waiting for transfers between devices, swap(): return lax.ppermute(array, ('chan', 'tm'), pairs)  6.71 us
    pallas_call x2, Pallas kernels, correlate(): pl.pallas_call(lambda *refs: correlate_kernel(norm, picked, adds, crossin...  4.74 us
    pallas_call x1, Pallas kernels, whiten(): pl.pallas_call(whiten_kernel, out_shape=jax.ShapeDtypeStruct((chans, bins...  1.29 us
  transfers between devices with their start and end apart: 11, of which 3 were waited for; matrix products, arithmetic and copies ran while one was open for 1% of the time, Pallas kernels for 7%

profile of v13, /device:TPU:1, one launch (start us, length us, event | category | flops | bytes accessed | tf_op | source)
XLA Modules:
  0.0 25.4 jit_solution(4531350003437755903)
XLA Ops:
  0.0 0.0 copy-start
  0.0 1.3 %whiten.1 = bf16[96,256]{1,0:T(8,128)(2,1)S(1)} custom-call(bf16[64,2,2,96]{3,2,1,0:T(2,128)(2,1)} %spectra_hbm.1, s32[1,96]{1,0:T(1,128)} %bitcast.10), custom_call_target="tpu_custom_call" | custom-call | tf_op jit(solution)/shard_map/whiten/pallas_call | solution.py:54
  1.3 2.8 %collective-permute-start.6 = (bf16[1,96,256]{2,1,0:T(8,128)(2,1)S(1)}, bf16[1,96,256]{2,1,0:T(8,128)(2,1)S(1)}, u32[]{:S(2)}, u32[]{:S(2)}) collective-permute-start(bf16[1,96,256]{2,1,0:T(8,128)(2,1)S(1)} %bitcast.6), channel_id=1, source_target_pairs={{0,5},{1,4},{2,7},{3,6},{4,1},{5,0},{6,3},{7,2},{8,13},{9,12},{10,... | collective-permute-start | bytes 147464 | tf_op jit(solution)/shard_map/ppermute | solution.py:197
  4.1 2.1 %collective-permute-start.1 = (bf16[1,96,256]{2,1,0:T(8,128)(2,1)S(1)}, bf16[1,96,256]{2,1,0:T(8,128)(2,1)S(1)}, u32[]{:S(2)}, u32[]{:S(2)}) collective-permute-start(bf16[1,96,256]{2,1,0:T(8,128)(2,1)S(1)} %bitcast.7), channel_id=1, source_target_pairs={{0,7},{1,6},{2,5},{3,4},{4,3},{5,2},{6,1},{7,0},{8,15},{9,14},{10,... | collective-permute-start | bytes 147464 | tf_op jit(solution)/shard_map/ppermute | solution.py:197
  6.2 0.0 collective-permute-start
  6.2 0.0 copy-done
  6.2 0.1 constant_dynamic-slice_fusion
  6.2 0.1 copy.4
  6.3 0.1 reshape.16
  6.4 0.1 add_bitcast_fusion.refs_2_.refs_0_
  6.5 0.0 collective-permute-done.6.refs_1_
  6.5 2.7 %collective-permute-start.9 = (bf16[2,96,256]{2,1,0:T(8,128)(2,1)S(1)}, bf16[2,96,256]{2,1,0:T(8,128)(2,1)S(1)}, u32[]{:S(2)}, u32[]{:S(2)}) collective-permute-start(bf16[2,96,256]{2,1,0:T(8,128)(2,1)S(1)} %stack.6.refs_0_), channel_id=1, source_target_pairs={{0,28},{1,29},{2,30},{3,31},{4,24},{5,25},{6,26},{7,27},{8,20},{9,... | collective-permute-start | bytes 294920 | tf_op jit(solution)/shard_map/ppermute | solution.py:197
  9.2 0.0 collective-permute-start.8
  9.2 0.7 %collective-permute-start.7 = (bf16[2,96,256]{2,1,0:T(8,128)(2,1)S(1)}, bf16[2,96,256]{2,1,0:T(8,128)(2,1)S(1)}, u32[]{:S(2)}, u32[]{:S(2)}) collective-permute-start(bf16[2,96,256]{2,1,0:T(8,128)(2,1)S(1)} %stack.6.refs_0_), channel_id=1, source_target_pairs={{0,12},{1,13},{2,14},{3,15},{4,8},{5,9},{6,10},{7,11},{8,4},{9,5},... | collective-permute-start | bytes 294920 | tf_op jit(solution)/shard_map/ppermute | solution.py:197
  10.0 0.0 collective-permute-done.1.refs_1_
  10.0 2.2 %collective-permute-done.refs_0_ = bf16[1,96,256]{2,1,0:T(8,128)(2,1)S(1)} collective-permute-done((bf16[1,96,256]{2,1,0:T(8,128)(2,1)S(1)}, bf16[1,96,256]{2,1,0:T(8,128)(2,1)S(1)}, u32[]{:S(2)}, u32[]{:S(2)}) %collective-permute-start) | collective-permute-done | bytes 49184 | tf_op jit(solution)/shard_map/ppermute | solution.py:197
  12.3 2.3 %collective-permute-start.4 = (bf16[2,96,256]{2,1,0:T(8,128)(2,1)S(1)}, bf16[2,96,256]{2,1,0:T(8,128)(2,1)S(1)}, u32[]{:S(2)}, u32[]{:S(2)}) collective-permute-start(bf16[2,96,256]{2,1,0:T(8,128)(2,1)S(1)} %stack.4.refs_0_), channel_id=1, source_target_pairs={{0,28},{1,29},{2,30},{3,31},{4,24},{5,25},{6,26},{7,27},{8,20},{9,... | collective-permute-start | bytes 294920 | tf_op jit(solution)/shard_map/ppermute | solution.py:197
  14.6 0.4 %collective-permute-start.3 = (bf16[2,96,256]{2,1,0:T(8,128)(2,1)S(1)}, bf16[2,96,256]{2,1,0:T(8,128)(2,1)S(1)}, u32[]{:S(2)}, u32[]{:S(2)}) collective-permute-start(bf16[2,96,256]{2,1,0:T(8,128)(2,1)S(1)} %stack.4.refs_0_), channel_id=1, source_target_pairs={{0,20},{1,21},{2,22},{3,23},{4,16},{5,17},{6,18},{7,19},{8,28},{9,... | collective-permute-start | bytes 294920 | tf_op jit(solution)/shard_map/ppermute | solution.py:197
  15.0 0.0 collective-permute-done.9.refs_3_
  15.0 0.3 %collective-permute-start.2 = (bf16[2,96,256]{2,1,0:T(8,128)(2,1)S(1)}, bf16[2,96,256]{2,1,0:T(8,128)(2,1)S(1)}, u32[]{:S(2)}, u32[]{:S(2)}) collective-permute-start(bf16[2,96,256]{2,1,0:T(8,128)(2,1)S(1)} %stack.4.refs_0_), channel_id=1, source_target_pairs={{0,12},{1,13},{2,14},{3,15},{4,8},{5,9},{6,10},{7,11},{8,4},{9,5},... | collective-permute-start | bytes 294920 | tf_op jit(solution)/shard_map/ppermute | solution.py:197
  15.3 0.0 collective-permute-done.8.refs_2_
  15.3 0.0 collective-permute-done.7.refs_1_
  15.4 0.4 %collective-permute-start.10 = (bf16[8,96,256]{2,1,0:T(8,128)(2,1)S(1)}, bf16[8,96,256]{2,1,0:T(8,128)(2,1)S(1)}, u32[]{:S(2)}, u32[]{:S(2)}) collective-permute-start(bf16[8,96,256]{2,1,0:T(8,128)(2,1)S(1)} %stack.7.refs_1_), channel_id=1, source_target_pairs={{0,4},{1,5},{2,6},{3,7},{4,0},{5,1},{6,2},{7,3},{8,12},{9,13},{10,... | collective-permute-start | bytes 1179656 | tf_op jit(solution)/shard_map/ppermute | solution.py:197
  15.7 2.1 %collective-permute-done.4.refs_3_ = bf16[2,96,256]{2,1,0:T(8,128)(2,1)S(1)} collective-permute-done((bf16[2,96,256]{2,1,0:T(8,128)(2,1)S(1)}, bf16[2,96,256]{2,1,0:T(8,128)(2,1)S(1)}, u32[]{:S(2)}, u32[]{:S(2)}) %collective-permute-start.4) | collective-permute-done | bytes 98336 | tf_op jit(solution)/shard_map/ppermute | solution.py:197
  17.9 2.3 %collective-permute-done.3.refs_2_ = bf16[2,96,256]{2,1,0:T(8,128)(2,1)S(1)} collective-permute-done((bf16[2,96,256]{2,1,0:T(8,128)(2,1)S(1)}, bf16[2,96,256]{2,1,0:T(8,128)(2,1)S(1)}, u32[]{:S(2)}, u32[]{:S(2)}) %collective-permute-start.3) | collective-permute-done | bytes 98336 | tf_op jit(solution)/shard_map/ppermute | solution.py:197
  20.2 0.0 collective-permute-done.2.refs_1_
  20.2 0.5 %collective-permute-start.5 = (bf16[8,96,256]{2,1,0:T(8,128)(2,1)S(1)}, bf16[8,96,256]{2,1,0:T(8,128)(2,1)S(1)}, u32[]{:S(2)}, u32[]{:S(2)}) collective-permute-start(bf16[8,96,256]{2,1,0:T(8,128)(2,1)S(1)} %stack.5.refs_1_), channel_id=1, source_target_pairs={{0,4},{1,5},{2,6},{3,7},{4,0},{5,1},{6,2},{7,3},{8,12},{9,13},{10,... | collective-permute-start | bytes 1179656 | tf_op jit(solution)/shard_map/ppermute | solution.py:197
  20.7 0.0 collective-permute-done.10.refs_2_
  20.7 1.7 %correlate.1.refs_3_ = f32[2,4,8,128,128]{4,3,2,1,0:T(8,128)S(1)} custom-call(s32[1,5]{1,0:T(1,128)S(1)} %add_bitcast_fusion.refs_2_.refs_0_, bf16[8,96,256]{2,1,0:T(8,128)(2,1)S(1)} %stack.7.refs_1_, bf16[8,96,256]{2,1,0:T(8,128)(2,1)S(1)} %collective-permute-done.10.refs_2_), custom_call_target="tpu_custom_call" | custom-call | tf_op jit(solution)/shard_map/correlate/pallas_call | solution.py:175
  22.4 0.0 collective-permute-done.5.refs_2_
  22.4 3.0 %correlate_add.1 = f32[2,4,8,128,128]{4,3,2,1,0:T(8,128)} custom-call(s32[1,5]{1,0:T(1,128)S(1)} %add_bitcast_fusion.refs_2_.refs_0_, bf16[8,96,256]{2,1,0:T(8,128)(2,1)S(1)} %stack.5.refs_1_, bf16[8,96,256]{2,1,0:T(8,128)(2,1)S(1)} %collective-permute-done.5.refs_2_, f32[2,4,8,128,128]{4,3,2,1,0:T(8,128)S(1)} %correlate.1.refs_3_), custom_call_target="tpu_custom_call" | custom-call | tf_op jit(solution)/shard_map/correlate_add/pallas_call | solution.py:175
  (4 shorter events, 0.1 us)
Async XLA Ops:
  0.0 6.2 %copy-start = (s32[8,2]{0,1:T(2,128)S(1)}, s32[8,2]{0,1:T(2,128)}, u32[]{:S(2)}) copy-start(s32[8,2]{0,1:T(2,128)} %param.5) | copy-start | bytes 196
  1.3 5.2 %collective-permute-start.6 = (bf16[1,96,256]{2,1,0:T(8,128)(2,1)S(1)}, bf16[1,96,256]{2,1,0:T(8,128)(2,1)S(1)}, u32[]{:S(2)}, u32[]{:S(2)}) collective-permute-start(bf16[1,96,256]{2,1,0:T(8,128)(2,1)S(1)} %bitcast.6), channel_id=1, source_target_pairs={{0,5},{1,4},{2,7},{3,6},{4,1},{5,0},{6,3},{7,2},{8,13},{9,12},{10,... | collective-permute-start | bytes 147464 | tf_op jit(solution)/shard_map/ppermute | solution.py:197
  4.1 5.9 %collective-permute-start.1 = (bf16[1,96,256]{2,1,0:T(8,128)(2,1)S(1)}, bf16[1,96,256]{2,1,0:T(8,128)(2,1)S(1)}, u32[]{:S(2)}, u32[]{:S(2)}) collective-permute-start(bf16[1,96,256]{2,1,0:T(8,128)(2,1)S(1)} %bitcast.7), channel_id=1, source_target_pairs={{0,7},{1,6},{2,5},{3,4},{4,3},{5,2},{6,1},{7,0},{8,15},{9,14},{10,... | collective-permute-start | bytes 147464 | tf_op jit(solution)/shard_map/ppermute | solution.py:197
  6.2 6.1 %collective-permute-start = (bf16[1,96,256]{2,1,0:T(8,128)(2,1)S(1)}, bf16[1,96,256]{2,1,0:T(8,128)(2,1)S(1)}, u32[]{:S(2)}, u32[]{:S(2)}) collective-permute-start(bf16[1,96,256]{2,1,0:T(8,128)(2,1)S(1)} %bitcast.8), channel_id=1, source_target_pairs={{0,6},{1,7},{2,4},{3,5},{4,2},{5,3},{6,0},{7,1},{8,14},{9,15},{10,... | collective-permute-start | bytes 147464 | tf_op jit(solution)/shard_map/ppermute | solution.py:197
  6.5 8.5 %collective-permute-start.9 = (bf16[2,96,256]{2,1,0:T(8,128)(2,1)S(1)}, bf16[2,96,256]{2,1,0:T(8,128)(2,1)S(1)}, u32[]{:S(2)}, u32[]{:S(2)}) collective-permute-start(bf16[2,96,256]{2,1,0:T(8,128)(2,1)S(1)} %stack.6.refs_0_), channel_id=1, source_target_pairs={{0,28},{1,29},{2,30},{3,31},{4,24},{5,25},{6,26},{7,27},{8,20},{9,... | collective-permute-start | bytes 294920 | tf_op jit(solution)/shard_map/ppermute | solution.py:197
  9.2 6.1 %collective-permute-start.8 = (bf16[2,96,256]{2,1,0:T(8,128)(2,1)S(1)}, bf16[2,96,256]{2,1,0:T(8,128)(2,1)S(1)}, u32[]{:S(2)}, u32[]{:S(2)}) collective-permute-start(bf16[2,96,256]{2,1,0:T(8,128)(2,1)S(1)} %stack.6.refs_0_), channel_id=1, source_target_pairs={{0,20},{1,21},{2,22},{3,23},{4,16},{5,17},{6,18},{7,19},{8,28},{9,... | collective-permute-start | bytes 294920 | tf_op jit(solution)/shard_map/ppermute | solution.py:197
  9.2 6.1 %collective-permute-start.7 = (bf16[2,96,256]{2,1,0:T(8,128)(2,1)S(1)}, bf16[2,96,256]{2,1,0:T(8,128)(2,1)S(1)}, u32[]{:S(2)}, u32[]{:S(2)}) collective-permute-start(bf16[2,96,256]{2,1,0:T(8,128)(2,1)S(1)} %stack.6.refs_0_), channel_id=1, source_target_pairs={{0,12},{1,13},{2,14},{3,15},{4,8},{5,9},{6,10},{7,11},{8,4},{9,5},... | collective-permute-start | bytes 294920 | tf_op jit(solution)/shard_map/ppermute | solution.py:197
  12.3 5.6 %collective-permute-start.4 = (bf16[2,96,256]{2,1,0:T(8,128)(2,1)S(1)}, bf16[2,96,256]{2,1,0:T(8,128)(2,1)S(1)}, u32[]{:S(2)}, u32[]{:S(2)}) collective-permute-start(bf16[2,96,256]{2,1,0:T(8,128)(2,1)S(1)} %stack.4.refs_0_), channel_id=1, source_target_pairs={{0,28},{1,29},{2,30},{3,31},{4,24},{5,25},{6,26},{7,27},{8,20},{9,... | collective-permute-start | bytes 294920 | tf_op jit(solution)/shard_map/ppermute | solution.py:197
  14.6 5.6 %collective-permute-start.3 = (bf16[2,96,256]{2,1,0:T(8,128)(2,1)S(1)}, bf16[2,96,256]{2,1,0:T(8,128)(2,1)S(1)}, u32[]{:S(2)}, u32[]{:S(2)}) collective-permute-start(bf16[2,96,256]{2,1,0:T(8,128)(2,1)S(1)} %stack.4.refs_0_), channel_id=1, source_target_pairs={{0,20},{1,21},{2,22},{3,23},{4,16},{5,17},{6,18},{7,19},{8,28},{9,... | collective-permute-start | bytes 294920 | tf_op jit(solution)/shard_map/ppermute | solution.py:197
  15.0 5.2 %collective-permute-start.2 = (bf16[2,96,256]{2,1,0:T(8,128)(2,1)S(1)}, bf16[2,96,256]{2,1,0:T(8,128)(2,1)S(1)}, u32[]{:S(2)}, u32[]{:S(2)}) collective-permute-start(bf16[2,96,256]{2,1,0:T(8,128)(2,1)S(1)} %stack.4.refs_0_), channel_id=1, source_target_pairs={{0,12},{1,13},{2,14},{3,15},{4,8},{5,9},{6,10},{7,11},{8,4},{9,5},... | collective-permute-start | bytes 294920 | tf_op jit(solution)/shard_map/ppermute | solution.py:197
  15.4 5.3 %collective-permute-start.10 = (bf16[8,96,256]{2,1,0:T(8,128)(2,1)S(1)}, bf16[8,96,256]{2,1,0:T(8,128)(2,1)S(1)}, u32[]{:S(2)}, u32[]{:S(2)}) collective-permute-start(bf16[8,96,256]{2,1,0:T(8,128)(2,1)S(1)} %stack.7.refs_1_), channel_id=1, source_target_pairs={{0,4},{1,5},{2,6},{3,7},{4,0},{5,1},{6,2},{7,3},{8,12},{9,13},{10,... | collective-permute-start | bytes 1179656 | tf_op jit(solution)/shard_map/ppermute | solution.py:197
  20.2 2.2 %collective-permute-start.5 = (bf16[8,96,256]{2,1,0:T(8,128)(2,1)S(1)}, bf16[8,96,256]{2,1,0:T(8,128)(2,1)S(1)}, u32[]{:S(2)}, u32[]{:S(2)}) collective-permute-start(bf16[8,96,256]{2,1,0:T(8,128)(2,1)S(1)} %stack.5.refs_1_), channel_id=1, source_target_pairs={{0,4},{1,5},{2,6},{3,7},{4,0},{5,1},{6,2},{7,3},{8,12},{9,13},{10,... | collective-permute-start | bytes 1179656 | tf_op jit(solution)/shard_map/ppermute | solution.py:197

commit v14 on v12

--- a/solution.py
+++ b/solution.py
@@ -133,25 +133,26 @@
                     forward, backward = turn_by(re, im, *table[j], True)
                     store(right_turned, slot, 2 * j, g, forward)
                     store(right_turned, slot, 2 * j + 1, g, backward)
-            total = lax.dot_general(
-                left_turned[slot],
-                right_turned[slot, 2 * j * TILE:2 * (j + 1) * TILE, :],
-                (((1,), (1,)), ((), ())),
-                preferred_element_type=jnp.float32,
-            )
-            for s in range(2):
-                fine = FINE_PAIRS[j][s] + 4
-                for u in range(len(COARSE)):
-                    value = total[u * TILE:(u + 1) * TILE, s * TILE:(s + 1) * TILE]
+            for u in range(0, len(COARSE), 2):
+                total = lax.dot_general(
+                    left_turned[slot, u * TILE:(u + 2) * TILE, :],
+                    right_turned[slot, 2 * j * TILE:2 * (j + 1) * TILE, :],
+                    (((1,), (1,)), ((), ())),
+                    preferred_element_type=jnp.float32,
+                )
+                for v, s in ((0, 0), (0, 1), (1, 0), (1, 1)):
+                    fine = FINE_PAIRS[j][s] + 4
+                    value = total[v * TILE:(v + 1) * TILE, s * TILE:(s + 1) * TILE]
                     if adds:
                         each = len(picked) // adds
-                        more[0][i, u, fine] = partials[i // each][i % each, u, fine] + value
+                        more[0][i, u + v, fine] = partials[i // each][i % each, u + v, fine] + value
                     else:
-                        out_ref[i, u, fine] = value
-                if adds:
-                    copy = pltpu.make_async_copy(more[0].at[i, :, fine], out_ref.at[i, :, fine], more[1])
-                    copy.start(priority=s)
-                    copies.append(copy)
+                        out_ref[i, u + v, fine] = value
+            for s in range(2 if adds else 0):
+                fine = FINE_PAIRS[j][s] + 4
+                copy = pltpu.make_async_copy(more[0].at[i, :, fine], out_ref.at[i, :, fine], more[1])
+                copy.start(priority=s)
+                copies.append(copy)
     for copy in copies:
         copy.wait()
 

time: 25.1 us -> 24.7 us (0.984)
  Pallas kernels: 6.11 us -> 5.63 us
    pallas_call x2, Pallas kernels: 4.75 us -> 4.27 us  [correlate(): pl.pallas_call(lambda *refs: correlate_kernel(norm, picked, adds, *refs),...]
where the time goes in v14:
time: 24.7 us; the launch traced here: 24.5 us
  starting transfers between devices  15.6 us (63%)
  Pallas kernels  5.63 us (23%)
  waiting for transfers between devices  2.9 us (12%)
  local copies, waits for them, and re-layouts  0.26 us (1%)
    ppermute x11, starting transfers between devices, swap(): lax.ppermute(array, axis, [(i, i ^ k) for i in range(lax.axis_size(axis))])  15.6 us
    pallas_call x2, Pallas kernels, correlate(): pl.pallas_call(lambda *refs: correlate_kernel(norm, picked, adds, *refs),...  4.27 us
    ppermute x11, waiting for transfers between devices, swap(): lax.ppermute(array, axis, [(i, i ^ k) for i in range(lax.axis_size(axis))])  2.9 us
    pallas_call x1, Pallas kernels, whiten(): pl.pallas_call(whiten_kernel, out_shape=jax.ShapeDtypeStruct((chans, bins...  1.29 us
  transfers between devices with their start and end apart: 11, of which 2 were waited for; matrix products, arithmetic and copies ran while one was open for 1% of the time, Pallas kernels for 7%

profile of v14, /device:TPU:1, one launch (start us, length us, event | category | flops | bytes accessed | tf_op | source)
XLA Modules:
  0.0 24.5 jit_solution(26186267660733998)
XLA Ops:
  0.0 0.0 copy-start
  0.0 1.3 %whiten.1 = bf16[96,256]{1,0:T(8,128)(2,1)S(1)} custom-call(bf16[64,2,2,96]{3,2,1,0:T(2,128)(2,1)} %spectra_hbm.1, s32[1,96]{1,0:T(1,128)} %bitcast.10), custom_call_target="tpu_custom_call" | custom-call | tf_op jit(solution)/shard_map/whiten/pallas_call | solution.py:54
  1.3 2.2 %collective-permute-start.6 = (bf16[1,96,256]{2,1,0:T(8,128)(2,1)S(1)}, bf16[1,96,256]{2,1,0:T(8,128)(2,1)S(1)}, u32[]{:S(2)}, u32[]{:S(2)}) collective-permute-start(bf16[1,96,256]{2,1,0:T(8,128)(2,1)S(1)} %bitcast.6), channel_id=1, source_target_pairs={{0,1},{1,0},{2,3},{3,2},{4,5},{5,4},{6,7},{7,6},{8,9},{9,8},{10,11... | collective-permute-start | bytes 147464 | tf_op jit(solution)/shard_map/ppermute | solution.py:191
  3.5 2.2 %collective-permute-start.1 = (bf16[1,96,256]{2,1,0:T(8,128)(2,1)S(1)}, bf16[1,96,256]{2,1,0:T(8,128)(2,1)S(1)}, u32[]{:S(2)}, u32[]{:S(2)}) collective-permute-start(bf16[1,96,256]{2,1,0:T(8,128)(2,1)S(1)} %bitcast.7), channel_id=1, source_target_pairs={{0,3},{1,2},{2,1},{3,0},{4,7},{5,6},{6,5},{7,4},{8,11},{9,10},{10,... | collective-permute-start | bytes 147464 | tf_op jit(solution)/shard_map/ppermute | solution.py:191
  5.7 0.1 collective-permute-start
  5.8 0.0 copy-done
  5.8 0.1 constant_dynamic-slice_fusion
  5.9 0.1 copy.4
  6.0 0.1 reshape.16
  6.1 0.1 add_bitcast_fusion.refs_2_.refs_0_
  6.1 0.0 collective-permute-done.6.refs_1_
  6.2 2.2 %collective-permute-start.9 = (bf16[2,96,256]{2,1,0:T(8,128)(2,1)S(1)}, bf16[2,96,256]{2,1,0:T(8,128)(2,1)S(1)}, u32[]{:S(2)}, u32[]{:S(2)}) collective-permute-start(bf16[2,96,256]{2,1,0:T(8,128)(2,1)S(1)} %stack.6.refs_0_), channel_id=1, source_target_pairs={{0,24},{4,28},{8,16},{12,20},{16,8},{20,12},{24,0},{28,4},{1,25},{... | collective-permute-start | bytes 294920 | tf_op jit(solution)/shard_map/ppermute | solution.py:191
  8.4 0.2 collective-permute-start.8
  8.6 0.3 %collective-permute-start.7 = (bf16[2,96,256]{2,1,0:T(8,128)(2,1)S(1)}, bf16[2,96,256]{2,1,0:T(8,128)(2,1)S(1)}, u32[]{:S(2)}, u32[]{:S(2)}) collective-permute-start(bf16[2,96,256]{2,1,0:T(8,128)(2,1)S(1)} %stack.6.refs_0_), channel_id=1, source_target_pairs={{0,8},{4,12},{8,0},{12,4},{16,24},{20,28},{24,16},{28,20},{1,9},{5... | collective-permute-start | bytes 294920 | tf_op jit(solution)/shard_map/ppermute | solution.py:191
  8.9 0.0 collective-permute-done.1.refs_1_
  8.9 1.7 %collective-permute-done.refs_0_ = bf16[1,96,256]{2,1,0:T(8,128)(2,1)S(1)} collective-permute-done((bf16[1,96,256]{2,1,0:T(8,128)(2,1)S(1)}, bf16[1,96,256]{2,1,0:T(8,128)(2,1)S(1)}, u32[]{:S(2)}, u32[]{:S(2)}) %collective-permute-start) | collective-permute-done | bytes 49184 | tf_op jit(solution)/shard_map/ppermute | solution.py:191
  10.6 2.2 %collective-permute-start.4 = (bf16[2,96,256]{2,1,0:T(8,128)(2,1)S(1)}, bf16[2,96,256]{2,1,0:T(8,128)(2,1)S(1)}, u32[]{:S(2)}, u32[]{:S(2)}) collective-permute-start(bf16[2,96,256]{2,1,0:T(8,128)(2,1)S(1)} %stack.4.refs_0_), channel_id=1, source_target_pairs={{0,24},{4,28},{8,16},{12,20},{16,8},{20,12},{24,0},{28,4},{1,25},{... | collective-permute-start | bytes 294920 | tf_op jit(solution)/shard_map/ppermute | solution.py:191
  12.8 0.2 collective-permute-start.3
  13.0 0.0 collective-permute-done.9.refs_3_
  13.1 0.3 %collective-permute-start.2 = (bf16[2,96,256]{2,1,0:T(8,128)(2,1)S(1)}, bf16[2,96,256]{2,1,0:T(8,128)(2,1)S(1)}, u32[]{:S(2)}, u32[]{:S(2)}) collective-permute-start(bf16[2,96,256]{2,1,0:T(8,128)(2,1)S(1)} %stack.4.refs_0_), channel_id=1, source_target_pairs={{0,8},{4,12},{8,0},{12,4},{16,24},{20,28},{24,16},{28,20},{1,9},{5... | collective-permute-start | bytes 294920 | tf_op jit(solution)/shard_map/ppermute | solution.py:191
  13.3 0.0 collective-permute-done.8.refs_2_
  13.3 0.0 collective-permute-done.7.refs_1_
  13.3 2.8 %collective-permute-start.10 = (bf16[8,96,256]{2,1,0:T(8,128)(2,1)S(1)}, bf16[8,96,256]{2,1,0:T(8,128)(2,1)S(1)}, u32[]{:S(2)}, u32[]{:S(2)}) collective-permute-start(bf16[8,96,256]{2,1,0:T(8,128)(2,1)S(1)} %stack.7.refs_1_), channel_id=1, source_target_pairs={{0,4},{4,0},{8,12},{12,8},{16,20},{20,16},{24,28},{28,24},{1,5},{5... | collective-permute-start | bytes 1179656 | tf_op jit(solution)/shard_map/ppermute | solution.py:191
  16.1 0.0 collective-permute-done.4.refs_3_
  16.1 1.2 %collective-permute-done.3.refs_2_ = bf16[2,96,256]{2,1,0:T(8,128)(2,1)S(1)} collective-permute-done((bf16[2,96,256]{2,1,0:T(8,128)(2,1)S(1)}, bf16[2,96,256]{2,1,0:T(8,128)(2,1)S(1)}, u32[]{:S(2)}, u32[]{:S(2)}) %collective-permute-start.3) | collective-permute-done | bytes 98336 | tf_op jit(solution)/shard_map/ppermute | solution.py:191
  17.3 0.0 collective-permute-done.2.refs_1_
  17.3 2.9 %collective-permute-start.5 = (bf16[8,96,256]{2,1,0:T(8,128)(2,1)S(1)}, bf16[8,96,256]{2,1,0:T(8,128)(2,1)S(1)}, u32[]{:S(2)}, u32[]{:S(2)}) collective-permute-start(bf16[8,96,256]{2,1,0:T(8,128)(2,1)S(1)} %stack.5.refs_1_), channel_id=1, source_target_pairs={{0,4},{4,0},{8,12},{12,8},{16,20},{20,16},{24,28},{28,24},{1,5},{5... | collective-permute-start | bytes 1179656 | tf_op jit(solution)/shard_map/ppermute | solution.py:191
  20.2 0.0 collective-permute-done.10.refs_2_
  20.2 1.6 %correlate.1.refs_3_ = f32[2,4,8,128,128]{4,3,2,1,0:T(8,128)S(1)} custom-call(s32[1,5]{1,0:T(1,128)S(1)} %add_bitcast_fusion.refs_2_.refs_0_, bf16[8,96,256]{2,1,0:T(8,128)(2,1)S(1)} %stack.7.refs_1_, bf16[8,96,256]{2,1,0:T(8,128)(2,1)S(1)} %collective-permute-done.10.refs_2_), custom_call_target="tpu_custom_call" | custom-call | tf_op jit(solution)/shard_map/correlate/pallas_call | solution.py:173
  21.8 0.0 collective-permute-done.5.refs_2_
  21.8 2.7 %correlate_add.1 = f32[2,4,8,128,128]{4,3,2,1,0:T(8,128)} custom-call(s32[1,5]{1,0:T(1,128)S(1)} %add_bitcast_fusion.refs_2_.refs_0_, bf16[8,96,256]{2,1,0:T(8,128)(2,1)S(1)} %stack.5.refs_1_, bf16[8,96,256]{2,1,0:T(8,128)(2,1)S(1)} %collective-permute-done.5.refs_2_, f32[2,4,8,128,128]{4,3,2,1,0:T(8,128)S(1)} %correlate.1.refs_3_), custom_call_target="tpu_custom_call" | custom-call | tf_op jit(solution)/shard_map/correlate_add/pallas_call | solution.py:173
  (4 shorter events, 0.1 us)
Async XLA Ops:
  0.0 5.8 %copy-start = (s32[8,2]{0,1:T(2,128)S(1)}, s32[8,2]{0,1:T(2,128)}, u32[]{:S(2)}) copy-start(s32[8,2]{0,1:T(2,128)} %param.5) | copy-start | bytes 196
  1.3 4.8 %collective-permute-start.6 = (bf16[1,96,256]{2,1,0:T(8,128)(2,1)S(1)}, bf16[1,96,256]{2,1,0:T(8,128)(2,1)S(1)}, u32[]{:S(2)}, u32[]{:S(2)}) collective-permute-start(bf16[1,96,256]{2,1,0:T(8,128)(2,1)S(1)} %bitcast.6), channel_id=1, source_target_pairs={{0,1},{1,0},{2,3},{3,2},{4,5},{5,4},{6,7},{7,6},{8,9},{9,8},{10,11... | collective-permute-start | bytes 147464 | tf_op jit(solution)/shard_map/ppermute | solution.py:191
  3.5 5.4 %collective-permute-start.1 = (bf16[1,96,256]{2,1,0:T(8,128)(2,1)S(1)}, bf16[1,96,256]{2,1,0:T(8,128)(2,1)S(1)}, u32[]{:S(2)}, u32[]{:S(2)}) collective-permute-start(bf16[1,96,256]{2,1,0:T(8,128)(2,1)S(1)} %bitcast.7), channel_id=1, source_target_pairs={{0,3},{1,2},{2,1},{3,0},{4,7},{5,6},{6,5},{7,4},{8,11},{9,10},{10,... | collective-permute-start | bytes 147464 | tf_op jit(solution)/shard_map/ppermute | solution.py:191
  5.7 4.9 %collective-permute-start = (bf16[1,96,256]{2,1,0:T(8,128)(2,1)S(1)}, bf16[1,96,256]{2,1,0:T(8,128)(2,1)S(1)}, u32[]{:S(2)}, u32[]{:S(2)}) collective-permute-start(bf16[1,96,256]{2,1,0:T(8,128)(2,1)S(1)} %bitcast.8), channel_id=1, source_target_pairs={{0,2},{1,3},{2,0},{3,1},{4,6},{5,7},{6,4},{7,5},{8,10},{9,11},{10,... | collective-permute-start | bytes 147464 | tf_op jit(solution)/shard_map/ppermute | solution.py:191
  6.2 6.9 %collective-permute-start.9 = (bf16[2,96,256]{2,1,0:T(8,128)(2,1)S(1)}, bf16[2,96,256]{2,1,0:T(8,128)(2,1)S(1)}, u32[]{:S(2)}, u32[]{:S(2)}) collective-permute-start(bf16[2,96,256]{2,1,0:T(8,128)(2,1)S(1)} %stack.6.refs_0_), channel_id=1, source_target_pairs={{0,24},{4,28},{8,16},{12,20},{16,8},{20,12},{24,0},{28,4},{1,25},{... | collective-permute-start | bytes 294920 | tf_op jit(solution)/shard_map/ppermute | solution.py:191
  8.4 4.9 %collective-permute-start.8 = (bf16[2,96,256]{2,1,0:T(8,128)(2,1)S(1)}, bf16[2,96,256]{2,1,0:T(8,128)(2,1)S(1)}, u32[]{:S(2)}, u32[]{:S(2)}) collective-permute-start(bf16[2,96,256]{2,1,0:T(8,128)(2,1)S(1)} %stack.6.refs_0_), channel_id=1, source_target_pairs={{0,16},{4,20},{8,24},{12,28},{16,0},{20,4},{24,8},{28,12},{1,17},{... | collective-permute-start | bytes 294920 | tf_op jit(solution)/shard_map/ppermute | solution.py:191
  8.6 4.7 %collective-permute-start.7 = (bf16[2,96,256]{2,1,0:T(8,128)(2,1)S(1)}, bf16[2,96,256]{2,1,0:T(8,128)(2,1)S(1)}, u32[]{:S(2)}, u32[]{:S(2)}) collective-permute-start(bf16[2,96,256]{2,1,0:T(8,128)(2,1)S(1)} %stack.6.refs_0_), channel_id=1, source_target_pairs={{0,8},{4,12},{8,0},{12,4},{16,24},{20,28},{24,16},{28,20},{1,9},{5... | collective-permute-start | bytes 294920 | tf_op jit(solution)/shard_map/ppermute | solution.py:191
  10.6 5.5 %collective-permute-start.4 = (bf16[2,96,256]{2,1,0:T(8,128)(2,1)S(1)}, bf16[2,96,256]{2,1,0:T(8,128)(2,1)S(1)}, u32[]{:S(2)}, u32[]{:S(2)}) collective-permute-start(bf16[2,96,256]{2,1,0:T(8,128)(2,1)S(1)} %stack.4.refs_0_), channel_id=1, source_target_pairs={{0,24},{4,28},{8,16},{12,20},{16,8},{20,12},{24,0},{28,4},{1,25},{... | collective-permute-start | bytes 294920 | tf_op jit(solution)/shard_map/ppermute | solution.py:191
  12.8 4.5 %collective-permute-start.3 = (bf16[2,96,256]{2,1,0:T(8,128)(2,1)S(1)}, bf16[2,96,256]{2,1,0:T(8,128)(2,1)S(1)}, u32[]{:S(2)}, u32[]{:S(2)}) collective-permute-start(bf16[2,96,256]{2,1,0:T(8,128)(2,1)S(1)} %stack.4.refs_0_), channel_id=1, source_target_pairs={{0,16},{4,20},{8,24},{12,28},{16,0},{20,4},{24,8},{28,12},{1,17},{... | collective-permute-start | bytes 294920 | tf_op jit(solution)/shard_map/ppermute | solution.py:191
  13.1 4.2 %collective-permute-start.2 = (bf16[2,96,256]{2,1,0:T(8,128)(2,1)S(1)}, bf16[2,96,256]{2,1,0:T(8,128)(2,1)S(1)}, u32[]{:S(2)}, u32[]{:S(2)}) collective-permute-start(bf16[2,96,256]{2,1,0:T(8,128)(2,1)S(1)} %stack.4.refs_0_), channel_id=1, source_target_pairs={{0,8},{4,12},{8,0},{12,4},{16,24},{20,28},{24,16},{28,20},{1,9},{5... | collective-permute-start | bytes 294920 | tf_op jit(solution)/shard_map/ppermute | solution.py:191
  13.3 6.8 %collective-permute-start.10 = (bf16[8,96,256]{2,1,0:T(8,128)(2,1)S(1)}, bf16[8,96,256]{2,1,0:T(8,128)(2,1)S(1)}, u32[]{:S(2)}, u32[]{:S(2)}) collective-permute-start(bf16[8,96,256]{2,1,0:T(8,128)(2,1)S(1)} %stack.7.refs_1_), channel_id=1, source_target_pairs={{0,4},{4,0},{8,12},{12,8},{16,20},{20,16},{24,28},{28,24},{1,5},{5... | collective-permute-start | bytes 1179656 | tf_op jit(solution)/shard_map/ppermute | solution.py:191
  17.3 4.5 %collective-permute-start.5 = (bf16[8,96,256]{2,1,0:T(8,128)(2,1)S(1)}, bf16[8,96,256]{2,1,0:T(8,128)(2,1)S(1)}, u32[]{:S(2)}, u32[]{:S(2)}) collective-permute-start(bf16[8,96,256]{2,1,0:T(8,128)(2,1)S(1)} %stack.5.refs_1_), channel_id=1, source_target_pairs={{0,4},{4,0},{8,12},{12,8},{16,20},{20,16},{24,28},{28,24},{1,5},{5... | collective-permute-start | bytes 1179656 | tf_op jit(solution)/shard_map/ppermute | solution.py:191

commit v15 on v14

--- a/solution.py
+++ b/solution.py
@@ -85,7 +85,8 @@
     return (forward, (rc + is_, ic - rs)) if both else (forward,)
 
 
-def correlate_kernel(norm, picked, adds, where_ref, own_ref, sib_ref, *refs):
+def correlate_kernel(norm, picked, adds, places, where_ref, *refs):
+    parts, refs = refs[:2 * len(places)], refs[2 * len(places):]
     partials = refs[:adds]
     out_ref = refs[adds]
     spectra, left_turned, right_turned, *more = refs[adds + 1:]
@@ -98,11 +99,11 @@
     table = {k: (cos[i:i + 1], sin[i:i + 1]) for k, i in ((1, 1), (2, 2), (3, 3), (4, 4), (12, 6))}
 
     chan = where_ref[0, 0]
-    rows = own_ref.shape[1]
-    for core, piece in enumerate((own_ref, sib_ref)):
-        for k in range(piece.shape[0] // groups):
-            place = pl.multiple_of((chan ^ (CORES * k + core)) * rows, 32)
-            spectra[:, pl.ds(place, rows), :] = piece[k * groups:(k + 1) * groups]
+    for i, piece in enumerate(parts):
+        rows = piece.shape[1]
+        for slot, k in enumerate(places[i // 2]):
+            place = pl.multiple_of((chan ^ (CORES * k + i % 2)) * rows, 32)
+            spectra[:, pl.ds(place, rows), :] = piece[slot * groups:(slot + 1) * groups]
 
     def load(block, g):
         whole = spectra[g, pl.ds(pl.multiple_of(block * TILE, TILE), TILE), :].astype(jnp.float32)
@@ -148,22 +149,24 @@
                         more[0][i, u + v, fine] = partials[i // each][i % each, u + v, fine] + value
                     else:
                         out_ref[i, u + v, fine] = value
-            for s in range(2 if adds else 0):
-                fine = FINE_PAIRS[j][s] + 4
-                copy = pltpu.make_async_copy(more[0].at[i, :, fine], out_ref.at[i, :, fine], more[1])
-                copy.start(priority=s)
-                copies.append(copy)
+                for s in range(2 if adds else 0):
+                    done = (i, pl.ds(u, 2), FINE_PAIRS[j][s] + 4)
+                    copy = pltpu.make_async_copy(more[0].at[done], out_ref.at[done], more[1])
+                    copy.start(priority=s)
+                    copies.append(copy)
     for copy in copies:
         copy.wait()
 
 
-def correlate(pieces, groups, where, picked, hours, partials=()):
-    depth, rows, lanes = pieces[0].shape
+def correlate(parts, groups, where, picked, hours, partials=()):
+    places = [part[0] for part in parts]
+    pieces = [piece for part in parts for piece in part[1:]]
+    _, rows, lanes = pieces[0].shape
     fine = 2 * len(FINE_PAIRS)
     shape = (len(picked), len(COARSE), fine, TILE, TILE)
     norm = 1.0 / math.sqrt(F * hours)
     slots = min(len(picked), 2)
-    chans = len(pieces) * depth // groups * rows
+    chans = CORES * sum(map(len, places)) * rows
     scratch = 2 * (groups * chans * lanes + slots * (len(COARSE) + fine) * TILE * groups * lanes)
     adds = len(partials)
     more = []
@@ -171,7 +174,7 @@
         more = [pltpu.VMEM(shape, jnp.float32), pltpu.SemaphoreType.DMA]
         scratch += 4 * math.prod(shape)
     return pl.pallas_call(
-        lambda *refs: correlate_kernel(norm, picked, adds, *refs),
+        lambda *refs: correlate_kernel(norm, picked, adds, places, *refs),
         out_shape=jax.ShapeDtypeStruct(shape, jnp.float32),
         in_specs=[VMEM] * (1 + len(pieces) + adds),
         out_specs=pl.BlockSpec(memory_space=pl.ANY) if adds else VMEM,
@@ -218,8 +221,17 @@
     return stack(blocks[:groups // 2], after=(where,)), stack(blocks[groups // 2:], flops=10**9)
 
 
-def between_chips(half):
-    return [half] + [swap(half, "chan", k) for k in range(CORES, lax.axis_size("chan"), CORES)]
+def between_chips(half, parts):
+    chips = lax.axis_size("chan") // CORES
+    places = [0, *range(chips - 1, 0, -1)]
+    blocks = [swap(half, "chan", CORES * k) if k else half for k in places]
+    each = chips // parts
+    return [(places[i:i + each], blocks[i:i + each]) for i in range(0, chips, each)]
+
+
+def between_cores(parts):
+    collected = [(places, stack(blocks)) for places, blocks in parts]
+    return [(places, own, swap(own, "chan", 1)) for places, own in collected]
 
 
 def per_device(spectra, bad_channels, tile_list):
@@ -229,11 +241,8 @@
     white = whiten(spectra, bad_channels)
     pairs = lax.dynamic_slice_in_dim(tile_list, lax.axis_index("tm") * tiles, tiles, axis=0)
     where = jnp.concatenate([lax.axis_index("chan").reshape(1), pairs.reshape(-1)]).astype(jnp.int32).reshape(1, -1)
-    near, far = [between_chips(half) for half in halves(white, where)]
-    near = stack(near)
-    near = (near, swap(near, "chan", 1))
-    far = stack(far)
-    far = (far, swap(far, "chan", 1))
+    near, far = halves(white, where)
+    near, far = between_cores(between_chips(near, 2)), between_cores(between_chips(far, 2))
     partial = correlate(near, groups // 2, where, range(tiles), hours)
     out = correlate(far, groups // 2, where, range(tiles), hours, [partial])
     return out.reshape(tiles, LAGS, TILE, TILE)

time: 24.7 us -> 24.8 us (level)
  waiting for transfers between devices: 2.9 us -> 1.74 us
  starting transfers between devices: 15.6 us -> 16.7 us
    ppermute x11 -> x13, starting transfers between devices: 15.6 us -> 16.7 us  [swap(): lax.ppermute(array, axis, [(i, i ^ k) for i in range(lax.axis_size(axis))])]
    ppermute x11 -> x13, waiting for transfers between devices: 2.9 us -> 1.74 us  [swap(): lax.ppermute(array, axis, [(i, i ^ k) for i in range(lax.axis_size(axis))])]
  transfers between devices with their start and end apart: 11 -> 13, of which waited for: 2 -> 1; matrix products, arithmetic and copies ran while one was open for 1% -> 1% of each run, Pallas kernels for 7% -> 7%
where the time goes in v15:
time: 24.8 us; the launch traced here: 24.6 us
  starting transfers between devices  16.7 us (67%)
  Pallas kernels  5.74 us (23%)
  waiting for transfers between devices  1.74 us (7%)
  local copies, waits for them, and re-layouts  0.26 us (1%)
    ppermute x13, starting transfers between devices, swap(): lax.ppermute(array, axis, [(i, i ^ k) for i in range(lax.axis_size(axis))])  16.7 us
    pallas_call x2, Pallas kernels, correlate(): pl.pallas_call(lambda *refs: correlate_kernel(norm, picked, adds, places,...  4.38 us
    ppermute x13, waiting for transfers between devices, swap(): lax.ppermute(array, axis, [(i, i ^ k) for i in range(lax.axis_size(axis))])  1.74 us
    pallas_call x1, Pallas kernels, whiten(): pl.pallas_call(whiten_kernel, out_shape=jax.ShapeDtypeStruct((chans, bins...  1.29 us
  transfers between devices with their start and end apart: 13, of which 1 were waited for; matrix products, arithmetic and copies ran while one was open for 1% of the time, Pallas kernels for 7%

profile of v15, /device:TPU:1, one launch (start us, length us, event | category | flops | bytes accessed | tf_op | source)
XLA Modules:
  0.0 24.6 jit_solution(15864632374123966118)
XLA Ops:
  0.0 0.0 copy-start
  0.0 1.3 %whiten.1 = bf16[96,256]{1,0:T(8,128)(2,1)S(1)} custom-call(bf16[64,2,2,96]{3,2,1,0:T(2,128)(2,1)} %spectra_hbm.1, s32[1,96]{1,0:T(1,128)} %bitcast.10), custom_call_target="tpu_custom_call" | custom-call | tf_op jit(solution)/shard_map/whiten/pallas_call | solution.py:54
  1.3 2.2 %collective-permute-start.7 = (bf16[1,96,256]{2,1,0:T(8,128)(2,1)S(1)}, bf16[1,96,256]{2,1,0:T(8,128)(2,1)S(1)}, u32[]{:S(2)}, u32[]{:S(2)}) collective-permute-start(bf16[1,96,256]{2,1,0:T(8,128)(2,1)S(1)} %bitcast.6), channel_id=1, source_target_pairs={{0,1},{1,0},{2,3},{3,2},{4,5},{5,4},{6,7},{7,6},{8,9},{9,8},{10,11... | collective-permute-start | bytes 147464 | tf_op jit(solution)/shard_map/ppermute | solution.py:194
  3.5 2.2 %collective-permute-start.1 = (bf16[1,96,256]{2,1,0:T(8,128)(2,1)S(1)}, bf16[1,96,256]{2,1,0:T(8,128)(2,1)S(1)}, u32[]{:S(2)}, u32[]{:S(2)}) collective-permute-start(bf16[1,96,256]{2,1,0:T(8,128)(2,1)S(1)} %bitcast.7), channel_id=1, source_target_pairs={{0,3},{1,2},{2,1},{3,0},{4,7},{5,6},{6,5},{7,4},{8,11},{9,10},{10,... | collective-permute-start | bytes 147464 | tf_op jit(solution)/shard_map/ppermute | solution.py:194
  5.7 0.1 collective-permute-start
  5.8 0.0 copy-done
  5.8 0.1 constant_dynamic-slice_fusion
  5.9 0.1 copy.4
  6.0 0.1 reshape.16
  6.1 0.1 add_bitcast_fusion.refs_2_.refs_0_
  6.1 0.0 collective-permute-done.7.refs_1_
  6.2 2.2 %collective-permute-start.8 = (bf16[2,96,256]{2,1,0:T(8,128)(2,1)S(1)}, bf16[2,96,256]{2,1,0:T(8,128)(2,1)S(1)}, u32[]{:S(2)}, u32[]{:S(2)}) collective-permute-start(bf16[2,96,256]{2,1,0:T(8,128)(2,1)S(1)} %stack.9.refs_0_), channel_id=1, source_target_pairs={{0,24},{4,28},{8,16},{12,20},{16,8},{20,12},{24,0},{28,4},{1,25},{... | collective-permute-start | bytes 294920 | tf_op jit(solution)/shard_map/ppermute | solution.py:194
  8.4 0.3 %collective-permute-start.11 = (bf16[2,96,256]{2,1,0:T(8,128)(2,1)S(1)}, bf16[2,96,256]{2,1,0:T(8,128)(2,1)S(1)}, u32[]{:S(2)}, u32[]{:S(2)}) collective-permute-start(bf16[2,96,256]{2,1,0:T(8,128)(2,1)S(1)} %stack.9.refs_0_), channel_id=1, source_target_pairs={{0,8},{4,12},{8,0},{12,4},{16,24},{20,28},{24,16},{28,20},{1,9},{5... | collective-permute-start | bytes 294920 | tf_op jit(solution)/shard_map/ppermute | solution.py:194
  8.6 0.2 collective-permute-start.10
  8.9 0.0 collective-permute-done.1.refs_1_
  8.9 1.7 %collective-permute-done.refs_0_ = bf16[1,96,256]{2,1,0:T(8,128)(2,1)S(1)} collective-permute-done((bf16[1,96,256]{2,1,0:T(8,128)(2,1)S(1)}, bf16[1,96,256]{2,1,0:T(8,128)(2,1)S(1)}, u32[]{:S(2)}, u32[]{:S(2)}) %collective-permute-start) | collective-permute-done | bytes 49184 | tf_op jit(solution)/shard_map/ppermute | solution.py:194
  10.6 2.2 %collective-permute-start.2 = (bf16[2,96,256]{2,1,0:T(8,128)(2,1)S(1)}, bf16[2,96,256]{2,1,0:T(8,128)(2,1)S(1)}, u32[]{:S(2)}, u32[]{:S(2)}) collective-permute-start(bf16[2,96,256]{2,1,0:T(8,128)(2,1)S(1)} %stack.6.refs_0_), channel_id=1, source_target_pairs={{0,24},{4,28},{8,16},{12,20},{16,8},{20,12},{24,0},{28,4},{1,25},{... | collective-permute-start | bytes 294920 | tf_op jit(solution)/shard_map/ppermute | solution.py:194
  12.8 0.3 %collective-permute-start.5 = (bf16[2,96,256]{2,1,0:T(8,128)(2,1)S(1)}, bf16[2,96,256]{2,1,0:T(8,128)(2,1)S(1)}, u32[]{:S(2)}, u32[]{:S(2)}) collective-permute-start(bf16[2,96,256]{2,1,0:T(8,128)(2,1)S(1)} %stack.6.refs_0_), channel_id=1, source_target_pairs={{0,8},{4,12},{8,0},{12,4},{16,24},{20,28},{24,16},{28,20},{1,9},{5... | collective-permute-start | bytes 294920 | tf_op jit(solution)/shard_map/ppermute | solution.py:194
  13.1 0.0 collective-permute-done.8.refs_1_
  13.1 0.2 collective-permute-start.4
  13.3 0.0 collective-permute-done.11.refs_1_
  13.3 2.8 %collective-permute-start.9 = (bf16[4,96,256]{2,1,0:T(8,128)(2,1)S(1)}, bf16[4,96,256]{2,1,0:T(8,128)(2,1)S(1)}, u32[]{:S(2)}, u32[]{:S(2)}) collective-permute-start(bf16[4,96,256]{2,1,0:T(8,128)(2,1)S(1)} %stack.10.refs_1_), channel_id=1, source_target_pairs={{0,4},{4,0},{8,12},{12,8},{16,20},{20,16},{24,28},{28,24},{1,5},{5... | collective-permute-start | bytes 589832 | tf_op jit(solution)/shard_map/ppermute | solution.py:194
  16.1 0.0 collective-permute-done.10.refs_0_
  16.1 0.1 collective-permute-start.12
  16.2 0.0 collective-permute-done.2.refs_1_
  16.2 2.0 %collective-permute-start.3 = (bf16[4,96,256]{2,1,0:T(8,128)(2,1)S(1)}, bf16[4,96,256]{2,1,0:T(8,128)(2,1)S(1)}, u32[]{:S(2)}, u32[]{:S(2)}) collective-permute-start(bf16[4,96,256]{2,1,0:T(8,128)(2,1)S(1)} %stack.7.refs_1_), channel_id=1, source_target_pairs={{0,4},{4,0},{8,12},{12,8},{16,20},{20,16},{24,28},{28,24},{1,5},{5... | collective-permute-start | bytes 589832 | tf_op jit(solution)/shard_map/ppermute | solution.py:194
  18.2 0.0 collective-permute-done.5.refs_1_
  18.2 0.0 collective-permute-done.4.refs_0_
  18.2 2.0 %collective-permute-start.6 = (bf16[4,96,256]{2,1,0:T(8,128)(2,1)S(1)}, bf16[4,96,256]{2,1,0:T(8,128)(2,1)S(1)}, u32[]{:S(2)}, u32[]{:S(2)}) collective-permute-start(bf16[4,96,256]{2,1,0:T(8,128)(2,1)S(1)} %stack.8.refs_3_), channel_id=1, source_target_pairs={{0,4},{4,0},{8,12},{12,8},{16,20},{20,16},{24,28},{28,24},{1,5},{5... | collective-permute-start | bytes 589832 | tf_op jit(solution)/shard_map/ppermute | solution.py:194
  20.2 0.0 collective-permute-done.9.refs_2_
  20.2 0.0 collective-permute-done.12.refs_4_
  20.2 1.6 %correlate.1.refs_5_ = f32[2,4,8,128,128]{4,3,2,1,0:T(8,128)S(1)} custom-call(s32[1,5]{1,0:T(1,128)S(1)} %add_bitcast_fusion.refs_2_.refs_0_, bf16[4,96,256]{2,1,0:T(8,128)(2,1)S(1)} %stack.10.refs_1_, bf16[4,96,256]{2,1,0:T(8,128)(2,1)S(1)} %collective-permute-done.9.refs_2_, bf16[4,96,256]{2,1,0:T(8,128)(2,1)S(1)} %stack.11.refs_3_, ...), custom_call_target="tpu_custom_call" | custom-call | tf_op jit(solution)/shard_map/correlate/pallas_call | solution.py:176
  21.8 0.0 collective-permute-done.3.refs_2_
  21.8 0.0 collective-permute-done.6.refs_4_
  21.8 2.8 %correlate_add.1 = f32[2,4,8,128,128]{4,3,2,1,0:T(8,128)} custom-call(s32[1,5]{1,0:T(1,128)S(1)} %add_bitcast_fusion.refs_2_.refs_0_, bf16[4,96,256]{2,1,0:T(8,128)(2,1)S(1)} %stack.7.refs_1_, bf16[4,96,256]{2,1,0:T(8,128)(2,1)S(1)} %collective-permute-done.3.refs_2_, bf16[4,96,256]{2,1,0:T(8,128)(2,1)S(1)} %stack.8.refs_3_, ...), custom_call_target="tpu_custom_call" | custom-call | tf_op jit(solution)/shard_map/correlate_add/pallas_call | solution.py:176
  (6 shorter events, 0.1 us)
Async XLA Ops:
  0.0 5.8 %copy-start = (s32[8,2]{0,1:T(2,128)S(1)}, s32[8,2]{0,1:T(2,128)}, u32[]{:S(2)}) copy-start(s32[8,2]{0,1:T(2,128)} %param.5) | copy-start | bytes 196
  1.3 4.8 %collective-permute-start.7 = (bf16[1,96,256]{2,1,0:T(8,128)(2,1)S(1)}, bf16[1,96,256]{2,1,0:T(8,128)(2,1)S(1)}, u32[]{:S(2)}, u32[]{:S(2)}) collective-permute-start(bf16[1,96,256]{2,1,0:T(8,128)(2,1)S(1)} %bitcast.6), channel_id=1, source_target_pairs={{0,1},{1,0},{2,3},{3,2},{4,5},{5,4},{6,7},{7,6},{8,9},{9,8},{10,11... | collective-permute-start | bytes 147464 | tf_op jit(solution)/shard_map/ppermute | solution.py:194
  3.5 5.4 %collective-permute-start.1 = (bf16[1,96,256]{2,1,0:T(8,128)(2,1)S(1)}, bf16[1,96,256]{2,1,0:T(8,128)(2,1)S(1)}, u32[]{:S(2)}, u32[]{:S(2)}) collective-permute-start(bf16[1,96,256]{2,1,0:T(8,128)(2,1)S(1)} %bitcast.7), channel_id=1, source_target_pairs={{0,3},{1,2},{2,1},{3,0},{4,7},{5,6},{6,5},{7,4},{8,11},{9,10},{10,... | collective-permute-start | bytes 147464 | tf_op jit(solution)/shard_map/ppermute | solution.py:194
  5.7 4.9 %collective-permute-start = (bf16[1,96,256]{2,1,0:T(8,128)(2,1)S(1)}, bf16[1,96,256]{2,1,0:T(8,128)(2,1)S(1)}, u32[]{:S(2)}, u32[]{:S(2)}) collective-permute-start(bf16[1,96,256]{2,1,0:T(8,128)(2,1)S(1)} %bitcast.8), channel_id=1, source_target_pairs={{0,2},{1,3},{2,0},{3,1},{4,6},{5,7},{6,4},{7,5},{8,10},{9,11},{10,... | collective-permute-start | bytes 147464 | tf_op jit(solution)/shard_map/ppermute | solution.py:194
  6.2 6.9 %collective-permute-start.8 = (bf16[2,96,256]{2,1,0:T(8,128)(2,1)S(1)}, bf16[2,96,256]{2,1,0:T(8,128)(2,1)S(1)}, u32[]{:S(2)}, u32[]{:S(2)}) collective-permute-start(bf16[2,96,256]{2,1,0:T(8,128)(2,1)S(1)} %stack.9.refs_0_), channel_id=1, source_target_pairs={{0,24},{4,28},{8,16},{12,20},{16,8},{20,12},{24,0},{28,4},{1,25},{... | collective-permute-start | bytes 294920 | tf_op jit(solution)/shard_map/ppermute | solution.py:194
  8.4 4.9 %collective-permute-start.11 = (bf16[2,96,256]{2,1,0:T(8,128)(2,1)S(1)}, bf16[2,96,256]{2,1,0:T(8,128)(2,1)S(1)}, u32[]{:S(2)}, u32[]{:S(2)}) collective-permute-start(bf16[2,96,256]{2,1,0:T(8,128)(2,1)S(1)} %stack.9.refs_0_), channel_id=1, source_target_pairs={{0,8},{4,12},{8,0},{12,4},{16,24},{20,28},{24,16},{28,20},{1,9},{5... | collective-permute-start | bytes 294920 | tf_op jit(solution)/shard_map/ppermute | solution.py:194
  8.6 7.5 %collective-permute-start.10 = (bf16[2,96,256]{2,1,0:T(8,128)(2,1)S(1)}, bf16[2,96,256]{2,1,0:T(8,128)(2,1)S(1)}, u32[]{:S(2)}, u32[]{:S(2)}) collective-permute-start(bf16[2,96,256]{2,1,0:T(8,128)(2,1)S(1)} %stack.9.refs_0_), channel_id=1, source_target_pairs={{0,16},{4,20},{8,24},{12,28},{16,0},{20,4},{24,8},{28,12},{1,17},{... | collective-permute-start | bytes 294920 | tf_op jit(solution)/shard_map/ppermute | solution.py:194
  10.6 5.6 %collective-permute-start.2 = (bf16[2,96,256]{2,1,0:T(8,128)(2,1)S(1)}, bf16[2,96,256]{2,1,0:T(8,128)(2,1)S(1)}, u32[]{:S(2)}, u32[]{:S(2)}) collective-permute-start(bf16[2,96,256]{2,1,0:T(8,128)(2,1)S(1)} %stack.6.refs_0_), channel_id=1, source_target_pairs={{0,24},{4,28},{8,16},{12,20},{16,8},{20,12},{24,0},{28,4},{1,25},{... | collective-permute-start | bytes 294920 | tf_op jit(solution)/shard_map/ppermute | solution.py:194
  12.8 5.4 %collective-permute-start.5 = (bf16[2,96,256]{2,1,0:T(8,128)(2,1)S(1)}, bf16[2,96,256]{2,1,0:T(8,128)(2,1)S(1)}, u32[]{:S(2)}, u32[]{:S(2)}) collective-permute-start(bf16[2,96,256]{2,1,0:T(8,128)(2,1)S(1)} %stack.6.refs_0_), channel_id=1, source_target_pairs={{0,8},{4,12},{8,0},{12,4},{16,24},{20,28},{24,16},{28,20},{1,9},{5... | collective-permute-start | bytes 294920 | tf_op jit(solution)/shard_map/ppermute | solution.py:194
  13.1 5.1 %collective-permute-start.4 = (bf16[2,96,256]{2,1,0:T(8,128)(2,1)S(1)}, bf16[2,96,256]{2,1,0:T(8,128)(2,1)S(1)}, u32[]{:S(2)}, u32[]{:S(2)}) collective-permute-start(bf16[2,96,256]{2,1,0:T(8,128)(2,1)S(1)} %stack.6.refs_0_), channel_id=1, source_target_pairs={{0,16},{4,20},{8,24},{12,28},{16,0},{20,4},{24,8},{28,12},{1,17},{... | collective-permute-start | bytes 294920 | tf_op jit(solution)/shard_map/ppermute | solution.py:194
  13.3 6.9 %collective-permute-start.9 = (bf16[4,96,256]{2,1,0:T(8,128)(2,1)S(1)}, bf16[4,96,256]{2,1,0:T(8,128)(2,1)S(1)}, u32[]{:S(2)}, u32[]{:S(2)}) collective-permute-start(bf16[4,96,256]{2,1,0:T(8,128)(2,1)S(1)} %stack.10.refs_1_), channel_id=1, source_target_pairs={{0,4},{4,0},{8,12},{12,8},{16,20},{20,16},{24,28},{28,24},{1,5},{5... | collective-permute-start | bytes 589832 | tf_op jit(solution)/shard_map/ppermute | solution.py:194
  16.1 4.1 %collective-permute-start.12 = (bf16[4,96,256]{2,1,0:T(8,128)(2,1)S(1)}, bf16[4,96,256]{2,1,0:T(8,128)(2,1)S(1)}, u32[]{:S(2)}, u32[]{:S(2)}) collective-permute-start(bf16[4,96,256]{2,1,0:T(8,128)(2,1)S(1)} %stack.11.refs_3_), channel_id=1, source_target_pairs={{0,4},{4,0},{8,12},{12,8},{16,20},{20,16},{24,28},{28,24},{1,5},{5... | collective-permute-start | bytes 589832 | tf_op jit(solution)/shard_map/ppermute | solution.py:194
  16.2 5.6 %collective-permute-start.3 = (bf16[4,96,256]{2,1,0:T(8,128)(2,1)S(1)}, bf16[4,96,256]{2,1,0:T(8,128)(2,1)S(1)}, u32[]{:S(2)}, u32[]{:S(2)}) collective-permute-start(bf16[4,96,256]{2,1,0:T(8,128)(2,1)S(1)} %stack.7.refs_1_), channel_id=1, source_target_pairs={{0,4},{4,0},{8,12},{12,8},{16,20},{20,16},{24,28},{28,24},{1,5},{5... | collective-permute-start | bytes 589832 | tf_op jit(solution)/shard_map/ppermute | solution.py:194
  18.2 3.6 %collective-permute-start.6 = (bf16[4,96,256]{2,1,0:T(8,128)(2,1)S(1)}, bf16[4,96,256]{2,1,0:T(8,128)(2,1)S(1)}, u32[]{:S(2)}, u32[]{:S(2)}) collective-permute-start(bf16[4,96,256]{2,1,0:T(8,128)(2,1)S(1)} %stack.8.refs_3_), channel_id=1, source_target_pairs={{0,4},{4,0},{8,12},{12,8},{16,20},{20,16},{24,28},{28,24},{1,5},{5... | collective-permute-start | bytes 589832 | tf_op jit(solution)/shard_map/ppermute | solution.py:194

commit v16 on v15

--- a/solution.py
+++ b/solution.py
@@ -15,7 +15,9 @@
 SMALL = 4 * 1024 * 1024
 VMEM = pl.BlockSpec(memory_space=pltpu.VMEM)
 COARSE = (-12, -4, 4, 12)
-FINE_PAIRS = ((-4, 0), (-1, 1), (-2, 2), (-3, 3))
+FINE = (-4, -3, -2, -1, 0, 1, 2, 3)
+LEFT_ORDER = (-4, 4, -12, 12)
+STEPS = (0, -2, 2, -4)
 
 
 def whiten_kernel(spectra_hbm, bad_hbm, out_ref, spectra_ref, bad_ref, sems):
@@ -114,46 +116,50 @@
         ref[slot, rows_at, g * lanes:g * lanes + half] = value[0].astype(jnp.bfloat16)
         ref[slot, rows_at, g * lanes + half:(g + 1) * lanes] = value[1].astype(jnp.bfloat16)
 
+    def turn_left(slot, block, k):
+        for g in range(groups):
+            forward, backward = turn_by(*load(block, g), *(norm * part for part in table[k]), True)
+            store(left_turned, slot, LEFT_ORDER.index(k), g, forward)
+            store(left_turned, slot, LEFT_ORDER.index(-k), g, backward)
+
+    def turn_right(slot, block, k):
+        for g in range(groups):
+            re, im = load(block, g)
+            if k == 1:
+                store(right_turned, slot, FINE.index(0), g, (re, im))
+            turns = turn_by(re, im, *table[k], k in FINE)
+            for lag, value in zip((-k, k), turns):
+                store(right_turned, slot, FINE.index(lag), g, value)
+
     copies = []
     for i, t in enumerate(picked):
         slot = i % left_turned.shape[0]
         left_block, right_block = where_ref[0, 1 + 2 * t], where_ref[0, 2 + 2 * t]
-        for g in range(groups):
-            re, im = load(left_block, g)
-            for k in (4, 12):
-                forward, backward = turn_by(re, im, *(norm * part for part in table[k]), True)
-                store(left_turned, slot, COARSE.index(k), g, forward)
-                store(left_turned, slot, COARSE.index(-k), g, backward)
-        for j in range(len(FINE_PAIRS)):
-            for g in range(groups):
-                re, im = load(right_block, g)
+        for j, lag in enumerate(STEPS):
+            fine = FINE.index(lag)
+            turn_right(slot, right_block, j + 1)
+            for first in range(0, len(COARSE), 2):
                 if j == 0:
-                    store(right_turned, slot, 0, g, turn_by(re, im, *table[4], False)[0])
-                    store(right_turned, slot, 1, g, (re, im))
-                else:
-                    forward, backward = turn_by(re, im, *table[j], True)
-                    store(right_turned, slot, 2 * j, g, forward)
-                    store(right_turned, slot, 2 * j + 1, g, backward)
-            for u in range(0, len(COARSE), 2):
+                    turn_left(slot, left_block, LEFT_ORDER[first + 1])
                 total = lax.dot_general(
-                    left_turned[slot, u * TILE:(u + 2) * TILE, :],
-                    right_turned[slot, 2 * j * TILE:2 * (j + 1) * TILE, :],
+                    left_turned[slot, first * TILE:(first + 2) * TILE, :],
+                    right_turned[slot, fine * TILE:(fine + 2) * TILE, :],
                     (((1,), (1,)), ((), ())),
                     preferred_element_type=jnp.float32,
                 )
                 for v, s in ((0, 0), (0, 1), (1, 0), (1, 1)):
-                    fine = FINE_PAIRS[j][s] + 4
+                    u = COARSE.index(LEFT_ORDER[first + v])
                     value = total[v * TILE:(v + 1) * TILE, s * TILE:(s + 1) * TILE]
                     if adds:
                         each = len(picked) // adds
-                        more[0][i, u + v, fine] = partials[i // each][i % each, u + v, fine] + value
+                        more[0][i, u, fine + s] = partials[i // each][i % each, u, fine + s] + value
                     else:
-                        out_ref[i, u + v, fine] = value
-                for s in range(2 if adds else 0):
-                    done = (i, pl.ds(u, 2), FINE_PAIRS[j][s] + 4)
-                    copy = pltpu.make_async_copy(more[0].at[done], out_ref.at[done], more[1])
-                    copy.start(priority=s)
-                    copies.append(copy)
+                        out_ref[i, u, fine + s] = value
+            if adds:
+                done = (i, slice(None), pl.ds(fine, 2))
+                copy = pltpu.make_async_copy(more[0].at[done], out_ref.at[done], more[1])
+                copy.start(priority=j % 2)
+                copies.append(copy)
     for copy in copies:
         copy.wait()
 
@@ -162,7 +168,7 @@
     places = [part[0] for part in parts]
     pieces = [piece for part in parts for piece in part[1:]]
     _, rows, lanes = pieces[0].shape
-    fine = 2 * len(FINE_PAIRS)
+    fine = len(FINE)
     shape = (len(picked), len(COARSE), fine, TILE, TILE)
     norm = 1.0 / math.sqrt(F * hours)
     slots = min(len(picked), 2)

time: 24.8 us -> 24.8 us (level)
  no operation moved by 1% of the time
where the time goes in v16:
time: 24.8 us; the launch traced here: 24.6 us
  starting transfers between devices  16.7 us (67%)
  Pallas kernels  5.74 us (23%)
  waiting for transfers between devices  1.74 us (7%)
  local copies, waits for them, and re-layouts  0.26 us (1%)
    ppermute x13, starting transfers between devices, swap(): lax.ppermute(array, axis, [(i, i ^ k) for i in range(lax.axis_size(axis))])  16.7 us
    pallas_call x2, Pallas kernels, correlate(): pl.pallas_call(lambda *refs: correlate_kernel(norm, picked, adds, places,...  4.39 us
    ppermute x13, waiting for transfers between devices, swap(): lax.ppermute(array, axis, [(i, i ^ k) for i in range(lax.axis_size(axis))])  1.74 us
    pallas_call x1, Pallas kernels, whiten(): pl.pallas_call(whiten_kernel, out_shape=jax.ShapeDtypeStruct((chans, bins...  1.29 us
  transfers between devices with their start and end apart: 13, of which 1 were waited for; matrix products, arithmetic and copies ran while one was open for 1% of the time, Pallas kernels for 7%

profile of v16, /device:TPU:1, one launch (start us, length us, event | category | flops | bytes accessed | tf_op | source)
XLA Modules:
  0.0 24.6 jit_solution(1115875373795634548)
XLA Ops:
  0.0 0.0 copy-start
  0.0 1.3 %whiten.1 = bf16[96,256]{1,0:T(8,128)(2,1)S(1)} custom-call(bf16[64,2,2,96]{3,2,1,0:T(2,128)(2,1)} %spectra_hbm.1, s32[1,96]{1,0:T(1,128)} %bitcast.10), custom_call_target="tpu_custom_call" | custom-call | tf_op jit(solution)/shard_map/whiten/pallas_call | solution.py:56
  1.3 2.2 %collective-permute-start.7 = (bf16[1,96,256]{2,1,0:T(8,128)(2,1)S(1)}, bf16[1,96,256]{2,1,0:T(8,128)(2,1)S(1)}, u32[]{:S(2)}, u32[]{:S(2)}) collective-permute-start(bf16[1,96,256]{2,1,0:T(8,128)(2,1)S(1)} %bitcast.6), channel_id=1, source_target_pairs={{0,1},{1,0},{2,3},{3,2},{4,5},{5,4},{6,7},{7,6},{8,9},{9,8},{10,11... | collective-permute-start | bytes 147464 | tf_op jit(solution)/shard_map/ppermute | solution.py:200
  3.5 2.2 %collective-permute-start.1 = (bf16[1,96,256]{2,1,0:T(8,128)(2,1)S(1)}, bf16[1,96,256]{2,1,0:T(8,128)(2,1)S(1)}, u32[]{:S(2)}, u32[]{:S(2)}) collective-permute-start(bf16[1,96,256]{2,1,0:T(8,128)(2,1)S(1)} %bitcast.7), channel_id=1, source_target_pairs={{0,3},{1,2},{2,1},{3,0},{4,7},{5,6},{6,5},{7,4},{8,11},{9,10},{10,... | collective-permute-start | bytes 147464 | tf_op jit(solution)/shard_map/ppermute | solution.py:200
  5.7 0.1 collective-permute-start
  5.8 0.0 copy-done
  5.8 0.1 constant_dynamic-slice_fusion
  5.9 0.1 copy.4
  6.0 0.1 reshape.16
  6.1 0.1 add_bitcast_fusion.refs_2_.refs_0_
  6.1 0.0 collective-permute-done.7.refs_1_
  6.2 2.2 %collective-permute-start.8 = (bf16[2,96,256]{2,1,0:T(8,128)(2,1)S(1)}, bf16[2,96,256]{2,1,0:T(8,128)(2,1)S(1)}, u32[]{:S(2)}, u32[]{:S(2)}) collective-permute-start(bf16[2,96,256]{2,1,0:T(8,128)(2,1)S(1)} %stack.9.refs_0_), channel_id=1, source_target_pairs={{0,24},{4,28},{8,16},{12,20},{16,8},{20,12},{24,0},{28,4},{1,25},{... | collective-permute-start | bytes 294920 | tf_op jit(solution)/shard_map/ppermute | solution.py:200
  8.4 0.3 %collective-permute-start.11 = (bf16[2,96,256]{2,1,0:T(8,128)(2,1)S(1)}, bf16[2,96,256]{2,1,0:T(8,128)(2,1)S(1)}, u32[]{:S(2)}, u32[]{:S(2)}) collective-permute-start(bf16[2,96,256]{2,1,0:T(8,128)(2,1)S(1)} %stack.9.refs_0_), channel_id=1, source_target_pairs={{0,8},{4,12},{8,0},{12,4},{16,24},{20,28},{24,16},{28,20},{1,9},{5... | collective-permute-start | bytes 294920 | tf_op jit(solution)/shard_map/ppermute | solution.py:200
  8.6 0.2 collective-permute-start.10
  8.9 0.0 collective-permute-done.1.refs_1_
  8.9 1.7 %collective-permute-done.refs_0_ = bf16[1,96,256]{2,1,0:T(8,128)(2,1)S(1)} collective-permute-done((bf16[1,96,256]{2,1,0:T(8,128)(2,1)S(1)}, bf16[1,96,256]{2,1,0:T(8,128)(2,1)S(1)}, u32[]{:S(2)}, u32[]{:S(2)}) %collective-permute-start) | collective-permute-done | bytes 49184 | tf_op jit(solution)/shard_map/ppermute | solution.py:200
  10.6 2.2 %collective-permute-start.2 = (bf16[2,96,256]{2,1,0:T(8,128)(2,1)S(1)}, bf16[2,96,256]{2,1,0:T(8,128)(2,1)S(1)}, u32[]{:S(2)}, u32[]{:S(2)}) collective-permute-start(bf16[2,96,256]{2,1,0:T(8,128)(2,1)S(1)} %stack.6.refs_0_), channel_id=1, source_target_pairs={{0,24},{4,28},{8,16},{12,20},{16,8},{20,12},{24,0},{28,4},{1,25},{... | collective-permute-start | bytes 294920 | tf_op jit(solution)/shard_map/ppermute | solution.py:200
  12.8 0.3 %collective-permute-start.5 = (bf16[2,96,256]{2,1,0:T(8,128)(2,1)S(1)}, bf16[2,96,256]{2,1,0:T(8,128)(2,1)S(1)}, u32[]{:S(2)}, u32[]{:S(2)}) collective-permute-start(bf16[2,96,256]{2,1,0:T(8,128)(2,1)S(1)} %stack.6.refs_0_), channel_id=1, source_target_pairs={{0,8},{4,12},{8,0},{12,4},{16,24},{20,28},{24,16},{28,20},{1,9},{5... | collective-permute-start | bytes 294920 | tf_op jit(solution)/shard_map/ppermute | solution.py:200
  13.1 0.0 collective-permute-done.8.refs_1_
  13.1 0.2 collective-permute-start.4
  13.3 0.0 collective-permute-done.11.refs_1_
  13.3 2.8 %collective-permute-start.9 = (bf16[4,96,256]{2,1,0:T(8,128)(2,1)S(1)}, bf16[4,96,256]{2,1,0:T(8,128)(2,1)S(1)}, u32[]{:S(2)}, u32[]{:S(2)}) collective-permute-start(bf16[4,96,256]{2,1,0:T(8,128)(2,1)S(1)} %stack.10.refs_1_), channel_id=1, source_target_pairs={{0,4},{4,0},{8,12},{12,8},{16,20},{20,16},{24,28},{28,24},{1,5},{5... | collective-permute-start | bytes 589832 | tf_op jit(solution)/shard_map/ppermute | solution.py:200
  16.1 0.0 collective-permute-done.10.refs_0_
  16.1 0.1 collective-permute-start.12
  16.2 0.0 collective-permute-done.2.refs_1_
  16.2 2.0 %collective-permute-start.3 = (bf16[4,96,256]{2,1,0:T(8,128)(2,1)S(1)}, bf16[4,96,256]{2,1,0:T(8,128)(2,1)S(1)}, u32[]{:S(2)}, u32[]{:S(2)}) collective-permute-start(bf16[4,96,256]{2,1,0:T(8,128)(2,1)S(1)} %stack.7.refs_1_), channel_id=1, source_target_pairs={{0,4},{4,0},{8,12},{12,8},{16,20},{20,16},{24,28},{28,24},{1,5},{5... | collective-permute-start | bytes 589832 | tf_op jit(solution)/shard_map/ppermute | solution.py:200
  18.2 0.0 collective-permute-done.5.refs_1_
  18.2 0.0 collective-permute-done.4.refs_0_
  18.2 2.0 %collective-permute-start.6 = (bf16[4,96,256]{2,1,0:T(8,128)(2,1)S(1)}, bf16[4,96,256]{2,1,0:T(8,128)(2,1)S(1)}, u32[]{:S(2)}, u32[]{:S(2)}) collective-permute-start(bf16[4,96,256]{2,1,0:T(8,128)(2,1)S(1)} %stack.8.refs_3_), channel_id=1, source_target_pairs={{0,4},{4,0},{8,12},{12,8},{16,20},{20,16},{24,28},{28,24},{1,5},{5... | collective-permute-start | bytes 589832 | tf_op jit(solution)/shard_map/ppermute | solution.py:200
  20.2 0.0 collective-permute-done.9.refs_2_
  20.2 0.0 collective-permute-done.12.refs_4_
  20.2 1.7 %correlate.1.refs_5_ = f32[2,4,8,128,128]{4,3,2,1,0:T(8,128)S(1)} custom-call(s32[1,5]{1,0:T(1,128)S(1)} %add_bitcast_fusion.refs_2_.refs_0_, bf16[4,96,256]{2,1,0:T(8,128)(2,1)S(1)} %stack.10.refs_1_, bf16[4,96,256]{2,1,0:T(8,128)(2,1)S(1)} %collective-permute-done.9.refs_2_, bf16[4,96,256]{2,1,0:T(8,128)(2,1)S(1)} %stack.11.refs_3_, ...), custom_call_target="tpu_custom_call" | custom-call | tf_op jit(solution)/shard_map/correlate/pallas_call | solution.py:182
  21.9 0.0 collective-permute-done.3.refs_2_
  21.9 0.0 collective-permute-done.6.refs_4_
  21.9 2.7 %correlate_add.1 = f32[2,4,8,128,128]{4,3,2,1,0:T(8,128)} custom-call(s32[1,5]{1,0:T(1,128)S(1)} %add_bitcast_fusion.refs_2_.refs_0_, bf16[4,96,256]{2,1,0:T(8,128)(2,1)S(1)} %stack.7.refs_1_, bf16[4,96,256]{2,1,0:T(8,128)(2,1)S(1)} %collective-permute-done.3.refs_2_, bf16[4,96,256]{2,1,0:T(8,128)(2,1)S(1)} %stack.8.refs_3_, ...), custom_call_target="tpu_custom_call" | custom-call | tf_op jit(solution)/shard_map/correlate_add/pallas_call | solution.py:182
  (6 shorter events, 0.1 us)
Async XLA Ops:
  0.0 5.8 %copy-start = (s32[8,2]{0,1:T(2,128)S(1)}, s32[8,2]{0,1:T(2,128)}, u32[]{:S(2)}) copy-start(s32[8,2]{0,1:T(2,128)} %param.5) | copy-start | bytes 196
  1.3 4.8 %collective-permute-start.7 = (bf16[1,96,256]{2,1,0:T(8,128)(2,1)S(1)}, bf16[1,96,256]{2,1,0:T(8,128)(2,1)S(1)}, u32[]{:S(2)}, u32[]{:S(2)}) collective-permute-start(bf16[1,96,256]{2,1,0:T(8,128)(2,1)S(1)} %bitcast.6), channel_id=1, source_target_pairs={{0,1},{1,0},{2,3},{3,2},{4,5},{5,4},{6,7},{7,6},{8,9},{9,8},{10,11... | collective-permute-start | bytes 147464 | tf_op jit(solution)/shard_map/ppermute | solution.py:200
  3.5 5.4 %collective-permute-start.1 = (bf16[1,96,256]{2,1,0:T(8,128)(2,1)S(1)}, bf16[1,96,256]{2,1,0:T(8,128)(2,1)S(1)}, u32[]{:S(2)}, u32[]{:S(2)}) collective-permute-start(bf16[1,96,256]{2,1,0:T(8,128)(2,1)S(1)} %bitcast.7), channel_id=1, source_target_pairs={{0,3},{1,2},{2,1},{3,0},{4,7},{5,6},{6,5},{7,4},{8,11},{9,10},{10,... | collective-permute-start | bytes 147464 | tf_op jit(solution)/shard_map/ppermute | solution.py:200
  5.7 4.9 %collective-permute-start = (bf16[1,96,256]{2,1,0:T(8,128)(2,1)S(1)}, bf16[1,96,256]{2,1,0:T(8,128)(2,1)S(1)}, u32[]{:S(2)}, u32[]{:S(2)}) collective-permute-start(bf16[1,96,256]{2,1,0:T(8,128)(2,1)S(1)} %bitcast.8), channel_id=1, source_target_pairs={{0,2},{1,3},{2,0},{3,1},{4,6},{5,7},{6,4},{7,5},{8,10},{9,11},{10,... | collective-permute-start | bytes 147464 | tf_op jit(solution)/shard_map/ppermute | solution.py:200
  6.2 6.9 %collective-permute-start.8 = (bf16[2,96,256]{2,1,0:T(8,128)(2,1)S(1)}, bf16[2,96,256]{2,1,0:T(8,128)(2,1)S(1)}, u32[]{:S(2)}, u32[]{:S(2)}) collective-permute-start(bf16[2,96,256]{2,1,0:T(8,128)(2,1)S(1)} %stack.9.refs_0_), channel_id=1, source_target_pairs={{0,24},{4,28},{8,16},{12,20},{16,8},{20,12},{24,0},{28,4},{1,25},{... | collective-permute-start | bytes 294920 | tf_op jit(solution)/shard_map/ppermute | solution.py:200
  8.4 4.9 %collective-permute-start.11 = (bf16[2,96,256]{2,1,0:T(8,128)(2,1)S(1)}, bf16[2,96,256]{2,1,0:T(8,128)(2,1)S(1)}, u32[]{:S(2)}, u32[]{:S(2)}) collective-permute-start(bf16[2,96,256]{2,1,0:T(8,128)(2,1)S(1)} %stack.9.refs_0_), channel_id=1, source_target_pairs={{0,8},{4,12},{8,0},{12,4},{16,24},{20,28},{24,16},{28,20},{1,9},{5... | collective-permute-start | bytes 294920 | tf_op jit(solution)/shard_map/ppermute | solution.py:200
  8.6 7.5 %collective-permute-start.10 = (bf16[2,96,256]{2,1,0:T(8,128)(2,1)S(1)}, bf16[2,96,256]{2,1,0:T(8,128)(2,1)S(1)}, u32[]{:S(2)}, u32[]{:S(2)}) collective-permute-start(bf16[2,96,256]{2,1,0:T(8,128)(2,1)S(1)} %stack.9.refs_0_), channel_id=1, source_target_pairs={{0,16},{4,20},{8,24},{12,28},{16,0},{20,4},{24,8},{28,12},{1,17},{... | collective-permute-start | bytes 294920 | tf_op jit(solution)/shard_map/ppermute | solution.py:200
  10.6 5.6 %collective-permute-start.2 = (bf16[2,96,256]{2,1,0:T(8,128)(2,1)S(1)}, bf16[2,96,256]{2,1,0:T(8,128)(2,1)S(1)}, u32[]{:S(2)}, u32[]{:S(2)}) collective-permute-start(bf16[2,96,256]{2,1,0:T(8,128)(2,1)S(1)} %stack.6.refs_0_), channel_id=1, source_target_pairs={{0,24},{4,28},{8,16},{12,20},{16,8},{20,12},{24,0},{28,4},{1,25},{... | collective-permute-start | bytes 294920 | tf_op jit(solution)/shard_map/ppermute | solution.py:200
  12.8 5.4 %collective-permute-start.5 = (bf16[2,96,256]{2,1,0:T(8,128)(2,1)S(1)}, bf16[2,96,256]{2,1,0:T(8,128)(2,1)S(1)}, u32[]{:S(2)}, u32[]{:S(2)}) collective-permute-start(bf16[2,96,256]{2,1,0:T(8,128)(2,1)S(1)} %stack.6.refs_0_), channel_id=1, source_target_pairs={{0,8},{4,12},{8,0},{12,4},{16,24},{20,28},{24,16},{28,20},{1,9},{5... | collective-permute-start | bytes 294920 | tf_op jit(solution)/shard_map/ppermute | solution.py:200
  13.1 5.1 %collective-permute-start.4 = (bf16[2,96,256]{2,1,0:T(8,128)(2,1)S(1)}, bf16[2,96,256]{2,1,0:T(8,128)(2,1)S(1)}, u32[]{:S(2)}, u32[]{:S(2)}) collective-permute-start(bf16[2,96,256]{2,1,0:T(8,128)(2,1)S(1)} %stack.6.refs_0_), channel_id=1, source_target_pairs={{0,16},{4,20},{8,24},{12,28},{16,0},{20,4},{24,8},{28,12},{1,17},{... | collective-permute-start | bytes 294920 | tf_op jit(solution)/shard_map/ppermute | solution.py:200
  13.3 6.9 %collective-permute-start.9 = (bf16[4,96,256]{2,1,0:T(8,128)(2,1)S(1)}, bf16[4,96,256]{2,1,0:T(8,128)(2,1)S(1)}, u32[]{:S(2)}, u32[]{:S(2)}) collective-permute-start(bf16[4,96,256]{2,1,0:T(8,128)(2,1)S(1)} %stack.10.refs_1_), channel_id=1, source_target_pairs={{0,4},{4,0},{8,12},{12,8},{16,20},{20,16},{24,28},{28,24},{1,5},{5... | collective-permute-start | bytes 589832 | tf_op jit(solution)/shard_map/ppermute | solution.py:200
  16.1 4.1 %collective-permute-start.12 = (bf16[4,96,256]{2,1,0:T(8,128)(2,1)S(1)}, bf16[4,96,256]{2,1,0:T(8,128)(2,1)S(1)}, u32[]{:S(2)}, u32[]{:S(2)}) collective-permute-start(bf16[4,96,256]{2,1,0:T(8,128)(2,1)S(1)} %stack.11.refs_3_), channel_id=1, source_target_pairs={{0,4},{4,0},{8,12},{12,8},{16,20},{20,16},{24,28},{28,24},{1,5},{5... | collective-permute-start | bytes 589832 | tf_op jit(solution)/shard_map/ppermute | solution.py:200
  16.2 5.7 %collective-permute-start.3 = (bf16[4,96,256]{2,1,0:T(8,128)(2,1)S(1)}, bf16[4,96,256]{2,1,0:T(8,128)(2,1)S(1)}, u32[]{:S(2)}, u32[]{:S(2)}) collective-permute-start(bf16[4,96,256]{2,1,0:T(8,128)(2,1)S(1)} %stack.7.refs_1_), channel_id=1, source_target_pairs={{0,4},{4,0},{8,12},{12,8},{16,20},{20,16},{24,28},{28,24},{1,5},{5... | collective-permute-start | bytes 589832 | tf_op jit(solution)/shard_map/ppermute | solution.py:200
  18.2 3.6 %collective-permute-start.6 = (bf16[4,96,256]{2,1,0:T(8,128)(2,1)S(1)}, bf16[4,96,256]{2,1,0:T(8,128)(2,1)S(1)}, u32[]{:S(2)}, u32[]{:S(2)}) collective-permute-start(bf16[4,96,256]{2,1,0:T(8,128)(2,1)S(1)} %stack.8.refs_3_), channel_id=1, source_target_pairs={{0,4},{4,0},{8,12},{12,8},{16,20},{20,16},{24,28},{28,24},{1,5},{5... | collective-permute-start | bytes 589832 | tf_op jit(solution)/shard_map/ppermute | solution.py:200

commit v17 on v16

--- a/solution.py
+++ b/solution.py
@@ -87,11 +87,11 @@
     return (forward, (rc + is_, ic - rs)) if both else (forward,)
 
 
-def correlate_kernel(norm, picked, adds, places, where_ref, *refs):
-    parts, refs = refs[:2 * len(places)], refs[2 * len(places):]
-    partials = refs[:adds]
-    out_ref = refs[adds]
-    spectra, left_turned, right_turned, *more = refs[adds + 1:]
+def correlate_kernel(norm, picked, adds, slots_of, where_ref, *refs):
+    partials, refs = refs[:adds], refs[adds:]
+    parts, refs = refs[:2 * len(slots_of)], refs[2 * len(slots_of):]
+    out_ref = refs[0]
+    spectra, left_turned, right_turned, *more = refs[1:]
     groups, _, lanes = spectra.shape
     half = lanes // 2
     hours_dev = half // F
@@ -103,9 +103,9 @@
     chan = where_ref[0, 0]
     for i, piece in enumerate(parts):
         rows = piece.shape[1]
-        for slot, k in enumerate(places[i // 2]):
+        for slot, (k, g) in enumerate(slots_of[i // 2]):
             place = pl.multiple_of((chan ^ (CORES * k + i % 2)) * rows, 32)
-            spectra[:, pl.ds(place, rows), :] = piece[slot * groups:(slot + 1) * groups]
+            spectra[g, pl.ds(place, rows), :] = piece[slot]
 
     def load(block, g):
         whole = spectra[g, pl.ds(pl.multiple_of(block * TILE, TILE), TILE), :].astype(jnp.float32)
@@ -165,14 +165,14 @@
 
 
 def correlate(parts, groups, where, picked, hours, partials=()):
-    places = [part[0] for part in parts]
+    slots_of = [part[0] for part in parts]
     pieces = [piece for part in parts for piece in part[1:]]
     _, rows, lanes = pieces[0].shape
     fine = len(FINE)
     shape = (len(picked), len(COARSE), fine, TILE, TILE)
     norm = 1.0 / math.sqrt(F * hours)
     slots = min(len(picked), 2)
-    chans = CORES * sum(map(len, places)) * rows
+    chans = lax.axis_size("chan") * rows
     scratch = 2 * (groups * chans * lanes + slots * (len(COARSE) + fine) * TILE * groups * lanes)
     adds = len(partials)
     more = []
@@ -180,7 +180,7 @@
         more = [pltpu.VMEM(shape, jnp.float32), pltpu.SemaphoreType.DMA]
         scratch += 4 * math.prod(shape)
     return pl.pallas_call(
-        lambda *refs: correlate_kernel(norm, picked, adds, places, *refs),
+        lambda *refs: correlate_kernel(norm, picked, adds, slots_of, *refs),
         out_shape=jax.ShapeDtypeStruct(shape, jnp.float32),
         in_specs=[VMEM] * (1 + len(pieces) + adds),
         out_specs=pl.BlockSpec(memory_space=pl.ANY) if adds else VMEM,
@@ -193,7 +193,7 @@
         compiler_params=pltpu.CompilerParams(vmem_limit_bytes=scratch + SMALL),
         cost_estimate=pl.CostEstimate(flops=0, bytes_accessed=0, transcendentals=0),
         name="correlate_add" if adds else "correlate",
-    )(where, *pieces, *partials)
+    )(where, *partials, *pieces)
 
 
 def swap(array, axis, k):
@@ -221,34 +221,32 @@
     )(*blocks, *after)
 
 
-def halves(white, where):
-    groups = lax.axis_size("tm")
-    blocks = [white[None]] + [swap(white[None], "tm", k) for k in range(1, groups)]
-    return stack(blocks[:groups // 2], after=(where,)), stack(blocks[groups // 2:], flops=10**9)
-
-
-def between_chips(half, parts):
+def between_chips(block):
     chips = lax.axis_size("chan") // CORES
-    places = [0, *range(chips - 1, 0, -1)]
-    blocks = [swap(half, "chan", CORES * k) if k else half for k in places]
-    each = chips // parts
-    return [(places[i:i + each], blocks[i:i + each]) for i in range(0, chips, each)]
-
-
-def between_cores(parts):
-    collected = [(places, stack(blocks)) for places, blocks in parts]
-    return [(places, own, swap(own, "chan", 1)) for places, own in collected]
+    return [(k, swap(block, "chan", CORES * k) if k else block) for k in (0, *range(chips - 1, 0, -1))]
+
+
+def both_cores(slots, own):
+    return slots, own, swap(own, "chan", 1)
 
 
 def per_device(spectra, bad_channels, tile_list):
     groups = lax.axis_size("tm")
     hours = spectra.shape[1] * groups
     tiles = tile_list.shape[0] // groups
-    white = whiten(spectra, bad_channels)
+    white = whiten(spectra, bad_channels)[None]
     pairs = lax.dynamic_slice_in_dim(tile_list, lax.axis_index("tm") * tiles, tiles, axis=0)
     where = jnp.concatenate([lax.axis_index("chan").reshape(1), pairs.reshape(-1)]).astype(jnp.int32).reshape(1, -1)
-    near, far = halves(white, where)
-    near, far = between_cores(between_chips(near, 2)), between_cores(between_chips(far, 2))
+    far = stack([swap(white, "tm", k) for k in range(groups // 2, groups)])
+    plane = between_chips(white)
+    own = stack([block for _, block in plane], after=(where,))
+    near = [own] + [swap(own, "tm", k) for k in range(1, groups // 2)]
+    near = [both_cores([(k, g) for k, _ in plane], block) for g, block in enumerate(near)]
+    plane = between_chips(far)
+    far = []
+    for part, flops in ((plane[:len(plane) // 2], 15 * 10**8), (plane[len(plane) // 2:], 0)):
+        slots = [(k, g) for k, _ in part for g in range(groups // 2)]
+        far.append(both_cores(slots, stack([block for _, block in part], flops=flops)))
     partial = correlate(near, groups // 2, where, range(tiles), hours)
     out = correlate(far, groups // 2, where, range(tiles), hours, [partial])
     return out.reshape(tiles, LAGS, TILE, TILE)

time: 24.8 us -> 26.7 us (1.077); the launches traced: 24.6 us -> 26.2 us
  starting transfers between devices: 16.7 us -> 17.8 us
  waiting for transfers between devices: 1.74 us -> 2.26 us
    ppermute x13, starting transfers between devices: 16.7 us -> 17.8 us  [swap(): lax.ppermute(array, axis, [(i, i ^ k) for i in range(lax.axis_size(axis))])]
    ppermute x13, waiting for transfers between devices: 1.74 us -> 2.26 us  [swap(): lax.ppermute(array, axis, [(i, i ^ k) for i in range(lax.axis_size(axis))])]
  transfers between devices with their start and end apart: 13 -> 13, of which waited for: 1 -> 2; matrix products, arithmetic and copies ran while one was open for 1% -> 1% of each run, Pallas kernels for 7% -> 7%
where the time goes in v17:
time: 26.7 us; the launch traced here: 26.2 us
  starting transfers between devices  17.8 us (67%)
  Pallas kernels  5.72 us (21%)
  waiting for transfers between devices  2.26 us (8%)
    ppermute x13, starting transfers between devices, swap(): lax.ppermute(array, axis, [(i, i ^ k) for i in range(lax.axis_size(axis))])  17.8 us
    pallas_call x2, Pallas kernels, correlate(): pl.pallas_call(lambda *refs: correlate_kernel(norm, picked, adds, slots_o...  4.38 us
    ppermute x13, waiting for transfers between devices, swap(): lax.ppermute(array, axis, [(i, i ^ k) for i in range(lax.axis_size(axis))])  2.26 us
    pallas_call x1, Pallas kernels, whiten(): pl.pallas_call(whiten_kernel, out_shape=jax.ShapeDtypeStruct((chans, bins...  1.29 us
  transfers between devices with their start and end apart: 13, of which 2 were waited for; matrix products, arithmetic and copies ran while one was open for 1% of the time, Pallas kernels for 7%

profile of v17, /device:TPU:1, one launch (start us, length us, event | category | flops | bytes accessed | tf_op | source)
XLA Modules:
  0.0 26.2 jit_solution(12468232059625245420)
XLA Ops:
  0.0 0.0 copy-start
  0.0 1.3 %whiten.1 = bf16[96,256]{1,0:T(8,128)(2,1)S(1)} custom-call(bf16[64,2,2,96]{3,2,1,0:T(2,128)(2,1)} %spectra_hbm.1, s32[1,96]{1,0:T(1,128)} %bitcast.12), custom_call_target="tpu_custom_call" | custom-call | tf_op jit(solution)/shard_map/whiten/pallas_call | solution.py:56
  1.3 4.2 %collective-permute-start.7 = (bf16[1,96,256]{2,1,0:T(8,128)(2,1)S(1)}, bf16[1,96,256]{2,1,0:T(8,128)(2,1)S(1)}, u32[]{:S(2)}, u32[]{:S(2)}) collective-permute-start(bf16[1,96,256]{2,1,0:T(8,128)(2,1)S(1)} %bitcast.6), channel_id=1, source_target_pairs={{0,3},{1,2},{2,1},{3,0},{4,7},{5,6},{6,5},{7,4},{8,11},{9,10},{10,... | collective-permute-start | bytes 147464 | tf_op jit(solution)/shard_map/ppermute | solution.py:200
  5.5 0.0 collective-permute-start.6
  5.5 1.2 %collective-permute-start.2 = (bf16[1,96,256]{2,1,0:T(8,128)(2,1)S(1)}, bf16[1,96,256]{2,1,0:T(8,128)(2,1)S(1)}, u32[]{:S(2)}, u32[]{:S(2)}) collective-permute-start(bf16[1,96,256]{2,1,0:T(8,128)(2,1)S(1)} %bitcast.8), channel_id=1, source_target_pairs={{0,8},{4,12},{8,0},{12,4},{16,24},{20,28},{24,16},{28,20},{1,9},{5... | collective-permute-start | bytes 147464 | tf_op jit(solution)/shard_map/ppermute | solution.py:200
  6.7 1.2 %collective-permute-start.1 = (bf16[1,96,256]{2,1,0:T(8,128)(2,1)S(1)}, bf16[1,96,256]{2,1,0:T(8,128)(2,1)S(1)}, u32[]{:S(2)}, u32[]{:S(2)}) collective-permute-start(bf16[1,96,256]{2,1,0:T(8,128)(2,1)S(1)} %bitcast.9), channel_id=1, source_target_pairs={{0,16},{4,20},{8,24},{12,28},{16,0},{20,4},{24,8},{28,12},{1,17},{... | collective-permute-start | bytes 147464 | tf_op jit(solution)/shard_map/ppermute | solution.py:200
  8.0 0.2 collective-permute-start
  8.2 0.0 copy-done
  8.2 0.1 constant_dynamic-slice_fusion
  8.2 0.1 copy.4
  8.3 0.1 reshape.16
  8.4 0.0 collective-permute-done.7.refs_1_
  8.4 1.5 %collective-permute-done.6.refs_0_ = bf16[1,96,256]{2,1,0:T(8,128)(2,1)S(1)} collective-permute-done((bf16[1,96,256]{2,1,0:T(8,128)(2,1)S(1)}, bf16[1,96,256]{2,1,0:T(8,128)(2,1)S(1)}, u32[]{:S(2)}, u32[]{:S(2)}) %collective-permute-start.6) | collective-permute-done | bytes 49184 | tf_op jit(solution)/shard_map/ppermute | solution.py:200
  9.9 2.2 %collective-permute-start.8 = (bf16[2,96,256]{2,1,0:T(8,128)(2,1)S(1)}, bf16[2,96,256]{2,1,0:T(8,128)(2,1)S(1)}, u32[]{:S(2)}, u32[]{:S(2)}) collective-permute-start(bf16[2,96,256]{2,1,0:T(8,128)(2,1)S(1)} %stack.5.refs_0_), channel_id=1, source_target_pairs={{0,24},{4,28},{8,16},{12,20},{16,8},{20,12},{24,0},{28,4},{1,25},{... | collective-permute-start | bytes 294920 | tf_op jit(solution)/shard_map/ppermute | solution.py:200
  12.1 0.1 add_bitcast_fusion.refs_4_.refs_0_
  12.2 0.0 collective-permute-done.2.refs_3_
  12.2 0.0 collective-permute-done.1.refs_2_
  12.2 0.0 collective-permute-done.refs_1_
  12.2 0.1 collective-permute-start.4
  12.4 0.6 %collective-permute-start.11 = (bf16[2,96,256]{2,1,0:T(8,128)(2,1)S(1)}, bf16[2,96,256]{2,1,0:T(8,128)(2,1)S(1)}, u32[]{:S(2)}, u32[]{:S(2)}) collective-permute-start(bf16[2,96,256]{2,1,0:T(8,128)(2,1)S(1)} %stack.5.refs_0_), channel_id=1, source_target_pairs={{0,8},{4,12},{8,0},{12,4},{16,24},{20,28},{24,16},{28,20},{1,9},{5... | collective-permute-start | bytes 294920 | tf_op jit(solution)/shard_map/ppermute | solution.py:200
  12.9 0.3 %collective-permute-start.10 = (bf16[2,96,256]{2,1,0:T(8,128)(2,1)S(1)}, bf16[2,96,256]{2,1,0:T(8,128)(2,1)S(1)}, u32[]{:S(2)}, u32[]{:S(2)}) collective-permute-start(bf16[2,96,256]{2,1,0:T(8,128)(2,1)S(1)} %stack.5.refs_0_), channel_id=1, source_target_pairs={{0,16},{4,20},{8,24},{12,28},{16,0},{20,4},{24,8},{28,12},{1,17},{... | collective-permute-start | bytes 294920 | tf_op jit(solution)/shard_map/ppermute | solution.py:200
  13.3 3.1 %collective-permute-start.3 = (bf16[4,96,256]{2,1,0:T(8,128)(2,1)S(1)}, bf16[4,96,256]{2,1,0:T(8,128)(2,1)S(1)}, u32[]{:S(2)}, u32[]{:S(2)}) collective-permute-start(bf16[4,96,256]{2,1,0:T(8,128)(2,1)S(1)} %stack.4.refs_1_), channel_id=1, source_target_pairs={{0,4},{4,0},{8,12},{12,8},{16,20},{20,16},{24,28},{28,24},{1,5},{5... | collective-permute-start | bytes 589832 | tf_op jit(solution)/shard_map/ppermute | solution.py:200
  16.3 0.0 collective-permute-done.8.refs_1_
  16.4 1.5 %collective-permute-start.9 = (bf16[4,96,256]{2,1,0:T(8,128)(2,1)S(1)}, bf16[4,96,256]{2,1,0:T(8,128)(2,1)S(1)}, u32[]{:S(2)}, u32[]{:S(2)}) collective-permute-start(bf16[4,96,256]{2,1,0:T(8,128)(2,1)S(1)} %stack.6.refs_2_), channel_id=1, source_target_pairs={{0,4},{4,0},{8,12},{12,8},{16,20},{20,16},{24,28},{28,24},{1,5},{5... | collective-permute-start | bytes 589832 | tf_op jit(solution)/shard_map/ppermute | solution.py:200
  17.8 0.0 collective-permute-done.4.refs_3_
  17.8 2.9 %collective-permute-start.5 = (bf16[4,96,256]{2,1,0:T(8,128)(2,1)S(1)}, bf16[4,96,256]{2,1,0:T(8,128)(2,1)S(1)}, u32[]{:S(2)}, u32[]{:S(2)}) collective-permute-start(bf16[4,96,256]{2,1,0:T(8,128)(2,1)S(1)} %collective-permute-done.4.refs_3_), channel_id=1, source_target_pairs={{0,4},{4,0},{8,12},{12,8},{16,20},{20,16},{24,28},{28,24},{1,5},{5... | collective-permute-start | bytes 589832 | tf_op jit(solution)/shard_map/ppermute | solution.py:200
  20.7 0.0 collective-permute-done.11.refs_1_
  20.7 0.0 collective-permute-done.10.refs_0_
  20.8 0.3 %collective-permute-start.12 = (bf16[4,96,256]{2,1,0:T(8,128)(2,1)S(1)}, bf16[4,96,256]{2,1,0:T(8,128)(2,1)S(1)}, u32[]{:S(2)}, u32[]{:S(2)}) collective-permute-start(bf16[4,96,256]{2,1,0:T(8,128)(2,1)S(1)} %stack.7.refs_4_), channel_id=1, source_target_pairs={{0,4},{4,0},{8,12},{12,8},{16,20},{20,16},{24,28},{28,24},{1,5},{5... | collective-permute-start | bytes 589832 | tf_op jit(solution)/shard_map/ppermute | solution.py:200
  21.0 0.0 collective-permute-done.3.refs_2_
  21.0 0.8 %collective-permute-done.5.refs_4_ = bf16[4,96,256]{2,1,0:T(8,128)(2,1)S(1)} collective-permute-done((bf16[4,96,256]{2,1,0:T(8,128)(2,1)S(1)}, bf16[4,96,256]{2,1,0:T(8,128)(2,1)S(1)}, u32[]{:S(2)}, u32[]{:S(2)}) %collective-permute-start.5) | collective-permute-done | bytes 196640 | tf_op jit(solution)/shard_map/ppermute | solution.py:200
  21.8 1.7 %correlate.1.refs_1_ = f32[2,4,8,128,128]{4,3,2,1,0:T(8,128)S(1)} custom-call(s32[1,5]{1,0:T(1,128)S(1)} %add_bitcast_fusion.refs_4_.refs_0_, bf16[4,96,256]{2,1,0:T(8,128)(2,1)S(1)} %stack.4.refs_1_, bf16[4,96,256]{2,1,0:T(8,128)(2,1)S(1)} %collective-permute-done.3.refs_2_, bf16[4,96,256]{2,1,0:T(8,128)(2,1)S(1)} %collective-permute-done.4.refs_3_, ...), custom_call_target="tpu_custom_call" | custom-call | tf_op jit(solution)/shard_map/correlate/pallas_call | solution.py:182
  23.5 0.0 collective-permute-done.9.refs_3_
  23.5 0.0 collective-permute-done.12.refs_5_
  23.5 2.7 %correlate_add.1 = f32[2,4,8,128,128]{4,3,2,1,0:T(8,128)} custom-call(s32[1,5]{1,0:T(1,128)S(1)} %add_bitcast_fusion.refs_4_.refs_0_, f32[2,4,8,128,128]{4,3,2,1,0:T(8,128)S(1)} %correlate.1.refs_1_, bf16[4,96,256]{2,1,0:T(8,128)(2,1)S(1)} %stack.6.refs_2_, bf16[4,96,256]{2,1,0:T(8,128)(2,1)S(1)} %collective-permute-done.9.refs_3_, ...), custom_call_target="tpu_custom_call" | custom-call | tf_op jit(solution)/shard_map/correlate_add/pallas_call | solution.py:182
  (4 shorter events, 0.1 us)
Async XLA Ops:
  0.0 8.2 %copy-start = (s32[8,2]{0,1:T(2,128)S(1)}, s32[8,2]{0,1:T(2,128)}, u32[]{:S(2)}) copy-start(s32[8,2]{0,1:T(2,128)} %param.5) | copy-start | bytes 196
  1.3 7.1 %collective-permute-start.7 = (bf16[1,96,256]{2,1,0:T(8,128)(2,1)S(1)}, bf16[1,96,256]{2,1,0:T(8,128)(2,1)S(1)}, u32[]{:S(2)}, u32[]{:S(2)}) collective-permute-start(bf16[1,96,256]{2,1,0:T(8,128)(2,1)S(1)} %bitcast.6), channel_id=1, source_target_pairs={{0,3},{1,2},{2,1},{3,0},{4,7},{5,6},{6,5},{7,4},{8,11},{9,10},{10,... | collective-permute-start | bytes 147464 | tf_op jit(solution)/shard_map/ppermute | solution.py:200
  5.5 4.4 %collective-permute-start.6 = (bf16[1,96,256]{2,1,0:T(8,128)(2,1)S(1)}, bf16[1,96,256]{2,1,0:T(8,128)(2,1)S(1)}, u32[]{:S(2)}, u32[]{:S(2)}) collective-permute-start(bf16[1,96,256]{2,1,0:T(8,128)(2,1)S(1)} %bitcast.7), channel_id=1, source_target_pairs={{0,2},{1,3},{2,0},{3,1},{4,6},{5,7},{6,4},{7,5},{8,10},{9,11},{10,... | collective-permute-start | bytes 147464 | tf_op jit(solution)/shard_map/ppermute | solution.py:200
  5.5 6.7 %collective-permute-start.2 = (bf16[1,96,256]{2,1,0:T(8,128)(2,1)S(1)}, bf16[1,96,256]{2,1,0:T(8,128)(2,1)S(1)}, u32[]{:S(2)}, u32[]{:S(2)}) collective-permute-start(bf16[1,96,256]{2,1,0:T(8,128)(2,1)S(1)} %bitcast.8), channel_id=1, source_target_pairs={{0,8},{4,12},{8,0},{12,4},{16,24},{20,28},{24,16},{28,20},{1,9},{5... | collective-permute-start | bytes 147464 | tf_op jit(solution)/shard_map/ppermute | solution.py:200
  6.7 5.5 %collective-permute-start.1 = (bf16[1,96,256]{2,1,0:T(8,128)(2,1)S(1)}, bf16[1,96,256]{2,1,0:T(8,128)(2,1)S(1)}, u32[]{:S(2)}, u32[]{:S(2)}) collective-permute-start(bf16[1,96,256]{2,1,0:T(8,128)(2,1)S(1)} %bitcast.9), channel_id=1, source_target_pairs={{0,16},{4,20},{8,24},{12,28},{16,0},{20,4},{24,8},{28,12},{1,17},{... | collective-permute-start | bytes 147464 | tf_op jit(solution)/shard_map/ppermute | solution.py:200
  8.0 4.2 %collective-permute-start = (bf16[1,96,256]{2,1,0:T(8,128)(2,1)S(1)}, bf16[1,96,256]{2,1,0:T(8,128)(2,1)S(1)}, u32[]{:S(2)}, u32[]{:S(2)}) collective-permute-start(bf16[1,96,256]{2,1,0:T(8,128)(2,1)S(1)} %bitcast.10), channel_id=1, source_target_pairs={{0,24},{4,28},{8,16},{12,20},{16,8},{20,12},{24,0},{28,4},{1,25},{... | collective-permute-start | bytes 147464 | tf_op jit(solution)/shard_map/ppermute | solution.py:200
  9.9 6.4 %collective-permute-start.8 = (bf16[2,96,256]{2,1,0:T(8,128)(2,1)S(1)}, bf16[2,96,256]{2,1,0:T(8,128)(2,1)S(1)}, u32[]{:S(2)}, u32[]{:S(2)}) collective-permute-start(bf16[2,96,256]{2,1,0:T(8,128)(2,1)S(1)} %stack.5.refs_0_), channel_id=1, source_target_pairs={{0,24},{4,28},{8,16},{12,20},{16,8},{20,12},{24,0},{28,4},{1,25},{... | collective-permute-start | bytes 294920 | tf_op jit(solution)/shard_map/ppermute | solution.py:200
  12.2 5.6 %collective-permute-start.4 = (bf16[4,96,256]{2,1,0:T(8,128)(2,1)S(1)}, bf16[4,96,256]{2,1,0:T(8,128)(2,1)S(1)}, u32[]{:S(2)}, u32[]{:S(2)}) collective-permute-start(bf16[4,96,256]{2,1,0:T(8,128)(2,1)S(1)} %stack.4.refs_1_), channel_id=1, source_target_pairs={{0,1},{1,0},{2,3},{3,2},{4,5},{5,4},{6,7},{7,6},{8,9},{9,8},{10,11... | collective-permute-start | bytes 589832 | tf_op jit(solution)/shard_map/ppermute | solution.py:200
  12.4 8.4 %collective-permute-start.11 = (bf16[2,96,256]{2,1,0:T(8,128)(2,1)S(1)}, bf16[2,96,256]{2,1,0:T(8,128)(2,1)S(1)}, u32[]{:S(2)}, u32[]{:S(2)}) collective-permute-start(bf16[2,96,256]{2,1,0:T(8,128)(2,1)S(1)} %stack.5.refs_0_), channel_id=1, source_target_pairs={{0,8},{4,12},{8,0},{12,4},{16,24},{20,28},{24,16},{28,20},{1,9},{5... | collective-permute-start | bytes 294920 | tf_op jit(solution)/shard_map/ppermute | solution.py:200
  12.9 7.8 %collective-permute-start.10 = (bf16[2,96,256]{2,1,0:T(8,128)(2,1)S(1)}, bf16[2,96,256]{2,1,0:T(8,128)(2,1)S(1)}, u32[]{:S(2)}, u32[]{:S(2)}) collective-permute-start(bf16[2,96,256]{2,1,0:T(8,128)(2,1)S(1)} %stack.5.refs_0_), channel_id=1, source_target_pairs={{0,16},{4,20},{8,24},{12,28},{16,0},{20,4},{24,8},{28,12},{1,17},{... | collective-permute-start | bytes 294920 | tf_op jit(solution)/shard_map/ppermute | solution.py:200
  13.3 7.8 %collective-permute-start.3 = (bf16[4,96,256]{2,1,0:T(8,128)(2,1)S(1)}, bf16[4,96,256]{2,1,0:T(8,128)(2,1)S(1)}, u32[]{:S(2)}, u32[]{:S(2)}) collective-permute-start(bf16[4,96,256]{2,1,0:T(8,128)(2,1)S(1)} %stack.4.refs_1_), channel_id=1, source_target_pairs={{0,4},{4,0},{8,12},{12,8},{16,20},{20,16},{24,28},{28,24},{1,5},{5... | collective-permute-start | bytes 589832 | tf_op jit(solution)/shard_map/ppermute | solution.py:200
  16.4 7.1 %collective-permute-start.9 = (bf16[4,96,256]{2,1,0:T(8,128)(2,1)S(1)}, bf16[4,96,256]{2,1,0:T(8,128)(2,1)S(1)}, u32[]{:S(2)}, u32[]{:S(2)}) collective-permute-start(bf16[4,96,256]{2,1,0:T(8,128)(2,1)S(1)} %stack.6.refs_2_), channel_id=1, source_target_pairs={{0,4},{4,0},{8,12},{12,8},{16,20},{20,16},{24,28},{28,24},{1,5},{5... | collective-permute-start | bytes 589832 | tf_op jit(solution)/shard_map/ppermute | solution.py:200
  17.8 4.0 %collective-permute-start.5 = (bf16[4,96,256]{2,1,0:T(8,128)(2,1)S(1)}, bf16[4,96,256]{2,1,0:T(8,128)(2,1)S(1)}, u32[]{:S(2)}, u32[]{:S(2)}) collective-permute-start(bf16[4,96,256]{2,1,0:T(8,128)(2,1)S(1)} %collective-permute-done.4.refs_3_), channel_id=1, source_target_pairs={{0,4},{4,0},{8,12},{12,8},{16,20},{20,16},{24,28},{28,24},{1,5},{5... | collective-permute-start | bytes 589832 | tf_op jit(solution)/shard_map/ppermute | solution.py:200
  20.8 2.7 %collective-permute-start.12 = (bf16[4,96,256]{2,1,0:T(8,128)(2,1)S(1)}, bf16[4,96,256]{2,1,0:T(8,128)(2,1)S(1)}, u32[]{:S(2)}, u32[]{:S(2)}) collective-permute-start(bf16[4,96,256]{2,1,0:T(8,128)(2,1)S(1)} %stack.7.refs_4_), channel_id=1, source_target_pairs={{0,4},{4,0},{8,12},{12,8},{16,20},{20,16},{24,28},{28,24},{1,5},{5... | collective-permute-start | bytes 589832 | tf_op jit(solution)/shard_map/ppermute | solution.py:200

commit v18 on v16

--- a/solution.py
+++ b/solution.py
@@ -227,17 +227,16 @@
     return stack(blocks[:groups // 2], after=(where,)), stack(blocks[groups // 2:], flops=10**9)
 
 
-def between_chips(half, parts):
-    chips = lax.axis_size("chan") // CORES
-    places = [0, *range(chips - 1, 0, -1)]
+def between_chips(half, parts, places):
     blocks = [swap(half, "chan", CORES * k) if k else half for k in places]
-    each = chips // parts
-    return [(places[i:i + each], blocks[i:i + each]) for i in range(0, chips, each)]
-
-
-def between_cores(parts):
-    collected = [(places, stack(blocks)) for places, blocks in parts]
-    return [(places, own, swap(own, "chan", 1)) for places, own in collected]
+    each = len(places) // parts
+    return [(places[i:i + each], blocks[i:i + each]) for i in range(0, len(places), each)]
+
+
+def between_cores(part, after=(), flops=0):
+    places, blocks = part
+    own = stack(blocks, after, flops)
+    return places, own, swap(own, "chan", 1)
 
 
 def per_device(spectra, bad_channels, tile_list):
@@ -248,8 +247,12 @@
     pairs = lax.dynamic_slice_in_dim(tile_list, lax.axis_index("tm") * tiles, tiles, axis=0)
     where = jnp.concatenate([lax.axis_index("chan").reshape(1), pairs.reshape(-1)]).astype(jnp.int32).reshape(1, -1)
     near, far = halves(white, where)
-    near, far = between_cores(between_chips(near, 2)), between_cores(between_chips(far, 2))
+    chips = lax.axis_size("chan") // CORES
+    near = [between_cores(part) for part in between_chips(near, 2, range(chips))]
+    *first, last = between_chips(far, 2, [0, *range(chips - 1, 0, -1)])
     partial = correlate(near, groups // 2, where, range(tiles), hours)
+    far = [between_cores(part, flops=3 * 10**9) for part in first]
+    far.append(between_cores(last, (partial,)))
     out = correlate(far, groups // 2, where, range(tiles), hours, [partial])
     return out.reshape(tiles, LAGS, TILE, TILE)
 

time: 24.8 us -> 25.5 us (1.028)
  waiting for transfers between devices: 1.74 us -> 3.33 us
  starting transfers between devices: 16.7 us -> 15.7 us
    ppermute x13, waiting for transfers between devices: 1.74 us -> 3.33 us  [swap(): lax.ppermute(array, axis, [(i, i ^ k) for i in range(lax.axis_size(axis))])]
    ppermute x13, starting transfers between devices: 16.7 us -> 15.7 us  [swap(): lax.ppermute(array, axis, [(i, i ^ k) for i in range(lax.axis_size(axis))])]
  transfers between devices with their start and end apart: 13 -> 13, of which waited for: 1 -> 4; matrix products, arithmetic and copies ran while one was open for 1% -> 1% of each run, Pallas kernels for 7% -> 7%
where the time goes in v18:
time: 25.5 us; the launch traced here: 25.2 us
  starting transfers between devices  15.7 us (62%)
  Pallas kernels  5.74 us (23%)
  waiting for transfers between devices  3.33 us (13%)
  local copies, waits for them, and re-layouts  0.26 us (1%)
    ppermute x13, starting transfers between devices, swap(): lax.ppermute(array, axis, [(i, i ^ k) for i in range(lax.axis_size(axis))])  15.7 us
    pallas_call x2, Pallas kernels, correlate(): pl.pallas_call(lambda *refs: correlate_kernel(norm, picked, adds, places,...  4.38 us
    ppermute x13, waiting for transfers between devices, swap(): lax.ppermute(array, axis, [(i, i ^ k) for i in range(lax.axis_size(axis))])  3.33 us
    pallas_call x1, Pallas kernels, whiten(): pl.pallas_call(whiten_kernel, out_shape=jax.ShapeDtypeStruct((chans, bins...  1.29 us
  transfers between devices with their start and end apart: 13, of which 4 were waited for; matrix products, arithmetic and copies ran while one was open for 1% of the time, Pallas kernels for 7%

profile of v18, /device:TPU:1, one launch (start us, length us, event | category | flops | bytes accessed | tf_op | source)
XLA Modules:
  0.0 25.2 jit_solution(6801932419895887720)
XLA Ops:
  0.0 0.0 copy-start
  0.0 1.3 %whiten.1 = bf16[96,256]{1,0:T(8,128)(2,1)S(1)} custom-call(bf16[64,2,2,96]{3,2,1,0:T(2,128)(2,1)} %spectra_hbm.1, s32[1,96]{1,0:T(1,128)} %bitcast.10), custom_call_target="tpu_custom_call" | custom-call | tf_op jit(solution)/shard_map/whiten/pallas_call | solution.py:56
  1.3 2.2 %collective-permute-start.6 = (bf16[1,96,256]{2,1,0:T(8,128)(2,1)S(1)}, bf16[1,96,256]{2,1,0:T(8,128)(2,1)S(1)}, u32[]{:S(2)}, u32[]{:S(2)}) collective-permute-start(bf16[1,96,256]{2,1,0:T(8,128)(2,1)S(1)} %bitcast.6), channel_id=1, source_target_pairs={{0,1},{1,0},{2,3},{3,2},{4,5},{5,4},{6,7},{7,6},{8,9},{9,8},{10,11... | collective-permute-start | bytes 147464 | tf_op jit(solution)/shard_map/ppermute | solution.py:200
  3.5 2.2 %collective-permute-start.1 = (bf16[1,96,256]{2,1,0:T(8,128)(2,1)S(1)}, bf16[1,96,256]{2,1,0:T(8,128)(2,1)S(1)}, u32[]{:S(2)}, u32[]{:S(2)}) collective-permute-start(bf16[1,96,256]{2,1,0:T(8,128)(2,1)S(1)} %bitcast.7), channel_id=1, source_target_pairs={{0,3},{1,2},{2,1},{3,0},{4,7},{5,6},{6,5},{7,4},{8,11},{9,10},{10,... | collective-permute-start | bytes 147464 | tf_op jit(solution)/shard_map/ppermute | solution.py:200
  5.7 0.1 collective-permute-start
  5.8 0.0 copy-done
  5.8 0.1 constant_dynamic-slice_fusion
  5.9 0.1 copy.4
  6.0 0.1 reshape.16
  6.1 0.1 add_bitcast_fusion.refs_2_.refs_0_
  6.1 0.0 collective-permute-done.6.refs_1_
  6.2 2.2 %collective-permute-start.10 = (bf16[2,96,256]{2,1,0:T(8,128)(2,1)S(1)}, bf16[2,96,256]{2,1,0:T(8,128)(2,1)S(1)}, u32[]{:S(2)}, u32[]{:S(2)}) collective-permute-start(bf16[2,96,256]{2,1,0:T(8,128)(2,1)S(1)} %stack.8.refs_0_), channel_id=1, source_target_pairs={{0,24},{4,28},{8,16},{12,20},{16,8},{20,12},{24,0},{28,4},{1,25},{... | collective-permute-start | bytes 294920 | tf_op jit(solution)/shard_map/ppermute | solution.py:200
  8.4 0.2 collective-permute-start.9
  8.6 0.3 %collective-permute-start.7 = (bf16[2,96,256]{2,1,0:T(8,128)(2,1)S(1)}, bf16[2,96,256]{2,1,0:T(8,128)(2,1)S(1)}, u32[]{:S(2)}, u32[]{:S(2)}) collective-permute-start(bf16[2,96,256]{2,1,0:T(8,128)(2,1)S(1)} %stack.8.refs_0_), channel_id=1, source_target_pairs={{0,8},{4,12},{8,0},{12,4},{16,24},{20,28},{24,16},{28,20},{1,9},{5... | collective-permute-start | bytes 294920 | tf_op jit(solution)/shard_map/ppermute | solution.py:200
  8.9 0.0 collective-permute-done.1.refs_1_
  8.9 1.7 %collective-permute-done.refs_0_ = bf16[1,96,256]{2,1,0:T(8,128)(2,1)S(1)} collective-permute-done((bf16[1,96,256]{2,1,0:T(8,128)(2,1)S(1)}, bf16[1,96,256]{2,1,0:T(8,128)(2,1)S(1)}, u32[]{:S(2)}, u32[]{:S(2)}) %collective-permute-start) | collective-permute-done | bytes 49184 | tf_op jit(solution)/shard_map/ppermute | solution.py:200
  10.6 2.2 %collective-permute-start.2 = (bf16[2,96,256]{2,1,0:T(8,128)(2,1)S(1)}, bf16[2,96,256]{2,1,0:T(8,128)(2,1)S(1)}, u32[]{:S(2)}, u32[]{:S(2)}) collective-permute-start(bf16[2,96,256]{2,1,0:T(8,128)(2,1)S(1)} %stack.6.refs_0_), channel_id=1, source_target_pairs={{0,24},{4,28},{8,16},{12,20},{16,8},{20,12},{24,0},{28,4},{1,25},{... | collective-permute-start | bytes 294920 | tf_op jit(solution)/shard_map/ppermute | solution.py:200
  12.8 0.3 %collective-permute-start.5 = (bf16[2,96,256]{2,1,0:T(8,128)(2,1)S(1)}, bf16[2,96,256]{2,1,0:T(8,128)(2,1)S(1)}, u32[]{:S(2)}, u32[]{:S(2)}) collective-permute-start(bf16[2,96,256]{2,1,0:T(8,128)(2,1)S(1)} %stack.6.refs_0_), channel_id=1, source_target_pairs={{0,8},{4,12},{8,0},{12,4},{16,24},{20,28},{24,16},{28,20},{1,9},{5... | collective-permute-start | bytes 294920 | tf_op jit(solution)/shard_map/ppermute | solution.py:200
  13.1 0.1 collective-permute-done.7.refs_1_
  13.2 0.7 %collective-permute-start.4 = (bf16[2,96,256]{2,1,0:T(8,128)(2,1)S(1)}, bf16[2,96,256]{2,1,0:T(8,128)(2,1)S(1)}, u32[]{:S(2)}, u32[]{:S(2)}) collective-permute-start(bf16[2,96,256]{2,1,0:T(8,128)(2,1)S(1)} %stack.6.refs_0_), channel_id=1, source_target_pairs={{0,16},{4,20},{8,24},{12,28},{16,0},{20,4},{24,8},{28,12},{1,17},{... | collective-permute-start | bytes 294920 | tf_op jit(solution)/shard_map/ppermute | solution.py:200
  13.9 0.0 collective-permute-done.10.refs_1_
  13.9 3.8 %collective-permute-start.8 = (bf16[4,96,256]{2,1,0:T(8,128)(2,1)S(1)}, bf16[4,96,256]{2,1,0:T(8,128)(2,1)S(1)}, u32[]{:S(2)}, u32[]{:S(2)}) collective-permute-start(bf16[4,96,256]{2,1,0:T(8,128)(2,1)S(1)} %stack.9.refs_1_), channel_id=1, source_target_pairs={{0,4},{4,0},{8,12},{12,8},{16,20},{20,16},{24,28},{28,24},{1,5},{5... | collective-permute-start | bytes 589832 | tf_op jit(solution)/shard_map/ppermute | solution.py:200
  17.7 0.0 collective-permute-done.9.refs_0_
  17.7 0.1 collective-permute-start.11
  17.8 0.0 collective-permute-done.2.refs_1_
  17.8 1.1 %collective-permute-start.3 = (bf16[4,96,256]{2,1,0:T(8,128)(2,1)S(1)}, bf16[4,96,256]{2,1,0:T(8,128)(2,1)S(1)}, u32[]{:S(2)}, u32[]{:S(2)}) collective-permute-start(bf16[4,96,256]{2,1,0:T(8,128)(2,1)S(1)} %stack.7.refs_1_), channel_id=1, source_target_pairs={{0,4},{4,0},{8,12},{12,8},{16,20},{20,16},{24,28},{28,24},{1,5},{5... | collective-permute-start | bytes 589832 | tf_op jit(solution)/shard_map/ppermute | solution.py:200
  19.0 0.0 collective-permute-done.8.refs_2_
  19.0 0.3 %collective-permute-done.11.refs_4_ = bf16[4,96,256]{2,1,0:T(8,128)(2,1)S(1)} collective-permute-done((bf16[4,96,256]{2,1,0:T(8,128)(2,1)S(1)}, bf16[4,96,256]{2,1,0:T(8,128)(2,1)S(1)}, u32[]{:S(2)}, u32[]{:S(2)}) %collective-permute-start.11) | collective-permute-done | bytes 196640 | tf_op jit(solution)/shard_map/ppermute | solution.py:200
  19.2 1.7 %correlate.1.refs_2_.refs_5_ = f32[2,4,8,128,128]{4,3,2,1,0:T(8,128)S(1)} custom-call(s32[1,5]{1,0:T(1,128)S(1)} %add_bitcast_fusion.refs_2_.refs_0_, bf16[4,96,256]{2,1,0:T(8,128)(2,1)S(1)} %stack.9.refs_1_, bf16[4,96,256]{2,1,0:T(8,128)(2,1)S(1)} %collective-permute-done.8.refs_2_, bf16[4,96,256]{2,1,0:T(8,128)(2,1)S(1)} %stack.10.refs_3_, ...), custom_call_target="tpu_custom_call" | custom-call | tf_op jit(solution)/shard_map/correlate/pallas_call | solution.py:182
  20.9 0.0 collective-permute-done.5.refs_1_
  20.9 0.0 collective-permute-done.4.refs_0_
  20.9 0.3 %collective-permute-start.12 = (bf16[4,96,256]{2,1,0:T(8,128)(2,1)S(1)}, bf16[4,96,256]{2,1,0:T(8,128)(2,1)S(1)}, u32[]{:S(2)}, u32[]{:S(2)}) collective-permute-start(bf16[4,96,256]{2,1,0:T(8,128)(2,1)S(1)} %stack.11.refs_3_), channel_id=1, source_target_pairs={{0,4},{4,0},{8,12},{12,8},{16,20},{20,16},{24,28},{28,24},{1,5},{5... | collective-permute-start | bytes 589832 | tf_op jit(solution)/shard_map/ppermute | solution.py:200
  21.2 0.0 collective-permute-done.3.refs_2_
  21.2 1.2 %collective-permute-done.12.refs_4_ = bf16[4,96,256]{2,1,0:T(8,128)(2,1)S(1)} collective-permute-done((bf16[4,96,256]{2,1,0:T(8,128)(2,1)S(1)}, bf16[4,96,256]{2,1,0:T(8,128)(2,1)S(1)}, u32[]{:S(2)}, u32[]{:S(2)}) %collective-permute-start.12) | collective-permute-done | bytes 196640 | tf_op jit(solution)/shard_map/ppermute | solution.py:200
  22.4 2.7 %correlate_add.1 = f32[2,4,8,128,128]{4,3,2,1,0:T(8,128)} custom-call(s32[1,5]{1,0:T(1,128)S(1)} %add_bitcast_fusion.refs_2_.refs_0_, bf16[4,96,256]{2,1,0:T(8,128)(2,1)S(1)} %stack.7.refs_1_, bf16[4,96,256]{2,1,0:T(8,128)(2,1)S(1)} %collective-permute-done.3.refs_2_, bf16[4,96,256]{2,1,0:T(8,128)(2,1)S(1)} %stack.11.refs_3_, ...), custom_call_target="tpu_custom_call" | custom-call | tf_op jit(solution)/shard_map/correlate_add/pallas_call | solution.py:182
  (6 shorter events, 0.1 us)
Async XLA Ops:
  0.0 5.8 %copy-start = (s32[8,2]{0,1:T(2,128)S(1)}, s32[8,2]{0,1:T(2,128)}, u32[]{:S(2)}) copy-start(s32[8,2]{0,1:T(2,128)} %param.5) | copy-start | bytes 196
  1.3 4.8 %collective-permute-start.6 = (bf16[1,96,256]{2,1,0:T(8,128)(2,1)S(1)}, bf16[1,96,256]{2,1,0:T(8,128)(2,1)S(1)}, u32[]{:S(2)}, u32[]{:S(2)}) collective-permute-start(bf16[1,96,256]{2,1,0:T(8,128)(2,1)S(1)} %bitcast.6), channel_id=1, source_target_pairs={{0,1},{1,0},{2,3},{3,2},{4,5},{5,4},{6,7},{7,6},{8,9},{9,8},{10,11... | collective-permute-start | bytes 147464 | tf_op jit(solution)/shard_map/ppermute | solution.py:200
  3.5 5.4 %collective-permute-start.1 = (bf16[1,96,256]{2,1,0:T(8,128)(2,1)S(1)}, bf16[1,96,256]{2,1,0:T(8,128)(2,1)S(1)}, u32[]{:S(2)}, u32[]{:S(2)}) collective-permute-start(bf16[1,96,256]{2,1,0:T(8,128)(2,1)S(1)} %bitcast.7), channel_id=1, source_target_pairs={{0,3},{1,2},{2,1},{3,0},{4,7},{5,6},{6,5},{7,4},{8,11},{9,10},{10,... | collective-permute-start | bytes 147464 | tf_op jit(solution)/shard_map/ppermute | solution.py:200
  5.7 4.9 %collective-permute-start = (bf16[1,96,256]{2,1,0:T(8,128)(2,1)S(1)}, bf16[1,96,256]{2,1,0:T(8,128)(2,1)S(1)}, u32[]{:S(2)}, u32[]{:S(2)}) collective-permute-start(bf16[1,96,256]{2,1,0:T(8,128)(2,1)S(1)} %bitcast.8), channel_id=1, source_target_pairs={{0,2},{1,3},{2,0},{3,1},{4,6},{5,7},{6,4},{7,5},{8,10},{9,11},{10,... | collective-permute-start | bytes 147464 | tf_op jit(solution)/shard_map/ppermute | solution.py:200
  6.2 7.8 %collective-permute-start.10 = (bf16[2,96,256]{2,1,0:T(8,128)(2,1)S(1)}, bf16[2,96,256]{2,1,0:T(8,128)(2,1)S(1)}, u32[]{:S(2)}, u32[]{:S(2)}) collective-permute-start(bf16[2,96,256]{2,1,0:T(8,128)(2,1)S(1)} %stack.8.refs_0_), channel_id=1, source_target_pairs={{0,24},{4,28},{8,16},{12,20},{16,8},{20,12},{24,0},{28,4},{1,25},{... | collective-permute-start | bytes 294920 | tf_op jit(solution)/shard_map/ppermute | solution.py:200
  8.4 9.3 %collective-permute-start.9 = (bf16[2,96,256]{2,1,0:T(8,128)(2,1)S(1)}, bf16[2,96,256]{2,1,0:T(8,128)(2,1)S(1)}, u32[]{:S(2)}, u32[]{:S(2)}) collective-permute-start(bf16[2,96,256]{2,1,0:T(8,128)(2,1)S(1)} %stack.8.refs_0_), channel_id=1, source_target_pairs={{0,16},{4,20},{8,24},{12,28},{16,0},{20,4},{24,8},{28,12},{1,17},{... | collective-permute-start | bytes 294920 | tf_op jit(solution)/shard_map/ppermute | solution.py:200
  8.6 4.6 %collective-permute-start.7 = (bf16[2,96,256]{2,1,0:T(8,128)(2,1)S(1)}, bf16[2,96,256]{2,1,0:T(8,128)(2,1)S(1)}, u32[]{:S(2)}, u32[]{:S(2)}) collective-permute-start(bf16[2,96,256]{2,1,0:T(8,128)(2,1)S(1)} %stack.8.refs_0_), channel_id=1, source_target_pairs={{0,8},{4,12},{8,0},{12,4},{16,24},{20,28},{24,16},{28,20},{1,9},{5... | collective-permute-start | bytes 294920 | tf_op jit(solution)/shard_map/ppermute | solution.py:200
  10.6 7.2 %collective-permute-start.2 = (bf16[2,96,256]{2,1,0:T(8,128)(2,1)S(1)}, bf16[2,96,256]{2,1,0:T(8,128)(2,1)S(1)}, u32[]{:S(2)}, u32[]{:S(2)}) collective-permute-start(bf16[2,96,256]{2,1,0:T(8,128)(2,1)S(1)} %stack.6.refs_0_), channel_id=1, source_target_pairs={{0,24},{4,28},{8,16},{12,20},{16,8},{20,12},{24,0},{28,4},{1,25},{... | collective-permute-start | bytes 294920 | tf_op jit(solution)/shard_map/ppermute | solution.py:200
  12.8 8.1 %collective-permute-start.5 = (bf16[2,96,256]{2,1,0:T(8,128)(2,1)S(1)}, bf16[2,96,256]{2,1,0:T(8,128)(2,1)S(1)}, u32[]{:S(2)}, u32[]{:S(2)}) collective-permute-start(bf16[2,96,256]{2,1,0:T(8,128)(2,1)S(1)} %stack.6.refs_0_), channel_id=1, source_target_pairs={{0,8},{4,12},{8,0},{12,4},{16,24},{20,28},{24,16},{28,20},{1,9},{5... | collective-permute-start | bytes 294920 | tf_op jit(solution)/shard_map/ppermute | solution.py:200
  13.2 7.7 %collective-permute-start.4 = (bf16[2,96,256]{2,1,0:T(8,128)(2,1)S(1)}, bf16[2,96,256]{2,1,0:T(8,128)(2,1)S(1)}, u32[]{:S(2)}, u32[]{:S(2)}) collective-permute-start(bf16[2,96,256]{2,1,0:T(8,128)(2,1)S(1)} %stack.6.refs_0_), channel_id=1, source_target_pairs={{0,16},{4,20},{8,24},{12,28},{16,0},{20,4},{24,8},{28,12},{1,17},{... | collective-permute-start | bytes 294920 | tf_op jit(solution)/shard_map/ppermute | solution.py:200
  13.9 5.0 %collective-permute-start.8 = (bf16[4,96,256]{2,1,0:T(8,128)(2,1)S(1)}, bf16[4,96,256]{2,1,0:T(8,128)(2,1)S(1)}, u32[]{:S(2)}, u32[]{:S(2)}) collective-permute-start(bf16[4,96,256]{2,1,0:T(8,128)(2,1)S(1)} %stack.9.refs_1_), channel_id=1, source_target_pairs={{0,4},{4,0},{8,12},{12,8},{16,20},{20,16},{24,28},{28,24},{1,5},{5... | collective-permute-start | bytes 589832 | tf_op jit(solution)/shard_map/ppermute | solution.py:200
  17.7 1.5 %collective-permute-start.11 = (bf16[4,96,256]{2,1,0:T(8,128)(2,1)S(1)}, bf16[4,96,256]{2,1,0:T(8,128)(2,1)S(1)}, u32[]{:S(2)}, u32[]{:S(2)}) collective-permute-start(bf16[4,96,256]{2,1,0:T(8,128)(2,1)S(1)} %stack.10.refs_3_), channel_id=1, source_target_pairs={{0,4},{4,0},{8,12},{12,8},{16,20},{20,16},{24,28},{28,24},{1,5},{5... | collective-permute-start | bytes 589832 | tf_op jit(solution)/shard_map/ppermute | solution.py:200
  17.8 3.4 %collective-permute-start.3 = (bf16[4,96,256]{2,1,0:T(8,128)(2,1)S(1)}, bf16[4,96,256]{2,1,0:T(8,128)(2,1)S(1)}, u32[]{:S(2)}, u32[]{:S(2)}) collective-permute-start(bf16[4,96,256]{2,1,0:T(8,128)(2,1)S(1)} %stack.7.refs_1_), channel_id=1, source_target_pairs={{0,4},{4,0},{8,12},{12,8},{16,20},{20,16},{24,28},{28,24},{1,5},{5... | collective-permute-start | bytes 589832 | tf_op jit(solution)/shard_map/ppermute | solution.py:200
  20.9 1.5 %collective-permute-start.12 = (bf16[4,96,256]{2,1,0:T(8,128)(2,1)S(1)}, bf16[4,96,256]{2,1,0:T(8,128)(2,1)S(1)}, u32[]{:S(2)}, u32[]{:S(2)}) collective-permute-start(bf16[4,96,256]{2,1,0:T(8,128)(2,1)S(1)} %stack.11.refs_3_), channel_id=1, source_target_pairs={{0,4},{4,0},{8,12},{12,8},{16,20},{20,16},{24,28},{28,24},{1,5},{5... | collective-permute-start | bytes 589832 | tf_op jit(solution)/shard_map/ppermute | solution.py:200

commit v19 on v16

--- a/solution.py
+++ b/solution.py
@@ -138,18 +138,18 @@
         for j, lag in enumerate(STEPS):
             fine = FINE.index(lag)
             turn_right(slot, right_block, j + 1)
-            for first in range(0, len(COARSE), 2):
-                if j == 0:
+            for first in range(len(COARSE)):
+                if j == 0 and first % 2 == 0:
                     turn_left(slot, left_block, LEFT_ORDER[first + 1])
                 total = lax.dot_general(
-                    left_turned[slot, first * TILE:(first + 2) * TILE, :],
+                    left_turned[slot, first * TILE:(first + 1) * TILE, :],
                     right_turned[slot, fine * TILE:(fine + 2) * TILE, :],
                     (((1,), (1,)), ((), ())),
                     preferred_element_type=jnp.float32,
                 )
-                for v, s in ((0, 0), (0, 1), (1, 0), (1, 1)):
-                    u = COARSE.index(LEFT_ORDER[first + v])
-                    value = total[v * TILE:(v + 1) * TILE, s * TILE:(s + 1) * TILE]
+                u = COARSE.index(LEFT_ORDER[first])
+                for s in range(2):
+                    value = total[:, s * TILE:(s + 1) * TILE]
                     if adds:
                         each = len(picked) // adds
                         more[0][i, u, fine + s] = partials[i // each][i % each, u, fine + s] + value

time: 24.8 us -> 27.5 us (1.11)
  Pallas kernels: 5.74 us -> 8.44 us
    pallas_call x2, Pallas kernels: 4.39 us -> 7.08 us  [correlate(): pl.pallas_call(lambda *refs: correlate_kernel(norm, picked, adds, places,...]
  transfers between devices with their start and end apart: 13 -> 13, of which waited for: 1 -> 1; matrix products, arithmetic and copies ran while one was open for 1% -> 1% of each run, Pallas kernels for 7% -> 12%
where the time goes in v19:
time: 27.5 us; the launch traced here: 27.3 us
  starting transfers between devices  16.7 us (61%)
  Pallas kernels  8.44 us (31%)
  waiting for transfers between devices  1.74 us (6%)
    ppermute x13, starting transfers between devices, swap(): lax.ppermute(array, axis, [(i, i ^ k) for i in range(lax.axis_size(axis))])  16.7 us
    pallas_call x2, Pallas kernels, correlate(): pl.pallas_call(lambda *refs: correlate_kernel(norm, picked, adds, places,...  7.08 us
    ppermute x13, waiting for transfers between devices, swap(): lax.ppermute(array, axis, [(i, i ^ k) for i in range(lax.axis_size(axis))])  1.74 us
    pallas_call x1, Pallas kernels, whiten(): pl.pallas_call(whiten_kernel, out_shape=jax.ShapeDtypeStruct((chans, bins...  1.29 us
  transfers between devices with their start and end apart: 13, of which 1 were waited for; matrix products, arithmetic and copies ran while one was open for 1% of the time, Pallas kernels for 12%

profile of v19, /device:TPU:1, one launch (start us, length us, event | category | flops | bytes accessed | tf_op | source)
XLA Modules:
  0.0 27.3 jit_solution(6945318445668439990)
XLA Ops:
  0.0 0.0 copy-start
  0.0 1.3 %whiten.1 = bf16[96,256]{1,0:T(8,128)(2,1)S(1)} custom-call(bf16[64,2,2,96]{3,2,1,0:T(2,128)(2,1)} %spectra_hbm.1, s32[1,96]{1,0:T(1,128)} %bitcast.10), custom_call_target="tpu_custom_call" | custom-call | tf_op jit(solution)/shard_map/whiten/pallas_call | solution.py:56
  1.3 2.2 %collective-permute-start.7 = (bf16[1,96,256]{2,1,0:T(8,128)(2,1)S(1)}, bf16[1,96,256]{2,1,0:T(8,128)(2,1)S(1)}, u32[]{:S(2)}, u32[]{:S(2)}) collective-permute-start(bf16[1,96,256]{2,1,0:T(8,128)(2,1)S(1)} %bitcast.6), channel_id=1, source_target_pairs={{0,1},{1,0},{2,3},{3,2},{4,5},{5,4},{6,7},{7,6},{8,9},{9,8},{10,11... | collective-permute-start | bytes 147464 | tf_op jit(solution)/shard_map/ppermute | solution.py:200
  3.5 2.2 %collective-permute-start.1 = (bf16[1,96,256]{2,1,0:T(8,128)(2,1)S(1)}, bf16[1,96,256]{2,1,0:T(8,128)(2,1)S(1)}, u32[]{:S(2)}, u32[]{:S(2)}) collective-permute-start(bf16[1,96,256]{2,1,0:T(8,128)(2,1)S(1)} %bitcast.7), channel_id=1, source_target_pairs={{0,3},{1,2},{2,1},{3,0},{4,7},{5,6},{6,5},{7,4},{8,11},{9,10},{10,... | collective-permute-start | bytes 147464 | tf_op jit(solution)/shard_map/ppermute | solution.py:200
  5.7 0.1 collective-permute-start
  5.8 0.0 copy-done
  5.8 0.1 constant_dynamic-slice_fusion
  5.9 0.1 copy.4
  6.0 0.1 reshape.16
  6.1 0.1 add_bitcast_fusion.refs_2_.refs_0_
  6.1 0.0 collective-permute-done.7.refs_1_
  6.2 2.2 %collective-permute-start.8 = (bf16[2,96,256]{2,1,0:T(8,128)(2,1)S(1)}, bf16[2,96,256]{2,1,0:T(8,128)(2,1)S(1)}, u32[]{:S(2)}, u32[]{:S(2)}) collective-permute-start(bf16[2,96,256]{2,1,0:T(8,128)(2,1)S(1)} %stack.9.refs_0_), channel_id=1, source_target_pairs={{0,24},{4,28},{8,16},{12,20},{16,8},{20,12},{24,0},{28,4},{1,25},{... | collective-permute-start | bytes 294920 | tf_op jit(solution)/shard_map/ppermute | solution.py:200
  8.4 0.3 collective-permute-start.11
  8.6 0.2 collective-permute-start.10
  8.9 0.0 collective-permute-done.1.refs_1_
  8.9 1.7 %collective-permute-done.refs_0_ = bf16[1,96,256]{2,1,0:T(8,128)(2,1)S(1)} collective-permute-done((bf16[1,96,256]{2,1,0:T(8,128)(2,1)S(1)}, bf16[1,96,256]{2,1,0:T(8,128)(2,1)S(1)}, u32[]{:S(2)}, u32[]{:S(2)}) %collective-permute-start) | collective-permute-done | bytes 49184 | tf_op jit(solution)/shard_map/ppermute | solution.py:200
  10.6 2.2 %collective-permute-start.2 = (bf16[2,96,256]{2,1,0:T(8,128)(2,1)S(1)}, bf16[2,96,256]{2,1,0:T(8,128)(2,1)S(1)}, u32[]{:S(2)}, u32[]{:S(2)}) collective-permute-start(bf16[2,96,256]{2,1,0:T(8,128)(2,1)S(1)} %stack.6.refs_0_), channel_id=1, source_target_pairs={{0,24},{4,28},{8,16},{12,20},{16,8},{20,12},{24,0},{28,4},{1,25},{... | collective-permute-start | bytes 294920 | tf_op jit(solution)/shard_map/ppermute | solution.py:200
  12.8 0.3 collective-permute-start.5
  13.1 0.0 collective-permute-done.8.refs_1_
  13.1 0.2 collective-permute-start.4
  13.3 0.0 collective-permute-done.11.refs_1_
  13.3 2.8 %collective-permute-start.9 = (bf16[4,96,256]{2,1,0:T(8,128)(2,1)S(1)}, bf16[4,96,256]{2,1,0:T(8,128)(2,1)S(1)}, u32[]{:S(2)}, u32[]{:S(2)}) collective-permute-start(bf16[4,96,256]{2,1,0:T(8,128)(2,1)S(1)} %stack.10.refs_1_), channel_id=1, source_target_pairs={{0,4},{4,0},{8,12},{12,8},{16,20},{20,16},{24,28},{28,24},{1,5},{5... | collective-permute-start | bytes 589832 | tf_op jit(solution)/shard_map/ppermute | solution.py:200
  16.1 0.0 collective-permute-done.10.refs_0_
  16.1 0.1 collective-permute-start.12
  16.2 0.0 collective-permute-done.2.refs_1_
  16.2 2.0 %collective-permute-start.3 = (bf16[4,96,256]{2,1,0:T(8,128)(2,1)S(1)}, bf16[4,96,256]{2,1,0:T(8,128)(2,1)S(1)}, u32[]{:S(2)}, u32[]{:S(2)}) collective-permute-start(bf16[4,96,256]{2,1,0:T(8,128)(2,1)S(1)} %stack.7.refs_1_), channel_id=1, source_target_pairs={{0,4},{4,0},{8,12},{12,8},{16,20},{20,16},{24,28},{28,24},{1,5},{5... | collective-permute-start | bytes 589832 | tf_op jit(solution)/shard_map/ppermute | solution.py:200
  18.2 0.0 collective-permute-done.5.refs_1_
  18.2 0.0 collective-permute-done.4.refs_0_
  18.2 2.0 %collective-permute-start.6 = (bf16[4,96,256]{2,1,0:T(8,128)(2,1)S(1)}, bf16[4,96,256]{2,1,0:T(8,128)(2,1)S(1)}, u32[]{:S(2)}, u32[]{:S(2)}) collective-permute-start(bf16[4,96,256]{2,1,0:T(8,128)(2,1)S(1)} %stack.8.refs_3_), channel_id=1, source_target_pairs={{0,4},{4,0},{8,12},{12,8},{16,20},{20,16},{24,28},{28,24},{1,5},{5... | collective-permute-start | bytes 589832 | tf_op jit(solution)/shard_map/ppermute | solution.py:200
  20.2 0.0 collective-permute-done.9.refs_2_
  20.2 0.0 collective-permute-done.12.refs_4_
  20.2 3.1 %correlate.1.refs_5_ = f32[2,4,8,128,128]{4,3,2,1,0:T(8,128)S(1)} custom-call(s32[1,5]{1,0:T(1,128)S(1)} %add_bitcast_fusion.refs_2_.refs_0_, bf16[4,96,256]{2,1,0:T(8,128)(2,1)S(1)} %stack.10.refs_1_, bf16[4,96,256]{2,1,0:T(8,128)(2,1)S(1)} %collective-permute-done.9.refs_2_, bf16[4,96,256]{2,1,0:T(8,128)(2,1)S(1)} %stack.11.refs_3_, ...), custom_call_target="tpu_custom_call" | custom-call | tf_op jit(solution)/shard_map/correlate/pallas_call | solution.py:182
  23.3 0.0 collective-permute-done.3.refs_2_
  23.3 0.0 collective-permute-done.6.refs_4_
  23.3 4.0 %correlate_add.1 = f32[2,4,8,128,128]{4,3,2,1,0:T(8,128)} custom-call(s32[1,5]{1,0:T(1,128)S(1)} %add_bitcast_fusion.refs_2_.refs_0_, bf16[4,96,256]{2,1,0:T(8,128)(2,1)S(1)} %stack.7.refs_1_, bf16[4,96,256]{2,1,0:T(8,128)(2,1)S(1)} %collective-permute-done.3.refs_2_, bf16[4,96,256]{2,1,0:T(8,128)(2,1)S(1)} %stack.8.refs_3_, ...), custom_call_target="tpu_custom_call" | custom-call | tf_op jit(solution)/shard_map/correlate_add/pallas_call | solution.py:182
  (6 shorter events, 0.1 us)
Async XLA Ops:
  0.0 5.8 %copy-start = (s32[8,2]{0,1:T(2,128)S(1)}, s32[8,2]{0,1:T(2,128)}, u32[]{:S(2)}) copy-start(s32[8,2]{0,1:T(2,128)} %param.5) | copy-start | bytes 196
  1.3 4.8 %collective-permute-start.7 = (bf16[1,96,256]{2,1,0:T(8,128)(2,1)S(1)}, bf16[1,96,256]{2,1,0:T(8,128)(2,1)S(1)}, u32[]{:S(2)}, u32[]{:S(2)}) collective-permute-start(bf16[1,96,256]{2,1,0:T(8,128)(2,1)S(1)} %bitcast.6), channel_id=1, source_target_pairs={{0,1},{1,0},{2,3},{3,2},{4,5},{5,4},{6,7},{7,6},{8,9},{9,8},{10,11... | collective-permute-start | bytes 147464 | tf_op jit(solution)/shard_map/ppermute | solution.py:200
  3.5 5.4 %collective-permute-start.1 = (bf16[1,96,256]{2,1,0:T(8,128)(2,1)S(1)}, bf16[1,96,256]{2,1,0:T(8,128)(2,1)S(1)}, u32[]{:S(2)}, u32[]{:S(2)}) collective-permute-start(bf16[1,96,256]{2,1,0:T(8,128)(2,1)S(1)} %bitcast.7), channel_id=1, source_target_pairs={{0,3},{1,2},{2,1},{3,0},{4,7},{5,6},{6,5},{7,4},{8,11},{9,10},{10,... | collective-permute-start | bytes 147464 | tf_op jit(solution)/shard_map/ppermute | solution.py:200
  5.7 4.9 %collective-permute-start = (bf16[1,96,256]{2,1,0:T(8,128)(2,1)S(1)}, bf16[1,96,256]{2,1,0:T(8,128)(2,1)S(1)}, u32[]{:S(2)}, u32[]{:S(2)}) collective-permute-start(bf16[1,96,256]{2,1,0:T(8,128)(2,1)S(1)} %bitcast.8), channel_id=1, source_target_pairs={{0,2},{1,3},{2,0},{3,1},{4,6},{5,7},{6,4},{7,5},{8,10},{9,11},{10,... | collective-permute-start | bytes 147464 | tf_op jit(solution)/shard_map/ppermute | solution.py:200
  6.2 6.9 %collective-permute-start.8 = (bf16[2,96,256]{2,1,0:T(8,128)(2,1)S(1)}, bf16[2,96,256]{2,1,0:T(8,128)(2,1)S(1)}, u32[]{:S(2)}, u32[]{:S(2)}) collective-permute-start(bf16[2,96,256]{2,1,0:T(8,128)(2,1)S(1)} %stack.9.refs_0_), channel_id=1, source_target_pairs={{0,24},{4,28},{8,16},{12,20},{16,8},{20,12},{24,0},{28,4},{1,25},{... | collective-permute-start | bytes 294920 | tf_op jit(solution)/shard_map/ppermute | solution.py:200
  8.4 4.9 %collective-permute-start.11 = (bf16[2,96,256]{2,1,0:T(8,128)(2,1)S(1)}, bf16[2,96,256]{2,1,0:T(8,128)(2,1)S(1)}, u32[]{:S(2)}, u32[]{:S(2)}) collective-permute-start(bf16[2,96,256]{2,1,0:T(8,128)(2,1)S(1)} %stack.9.refs_0_), channel_id=1, source_target_pairs={{0,8},{4,12},{8,0},{12,4},{16,24},{20,28},{24,16},{28,20},{1,9},{5... | collective-permute-start | bytes 294920 | tf_op jit(solution)/shard_map/ppermute | solution.py:200
  8.6 7.5 %collective-permute-start.10 = (bf16[2,96,256]{2,1,0:T(8,128)(2,1)S(1)}, bf16[2,96,256]{2,1,0:T(8,128)(2,1)S(1)}, u32[]{:S(2)}, u32[]{:S(2)}) collective-permute-start(bf16[2,96,256]{2,1,0:T(8,128)(2,1)S(1)} %stack.9.refs_0_), channel_id=1, source_target_pairs={{0,16},{4,20},{8,24},{12,28},{16,0},{20,4},{24,8},{28,12},{1,17},{... | collective-permute-start | bytes 294920 | tf_op jit(solution)/shard_map/ppermute | solution.py:200
  10.6 5.6 %collective-permute-start.2 = (bf16[2,96,256]{2,1,0:T(8,128)(2,1)S(1)}, bf16[2,96,256]{2,1,0:T(8,128)(2,1)S(1)}, u32[]{:S(2)}, u32[]{:S(2)}) collective-permute-start(bf16[2,96,256]{2,1,0:T(8,128)(2,1)S(1)} %stack.6.refs_0_), channel_id=1, source_target_pairs={{0,24},{4,28},{8,16},{12,20},{16,8},{20,12},{24,0},{28,4},{1,25},{... | collective-permute-start | bytes 294920 | tf_op jit(solution)/shard_map/ppermute | solution.py:200
  12.8 5.4 %collective-permute-start.5 = (bf16[2,96,256]{2,1,0:T(8,128)(2,1)S(1)}, bf16[2,96,256]{2,1,0:T(8,128)(2,1)S(1)}, u32[]{:S(2)}, u32[]{:S(2)}) collective-permute-start(bf16[2,96,256]{2,1,0:T(8,128)(2,1)S(1)} %stack.6.refs_0_), channel_id=1, source_target_pairs={{0,8},{4,12},{8,0},{12,4},{16,24},{20,28},{24,16},{28,20},{1,9},{5... | collective-permute-start | bytes 294920 | tf_op jit(solution)/shard_map/ppermute | solution.py:200
  13.1 5.1 %collective-permute-start.4 = (bf16[2,96,256]{2,1,0:T(8,128)(2,1)S(1)}, bf16[2,96,256]{2,1,0:T(8,128)(2,1)S(1)}, u32[]{:S(2)}, u32[]{:S(2)}) collective-permute-start(bf16[2,96,256]{2,1,0:T(8,128)(2,1)S(1)} %stack.6.refs_0_), channel_id=1, source_target_pairs={{0,16},{4,20},{8,24},{12,28},{16,0},{20,4},{24,8},{28,12},{1,17},{... | collective-permute-start | bytes 294920 | tf_op jit(solution)/shard_map/ppermute | solution.py:200
  13.3 6.9 %collective-permute-start.9 = (bf16[4,96,256]{2,1,0:T(8,128)(2,1)S(1)}, bf16[4,96,256]{2,1,0:T(8,128)(2,1)S(1)}, u32[]{:S(2)}, u32[]{:S(2)}) collective-permute-start(bf16[4,96,256]{2,1,0:T(8,128)(2,1)S(1)} %stack.10.refs_1_), channel_id=1, source_target_pairs={{0,4},{4,0},{8,12},{12,8},{16,20},{20,16},{24,28},{28,24},{1,5},{5... | collective-permute-start | bytes 589832 | tf_op jit(solution)/shard_map/ppermute | solution.py:200
  16.1 4.1 %collective-permute-start.12 = (bf16[4,96,256]{2,1,0:T(8,128)(2,1)S(1)}, bf16[4,96,256]{2,1,0:T(8,128)(2,1)S(1)}, u32[]{:S(2)}, u32[]{:S(2)}) collective-permute-start(bf16[4,96,256]{2,1,0:T(8,128)(2,1)S(1)} %stack.11.refs_3_), channel_id=1, source_target_pairs={{0,4},{4,0},{8,12},{12,8},{16,20},{20,16},{24,28},{28,24},{1,5},{5... | collective-permute-start | bytes 589832 | tf_op jit(solution)/shard_map/ppermute | solution.py:200
  16.2 7.1 %collective-permute-start.3 = (bf16[4,96,256]{2,1,0:T(8,128)(2,1)S(1)}, bf16[4,96,256]{2,1,0:T(8,128)(2,1)S(1)}, u32[]{:S(2)}, u32[]{:S(2)}) collective-permute-start(bf16[4,96,256]{2,1,0:T(8,128)(2,1)S(1)} %stack.7.refs_1_), channel_id=1, source_target_pairs={{0,4},{4,0},{8,12},{12,8},{16,20},{20,16},{24,28},{28,24},{1,5},{5... | collective-permute-start | bytes 589832 | tf_op jit(solution)/shard_map/ppermute | solution.py:200
  18.2 5.1 %collective-permute-start.6 = (bf16[4,96,256]{2,1,0:T(8,128)(2,1)S(1)}, bf16[4,96,256]{2,1,0:T(8,128)(2,1)S(1)}, u32[]{:S(2)}, u32[]{:S(2)}) collective-permute-start(bf16[4,96,256]{2,1,0:T(8,128)(2,1)S(1)} %stack.8.refs_3_), channel_id=1, source_target_pairs={{0,4},{4,0},{8,12},{12,8},{16,20},{20,16},{24,28},{28,24},{1,5},{5... | collective-permute-start | bytes 589832 | tf_op jit(solution)/shard_map/ppermute | solution.py:200

commit v20 on v16

--- a/solution.py
+++ b/solution.py
@@ -98,7 +98,12 @@
     bin_number = lax.broadcasted_iota(jnp.int32, (8, half), 1) // hours_dev + 1
     step = lax.broadcasted_iota(jnp.int32, (8, half), 0)
     cos, sin = cos_sin(jnp.where(step == 6, 12, step) * bin_number)
-    table = {k: (cos[i:i + 1], sin[i:i + 1]) for k, i in ((1, 1), (2, 2), (3, 3), (4, 4), (12, 6))}
+    table = {k: (cos[i:i + 1], sin[i:i + 1]) for k, i in ((4, 4), (12, 6))}
+    bin_number = lax.broadcasted_iota(jnp.int32, (half, 8), 0) // hours_dev + 1
+    cos, sin = cos_sin(lax.broadcasted_iota(jnp.int32, (half, 8), 1) * bin_number)
+    columns = {
+        k: tuple(jnp.broadcast_to(part[:, k:k + 1], (half, TILE)) for part in (cos, sin)) for k in range(1, len(STEPS) + 1)
+    }
 
     chan = where_ref[0, 0]
     for i, piece in enumerate(parts):
@@ -111,25 +116,27 @@
         whole = spectra[g, pl.ds(pl.multiple_of(block * TILE, TILE), TILE), :].astype(jnp.float32)
         return whole[:, :half], whole[:, half:]
 
-    def store(ref, slot, index, g, value):
-        rows_at = pl.ds(index * TILE, TILE)
-        ref[slot, rows_at, g * lanes:g * lanes + half] = value[0].astype(jnp.bfloat16)
-        ref[slot, rows_at, g * lanes + half:(g + 1) * lanes] = value[1].astype(jnp.bfloat16)
-
     def turn_left(slot, block, k):
-        for g in range(groups):
-            forward, backward = turn_by(*load(block, g), *(norm * part for part in table[k]), True)
-            store(left_turned, slot, LEFT_ORDER.index(k), g, forward)
-            store(left_turned, slot, LEFT_ORDER.index(-k), g, backward)
+        turns = [turn_by(*load(block, g), *(norm * part for part in table[k]), True) for g in range(groups)]
+        for g, turn in enumerate(turns):
+            for lag, value in zip((k, -k), turn):
+                rows_at = pl.ds(LEFT_ORDER.index(lag) * TILE, TILE)
+                for part in range(2):
+                    at = g * lanes + part * half
+                    left_turned[slot, rows_at, at:at + half] = value[part].astype(jnp.bfloat16)
 
     def turn_right(slot, block, k):
         for g in range(groups):
-            re, im = load(block, g)
+            at = [pl.ds(g * lanes + part * half, half) for part in range(2)]
+            plain = pl.ds(FINE.index(0) * TILE, TILE)
             if k == 1:
-                store(right_turned, slot, FINE.index(0), g, (re, im))
-            turns = turn_by(re, im, *table[k], k in FINE)
-            for lag, value in zip((-k, k), turns):
-                store(right_turned, slot, FINE.index(lag), g, value)
+                for part, value in enumerate(load(block, g)):
+                    right_turned[slot, at[part], plain] = value.T.astype(jnp.bfloat16)
+            re, im = (right_turned[slot, rows_at, plain].astype(jnp.float32) for rows_at in at)
+            for lag, value in zip((-k, k), turn_by(re, im, *columns[k], k in FINE)):
+                for part in range(2):
+                    column = pl.ds(FINE.index(lag) * TILE, TILE)
+                    right_turned[slot, at[part], column] = value[part].astype(jnp.bfloat16)
 
     copies = []
     for i, t in enumerate(picked):
@@ -143,8 +150,8 @@
                     turn_left(slot, left_block, LEFT_ORDER[first + 1])
                 total = lax.dot_general(
                     left_turned[slot, first * TILE:(first + 2) * TILE, :],
-                    right_turned[slot, fine * TILE:(fine + 2) * TILE, :],
-                    (((1,), (1,)), ((), ())),
+                    right_turned[slot, :, fine * TILE:(fine + 2) * TILE],
+                    (((1,), (0,)), ((), ())),
                     preferred_element_type=jnp.float32,
                 )
                 for v, s in ((0, 0), (0, 1), (1, 0), (1, 1)):
@@ -187,7 +194,7 @@
         scratch_shapes=[
             pltpu.VMEM((groups, chans, lanes), jnp.bfloat16),
             pltpu.VMEM((slots, len(COARSE) * TILE, groups * lanes), jnp.bfloat16),
-            pltpu.VMEM((slots, fine * TILE, groups * lanes), jnp.bfloat16),
+            pltpu.VMEM((slots, groups * lanes, fine * TILE), jnp.bfloat16),
             *more,
         ],
         compiler_params=pltpu.CompilerParams(vmem_limit_bytes=scratch + SMALL),

time: 24.8 us -> 25.5 us (1.028)
  Pallas kernels: 5.74 us -> 6.5 us
    pallas_call x2, Pallas kernels: 4.39 us -> 5.14 us  [correlate(): pl.pallas_call(lambda *refs: correlate_kernel(norm, picked, adds, places,...]
  transfers between devices with their start and end apart: 13 -> 13, of which waited for: 1 -> 1; matrix products, arithmetic and copies ran while one was open for 1% -> 1% of each run, Pallas kernels for 7% -> 8%
where the time goes in v20:
time: 25.5 us; the launch traced here: 25.4 us
  starting transfers between devices  16.7 us (65%)
  Pallas kernels  6.5 us (25%)
  waiting for transfers between devices  1.74 us (7%)
  local copies, waits for them, and re-layouts  0.26 us (1%)
    ppermute x13, starting transfers between devices, swap(): lax.ppermute(array, axis, [(i, i ^ k) for i in range(lax.axis_size(axis))])  16.7 us
    pallas_call x2, Pallas kernels, correlate(): pl.pallas_call(lambda *refs: correlate_kernel(norm, picked, adds, places,...  5.14 us
    ppermute x13, waiting for transfers between devices, swap(): lax.ppermute(array, axis, [(i, i ^ k) for i in range(lax.axis_size(axis))])  1.74 us
    pallas_call x1, Pallas kernels, whiten(): pl.pallas_call(whiten_kernel, out_shape=jax.ShapeDtypeStruct((chans, bins...  1.29 us
  transfers between devices with their start and end apart: 13, of which 1 were waited for; matrix products, arithmetic and copies ran while one was open for 1% of the time, Pallas kernels for 8%

profile of v20, /device:TPU:1, one launch (start us, length us, event | category | flops | bytes accessed | tf_op | source)
XLA Modules:
  0.0 25.4 jit_solution(6486699142746499568)
XLA Ops:
  0.0 0.0 copy-start
  0.0 1.3 %whiten.1 = bf16[96,256]{1,0:T(8,128)(2,1)S(1)} custom-call(bf16[64,2,2,96]{3,2,1,0:T(2,128)(2,1)} %spectra_hbm.1, s32[1,96]{1,0:T(1,128)} %bitcast.10), custom_call_target="tpu_custom_call" | custom-call | tf_op jit(solution)/shard_map/whiten/pallas_call | solution.py:56
  1.3 2.2 %collective-permute-start.7 = (bf16[1,96,256]{2,1,0:T(8,128)(2,1)S(1)}, bf16[1,96,256]{2,1,0:T(8,128)(2,1)S(1)}, u32[]{:S(2)}, u32[]{:S(2)}) collective-permute-start(bf16[1,96,256]{2,1,0:T(8,128)(2,1)S(1)} %bitcast.6), channel_id=1, source_target_pairs={{0,1},{1,0},{2,3},{3,2},{4,5},{5,4},{6,7},{7,6},{8,9},{9,8},{10,11... | collective-permute-start | bytes 147464 | tf_op jit(solution)/shard_map/ppermute | solution.py:207
  3.5 2.2 %collective-permute-start.1 = (bf16[1,96,256]{2,1,0:T(8,128)(2,1)S(1)}, bf16[1,96,256]{2,1,0:T(8,128)(2,1)S(1)}, u32[]{:S(2)}, u32[]{:S(2)}) collective-permute-start(bf16[1,96,256]{2,1,0:T(8,128)(2,1)S(1)} %bitcast.7), channel_id=1, source_target_pairs={{0,3},{1,2},{2,1},{3,0},{4,7},{5,6},{6,5},{7,4},{8,11},{9,10},{10,... | collective-permute-start | bytes 147464 | tf_op jit(solution)/shard_map/ppermute | solution.py:207
  5.7 0.1 collective-permute-start
  5.8 0.0 copy-done
  5.8 0.1 constant_dynamic-slice_fusion
  5.9 0.1 copy.4
  6.0 0.1 reshape.16
  6.1 0.1 add_bitcast_fusion.refs_2_.refs_0_
  6.1 0.0 collective-permute-done.7.refs_1_
  6.2 2.2 %collective-permute-start.8 = (bf16[2,96,256]{2,1,0:T(8,128)(2,1)S(1)}, bf16[2,96,256]{2,1,0:T(8,128)(2,1)S(1)}, u32[]{:S(2)}, u32[]{:S(2)}) collective-permute-start(bf16[2,96,256]{2,1,0:T(8,128)(2,1)S(1)} %stack.9.refs_0_), channel_id=1, source_target_pairs={{0,24},{4,28},{8,16},{12,20},{16,8},{20,12},{24,0},{28,4},{1,25},{... | collective-permute-start | bytes 294920 | tf_op jit(solution)/shard_map/ppermute | solution.py:207
  8.4 0.3 %collective-permute-start.11 = (bf16[2,96,256]{2,1,0:T(8,128)(2,1)S(1)}, bf16[2,96,256]{2,1,0:T(8,128)(2,1)S(1)}, u32[]{:S(2)}, u32[]{:S(2)}) collective-permute-start(bf16[2,96,256]{2,1,0:T(8,128)(2,1)S(1)} %stack.9.refs_0_), channel_id=1, source_target_pairs={{0,8},{4,12},{8,0},{12,4},{16,24},{20,28},{24,16},{28,20},{1,9},{5... | collective-permute-start | bytes 294920 | tf_op jit(solution)/shard_map/ppermute | solution.py:207
  8.6 0.2 collective-permute-start.10
  8.9 0.0 collective-permute-done.1.refs_1_
  8.9 1.7 %collective-permute-done.refs_0_ = bf16[1,96,256]{2,1,0:T(8,128)(2,1)S(1)} collective-permute-done((bf16[1,96,256]{2,1,0:T(8,128)(2,1)S(1)}, bf16[1,96,256]{2,1,0:T(8,128)(2,1)S(1)}, u32[]{:S(2)}, u32[]{:S(2)}) %collective-permute-start) | collective-permute-done | bytes 49184 | tf_op jit(solution)/shard_map/ppermute | solution.py:207
  10.6 2.2 %collective-permute-start.2 = (bf16[2,96,256]{2,1,0:T(8,128)(2,1)S(1)}, bf16[2,96,256]{2,1,0:T(8,128)(2,1)S(1)}, u32[]{:S(2)}, u32[]{:S(2)}) collective-permute-start(bf16[2,96,256]{2,1,0:T(8,128)(2,1)S(1)} %stack.6.refs_0_), channel_id=1, source_target_pairs={{0,24},{4,28},{8,16},{12,20},{16,8},{20,12},{24,0},{28,4},{1,25},{... | collective-permute-start | bytes 294920 | tf_op jit(solution)/shard_map/ppermute | solution.py:207
  12.8 0.3 %collective-permute-start.5 = (bf16[2,96,256]{2,1,0:T(8,128)(2,1)S(1)}, bf16[2,96,256]{2,1,0:T(8,128)(2,1)S(1)}, u32[]{:S(2)}, u32[]{:S(2)}) collective-permute-start(bf16[2,96,256]{2,1,0:T(8,128)(2,1)S(1)} %stack.6.refs_0_), channel_id=1, source_target_pairs={{0,8},{4,12},{8,0},{12,4},{16,24},{20,28},{24,16},{28,20},{1,9},{5... | collective-permute-start | bytes 294920 | tf_op jit(solution)/shard_map/ppermute | solution.py:207
  13.1 0.0 collective-permute-done.8.refs_1_
  13.1 0.2 collective-permute-start.4
  13.3 0.0 collective-permute-done.11.refs_1_
  13.3 2.8 %collective-permute-start.9 = (bf16[4,96,256]{2,1,0:T(8,128)(2,1)S(1)}, bf16[4,96,256]{2,1,0:T(8,128)(2,1)S(1)}, u32[]{:S(2)}, u32[]{:S(2)}) collective-permute-start(bf16[4,96,256]{2,1,0:T(8,128)(2,1)S(1)} %stack.10.refs_1_), channel_id=1, source_target_pairs={{0,4},{4,0},{8,12},{12,8},{16,20},{20,16},{24,28},{28,24},{1,5},{5... | collective-permute-start | bytes 589832 | tf_op jit(solution)/shard_map/ppermute | solution.py:207
  16.1 0.0 collective-permute-done.10.refs_0_
  16.1 0.1 collective-permute-start.12
  16.2 0.0 collective-permute-done.2.refs_1_
  16.2 2.0 %collective-permute-start.3 = (bf16[4,96,256]{2,1,0:T(8,128)(2,1)S(1)}, bf16[4,96,256]{2,1,0:T(8,128)(2,1)S(1)}, u32[]{:S(2)}, u32[]{:S(2)}) collective-permute-start(bf16[4,96,256]{2,1,0:T(8,128)(2,1)S(1)} %stack.7.refs_1_), channel_id=1, source_target_pairs={{0,4},{4,0},{8,12},{12,8},{16,20},{20,16},{24,28},{28,24},{1,5},{5... | collective-permute-start | bytes 589832 | tf_op jit(solution)/shard_map/ppermute | solution.py:207
  18.2 0.0 collective-permute-done.5.refs_1_
  18.2 0.0 collective-permute-done.4.refs_0_
  18.2 2.0 %collective-permute-start.6 = (bf16[4,96,256]{2,1,0:T(8,128)(2,1)S(1)}, bf16[4,96,256]{2,1,0:T(8,128)(2,1)S(1)}, u32[]{:S(2)}, u32[]{:S(2)}) collective-permute-start(bf16[4,96,256]{2,1,0:T(8,128)(2,1)S(1)} %stack.8.refs_3_), channel_id=1, source_target_pairs={{0,4},{4,0},{8,12},{12,8},{16,20},{20,16},{24,28},{28,24},{1,5},{5... | collective-permute-start | bytes 589832 | tf_op jit(solution)/shard_map/ppermute | solution.py:207
  20.2 0.0 collective-permute-done.9.refs_2_
  20.2 0.0 collective-permute-done.12.refs_4_
  20.2 2.0 %correlate.1.refs_5_ = f32[2,4,8,128,128]{4,3,2,1,0:T(8,128)S(1)} custom-call(s32[1,5]{1,0:T(1,128)S(1)} %add_bitcast_fusion.refs_2_.refs_0_, bf16[4,96,256]{2,1,0:T(8,128)(2,1)S(1)} %stack.10.refs_1_, bf16[4,96,256]{2,1,0:T(8,128)(2,1)S(1)} %collective-permute-done.9.refs_2_, bf16[4,96,256]{2,1,0:T(8,128)(2,1)S(1)} %stack.11.refs_3_, ...), custom_call_target="tpu_custom_call" | custom-call | tf_op jit(solution)/shard_map/correlate/pallas_call | solution.py:189
  22.3 0.0 collective-permute-done.3.refs_2_
  22.3 0.0 collective-permute-done.6.refs_4_
  22.3 3.1 %correlate_add.1 = f32[2,4,8,128,128]{4,3,2,1,0:T(8,128)} custom-call(s32[1,5]{1,0:T(1,128)S(1)} %add_bitcast_fusion.refs_2_.refs_0_, bf16[4,96,256]{2,1,0:T(8,128)(2,1)S(1)} %stack.7.refs_1_, bf16[4,96,256]{2,1,0:T(8,128)(2,1)S(1)} %collective-permute-done.3.refs_2_, bf16[4,96,256]{2,1,0:T(8,128)(2,1)S(1)} %stack.8.refs_3_, ...), custom_call_target="tpu_custom_call" | custom-call | tf_op jit(solution)/shard_map/correlate_add/pallas_call | solution.py:189
  (6 shorter events, 0.1 us)
Async XLA Ops:
  0.0 5.8 %copy-start = (s32[8,2]{0,1:T(2,128)S(1)}, s32[8,2]{0,1:T(2,128)}, u32[]{:S(2)}) copy-start(s32[8,2]{0,1:T(2,128)} %param.5) | copy-start | bytes 196
  1.3 4.8 %collective-permute-start.7 = (bf16[1,96,256]{2,1,0:T(8,128)(2,1)S(1)}, bf16[1,96,256]{2,1,0:T(8,128)(2,1)S(1)}, u32[]{:S(2)}, u32[]{:S(2)}) collective-permute-start(bf16[1,96,256]{2,1,0:T(8,128)(2,1)S(1)} %bitcast.6), channel_id=1, source_target_pairs={{0,1},{1,0},{2,3},{3,2},{4,5},{5,4},{6,7},{7,6},{8,9},{9,8},{10,11... | collective-permute-start | bytes 147464 | tf_op jit(solution)/shard_map/ppermute | solution.py:207
  3.5 5.4 %collective-permute-start.1 = (bf16[1,96,256]{2,1,0:T(8,128)(2,1)S(1)}, bf16[1,96,256]{2,1,0:T(8,128)(2,1)S(1)}, u32[]{:S(2)}, u32[]{:S(2)}) collective-permute-start(bf16[1,96,256]{2,1,0:T(8,128)(2,1)S(1)} %bitcast.7), channel_id=1, source_target_pairs={{0,3},{1,2},{2,1},{3,0},{4,7},{5,6},{6,5},{7,4},{8,11},{9,10},{10,... | collective-permute-start | bytes 147464 | tf_op jit(solution)/shard_map/ppermute | solution.py:207
  5.7 4.9 %collective-permute-start = (bf16[1,96,256]{2,1,0:T(8,128)(2,1)S(1)}, bf16[1,96,256]{2,1,0:T(8,128)(2,1)S(1)}, u32[]{:S(2)}, u32[]{:S(2)}) collective-permute-start(bf16[1,96,256]{2,1,0:T(8,128)(2,1)S(1)} %bitcast.8), channel_id=1, source_target_pairs={{0,2},{1,3},{2,0},{3,1},{4,6},{5,7},{6,4},{7,5},{8,10},{9,11},{10,... | collective-permute-start | bytes 147464 | tf_op jit(solution)/shard_map/ppermute | solution.py:207
  6.2 6.9 %collective-permute-start.8 = (bf16[2,96,256]{2,1,0:T(8,128)(2,1)S(1)}, bf16[2,96,256]{2,1,0:T(8,128)(2,1)S(1)}, u32[]{:S(2)}, u32[]{:S(2)}) collective-permute-start(bf16[2,96,256]{2,1,0:T(8,128)(2,1)S(1)} %stack.9.refs_0_), channel_id=1, source_target_pairs={{0,24},{4,28},{8,16},{12,20},{16,8},{20,12},{24,0},{28,4},{1,25},{... | collective-permute-start | bytes 294920 | tf_op jit(solution)/shard_map/ppermute | solution.py:207
  8.4 4.9 %collective-permute-start.11 = (bf16[2,96,256]{2,1,0:T(8,128)(2,1)S(1)}, bf16[2,96,256]{2,1,0:T(8,128)(2,1)S(1)}, u32[]{:S(2)}, u32[]{:S(2)}) collective-permute-start(bf16[2,96,256]{2,1,0:T(8,128)(2,1)S(1)} %stack.9.refs_0_), channel_id=1, source_target_pairs={{0,8},{4,12},{8,0},{12,4},{16,24},{20,28},{24,16},{28,20},{1,9},{5... | collective-permute-start | bytes 294920 | tf_op jit(solution)/shard_map/ppermute | solution.py:207
  8.6 7.5 %collective-permute-start.10 = (bf16[2,96,256]{2,1,0:T(8,128)(2,1)S(1)}, bf16[2,96,256]{2,1,0:T(8,128)(2,1)S(1)}, u32[]{:S(2)}, u32[]{:S(2)}) collective-permute-start(bf16[2,96,256]{2,1,0:T(8,128)(2,1)S(1)} %stack.9.refs_0_), channel_id=1, source_target_pairs={{0,16},{4,20},{8,24},{12,28},{16,0},{20,4},{24,8},{28,12},{1,17},{... | collective-permute-start | bytes 294920 | tf_op jit(solution)/shard_map/ppermute | solution.py:207
  10.6 5.6 %collective-permute-start.2 = (bf16[2,96,256]{2,1,0:T(8,128)(2,1)S(1)}, bf16[2,96,256]{2,1,0:T(8,128)(2,1)S(1)}, u32[]{:S(2)}, u32[]{:S(2)}) collective-permute-start(bf16[2,96,256]{2,1,0:T(8,128)(2,1)S(1)} %stack.6.refs_0_), channel_id=1, source_target_pairs={{0,24},{4,28},{8,16},{12,20},{16,8},{20,12},{24,0},{28,4},{1,25},{... | collective-permute-start | bytes 294920 | tf_op jit(solution)/shard_map/ppermute | solution.py:207
  12.8 5.4 %collective-permute-start.5 = (bf16[2,96,256]{2,1,0:T(8,128)(2,1)S(1)}, bf16[2,96,256]{2,1,0:T(8,128)(2,1)S(1)}, u32[]{:S(2)}, u32[]{:S(2)}) collective-permute-start(bf16[2,96,256]{2,1,0:T(8,128)(2,1)S(1)} %stack.6.refs_0_), channel_id=1, source_target_pairs={{0,8},{4,12},{8,0},{12,4},{16,24},{20,28},{24,16},{28,20},{1,9},{5... | collective-permute-start | bytes 294920 | tf_op jit(solution)/shard_map/ppermute | solution.py:207
  13.1 5.1 %collective-permute-start.4 = (bf16[2,96,256]{2,1,0:T(8,128)(2,1)S(1)}, bf16[2,96,256]{2,1,0:T(8,128)(2,1)S(1)}, u32[]{:S(2)}, u32[]{:S(2)}) collective-permute-start(bf16[2,96,256]{2,1,0:T(8,128)(2,1)S(1)} %stack.6.refs_0_), channel_id=1, source_target_pairs={{0,16},{4,20},{8,24},{12,28},{16,0},{20,4},{24,8},{28,12},{1,17},{... | collective-permute-start | bytes 294920 | tf_op jit(solution)/shard_map/ppermute | solution.py:207
  13.3 6.9 %collective-permute-start.9 = (bf16[4,96,256]{2,1,0:T(8,128)(2,1)S(1)}, bf16[4,96,256]{2,1,0:T(8,128)(2,1)S(1)}, u32[]{:S(2)}, u32[]{:S(2)}) collective-permute-start(bf16[4,96,256]{2,1,0:T(8,128)(2,1)S(1)} %stack.10.refs_1_), channel_id=1, source_target_pairs={{0,4},{4,0},{8,12},{12,8},{16,20},{20,16},{24,28},{28,24},{1,5},{5... | collective-permute-start | bytes 589832 | tf_op jit(solution)/shard_map/ppermute | solution.py:207
  16.1 4.1 %collective-permute-start.12 = (bf16[4,96,256]{2,1,0:T(8,128)(2,1)S(1)}, bf16[4,96,256]{2,1,0:T(8,128)(2,1)S(1)}, u32[]{:S(2)}, u32[]{:S(2)}) collective-permute-start(bf16[4,96,256]{2,1,0:T(8,128)(2,1)S(1)} %stack.11.refs_3_), channel_id=1, source_target_pairs={{0,4},{4,0},{8,12},{12,8},{16,20},{20,16},{24,28},{28,24},{1,5},{5... | collective-permute-start | bytes 589832 | tf_op jit(solution)/shard_map/ppermute | solution.py:207
  16.2 6.0 %collective-permute-start.3 = (bf16[4,96,256]{2,1,0:T(8,128)(2,1)S(1)}, bf16[4,96,256]{2,1,0:T(8,128)(2,1)S(1)}, u32[]{:S(2)}, u32[]{:S(2)}) collective-permute-start(bf16[4,96,256]{2,1,0:T(8,128)(2,1)S(1)} %stack.7.refs_1_), channel_id=1, source_target_pairs={{0,4},{4,0},{8,12},{12,8},{16,20},{20,16},{24,28},{28,24},{1,5},{5... | collective-permute-start | bytes 589832 | tf_op jit(solution)/shard_map/ppermute | solution.py:207
  18.2 4.0 %collective-permute-start.6 = (bf16[4,96,256]{2,1,0:T(8,128)(2,1)S(1)}, bf16[4,96,256]{2,1,0:T(8,128)(2,1)S(1)}, u32[]{:S(2)}, u32[]{:S(2)}) collective-permute-start(bf16[4,96,256]{2,1,0:T(8,128)(2,1)S(1)} %stack.8.refs_3_), channel_id=1, source_target_pairs={{0,4},{4,0},{8,12},{12,8},{16,20},{20,16},{24,28},{28,24},{1,5},{5... | collective-permute-start | bytes 589832 | tf_op jit(solution)/shard_map/ppermute | solution.py:207

commit v21 on v16

--- a/solution.py
+++ b/solution.py
@@ -27,8 +27,9 @@
     ]
     for copy in copies:
         copy.start()
-    bins, hours, _, chans = spectra_ref.shape
-    rows = bins * hours * 2
+    rows, chans = spectra_ref.shape
+    bins = F
+    hours = rows // (2 * bins)
     row = lax.broadcasted_iota(jnp.int32, (rows, chans), 0)
     hour = (row // 2) % hours
     src = lax.broadcasted_iota(jnp.int32, (rows, rows), 0)
@@ -36,7 +37,7 @@
     move = jnp.where((src % 2) * (rows // 2) + src // 2 == dst, 1.0, 0.0).astype(jnp.bfloat16)
     for copy in copies:
         copy.wait()
-    values = spectra_ref[...].reshape(rows, chans).astype(jnp.float32)
+    values = spectra_ref[...].astype(jnp.float32)
     keep = (1 - bad_ref[...]).astype(jnp.float32)
     squares = values * values
     scale = jnp.zeros((rows, chans), jnp.float32)
@@ -50,12 +51,13 @@
 
 
 def whiten(spectra, bad_channels):
-    bins, hours, _, chans = spectra.shape
+    chans = spectra.shape[-1]
+    spectra = spectra.reshape(-1, chans)
     spectra = pltpu.with_memory_space_constraint(spectra, pltpu.HBM)
     bad_channels = pltpu.with_memory_space_constraint(bad_channels.reshape(1, chans), pltpu.HBM)
     return pl.pallas_call(
         whiten_kernel,
-        out_shape=jax.ShapeDtypeStruct((chans, bins * hours * 2), jnp.bfloat16),
+        out_shape=jax.ShapeDtypeStruct((chans, spectra.shape[0]), jnp.bfloat16),
         in_specs=[pl.BlockSpec(memory_space=pltpu.HBM)] * 2,
         out_specs=VMEM,
         scratch_shapes=[

time: 24.8 us -> 24.6 us (level)
  no operation moved by 1% of the time
where the time goes in v21:
time: 24.6 us; the launch traced here: 24.5 us
  starting transfers between devices  16.7 us (68%)
  Pallas kernels  5.61 us (23%)
  waiting for transfers between devices  1.74 us (7%)
  local copies, waits for them, and re-layouts  0.26 us (1%)
    ppermute x13, starting transfers between devices, swap(): lax.ppermute(array, axis, [(i, i ^ k) for i in range(lax.axis_size(axis))])  16.7 us
    pallas_call x2, Pallas kernels, correlate(): pl.pallas_call(lambda *refs: correlate_kernel(norm, picked, adds, places,...  4.39 us
    ppermute x13, waiting for transfers between devices, swap(): lax.ppermute(array, axis, [(i, i ^ k) for i in range(lax.axis_size(axis))])  1.74 us
    pallas_call x1, Pallas kernels, whiten(): pl.pallas_call(whiten_kernel, out_shape=jax.ShapeDtypeStruct((chans, spec...  1.15 us
  transfers between devices with their start and end apart: 13, of which 1 were waited for; matrix products, arithmetic and copies ran while one was open for 1% of the time, Pallas kernels for 7%

profile of v21, /device:TPU:1, one launch (start us, length us, event | category | flops | bytes accessed | tf_op | source)
XLA Modules:
  0.0 24.5 jit_solution(123549846154017915)
XLA Ops:
  0.0 0.0 copy-start
  0.0 1.2 %whiten.1 = bf16[96,256]{1,0:T(8,128)(2,1)S(1)} custom-call(bf16[256,96]{1,0:T(8,128)(2,1)} %bitcast.11, s32[1,96]{1,0:T(1,128)} %bitcast.12), custom_call_target="tpu_custom_call" | custom-call | tf_op jit(solution)/shard_map/whiten/pallas_call | solution.py:58
  1.2 2.2 %collective-permute-start.7 = (bf16[1,96,256]{2,1,0:T(8,128)(2,1)S(1)}, bf16[1,96,256]{2,1,0:T(8,128)(2,1)S(1)}, u32[]{:S(2)}, u32[]{:S(2)}) collective-permute-start(bf16[1,96,256]{2,1,0:T(8,128)(2,1)S(1)} %bitcast.7), channel_id=1, source_target_pairs={{0,1},{1,0},{2,3},{3,2},{4,5},{5,4},{6,7},{7,6},{8,9},{9,8},{10,11... | collective-permute-start | bytes 147464 | tf_op jit(solution)/shard_map/ppermute | solution.py:202
  3.4 2.2 %collective-permute-start.1 = (bf16[1,96,256]{2,1,0:T(8,128)(2,1)S(1)}, bf16[1,96,256]{2,1,0:T(8,128)(2,1)S(1)}, u32[]{:S(2)}, u32[]{:S(2)}) collective-permute-start(bf16[1,96,256]{2,1,0:T(8,128)(2,1)S(1)} %bitcast.8), channel_id=1, source_target_pairs={{0,3},{1,2},{2,1},{3,0},{4,7},{5,6},{6,5},{7,4},{8,11},{9,10},{10,... | collective-permute-start | bytes 147464 | tf_op jit(solution)/shard_map/ppermute | solution.py:202
  5.6 0.1 collective-permute-start
  5.7 0.0 copy-done
  5.7 0.1 constant_dynamic-slice_fusion
  5.7 0.1 copy.4
  5.8 0.1 reshape.19
  5.9 0.1 add_bitcast_fusion.refs_2_.refs_0_
  6.0 0.0 collective-permute-done.7.refs_1_
  6.0 2.2 %collective-permute-start.8 = (bf16[2,96,256]{2,1,0:T(8,128)(2,1)S(1)}, bf16[2,96,256]{2,1,0:T(8,128)(2,1)S(1)}, u32[]{:S(2)}, u32[]{:S(2)}) collective-permute-start(bf16[2,96,256]{2,1,0:T(8,128)(2,1)S(1)} %stack.9.refs_0_), channel_id=1, source_target_pairs={{0,24},{4,28},{8,16},{12,20},{16,8},{20,12},{24,0},{28,4},{1,25},{... | collective-permute-start | bytes 294920 | tf_op jit(solution)/shard_map/ppermute | solution.py:202
  8.3 0.3 %collective-permute-start.11 = (bf16[2,96,256]{2,1,0:T(8,128)(2,1)S(1)}, bf16[2,96,256]{2,1,0:T(8,128)(2,1)S(1)}, u32[]{:S(2)}, u32[]{:S(2)}) collective-permute-start(bf16[2,96,256]{2,1,0:T(8,128)(2,1)S(1)} %stack.9.refs_0_), channel_id=1, source_target_pairs={{0,8},{4,12},{8,0},{12,4},{16,24},{20,28},{24,16},{28,20},{1,9},{5... | collective-permute-start | bytes 294920 | tf_op jit(solution)/shard_map/ppermute | solution.py:202
  8.5 0.2 collective-permute-start.10
  8.7 0.0 collective-permute-done.1.refs_1_
  8.7 1.7 %collective-permute-done.refs_0_ = bf16[1,96,256]{2,1,0:T(8,128)(2,1)S(1)} collective-permute-done((bf16[1,96,256]{2,1,0:T(8,128)(2,1)S(1)}, bf16[1,96,256]{2,1,0:T(8,128)(2,1)S(1)}, u32[]{:S(2)}, u32[]{:S(2)}) %collective-permute-start) | collective-permute-done | bytes 49184 | tf_op jit(solution)/shard_map/ppermute | solution.py:202
  10.5 2.2 %collective-permute-start.2 = (bf16[2,96,256]{2,1,0:T(8,128)(2,1)S(1)}, bf16[2,96,256]{2,1,0:T(8,128)(2,1)S(1)}, u32[]{:S(2)}, u32[]{:S(2)}) collective-permute-start(bf16[2,96,256]{2,1,0:T(8,128)(2,1)S(1)} %stack.6.refs_0_), channel_id=1, source_target_pairs={{0,24},{4,28},{8,16},{12,20},{16,8},{20,12},{24,0},{28,4},{1,25},{... | collective-permute-start | bytes 294920 | tf_op jit(solution)/shard_map/ppermute | solution.py:202
  12.7 0.3 %collective-permute-start.5 = (bf16[2,96,256]{2,1,0:T(8,128)(2,1)S(1)}, bf16[2,96,256]{2,1,0:T(8,128)(2,1)S(1)}, u32[]{:S(2)}, u32[]{:S(2)}) collective-permute-start(bf16[2,96,256]{2,1,0:T(8,128)(2,1)S(1)} %stack.6.refs_0_), channel_id=1, source_target_pairs={{0,8},{4,12},{8,0},{12,4},{16,24},{20,28},{24,16},{28,20},{1,9},{5... | collective-permute-start | bytes 294920 | tf_op jit(solution)/shard_map/ppermute | solution.py:202
  12.9 0.0 collective-permute-done.8.refs_1_
  12.9 0.2 collective-permute-start.4
  13.2 0.0 collective-permute-done.11.refs_1_
  13.2 2.8 %collective-permute-start.9 = (bf16[4,96,256]{2,1,0:T(8,128)(2,1)S(1)}, bf16[4,96,256]{2,1,0:T(8,128)(2,1)S(1)}, u32[]{:S(2)}, u32[]{:S(2)}) collective-permute-start(bf16[4,96,256]{2,1,0:T(8,128)(2,1)S(1)} %stack.10.refs_1_), channel_id=1, source_target_pairs={{0,4},{4,0},{8,12},{12,8},{16,20},{20,16},{24,28},{28,24},{1,5},{5... | collective-permute-start | bytes 589832 | tf_op jit(solution)/shard_map/ppermute | solution.py:202
  16.0 0.0 collective-permute-done.10.refs_0_
  16.0 0.1 collective-permute-start.12
  16.1 0.0 collective-permute-done.2.refs_1_
  16.1 2.0 %collective-permute-start.3 = (bf16[4,96,256]{2,1,0:T(8,128)(2,1)S(1)}, bf16[4,96,256]{2,1,0:T(8,128)(2,1)S(1)}, u32[]{:S(2)}, u32[]{:S(2)}) collective-permute-start(bf16[4,96,256]{2,1,0:T(8,128)(2,1)S(1)} %stack.7.refs_1_), channel_id=1, source_target_pairs={{0,4},{4,0},{8,12},{12,8},{16,20},{20,16},{24,28},{28,24},{1,5},{5... | collective-permute-start | bytes 589832 | tf_op jit(solution)/shard_map/ppermute | solution.py:202
  18.1 0.0 collective-permute-done.5.refs_1_
  18.1 0.0 collective-permute-done.4.refs_0_
  18.1 2.0 %collective-permute-start.6 = (bf16[4,96,256]{2,1,0:T(8,128)(2,1)S(1)}, bf16[4,96,256]{2,1,0:T(8,128)(2,1)S(1)}, u32[]{:S(2)}, u32[]{:S(2)}) collective-permute-start(bf16[4,96,256]{2,1,0:T(8,128)(2,1)S(1)} %stack.8.refs_3_), channel_id=1, source_target_pairs={{0,4},{4,0},{8,12},{12,8},{16,20},{20,16},{24,28},{28,24},{1,5},{5... | collective-permute-start | bytes 589832 | tf_op jit(solution)/shard_map/ppermute | solution.py:202
  20.1 0.0 collective-permute-done.9.refs_2_
  20.1 0.0 collective-permute-done.12.refs_4_
  20.1 1.7 %correlate.1.refs_5_ = f32[2,4,8,128,128]{4,3,2,1,0:T(8,128)S(1)} custom-call(s32[1,5]{1,0:T(1,128)S(1)} %add_bitcast_fusion.refs_2_.refs_0_, bf16[4,96,256]{2,1,0:T(8,128)(2,1)S(1)} %stack.10.refs_1_, bf16[4,96,256]{2,1,0:T(8,128)(2,1)S(1)} %collective-permute-done.9.refs_2_, bf16[4,96,256]{2,1,0:T(8,128)(2,1)S(1)} %stack.11.refs_3_, ...), custom_call_target="tpu_custom_call" | custom-call | tf_op jit(solution)/shard_map/correlate/pallas_call | solution.py:184
  21.7 0.0 collective-permute-done.3.refs_2_
  21.8 0.0 collective-permute-done.6.refs_4_
  21.8 2.7 %correlate_add.1 = f32[2,4,8,128,128]{4,3,2,1,0:T(8,128)} custom-call(s32[1,5]{1,0:T(1,128)S(1)} %add_bitcast_fusion.refs_2_.refs_0_, bf16[4,96,256]{2,1,0:T(8,128)(2,1)S(1)} %stack.7.refs_1_, bf16[4,96,256]{2,1,0:T(8,128)(2,1)S(1)} %collective-permute-done.3.refs_2_, bf16[4,96,256]{2,1,0:T(8,128)(2,1)S(1)} %stack.8.refs_3_, ...), custom_call_target="tpu_custom_call" | custom-call | tf_op jit(solution)/shard_map/correlate_add/pallas_call | solution.py:184
  (6 shorter events, 0.1 us)
Async XLA Ops:
  0.0 5.7 %copy-start = (s32[8,2]{0,1:T(2,128)S(1)}, s32[8,2]{0,1:T(2,128)}, u32[]{:S(2)}) copy-start(s32[8,2]{0,1:T(2,128)} %param.5) | copy-start | bytes 196
  1.2 4.8 %collective-permute-start.7 = (bf16[1,96,256]{2,1,0:T(8,128)(2,1)S(1)}, bf16[1,96,256]{2,1,0:T(8,128)(2,1)S(1)}, u32[]{:S(2)}, u32[]{:S(2)}) collective-permute-start(bf16[1,96,256]{2,1,0:T(8,128)(2,1)S(1)} %bitcast.7), channel_id=1, source_target_pairs={{0,1},{1,0},{2,3},{3,2},{4,5},{5,4},{6,7},{7,6},{8,9},{9,8},{10,11... | collective-permute-start | bytes 147464 | tf_op jit(solution)/shard_map/ppermute | solution.py:202
  3.4 5.4 %collective-permute-start.1 = (bf16[1,96,256]{2,1,0:T(8,128)(2,1)S(1)}, bf16[1,96,256]{2,1,0:T(8,128)(2,1)S(1)}, u32[]{:S(2)}, u32[]{:S(2)}) collective-permute-start(bf16[1,96,256]{2,1,0:T(8,128)(2,1)S(1)} %bitcast.8), channel_id=1, source_target_pairs={{0,3},{1,2},{2,1},{3,0},{4,7},{5,6},{6,5},{7,4},{8,11},{9,10},{10,... | collective-permute-start | bytes 147464 | tf_op jit(solution)/shard_map/ppermute | solution.py:202
  5.6 4.9 %collective-permute-start = (bf16[1,96,256]{2,1,0:T(8,128)(2,1)S(1)}, bf16[1,96,256]{2,1,0:T(8,128)(2,1)S(1)}, u32[]{:S(2)}, u32[]{:S(2)}) collective-permute-start(bf16[1,96,256]{2,1,0:T(8,128)(2,1)S(1)} %bitcast.9), channel_id=1, source_target_pairs={{0,2},{1,3},{2,0},{3,1},{4,6},{5,7},{6,4},{7,5},{8,10},{9,11},{10,... | collective-permute-start | bytes 147464 | tf_op jit(solution)/shard_map/ppermute | solution.py:202
  6.0 6.9 %collective-permute-start.8 = (bf16[2,96,256]{2,1,0:T(8,128)(2,1)S(1)}, bf16[2,96,256]{2,1,0:T(8,128)(2,1)S(1)}, u32[]{:S(2)}, u32[]{:S(2)}) collective-permute-start(bf16[2,96,256]{2,1,0:T(8,128)(2,1)S(1)} %stack.9.refs_0_), channel_id=1, source_target_pairs={{0,24},{4,28},{8,16},{12,20},{16,8},{20,12},{24,0},{28,4},{1,25},{... | collective-permute-start | bytes 294920 | tf_op jit(solution)/shard_map/ppermute | solution.py:202
  8.3 4.9 %collective-permute-start.11 = (bf16[2,96,256]{2,1,0:T(8,128)(2,1)S(1)}, bf16[2,96,256]{2,1,0:T(8,128)(2,1)S(1)}, u32[]{:S(2)}, u32[]{:S(2)}) collective-permute-start(bf16[2,96,256]{2,1,0:T(8,128)(2,1)S(1)} %stack.9.refs_0_), channel_id=1, source_target_pairs={{0,8},{4,12},{8,0},{12,4},{16,24},{20,28},{24,16},{28,20},{1,9},{5... | collective-permute-start | bytes 294920 | tf_op jit(solution)/shard_map/ppermute | solution.py:202
  8.5 7.5 %collective-permute-start.10 = (bf16[2,96,256]{2,1,0:T(8,128)(2,1)S(1)}, bf16[2,96,256]{2,1,0:T(8,128)(2,1)S(1)}, u32[]{:S(2)}, u32[]{:S(2)}) collective-permute-start(bf16[2,96,256]{2,1,0:T(8,128)(2,1)S(1)} %stack.9.refs_0_), channel_id=1, source_target_pairs={{0,16},{4,20},{8,24},{12,28},{16,0},{20,4},{24,8},{28,12},{1,17},{... | collective-permute-start | bytes 294920 | tf_op jit(solution)/shard_map/ppermute | solution.py:202
  10.5 5.6 %collective-permute-start.2 = (bf16[2,96,256]{2,1,0:T(8,128)(2,1)S(1)}, bf16[2,96,256]{2,1,0:T(8,128)(2,1)S(1)}, u32[]{:S(2)}, u32[]{:S(2)}) collective-permute-start(bf16[2,96,256]{2,1,0:T(8,128)(2,1)S(1)} %stack.6.refs_0_), channel_id=1, source_target_pairs={{0,24},{4,28},{8,16},{12,20},{16,8},{20,12},{24,0},{28,4},{1,25},{... | collective-permute-start | bytes 294920 | tf_op jit(solution)/shard_map/ppermute | solution.py:202
  12.7 5.4 %collective-permute-start.5 = (bf16[2,96,256]{2,1,0:T(8,128)(2,1)S(1)}, bf16[2,96,256]{2,1,0:T(8,128)(2,1)S(1)}, u32[]{:S(2)}, u32[]{:S(2)}) collective-permute-start(bf16[2,96,256]{2,1,0:T(8,128)(2,1)S(1)} %stack.6.refs_0_), channel_id=1, source_target_pairs={{0,8},{4,12},{8,0},{12,4},{16,24},{20,28},{24,16},{28,20},{1,9},{5... | collective-permute-start | bytes 294920 | tf_op jit(solution)/shard_map/ppermute | solution.py:202
  12.9 5.1 %collective-permute-start.4 = (bf16[2,96,256]{2,1,0:T(8,128)(2,1)S(1)}, bf16[2,96,256]{2,1,0:T(8,128)(2,1)S(1)}, u32[]{:S(2)}, u32[]{:S(2)}) collective-permute-start(bf16[2,96,256]{2,1,0:T(8,128)(2,1)S(1)} %stack.6.refs_0_), channel_id=1, source_target_pairs={{0,16},{4,20},{8,24},{12,28},{16,0},{20,4},{24,8},{28,12},{1,17},{... | collective-permute-start | bytes 294920 | tf_op jit(solution)/shard_map/ppermute | solution.py:202
  13.2 6.9 %collective-permute-start.9 = (bf16[4,96,256]{2,1,0:T(8,128)(2,1)S(1)}, bf16[4,96,256]{2,1,0:T(8,128)(2,1)S(1)}, u32[]{:S(2)}, u32[]{:S(2)}) collective-permute-start(bf16[4,96,256]{2,1,0:T(8,128)(2,1)S(1)} %stack.10.refs_1_), channel_id=1, source_target_pairs={{0,4},{4,0},{8,12},{12,8},{16,20},{20,16},{24,28},{28,24},{1,5},{5... | collective-permute-start | bytes 589832 | tf_op jit(solution)/shard_map/ppermute | solution.py:202
  16.0 4.1 %collective-permute-start.12 = (bf16[4,96,256]{2,1,0:T(8,128)(2,1)S(1)}, bf16[4,96,256]{2,1,0:T(8,128)(2,1)S(1)}, u32[]{:S(2)}, u32[]{:S(2)}) collective-permute-start(bf16[4,96,256]{2,1,0:T(8,128)(2,1)S(1)} %stack.11.refs_3_), channel_id=1, source_target_pairs={{0,4},{4,0},{8,12},{12,8},{16,20},{20,16},{24,28},{28,24},{1,5},{5... | collective-permute-start | bytes 589832 | tf_op jit(solution)/shard_map/ppermute | solution.py:202
  16.1 5.7 %collective-permute-start.3 = (bf16[4,96,256]{2,1,0:T(8,128)(2,1)S(1)}, bf16[4,96,256]{2,1,0:T(8,128)(2,1)S(1)}, u32[]{:S(2)}, u32[]{:S(2)}) collective-permute-start(bf16[4,96,256]{2,1,0:T(8,128)(2,1)S(1)} %stack.7.refs_1_), channel_id=1, source_target_pairs={{0,4},{4,0},{8,12},{12,8},{16,20},{20,16},{24,28},{28,24},{1,5},{5... | collective-permute-start | bytes 589832 | tf_op jit(solution)/shard_map/ppermute | solution.py:202
  18.1 3.6 %collective-permute-start.6 = (bf16[4,96,256]{2,1,0:T(8,128)(2,1)S(1)}, bf16[4,96,256]{2,1,0:T(8,128)(2,1)S(1)}, u32[]{:S(2)}, u32[]{:S(2)}) collective-permute-start(bf16[4,96,256]{2,1,0:T(8,128)(2,1)S(1)} %stack.8.refs_3_), channel_id=1, source_target_pairs={{0,4},{4,0},{8,12},{12,8},{16,20},{20,16},{24,28},{28,24},{1,5},{5... | collective-permute-start | bytes 589832 | tf_op jit(solution)/shard_map/ppermute | solution.py:202

commit v22 on v15

--- a/solution.py
+++ b/solution.py
@@ -25,8 +25,9 @@
     ]
     for copy in copies:
         copy.start()
-    bins, hours, _, chans = spectra_ref.shape
-    rows = bins * hours * 2
+    rows, chans = spectra_ref.shape
+    bins = F
+    hours = rows // (2 * bins)
     row = lax.broadcasted_iota(jnp.int32, (rows, chans), 0)
     hour = (row // 2) % hours
     src = lax.broadcasted_iota(jnp.int32, (rows, rows), 0)
@@ -34,7 +35,7 @@
     move = jnp.where((src % 2) * (rows // 2) + src // 2 == dst, 1.0, 0.0).astype(jnp.bfloat16)
     for copy in copies:
         copy.wait()
-    values = spectra_ref[...].reshape(rows, chans).astype(jnp.float32)
+    values = spectra_ref[...].astype(jnp.float32)
     keep = (1 - bad_ref[...]).astype(jnp.float32)
     squares = values * values
     scale = jnp.zeros((rows, chans), jnp.float32)
@@ -48,12 +49,13 @@
 
 
 def whiten(spectra, bad_channels):
-    bins, hours, _, chans = spectra.shape
+    chans = spectra.shape[-1]
+    spectra = spectra.reshape(-1, chans)
     spectra = pltpu.with_memory_space_constraint(spectra, pltpu.HBM)
     bad_channels = pltpu.with_memory_space_constraint(bad_channels.reshape(1, chans), pltpu.HBM)
     return pl.pallas_call(
         whiten_kernel,
-        out_shape=jax.ShapeDtypeStruct((chans, bins * hours * 2), jnp.bfloat16),
+        out_shape=jax.ShapeDtypeStruct((chans, spectra.shape[0]), jnp.bfloat16),
         in_specs=[pl.BlockSpec(memory_space=pltpu.HBM)] * 2,
         out_specs=VMEM,
         scratch_shapes=[
@@ -149,11 +151,11 @@
                         more[0][i, u + v, fine] = partials[i // each][i % each, u + v, fine] + value
                     else:
                         out_ref[i, u + v, fine] = value
-                for s in range(2 if adds else 0):
-                    done = (i, pl.ds(u, 2), FINE_PAIRS[j][s] + 4)
-                    copy = pltpu.make_async_copy(more[0].at[done], out_ref.at[done], more[1])
-                    copy.start(priority=s)
-                    copies.append(copy)
+            for s in range(2 if adds else 0):
+                done = (i, slice(None), FINE_PAIRS[j][s] + 4)
+                copy = pltpu.make_async_copy(more[0].at[done], out_ref.at[done], more[1])
+                copy.start(priority=s)
+                copies.append(copy)
     for copy in copies:
         copy.wait()
 
@@ -218,7 +220,7 @@
 def halves(white, where):
     groups = lax.axis_size("tm")
     blocks = [white[None]] + [swap(white[None], "tm", k) for k in range(1, groups)]
-    return stack(blocks[:groups // 2], after=(where,)), stack(blocks[groups // 2:], flops=10**9)
+    return stack(blocks[:groups // 2]), stack(blocks[groups // 2:], after=(where,), flops=10**9)
 
 
 def between_chips(half, parts):

time: 24.8 us -> 24.5 us (0.988)
  no operation moved by 1% of the time
where the time goes in v22:
time: 24.5 us; the launch traced here: 24.4 us
  starting transfers between devices  16.7 us (68%)
  Pallas kernels  5.5 us (22%)
  waiting for transfers between devices  1.74 us (7%)
  local copies, waits for them, and re-layouts  0.26 us (1%)
    ppermute x13, starting transfers between devices, swap(): lax.ppermute(array, axis, [(i, i ^ k) for i in range(lax.axis_size(axis))])  16.7 us
    pallas_call x2, Pallas kernels, correlate(): pl.pallas_call(lambda *refs: correlate_kernel(norm, picked, adds, places,...  4.28 us
    ppermute x13, waiting for transfers between devices, swap(): lax.ppermute(array, axis, [(i, i ^ k) for i in range(lax.axis_size(axis))])  1.74 us
    pallas_call x1, Pallas kernels, whiten(): pl.pallas_call(whiten_kernel, out_shape=jax.ShapeDtypeStruct((chans, spec...  1.15 us
  transfers between devices with their start and end apart: 13, of which 1 were waited for; matrix products, arithmetic and copies ran while one was open for 1% of the time, Pallas kernels for 7%

profile of v22, /device:TPU:1, one launch (start us, length us, event | category | flops | bytes accessed | tf_op | source)
XLA Modules:
  0.0 24.4 jit_solution(9341026699731035875)
XLA Ops:
  0.0 0.0 copy-start
  0.0 1.2 %whiten.1 = bf16[96,256]{1,0:T(8,128)(2,1)S(1)} custom-call(bf16[256,96]{1,0:T(8,128)(2,1)} %bitcast.11, s32[1,96]{1,0:T(1,128)} %bitcast.12), custom_call_target="tpu_custom_call" | custom-call | tf_op jit(solution)/shard_map/whiten/pallas_call | solution.py:56
  1.2 2.2 %collective-permute-start.7 = (bf16[1,96,256]{2,1,0:T(8,128)(2,1)S(1)}, bf16[1,96,256]{2,1,0:T(8,128)(2,1)S(1)}, u32[]{:S(2)}, u32[]{:S(2)}) collective-permute-start(bf16[1,96,256]{2,1,0:T(8,128)(2,1)S(1)} %bitcast.7), channel_id=1, source_target_pairs={{0,1},{1,0},{2,3},{3,2},{4,5},{5,4},{6,7},{7,6},{8,9},{9,8},{10,11... | collective-permute-start | bytes 147464 | tf_op jit(solution)/shard_map/ppermute | solution.py:196
  3.4 2.2 %collective-permute-start.1 = (bf16[1,96,256]{2,1,0:T(8,128)(2,1)S(1)}, bf16[1,96,256]{2,1,0:T(8,128)(2,1)S(1)}, u32[]{:S(2)}, u32[]{:S(2)}) collective-permute-start(bf16[1,96,256]{2,1,0:T(8,128)(2,1)S(1)} %bitcast.8), channel_id=1, source_target_pairs={{0,3},{1,2},{2,1},{3,0},{4,7},{5,6},{6,5},{7,4},{8,11},{9,10},{10,... | collective-permute-start | bytes 147464 | tf_op jit(solution)/shard_map/ppermute | solution.py:196
  5.6 0.1 collective-permute-start
  5.7 0.0 copy-done
  5.7 0.1 constant_dynamic-slice_fusion
  5.7 0.1 copy.4
  5.8 0.1 reshape.19
  5.9 0.0 collective-permute-done.7.refs_1_
  5.9 2.2 %collective-permute-start.8 = (bf16[2,96,256]{2,1,0:T(8,128)(2,1)S(1)}, bf16[2,96,256]{2,1,0:T(8,128)(2,1)S(1)}, u32[]{:S(2)}, u32[]{:S(2)}) collective-permute-start(bf16[2,96,256]{2,1,0:T(8,128)(2,1)S(1)} %stack.9.refs_0_), channel_id=1, source_target_pairs={{0,24},{4,28},{8,16},{12,20},{16,8},{20,12},{24,0},{28,4},{1,25},{... | collective-permute-start | bytes 294920 | tf_op jit(solution)/shard_map/ppermute | solution.py:196
  8.2 0.1 add_bitcast_fusion.refs_2_.refs_0_
  8.2 0.3 %collective-permute-start.11 = (bf16[2,96,256]{2,1,0:T(8,128)(2,1)S(1)}, bf16[2,96,256]{2,1,0:T(8,128)(2,1)S(1)}, u32[]{:S(2)}, u32[]{:S(2)}) collective-permute-start(bf16[2,96,256]{2,1,0:T(8,128)(2,1)S(1)} %stack.9.refs_0_), channel_id=1, source_target_pairs={{0,8},{4,12},{8,0},{12,4},{16,24},{20,28},{24,16},{28,20},{1,9},{5... | collective-permute-start | bytes 294920 | tf_op jit(solution)/shard_map/ppermute | solution.py:196
  8.5 0.2 collective-permute-start.10
  8.7 0.0 collective-permute-done.1.refs_1_
  8.7 1.7 %collective-permute-done.refs_0_ = bf16[1,96,256]{2,1,0:T(8,128)(2,1)S(1)} collective-permute-done((bf16[1,96,256]{2,1,0:T(8,128)(2,1)S(1)}, bf16[1,96,256]{2,1,0:T(8,128)(2,1)S(1)}, u32[]{:S(2)}, u32[]{:S(2)}) %collective-permute-start) | collective-permute-done | bytes 49184 | tf_op jit(solution)/shard_map/ppermute | solution.py:196
  10.5 2.2 %collective-permute-start.2 = (bf16[2,96,256]{2,1,0:T(8,128)(2,1)S(1)}, bf16[2,96,256]{2,1,0:T(8,128)(2,1)S(1)}, u32[]{:S(2)}, u32[]{:S(2)}) collective-permute-start(bf16[2,96,256]{2,1,0:T(8,128)(2,1)S(1)} %stack.6.refs_0_), channel_id=1, source_target_pairs={{0,24},{4,28},{8,16},{12,20},{16,8},{20,12},{24,0},{28,4},{1,25},{... | collective-permute-start | bytes 294920 | tf_op jit(solution)/shard_map/ppermute | solution.py:196
  12.7 0.3 %collective-permute-start.5 = (bf16[2,96,256]{2,1,0:T(8,128)(2,1)S(1)}, bf16[2,96,256]{2,1,0:T(8,128)(2,1)S(1)}, u32[]{:S(2)}, u32[]{:S(2)}) collective-permute-start(bf16[2,96,256]{2,1,0:T(8,128)(2,1)S(1)} %stack.6.refs_0_), channel_id=1, source_target_pairs={{0,8},{4,12},{8,0},{12,4},{16,24},{20,28},{24,16},{28,20},{1,9},{5... | collective-permute-start | bytes 294920 | tf_op jit(solution)/shard_map/ppermute | solution.py:196
  12.9 0.0 collective-permute-done.8.refs_1_
  12.9 0.2 collective-permute-start.4
  13.2 0.0 collective-permute-done.11.refs_1_
  13.2 2.8 %collective-permute-start.9 = (bf16[4,96,256]{2,1,0:T(8,128)(2,1)S(1)}, bf16[4,96,256]{2,1,0:T(8,128)(2,1)S(1)}, u32[]{:S(2)}, u32[]{:S(2)}) collective-permute-start(bf16[4,96,256]{2,1,0:T(8,128)(2,1)S(1)} %stack.10.refs_1_), channel_id=1, source_target_pairs={{0,4},{4,0},{8,12},{12,8},{16,20},{20,16},{24,28},{28,24},{1,5},{5... | collective-permute-start | bytes 589832 | tf_op jit(solution)/shard_map/ppermute | solution.py:196
  16.0 0.0 collective-permute-done.10.refs_0_
  16.0 0.1 collective-permute-start.12
  16.1 0.0 collective-permute-done.2.refs_1_
  16.1 2.0 %collective-permute-start.3 = (bf16[4,96,256]{2,1,0:T(8,128)(2,1)S(1)}, bf16[4,96,256]{2,1,0:T(8,128)(2,1)S(1)}, u32[]{:S(2)}, u32[]{:S(2)}) collective-permute-start(bf16[4,96,256]{2,1,0:T(8,128)(2,1)S(1)} %stack.7.refs_1_), channel_id=1, source_target_pairs={{0,4},{4,0},{8,12},{12,8},{16,20},{20,16},{24,28},{28,24},{1,5},{5... | collective-permute-start | bytes 589832 | tf_op jit(solution)/shard_map/ppermute | solution.py:196
  18.1 0.0 collective-permute-done.5.refs_1_
  18.1 0.0 collective-permute-done.4.refs_0_
  18.1 2.0 %collective-permute-start.6 = (bf16[4,96,256]{2,1,0:T(8,128)(2,1)S(1)}, bf16[4,96,256]{2,1,0:T(8,128)(2,1)S(1)}, u32[]{:S(2)}, u32[]{:S(2)}) collective-permute-start(bf16[4,96,256]{2,1,0:T(8,128)(2,1)S(1)} %stack.8.refs_3_), channel_id=1, source_target_pairs={{0,4},{4,0},{8,12},{12,8},{16,20},{20,16},{24,28},{28,24},{1,5},{5... | collective-permute-start | bytes 589832 | tf_op jit(solution)/shard_map/ppermute | solution.py:196
  20.1 0.0 collective-permute-done.9.refs_2_
  20.1 0.0 collective-permute-done.12.refs_4_
  20.1 1.6 %correlate.1.refs_5_ = f32[2,4,8,128,128]{4,3,2,1,0:T(8,128)S(1)} custom-call(s32[1,5]{1,0:T(1,128)S(1)} %add_bitcast_fusion.refs_2_.refs_0_, bf16[4,96,256]{2,1,0:T(8,128)(2,1)S(1)} %stack.10.refs_1_, bf16[4,96,256]{2,1,0:T(8,128)(2,1)S(1)} %collective-permute-done.9.refs_2_, bf16[4,96,256]{2,1,0:T(8,128)(2,1)S(1)} %stack.11.refs_3_, ...), custom_call_target="tpu_custom_call" | custom-call | tf_op jit(solution)/shard_map/correlate/pallas_call | solution.py:178
  21.7 0.0 collective-permute-done.3.refs_2_
  21.7 0.0 collective-permute-done.6.refs_4_
  21.7 2.7 %correlate_add.1 = f32[2,4,8,128,128]{4,3,2,1,0:T(8,128)} custom-call(s32[1,5]{1,0:T(1,128)S(1)} %add_bitcast_fusion.refs_2_.refs_0_, bf16[4,96,256]{2,1,0:T(8,128)(2,1)S(1)} %stack.7.refs_1_, bf16[4,96,256]{2,1,0:T(8,128)(2,1)S(1)} %collective-permute-done.3.refs_2_, bf16[4,96,256]{2,1,0:T(8,128)(2,1)S(1)} %stack.8.refs_3_, ...), custom_call_target="tpu_custom_call" | custom-call | tf_op jit(solution)/shard_map/correlate_add/pallas_call | solution.py:178
  (6 shorter events, 0.1 us)
Async XLA Ops:
  0.0 5.7 %copy-start = (s32[8,2]{0,1:T(2,128)S(1)}, s32[8,2]{0,1:T(2,128)}, u32[]{:S(2)}) copy-start(s32[8,2]{0,1:T(2,128)} %param.5) | copy-start | bytes 196
  1.2 4.8 %collective-permute-start.7 = (bf16[1,96,256]{2,1,0:T(8,128)(2,1)S(1)}, bf16[1,96,256]{2,1,0:T(8,128)(2,1)S(1)}, u32[]{:S(2)}, u32[]{:S(2)}) collective-permute-start(bf16[1,96,256]{2,1,0:T(8,128)(2,1)S(1)} %bitcast.7), channel_id=1, source_target_pairs={{0,1},{1,0},{2,3},{3,2},{4,5},{5,4},{6,7},{7,6},{8,9},{9,8},{10,11... | collective-permute-start | bytes 147464 | tf_op jit(solution)/shard_map/ppermute | solution.py:196
  3.4 5.4 %collective-permute-start.1 = (bf16[1,96,256]{2,1,0:T(8,128)(2,1)S(1)}, bf16[1,96,256]{2,1,0:T(8,128)(2,1)S(1)}, u32[]{:S(2)}, u32[]{:S(2)}) collective-permute-start(bf16[1,96,256]{2,1,0:T(8,128)(2,1)S(1)} %bitcast.8), channel_id=1, source_target_pairs={{0,3},{1,2},{2,1},{3,0},{4,7},{5,6},{6,5},{7,4},{8,11},{9,10},{10,... | collective-permute-start | bytes 147464 | tf_op jit(solution)/shard_map/ppermute | solution.py:196
  5.6 4.9 %collective-permute-start = (bf16[1,96,256]{2,1,0:T(8,128)(2,1)S(1)}, bf16[1,96,256]{2,1,0:T(8,128)(2,1)S(1)}, u32[]{:S(2)}, u32[]{:S(2)}) collective-permute-start(bf16[1,96,256]{2,1,0:T(8,128)(2,1)S(1)} %bitcast.9), channel_id=1, source_target_pairs={{0,2},{1,3},{2,0},{3,1},{4,6},{5,7},{6,4},{7,5},{8,10},{9,11},{10,... | collective-permute-start | bytes 147464 | tf_op jit(solution)/shard_map/ppermute | solution.py:196
  5.9 7.0 %collective-permute-start.8 = (bf16[2,96,256]{2,1,0:T(8,128)(2,1)S(1)}, bf16[2,96,256]{2,1,0:T(8,128)(2,1)S(1)}, u32[]{:S(2)}, u32[]{:S(2)}) collective-permute-start(bf16[2,96,256]{2,1,0:T(8,128)(2,1)S(1)} %stack.9.refs_0_), channel_id=1, source_target_pairs={{0,24},{4,28},{8,16},{12,20},{16,8},{20,12},{24,0},{28,4},{1,25},{... | collective-permute-start | bytes 294920 | tf_op jit(solution)/shard_map/ppermute | solution.py:196
  8.2 4.9 %collective-permute-start.11 = (bf16[2,96,256]{2,1,0:T(8,128)(2,1)S(1)}, bf16[2,96,256]{2,1,0:T(8,128)(2,1)S(1)}, u32[]{:S(2)}, u32[]{:S(2)}) collective-permute-start(bf16[2,96,256]{2,1,0:T(8,128)(2,1)S(1)} %stack.9.refs_0_), channel_id=1, source_target_pairs={{0,8},{4,12},{8,0},{12,4},{16,24},{20,28},{24,16},{28,20},{1,9},{5... | collective-permute-start | bytes 294920 | tf_op jit(solution)/shard_map/ppermute | solution.py:196
  8.5 7.5 %collective-permute-start.10 = (bf16[2,96,256]{2,1,0:T(8,128)(2,1)S(1)}, bf16[2,96,256]{2,1,0:T(8,128)(2,1)S(1)}, u32[]{:S(2)}, u32[]{:S(2)}) collective-permute-start(bf16[2,96,256]{2,1,0:T(8,128)(2,1)S(1)} %stack.9.refs_0_), channel_id=1, source_target_pairs={{0,16},{4,20},{8,24},{12,28},{16,0},{20,4},{24,8},{28,12},{1,17},{... | collective-permute-start | bytes 294920 | tf_op jit(solution)/shard_map/ppermute | solution.py:196
  10.5 5.6 %collective-permute-start.2 = (bf16[2,96,256]{2,1,0:T(8,128)(2,1)S(1)}, bf16[2,96,256]{2,1,0:T(8,128)(2,1)S(1)}, u32[]{:S(2)}, u32[]{:S(2)}) collective-permute-start(bf16[2,96,256]{2,1,0:T(8,128)(2,1)S(1)} %stack.6.refs_0_), channel_id=1, source_target_pairs={{0,24},{4,28},{8,16},{12,20},{16,8},{20,12},{24,0},{28,4},{1,25},{... | collective-permute-start | bytes 294920 | tf_op jit(solution)/shard_map/ppermute | solution.py:196
  12.7 5.4 %collective-permute-start.5 = (bf16[2,96,256]{2,1,0:T(8,128)(2,1)S(1)}, bf16[2,96,256]{2,1,0:T(8,128)(2,1)S(1)}, u32[]{:S(2)}, u32[]{:S(2)}) collective-permute-start(bf16[2,96,256]{2,1,0:T(8,128)(2,1)S(1)} %stack.6.refs_0_), channel_id=1, source_target_pairs={{0,8},{4,12},{8,0},{12,4},{16,24},{20,28},{24,16},{28,20},{1,9},{5... | collective-permute-start | bytes 294920 | tf_op jit(solution)/shard_map/ppermute | solution.py:196
  12.9 5.1 %collective-permute-start.4 = (bf16[2,96,256]{2,1,0:T(8,128)(2,1)S(1)}, bf16[2,96,256]{2,1,0:T(8,128)(2,1)S(1)}, u32[]{:S(2)}, u32[]{:S(2)}) collective-permute-start(bf16[2,96,256]{2,1,0:T(8,128)(2,1)S(1)} %stack.6.refs_0_), channel_id=1, source_target_pairs={{0,16},{4,20},{8,24},{12,28},{16,0},{20,4},{24,8},{28,12},{1,17},{... | collective-permute-start | bytes 294920 | tf_op jit(solution)/shard_map/ppermute | solution.py:196
  13.2 6.9 %collective-permute-start.9 = (bf16[4,96,256]{2,1,0:T(8,128)(2,1)S(1)}, bf16[4,96,256]{2,1,0:T(8,128)(2,1)S(1)}, u32[]{:S(2)}, u32[]{:S(2)}) collective-permute-start(bf16[4,96,256]{2,1,0:T(8,128)(2,1)S(1)} %stack.10.refs_1_), channel_id=1, source_target_pairs={{0,4},{4,0},{8,12},{12,8},{16,20},{20,16},{24,28},{28,24},{1,5},{5... | collective-permute-start | bytes 589832 | tf_op jit(solution)/shard_map/ppermute | solution.py:196
  16.0 4.1 %collective-permute-start.12 = (bf16[4,96,256]{2,1,0:T(8,128)(2,1)S(1)}, bf16[4,96,256]{2,1,0:T(8,128)(2,1)S(1)}, u32[]{:S(2)}, u32[]{:S(2)}) collective-permute-start(bf16[4,96,256]{2,1,0:T(8,128)(2,1)S(1)} %stack.11.refs_3_), channel_id=1, source_target_pairs={{0,4},{4,0},{8,12},{12,8},{16,20},{20,16},{24,28},{28,24},{1,5},{5... | collective-permute-start | bytes 589832 | tf_op jit(solution)/shard_map/ppermute | solution.py:196
  16.1 5.6 %collective-permute-start.3 = (bf16[4,96,256]{2,1,0:T(8,128)(2,1)S(1)}, bf16[4,96,256]{2,1,0:T(8,128)(2,1)S(1)}, u32[]{:S(2)}, u32[]{:S(2)}) collective-permute-start(bf16[4,96,256]{2,1,0:T(8,128)(2,1)S(1)} %stack.7.refs_1_), channel_id=1, source_target_pairs={{0,4},{4,0},{8,12},{12,8},{16,20},{20,16},{24,28},{28,24},{1,5},{5... | collective-permute-start | bytes 589832 | tf_op jit(solution)/shard_map/ppermute | solution.py:196
  18.1 3.6 %collective-permute-start.6 = (bf16[4,96,256]{2,1,0:T(8,128)(2,1)S(1)}, bf16[4,96,256]{2,1,0:T(8,128)(2,1)S(1)}, u32[]{:S(2)}, u32[]{:S(2)}) collective-permute-start(bf16[4,96,256]{2,1,0:T(8,128)(2,1)S(1)} %stack.8.refs_3_), channel_id=1, source_target_pairs={{0,4},{4,0},{8,12},{12,8},{16,20},{20,16},{24,28},{28,24},{1,5},{5... | collective-permute-start | bytes 589832 | tf_op jit(solution)/shard_map/ppermute | solution.py:196

commit v23 on v22

--- a/solution.py
+++ b/solution.py
@@ -126,35 +126,36 @@
                 forward, backward = turn_by(re, im, *(norm * part for part in table[k]), True)
                 store(left_turned, slot, COARSE.index(k), g, forward)
                 store(left_turned, slot, COARSE.index(-k), g, backward)
-        for j in range(len(FINE_PAIRS)):
+        for j in range(0, len(FINE_PAIRS), 2):
             for g in range(groups):
                 re, im = load(right_block, g)
-                if j == 0:
-                    store(right_turned, slot, 0, g, turn_by(re, im, *table[4], False)[0])
-                    store(right_turned, slot, 1, g, (re, im))
-                else:
-                    forward, backward = turn_by(re, im, *table[j], True)
-                    store(right_turned, slot, 2 * j, g, forward)
-                    store(right_turned, slot, 2 * j + 1, g, backward)
+                for pair in (j, j + 1):
+                    if pair == 0:
+                        turns = (turn_by(re, im, *table[4], False)[0], (re, im))
+                    else:
+                        turns = turn_by(re, im, *table[pair], True)
+                    for s in range(2):
+                        store(right_turned, slot, 2 * pair + s, g, turns[s])
             for u in range(0, len(COARSE), 2):
                 total = lax.dot_general(
                     left_turned[slot, u * TILE:(u + 2) * TILE, :],
-                    right_turned[slot, 2 * j * TILE:2 * (j + 1) * TILE, :],
+                    right_turned[slot, 2 * j * TILE:2 * (j + 2) * TILE, :],
                     (((1,), (1,)), ((), ())),
                     preferred_element_type=jnp.float32,
                 )
-                for v, s in ((0, 0), (0, 1), (1, 0), (1, 1)):
-                    fine = FINE_PAIRS[j][s] + 4
-                    value = total[v * TILE:(v + 1) * TILE, s * TILE:(s + 1) * TILE]
-                    if adds:
-                        each = len(picked) // adds
-                        more[0][i, u + v, fine] = partials[i // each][i % each, u + v, fine] + value
-                    else:
-                        out_ref[i, u + v, fine] = value
-            for s in range(2 if adds else 0):
-                done = (i, slice(None), FINE_PAIRS[j][s] + 4)
+                for v in range(2):
+                    for s in range(4):
+                        fine = FINE_PAIRS[j + s // 2][s % 2] + 4
+                        value = total[v * TILE:(v + 1) * TILE, s * TILE:(s + 1) * TILE]
+                        if adds:
+                            each = len(picked) // adds
+                            more[0][i, u + v, fine] = partials[i // each][i % each, u + v, fine] + value
+                        else:
+                            out_ref[i, u + v, fine] = value
+            for s in range(4 if adds else 0):
+                done = (i, slice(None), FINE_PAIRS[j + s // 2][s % 2] + 4)
                 copy = pltpu.make_async_copy(more[0].at[done], out_ref.at[done], more[1])
-                copy.start(priority=s)
+                copy.start(priority=s % 2)
                 copies.append(copy)
     for copy in copies:
         copy.wait()

time: 24.5 us -> 24.9 us (1.016)
  Pallas kernels: 5.5 us -> 5.87 us
    pallas_call x2, Pallas kernels: 4.28 us -> 4.65 us  [correlate(): pl.pallas_call(lambda *refs: correlate_kernel(norm, picked, adds, places,...]
where the time goes in v23:
time: 24.9 us; the launch traced here: 24.7 us
  starting transfers between devices  16.7 us (67%)
  Pallas kernels  5.87 us (24%)
  waiting for transfers between devices  1.74 us (7%)
  local copies, waits for them, and re-layouts  0.26 us (1%)
    ppermute x13, starting transfers between devices, swap(): lax.ppermute(array, axis, [(i, i ^ k) for i in range(lax.axis_size(axis))])  16.7 us
    pallas_call x2, Pallas kernels, correlate(): pl.pallas_call(lambda *refs: correlate_kernel(norm, picked, adds, places,...  4.65 us
    ppermute x13, waiting for transfers between devices, swap(): lax.ppermute(array, axis, [(i, i ^ k) for i in range(lax.axis_size(axis))])  1.74 us
    pallas_call x1, Pallas kernels, whiten(): pl.pallas_call(whiten_kernel, out_shape=jax.ShapeDtypeStruct((chans, spec...  1.15 us
  transfers between devices with their start and end apart: 13, of which 1 were waited for; matrix products, arithmetic and copies ran while one was open for 1% of the time, Pallas kernels for 7%

profile of v23, /device:TPU:1, one launch (start us, length us, event | category | flops | bytes accessed | tf_op | source)
XLA Modules:
  0.0 24.7 jit_solution(3432595474451490529)
XLA Ops:
  0.0 0.0 copy-start
  0.0 1.2 %whiten.1 = bf16[96,256]{1,0:T(8,128)(2,1)S(1)} custom-call(bf16[256,96]{1,0:T(8,128)(2,1)} %bitcast.11, s32[1,96]{1,0:T(1,128)} %bitcast.12), custom_call_target="tpu_custom_call" | custom-call | tf_op jit(solution)/shard_map/whiten/pallas_call | solution.py:56
  1.2 2.2 %collective-permute-start.7 = (bf16[1,96,256]{2,1,0:T(8,128)(2,1)S(1)}, bf16[1,96,256]{2,1,0:T(8,128)(2,1)S(1)}, u32[]{:S(2)}, u32[]{:S(2)}) collective-permute-start(bf16[1,96,256]{2,1,0:T(8,128)(2,1)S(1)} %bitcast.7), channel_id=1, source_target_pairs={{0,1},{1,0},{2,3},{3,2},{4,5},{5,4},{6,7},{7,6},{8,9},{9,8},{10,11... | collective-permute-start | bytes 147464 | tf_op jit(solution)/shard_map/ppermute | solution.py:197
  3.4 2.2 %collective-permute-start.1 = (bf16[1,96,256]{2,1,0:T(8,128)(2,1)S(1)}, bf16[1,96,256]{2,1,0:T(8,128)(2,1)S(1)}, u32[]{:S(2)}, u32[]{:S(2)}) collective-permute-start(bf16[1,96,256]{2,1,0:T(8,128)(2,1)S(1)} %bitcast.8), channel_id=1, source_target_pairs={{0,3},{1,2},{2,1},{3,0},{4,7},{5,6},{6,5},{7,4},{8,11},{9,10},{10,... | collective-permute-start | bytes 147464 | tf_op jit(solution)/shard_map/ppermute | solution.py:197
  5.6 0.1 collective-permute-start
  5.7 0.0 copy-done
  5.7 0.1 constant_dynamic-slice_fusion
  5.7 0.1 copy.4
  5.8 0.1 reshape.19
  5.9 0.0 collective-permute-done.7.refs_1_
  5.9 2.2 %collective-permute-start.8 = (bf16[2,96,256]{2,1,0:T(8,128)(2,1)S(1)}, bf16[2,96,256]{2,1,0:T(8,128)(2,1)S(1)}, u32[]{:S(2)}, u32[]{:S(2)}) collective-permute-start(bf16[2,96,256]{2,1,0:T(8,128)(2,1)S(1)} %stack.9.refs_0_), channel_id=1, source_target_pairs={{0,24},{4,28},{8,16},{12,20},{16,8},{20,12},{24,0},{28,4},{1,25},{... | collective-permute-start | bytes 294920 | tf_op jit(solution)/shard_map/ppermute | solution.py:197
  8.2 0.1 add_bitcast_fusion.refs_2_.refs_0_
  8.2 0.3 %collective-permute-start.11 = (bf16[2,96,256]{2,1,0:T(8,128)(2,1)S(1)}, bf16[2,96,256]{2,1,0:T(8,128)(2,1)S(1)}, u32[]{:S(2)}, u32[]{:S(2)}) collective-permute-start(bf16[2,96,256]{2,1,0:T(8,128)(2,1)S(1)} %stack.9.refs_0_), channel_id=1, source_target_pairs={{0,8},{4,12},{8,0},{12,4},{16,24},{20,28},{24,16},{28,20},{1,9},{5... | collective-permute-start | bytes 294920 | tf_op jit(solution)/shard_map/ppermute | solution.py:197
  8.5 0.2 collective-permute-start.10
  8.7 0.0 collective-permute-done.1.refs_1_
  8.7 1.7 %collective-permute-done.refs_0_ = bf16[1,96,256]{2,1,0:T(8,128)(2,1)S(1)} collective-permute-done((bf16[1,96,256]{2,1,0:T(8,128)(2,1)S(1)}, bf16[1,96,256]{2,1,0:T(8,128)(2,1)S(1)}, u32[]{:S(2)}, u32[]{:S(2)}) %collective-permute-start) | collective-permute-done | bytes 49184 | tf_op jit(solution)/shard_map/ppermute | solution.py:197
  10.5 2.2 %collective-permute-start.2 = (bf16[2,96,256]{2,1,0:T(8,128)(2,1)S(1)}, bf16[2,96,256]{2,1,0:T(8,128)(2,1)S(1)}, u32[]{:S(2)}, u32[]{:S(2)}) collective-permute-start(bf16[2,96,256]{2,1,0:T(8,128)(2,1)S(1)} %stack.6.refs_0_), channel_id=1, source_target_pairs={{0,24},{4,28},{8,16},{12,20},{16,8},{20,12},{24,0},{28,4},{1,25},{... | collective-permute-start | bytes 294920 | tf_op jit(solution)/shard_map/ppermute | solution.py:197
  12.7 0.3 %collective-permute-start.5 = (bf16[2,96,256]{2,1,0:T(8,128)(2,1)S(1)}, bf16[2,96,256]{2,1,0:T(8,128)(2,1)S(1)}, u32[]{:S(2)}, u32[]{:S(2)}) collective-permute-start(bf16[2,96,256]{2,1,0:T(8,128)(2,1)S(1)} %stack.6.refs_0_), channel_id=1, source_target_pairs={{0,8},{4,12},{8,0},{12,4},{16,24},{20,28},{24,16},{28,20},{1,9},{5... | collective-permute-start | bytes 294920 | tf_op jit(solution)/shard_map/ppermute | solution.py:197
  12.9 0.0 collective-permute-done.8.refs_1_
  12.9 0.2 collective-permute-start.4
  13.2 0.0 collective-permute-done.11.refs_1_
  13.2 2.8 %collective-permute-start.9 = (bf16[4,96,256]{2,1,0:T(8,128)(2,1)S(1)}, bf16[4,96,256]{2,1,0:T(8,128)(2,1)S(1)}, u32[]{:S(2)}, u32[]{:S(2)}) collective-permute-start(bf16[4,96,256]{2,1,0:T(8,128)(2,1)S(1)} %stack.10.refs_1_), channel_id=1, source_target_pairs={{0,4},{4,0},{8,12},{12,8},{16,20},{20,16},{24,28},{28,24},{1,5},{5... | collective-permute-start | bytes 589832 | tf_op jit(solution)/shard_map/ppermute | solution.py:197
  16.0 0.0 collective-permute-done.10.refs_0_
  16.0 0.1 collective-permute-start.12
  16.1 0.0 collective-permute-done.2.refs_1_
  16.1 2.0 %collective-permute-start.3 = (bf16[4,96,256]{2,1,0:T(8,128)(2,1)S(1)}, bf16[4,96,256]{2,1,0:T(8,128)(2,1)S(1)}, u32[]{:S(2)}, u32[]{:S(2)}) collective-permute-start(bf16[4,96,256]{2,1,0:T(8,128)(2,1)S(1)} %stack.7.refs_1_), channel_id=1, source_target_pairs={{0,4},{4,0},{8,12},{12,8},{16,20},{20,16},{24,28},{28,24},{1,5},{5... | collective-permute-start | bytes 589832 | tf_op jit(solution)/shard_map/ppermute | solution.py:197
  18.1 0.0 collective-permute-done.5.refs_1_
  18.1 0.0 collective-permute-done.4.refs_0_
  18.1 2.0 %collective-permute-start.6 = (bf16[4,96,256]{2,1,0:T(8,128)(2,1)S(1)}, bf16[4,96,256]{2,1,0:T(8,128)(2,1)S(1)}, u32[]{:S(2)}, u32[]{:S(2)}) collective-permute-start(bf16[4,96,256]{2,1,0:T(8,128)(2,1)S(1)} %stack.8.refs_3_), channel_id=1, source_target_pairs={{0,4},{4,0},{8,12},{12,8},{16,20},{20,16},{24,28},{28,24},{1,5},{5... | collective-permute-start | bytes 589832 | tf_op jit(solution)/shard_map/ppermute | solution.py:197
  20.1 0.0 collective-permute-done.9.refs_2_
  20.1 0.0 collective-permute-done.12.refs_4_
  20.1 1.7 %correlate.1.refs_5_ = f32[2,4,8,128,128]{4,3,2,1,0:T(8,128)S(1)} custom-call(s32[1,5]{1,0:T(1,128)S(1)} %add_bitcast_fusion.refs_2_.refs_0_, bf16[4,96,256]{2,1,0:T(8,128)(2,1)S(1)} %stack.10.refs_1_, bf16[4,96,256]{2,1,0:T(8,128)(2,1)S(1)} %collective-permute-done.9.refs_2_, bf16[4,96,256]{2,1,0:T(8,128)(2,1)S(1)} %stack.11.refs_3_, ...), custom_call_target="tpu_custom_call" | custom-call | tf_op jit(solution)/shard_map/correlate/pallas_call | solution.py:179
  21.8 0.0 collective-permute-done.3.refs_2_
  21.8 0.0 collective-permute-done.6.refs_4_
  21.8 2.9 %correlate_add.1 = f32[2,4,8,128,128]{4,3,2,1,0:T(8,128)} custom-call(s32[1,5]{1,0:T(1,128)S(1)} %add_bitcast_fusion.refs_2_.refs_0_, bf16[4,96,256]{2,1,0:T(8,128)(2,1)S(1)} %stack.7.refs_1_, bf16[4,96,256]{2,1,0:T(8,128)(2,1)S(1)} %collective-permute-done.3.refs_2_, bf16[4,96,256]{2,1,0:T(8,128)(2,1)S(1)} %stack.8.refs_3_, ...), custom_call_target="tpu_custom_call" | custom-call | tf_op jit(solution)/shard_map/correlate_add/pallas_call | solution.py:179
  (6 shorter events, 0.1 us)
Async XLA Ops:
  0.0 5.7 %copy-start = (s32[8,2]{0,1:T(2,128)S(1)}, s32[8,2]{0,1:T(2,128)}, u32[]{:S(2)}) copy-start(s32[8,2]{0,1:T(2,128)} %param.5) | copy-start | bytes 196
  1.2 4.8 %collective-permute-start.7 = (bf16[1,96,256]{2,1,0:T(8,128)(2,1)S(1)}, bf16[1,96,256]{2,1,0:T(8,128)(2,1)S(1)}, u32[]{:S(2)}, u32[]{:S(2)}) collective-permute-start(bf16[1,96,256]{2,1,0:T(8,128)(2,1)S(1)} %bitcast.7), channel_id=1, source_target_pairs={{0,1},{1,0},{2,3},{3,2},{4,5},{5,4},{6,7},{7,6},{8,9},{9,8},{10,11... | collective-permute-start | bytes 147464 | tf_op jit(solution)/shard_map/ppermute | solution.py:197
  3.4 5.4 %collective-permute-start.1 = (bf16[1,96,256]{2,1,0:T(8,128)(2,1)S(1)}, bf16[1,96,256]{2,1,0:T(8,128)(2,1)S(1)}, u32[]{:S(2)}, u32[]{:S(2)}) collective-permute-start(bf16[1,96,256]{2,1,0:T(8,128)(2,1)S(1)} %bitcast.8), channel_id=1, source_target_pairs={{0,3},{1,2},{2,1},{3,0},{4,7},{5,6},{6,5},{7,4},{8,11},{9,10},{10,... | collective-permute-start | bytes 147464 | tf_op jit(solution)/shard_map/ppermute | solution.py:197
  5.6 4.9 %collective-permute-start = (bf16[1,96,256]{2,1,0:T(8,128)(2,1)S(1)}, bf16[1,96,256]{2,1,0:T(8,128)(2,1)S(1)}, u32[]{:S(2)}, u32[]{:S(2)}) collective-permute-start(bf16[1,96,256]{2,1,0:T(8,128)(2,1)S(1)} %bitcast.9), channel_id=1, source_target_pairs={{0,2},{1,3},{2,0},{3,1},{4,6},{5,7},{6,4},{7,5},{8,10},{9,11},{10,... | collective-permute-start | bytes 147464 | tf_op jit(solution)/shard_map/ppermute | solution.py:197
  5.9 7.0 %collective-permute-start.8 = (bf16[2,96,256]{2,1,0:T(8,128)(2,1)S(1)}, bf16[2,96,256]{2,1,0:T(8,128)(2,1)S(1)}, u32[]{:S(2)}, u32[]{:S(2)}) collective-permute-start(bf16[2,96,256]{2,1,0:T(8,128)(2,1)S(1)} %stack.9.refs_0_), channel_id=1, source_target_pairs={{0,24},{4,28},{8,16},{12,20},{16,8},{20,12},{24,0},{28,4},{1,25},{... | collective-permute-start | bytes 294920 | tf_op jit(solution)/shard_map/ppermute | solution.py:197
  8.2 4.9 %collective-permute-start.11 = (bf16[2,96,256]{2,1,0:T(8,128)(2,1)S(1)}, bf16[2,96,256]{2,1,0:T(8,128)(2,1)S(1)}, u32[]{:S(2)}, u32[]{:S(2)}) collective-permute-start(bf16[2,96,256]{2,1,0:T(8,128)(2,1)S(1)} %stack.9.refs_0_), channel_id=1, source_target_pairs={{0,8},{4,12},{8,0},{12,4},{16,24},{20,28},{24,16},{28,20},{1,9},{5... | collective-permute-start | bytes 294920 | tf_op jit(solution)/shard_map/ppermute | solution.py:197
  8.5 7.5 %collective-permute-start.10 = (bf16[2,96,256]{2,1,0:T(8,128)(2,1)S(1)}, bf16[2,96,256]{2,1,0:T(8,128)(2,1)S(1)}, u32[]{:S(2)}, u32[]{:S(2)}) collective-permute-start(bf16[2,96,256]{2,1,0:T(8,128)(2,1)S(1)} %stack.9.refs_0_), channel_id=1, source_target_pairs={{0,16},{4,20},{8,24},{12,28},{16,0},{20,4},{24,8},{28,12},{1,17},{... | collective-permute-start | bytes 294920 | tf_op jit(solution)/shard_map/ppermute | solution.py:197
  10.5 5.6 %collective-permute-start.2 = (bf16[2,96,256]{2,1,0:T(8,128)(2,1)S(1)}, bf16[2,96,256]{2,1,0:T(8,128)(2,1)S(1)}, u32[]{:S(2)}, u32[]{:S(2)}) collective-permute-start(bf16[2,96,256]{2,1,0:T(8,128)(2,1)S(1)} %stack.6.refs_0_), channel_id=1, source_target_pairs={{0,24},{4,28},{8,16},{12,20},{16,8},{20,12},{24,0},{28,4},{1,25},{... | collective-permute-start | bytes 294920 | tf_op jit(solution)/shard_map/ppermute | solution.py:197
  12.7 5.4 %collective-permute-start.5 = (bf16[2,96,256]{2,1,0:T(8,128)(2,1)S(1)}, bf16[2,96,256]{2,1,0:T(8,128)(2,1)S(1)}, u32[]{:S(2)}, u32[]{:S(2)}) collective-permute-start(bf16[2,96,256]{2,1,0:T(8,128)(2,1)S(1)} %stack.6.refs_0_), channel_id=1, source_target_pairs={{0,8},{4,12},{8,0},{12,4},{16,24},{20,28},{24,16},{28,20},{1,9},{5... | collective-permute-start | bytes 294920 | tf_op jit(solution)/shard_map/ppermute | solution.py:197
  12.9 5.1 %collective-permute-start.4 = (bf16[2,96,256]{2,1,0:T(8,128)(2,1)S(1)}, bf16[2,96,256]{2,1,0:T(8,128)(2,1)S(1)}, u32[]{:S(2)}, u32[]{:S(2)}) collective-permute-start(bf16[2,96,256]{2,1,0:T(8,128)(2,1)S(1)} %stack.6.refs_0_), channel_id=1, source_target_pairs={{0,16},{4,20},{8,24},{12,28},{16,0},{20,4},{24,8},{28,12},{1,17},{... | collective-permute-start | bytes 294920 | tf_op jit(solution)/shard_map/ppermute | solution.py:197
  13.2 6.9 %collective-permute-start.9 = (bf16[4,96,256]{2,1,0:T(8,128)(2,1)S(1)}, bf16[4,96,256]{2,1,0:T(8,128)(2,1)S(1)}, u32[]{:S(2)}, u32[]{:S(2)}) collective-permute-start(bf16[4,96,256]{2,1,0:T(8,128)(2,1)S(1)} %stack.10.refs_1_), channel_id=1, source_target_pairs={{0,4},{4,0},{8,12},{12,8},{16,20},{20,16},{24,28},{28,24},{1,5},{5... | collective-permute-start | bytes 589832 | tf_op jit(solution)/shard_map/ppermute | solution.py:197
  16.0 4.1 %collective-permute-start.12 = (bf16[4,96,256]{2,1,0:T(8,128)(2,1)S(1)}, bf16[4,96,256]{2,1,0:T(8,128)(2,1)S(1)}, u32[]{:S(2)}, u32[]{:S(2)}) collective-permute-start(bf16[4,96,256]{2,1,0:T(8,128)(2,1)S(1)} %stack.11.refs_3_), channel_id=1, source_target_pairs={{0,4},{4,0},{8,12},{12,8},{16,20},{20,16},{24,28},{28,24},{1,5},{5... | collective-permute-start | bytes 589832 | tf_op jit(solution)/shard_map/ppermute | solution.py:197
  16.1 5.7 %collective-permute-start.3 = (bf16[4,96,256]{2,1,0:T(8,128)(2,1)S(1)}, bf16[4,96,256]{2,1,0:T(8,128)(2,1)S(1)}, u32[]{:S(2)}, u32[]{:S(2)}) collective-permute-start(bf16[4,96,256]{2,1,0:T(8,128)(2,1)S(1)} %stack.7.refs_1_), channel_id=1, source_target_pairs={{0,4},{4,0},{8,12},{12,8},{16,20},{20,16},{24,28},{28,24},{1,5},{5... | collective-permute-start | bytes 589832 | tf_op jit(solution)/shard_map/ppermute | solution.py:197
  18.1 3.7 %collective-permute-start.6 = (bf16[4,96,256]{2,1,0:T(8,128)(2,1)S(1)}, bf16[4,96,256]{2,1,0:T(8,128)(2,1)S(1)}, u32[]{:S(2)}, u32[]{:S(2)}) collective-permute-start(bf16[4,96,256]{2,1,0:T(8,128)(2,1)S(1)} %stack.8.refs_3_), channel_id=1, source_target_pairs={{0,4},{4,0},{8,12},{12,8},{16,20},{20,16},{24,28},{28,24},{1,5},{5... | collective-permute-start | bytes 589832 | tf_op jit(solution)/shard_map/ppermute | solution.py:197

commit v24 on v22

--- a/solution.py
+++ b/solution.py
@@ -116,46 +116,54 @@
         ref[slot, rows_at, g * lanes:g * lanes + half] = value[0].astype(jnp.bfloat16)
         ref[slot, rows_at, g * lanes + half:(g + 1) * lanes] = value[1].astype(jnp.bfloat16)
 
-    copies = []
-    for i, t in enumerate(picked):
-        slot = i % left_turned.shape[0]
-        left_block, right_block = where_ref[0, 1 + 2 * t], where_ref[0, 2 + 2 * t]
+    def turn_left(i):
         for g in range(groups):
-            re, im = load(left_block, g)
+            re, im = load(where_ref[0, 1 + 2 * picked[i]], g)
             for k in (4, 12):
                 forward, backward = turn_by(re, im, *(norm * part for part in table[k]), True)
-                store(left_turned, slot, COARSE.index(k), g, forward)
-                store(left_turned, slot, COARSE.index(-k), g, backward)
-        for j in range(len(FINE_PAIRS)):
-            for g in range(groups):
-                re, im = load(right_block, g)
-                if j == 0:
-                    store(right_turned, slot, 0, g, turn_by(re, im, *table[4], False)[0])
-                    store(right_turned, slot, 1, g, (re, im))
+                store(left_turned, i % slots, COARSE.index(k), g, forward)
+                store(left_turned, i % slots, COARSE.index(-k), g, backward)
+
+    def turn_right(i, j):
+        for g in range(groups):
+            re, im = load(where_ref[0, 2 + 2 * picked[i]], g)
+            if j == 0:
+                turns = (turn_by(re, im, *table[4], False)[0], (re, im))
+            else:
+                turns = turn_by(re, im, *table[j], True)
+            for s in range(2):
+                store(right_turned, i % slots, 2 * j + s, g, turns[s])
+
+    slots = left_turned.shape[0]
+    copies = []
+    steps = [(i, j) for i in range(len(picked)) for j in range(len(FINE_PAIRS))]
+    turn_left(0)
+    turn_right(0, 0)
+    for (i, j), after in zip(steps, steps[1:] + [None]):
+        for u in range(0, len(COARSE), 2):
+            if u and after:
+                if after[1] == 0:
+                    turn_left(after[0])
+                turn_right(*after)
+            total = lax.dot_general(
+                left_turned[i % slots, u * TILE:(u + 2) * TILE, :],
+                right_turned[i % slots, 2 * j * TILE:2 * (j + 1) * TILE, :],
+                (((1,), (1,)), ((), ())),
+                preferred_element_type=jnp.float32,
+            )
+            for v, s in ((0, 0), (0, 1), (1, 0), (1, 1)):
+                fine = FINE_PAIRS[j][s] + 4
+                value = total[v * TILE:(v + 1) * TILE, s * TILE:(s + 1) * TILE]
+                if adds:
+                    each = len(picked) // adds
+                    more[0][i, u + v, fine] = partials[i // each][i % each, u + v, fine] + value
                 else:
-                    forward, backward = turn_by(re, im, *table[j], True)
-                    store(right_turned, slot, 2 * j, g, forward)
-                    store(right_turned, slot, 2 * j + 1, g, backward)
-            for u in range(0, len(COARSE), 2):
-                total = lax.dot_general(
-                    left_turned[slot, u * TILE:(u + 2) * TILE, :],
-                    right_turned[slot, 2 * j * TILE:2 * (j + 1) * TILE, :],
-                    (((1,), (1,)), ((), ())),
-                    preferred_element_type=jnp.float32,
-                )
-                for v, s in ((0, 0), (0, 1), (1, 0), (1, 1)):
-                    fine = FINE_PAIRS[j][s] + 4
-                    value = total[v * TILE:(v + 1) * TILE, s * TILE:(s + 1) * TILE]
-                    if adds:
-                        each = len(picked) // adds
-                        more[0][i, u + v, fine] = partials[i // each][i % each, u + v, fine] + value
-                    else:
-                        out_ref[i, u + v, fine] = value
-            for s in range(2 if adds else 0):
-                done = (i, slice(None), FINE_PAIRS[j][s] + 4)
-                copy = pltpu.make_async_copy(more[0].at[done], out_ref.at[done], more[1])
-                copy.start(priority=s)
-                copies.append(copy)
+                    out_ref[i, u + v, fine] = value
+        for s in range(2 if adds else 0):
+            done = (i, slice(None), FINE_PAIRS[j][s] + 4)
+            copy = pltpu.make_async_copy(more[0].at[done], out_ref.at[done], more[1])
+            copy.start(priority=s)
+            copies.append(copy)
     for copy in copies:
         copy.wait()
 

time: 24.5 us -> 24.5 us (level)
  no operation moved by 1% of the time
where the time goes in v24:
time: 24.5 us; the launch traced here: 24.4 us
  starting transfers between devices  16.7 us (68%)
  Pallas kernels  5.5 us (22%)
  waiting for transfers between devices  1.74 us (7%)
  local copies, waits for them, and re-layouts  0.26 us (1%)
    ppermute x13, starting transfers between devices, swap(): lax.ppermute(array, axis, [(i, i ^ k) for i in range(lax.axis_size(axis))])  16.7 us
    pallas_call x2, Pallas kernels, correlate(): pl.pallas_call(lambda *refs: correlate_kernel(norm, picked, adds, places,...  4.27 us
    ppermute x13, waiting for transfers between devices, swap(): lax.ppermute(array, axis, [(i, i ^ k) for i in range(lax.axis_size(axis))])  1.74 us
    pallas_call x1, Pallas kernels, whiten(): pl.pallas_call(whiten_kernel, out_shape=jax.ShapeDtypeStruct((chans, spec...  1.15 us
  transfers between devices with their start and end apart: 13, of which 1 were waited for; matrix products, arithmetic and copies ran while one was open for 1% of the time, Pallas kernels for 7%

profile of v24, /device:TPU:1, one launch (start us, length us, event | category | flops | bytes accessed | tf_op | source)
XLA Modules:
  0.0 24.4 jit_solution(5276281090176931394)
XLA Ops:
  0.0 0.0 copy-start
  0.0 1.2 %whiten.1 = bf16[96,256]{1,0:T(8,128)(2,1)S(1)} custom-call(bf16[256,96]{1,0:T(8,128)(2,1)} %bitcast.11, s32[1,96]{1,0:T(1,128)} %bitcast.12), custom_call_target="tpu_custom_call" | custom-call | tf_op jit(solution)/shard_map/whiten/pallas_call | solution.py:56
  1.2 2.2 %collective-permute-start.7 = (bf16[1,96,256]{2,1,0:T(8,128)(2,1)S(1)}, bf16[1,96,256]{2,1,0:T(8,128)(2,1)S(1)}, u32[]{:S(2)}, u32[]{:S(2)}) collective-permute-start(bf16[1,96,256]{2,1,0:T(8,128)(2,1)S(1)} %bitcast.7), channel_id=1, source_target_pairs={{0,1},{1,0},{2,3},{3,2},{4,5},{5,4},{6,7},{7,6},{8,9},{9,8},{10,11... | collective-permute-start | bytes 147464 | tf_op jit(solution)/shard_map/ppermute | solution.py:204
  3.4 2.2 %collective-permute-start.1 = (bf16[1,96,256]{2,1,0:T(8,128)(2,1)S(1)}, bf16[1,96,256]{2,1,0:T(8,128)(2,1)S(1)}, u32[]{:S(2)}, u32[]{:S(2)}) collective-permute-start(bf16[1,96,256]{2,1,0:T(8,128)(2,1)S(1)} %bitcast.8), channel_id=1, source_target_pairs={{0,3},{1,2},{2,1},{3,0},{4,7},{5,6},{6,5},{7,4},{8,11},{9,10},{10,... | collective-permute-start | bytes 147464 | tf_op jit(solution)/shard_map/ppermute | solution.py:204
  5.6 0.1 collective-permute-start
  5.7 0.0 copy-done
  5.7 0.1 constant_dynamic-slice_fusion
  5.7 0.1 copy.4
  5.8 0.1 reshape.19
  5.9 0.0 collective-permute-done.7.refs_1_
  5.9 2.2 %collective-permute-start.8 = (bf16[2,96,256]{2,1,0:T(8,128)(2,1)S(1)}, bf16[2,96,256]{2,1,0:T(8,128)(2,1)S(1)}, u32[]{:S(2)}, u32[]{:S(2)}) collective-permute-start(bf16[2,96,256]{2,1,0:T(8,128)(2,1)S(1)} %stack.9.refs_0_), channel_id=1, source_target_pairs={{0,24},{4,28},{8,16},{12,20},{16,8},{20,12},{24,0},{28,4},{1,25},{... | collective-permute-start | bytes 294920 | tf_op jit(solution)/shard_map/ppermute | solution.py:204
  8.2 0.1 add_bitcast_fusion.refs_2_.refs_0_
  8.2 0.3 %collective-permute-start.11 = (bf16[2,96,256]{2,1,0:T(8,128)(2,1)S(1)}, bf16[2,96,256]{2,1,0:T(8,128)(2,1)S(1)}, u32[]{:S(2)}, u32[]{:S(2)}) collective-permute-start(bf16[2,96,256]{2,1,0:T(8,128)(2,1)S(1)} %stack.9.refs_0_), channel_id=1, source_target_pairs={{0,8},{4,12},{8,0},{12,4},{16,24},{20,28},{24,16},{28,20},{1,9},{5... | collective-permute-start | bytes 294920 | tf_op jit(solution)/shard_map/ppermute | solution.py:204
  8.5 0.2 collective-permute-start.10
  8.7 0.0 collective-permute-done.1.refs_1_
  8.7 1.7 %collective-permute-done.refs_0_ = bf16[1,96,256]{2,1,0:T(8,128)(2,1)S(1)} collective-permute-done((bf16[1,96,256]{2,1,0:T(8,128)(2,1)S(1)}, bf16[1,96,256]{2,1,0:T(8,128)(2,1)S(1)}, u32[]{:S(2)}, u32[]{:S(2)}) %collective-permute-start) | collective-permute-done | bytes 49184 | tf_op jit(solution)/shard_map/ppermute | solution.py:204
  10.5 2.2 %collective-permute-start.2 = (bf16[2,96,256]{2,1,0:T(8,128)(2,1)S(1)}, bf16[2,96,256]{2,1,0:T(8,128)(2,1)S(1)}, u32[]{:S(2)}, u32[]{:S(2)}) collective-permute-start(bf16[2,96,256]{2,1,0:T(8,128)(2,1)S(1)} %stack.6.refs_0_), channel_id=1, source_target_pairs={{0,24},{4,28},{8,16},{12,20},{16,8},{20,12},{24,0},{28,4},{1,25},{... | collective-permute-start | bytes 294920 | tf_op jit(solution)/shard_map/ppermute | solution.py:204
  12.7 0.3 %collective-permute-start.5 = (bf16[2,96,256]{2,1,0:T(8,128)(2,1)S(1)}, bf16[2,96,256]{2,1,0:T(8,128)(2,1)S(1)}, u32[]{:S(2)}, u32[]{:S(2)}) collective-permute-start(bf16[2,96,256]{2,1,0:T(8,128)(2,1)S(1)} %stack.6.refs_0_), channel_id=1, source_target_pairs={{0,8},{4,12},{8,0},{12,4},{16,24},{20,28},{24,16},{28,20},{1,9},{5... | collective-permute-start | bytes 294920 | tf_op jit(solution)/shard_map/ppermute | solution.py:204
  12.9 0.0 collective-permute-done.8.refs_1_
  12.9 0.2 collective-permute-start.4
  13.2 0.0 collective-permute-done.11.refs_1_
  13.2 2.8 %collective-permute-start.9 = (bf16[4,96,256]{2,1,0:T(8,128)(2,1)S(1)}, bf16[4,96,256]{2,1,0:T(8,128)(2,1)S(1)}, u32[]{:S(2)}, u32[]{:S(2)}) collective-permute-start(bf16[4,96,256]{2,1,0:T(8,128)(2,1)S(1)} %stack.10.refs_1_), channel_id=1, source_target_pairs={{0,4},{4,0},{8,12},{12,8},{16,20},{20,16},{24,28},{28,24},{1,5},{5... | collective-permute-start | bytes 589832 | tf_op jit(solution)/shard_map/ppermute | solution.py:204
  16.0 0.0 collective-permute-done.10.refs_0_
  16.0 0.1 collective-permute-start.12
  16.1 0.0 collective-permute-done.2.refs_1_
  16.1 2.0 %collective-permute-start.3 = (bf16[4,96,256]{2,1,0:T(8,128)(2,1)S(1)}, bf16[4,96,256]{2,1,0:T(8,128)(2,1)S(1)}, u32[]{:S(2)}, u32[]{:S(2)}) collective-permute-start(bf16[4,96,256]{2,1,0:T(8,128)(2,1)S(1)} %stack.7.refs_1_), channel_id=1, source_target_pairs={{0,4},{4,0},{8,12},{12,8},{16,20},{20,16},{24,28},{28,24},{1,5},{5... | collective-permute-start | bytes 589832 | tf_op jit(solution)/shard_map/ppermute | solution.py:204
  18.1 0.0 collective-permute-done.5.refs_1_
  18.1 0.0 collective-permute-done.4.refs_0_
  18.1 2.0 %collective-permute-start.6 = (bf16[4,96,256]{2,1,0:T(8,128)(2,1)S(1)}, bf16[4,96,256]{2,1,0:T(8,128)(2,1)S(1)}, u32[]{:S(2)}, u32[]{:S(2)}) collective-permute-start(bf16[4,96,256]{2,1,0:T(8,128)(2,1)S(1)} %stack.8.refs_3_), channel_id=1, source_target_pairs={{0,4},{4,0},{8,12},{12,8},{16,20},{20,16},{24,28},{28,24},{1,5},{5... | collective-permute-start | bytes 589832 | tf_op jit(solution)/shard_map/ppermute | solution.py:204
  20.1 0.0 collective-permute-done.9.refs_2_
  20.1 0.0 collective-permute-done.12.refs_4_
  20.1 1.6 %correlate.1.refs_5_ = f32[2,4,8,128,128]{4,3,2,1,0:T(8,128)S(1)} custom-call(s32[1,5]{1,0:T(1,128)S(1)} %add_bitcast_fusion.refs_2_.refs_0_, bf16[4,96,256]{2,1,0:T(8,128)(2,1)S(1)} %stack.10.refs_1_, bf16[4,96,256]{2,1,0:T(8,128)(2,1)S(1)} %collective-permute-done.9.refs_2_, bf16[4,96,256]{2,1,0:T(8,128)(2,1)S(1)} %stack.11.refs_3_, ...), custom_call_target="tpu_custom_call" | custom-call | tf_op jit(solution)/shard_map/correlate/pallas_call | solution.py:186
  21.7 0.0 collective-permute-done.3.refs_2_
  21.7 0.0 collective-permute-done.6.refs_4_
  21.7 2.7 %correlate_add.1 = f32[2,4,8,128,128]{4,3,2,1,0:T(8,128)} custom-call(s32[1,5]{1,0:T(1,128)S(1)} %add_bitcast_fusion.refs_2_.refs_0_, bf16[4,96,256]{2,1,0:T(8,128)(2,1)S(1)} %stack.7.refs_1_, bf16[4,96,256]{2,1,0:T(8,128)(2,1)S(1)} %collective-permute-done.3.refs_2_, bf16[4,96,256]{2,1,0:T(8,128)(2,1)S(1)} %stack.8.refs_3_, ...), custom_call_target="tpu_custom_call" | custom-call | tf_op jit(solution)/shard_map/correlate_add/pallas_call | solution.py:186
  (6 shorter events, 0.1 us)
Async XLA Ops:
  0.0 5.7 %copy-start = (s32[8,2]{0,1:T(2,128)S(1)}, s32[8,2]{0,1:T(2,128)}, u32[]{:S(2)}) copy-start(s32[8,2]{0,1:T(2,128)} %param.5) | copy-start | bytes 196
  1.2 4.8 %collective-permute-start.7 = (bf16[1,96,256]{2,1,0:T(8,128)(2,1)S(1)}, bf16[1,96,256]{2,1,0:T(8,128)(2,1)S(1)}, u32[]{:S(2)}, u32[]{:S(2)}) collective-permute-start(bf16[1,96,256]{2,1,0:T(8,128)(2,1)S(1)} %bitcast.7), channel_id=1, source_target_pairs={{0,1},{1,0},{2,3},{3,2},{4,5},{5,4},{6,7},{7,6},{8,9},{9,8},{10,11... | collective-permute-start | bytes 147464 | tf_op jit(solution)/shard_map/ppermute | solution.py:204
  3.4 5.4 %collective-permute-start.1 = (bf16[1,96,256]{2,1,0:T(8,128)(2,1)S(1)}, bf16[1,96,256]{2,1,0:T(8,128)(2,1)S(1)}, u32[]{:S(2)}, u32[]{:S(2)}) collective-permute-start(bf16[1,96,256]{2,1,0:T(8,128)(2,1)S(1)} %bitcast.8), channel_id=1, source_target_pairs={{0,3},{1,2},{2,1},{3,0},{4,7},{5,6},{6,5},{7,4},{8,11},{9,10},{10,... | collective-permute-start | bytes 147464 | tf_op jit(solution)/shard_map/ppermute | solution.py:204
  5.6 4.9 %collective-permute-start = (bf16[1,96,256]{2,1,0:T(8,128)(2,1)S(1)}, bf16[1,96,256]{2,1,0:T(8,128)(2,1)S(1)}, u32[]{:S(2)}, u32[]{:S(2)}) collective-permute-start(bf16[1,96,256]{2,1,0:T(8,128)(2,1)S(1)} %bitcast.9), channel_id=1, source_target_pairs={{0,2},{1,3},{2,0},{3,1},{4,6},{5,7},{6,4},{7,5},{8,10},{9,11},{10,... | collective-permute-start | bytes 147464 | tf_op jit(solution)/shard_map/ppermute | solution.py:204
  5.9 7.0 %collective-permute-start.8 = (bf16[2,96,256]{2,1,0:T(8,128)(2,1)S(1)}, bf16[2,96,256]{2,1,0:T(8,128)(2,1)S(1)}, u32[]{:S(2)}, u32[]{:S(2)}) collective-permute-start(bf16[2,96,256]{2,1,0:T(8,128)(2,1)S(1)} %stack.9.refs_0_), channel_id=1, source_target_pairs={{0,24},{4,28},{8,16},{12,20},{16,8},{20,12},{24,0},{28,4},{1,25},{... | collective-permute-start | bytes 294920 | tf_op jit(solution)/shard_map/ppermute | solution.py:204
  8.2 4.9 %collective-permute-start.11 = (bf16[2,96,256]{2,1,0:T(8,128)(2,1)S(1)}, bf16[2,96,256]{2,1,0:T(8,128)(2,1)S(1)}, u32[]{:S(2)}, u32[]{:S(2)}) collective-permute-start(bf16[2,96,256]{2,1,0:T(8,128)(2,1)S(1)} %stack.9.refs_0_), channel_id=1, source_target_pairs={{0,8},{4,12},{8,0},{12,4},{16,24},{20,28},{24,16},{28,20},{1,9},{5... | collective-permute-start | bytes 294920 | tf_op jit(solution)/shard_map/ppermute | solution.py:204
  8.5 7.5 %collective-permute-start.10 = (bf16[2,96,256]{2,1,0:T(8,128)(2,1)S(1)}, bf16[2,96,256]{2,1,0:T(8,128)(2,1)S(1)}, u32[]{:S(2)}, u32[]{:S(2)}) collective-permute-start(bf16[2,96,256]{2,1,0:T(8,128)(2,1)S(1)} %stack.9.refs_0_), channel_id=1, source_target_pairs={{0,16},{4,20},{8,24},{12,28},{16,0},{20,4},{24,8},{28,12},{1,17},{... | collective-permute-start | bytes 294920 | tf_op jit(solution)/shard_map/ppermute | solution.py:204
  10.5 5.6 %collective-permute-start.2 = (bf16[2,96,256]{2,1,0:T(8,128)(2,1)S(1)}, bf16[2,96,256]{2,1,0:T(8,128)(2,1)S(1)}, u32[]{:S(2)}, u32[]{:S(2)}) collective-permute-start(bf16[2,96,256]{2,1,0:T(8,128)(2,1)S(1)} %stack.6.refs_0_), channel_id=1, source_target_pairs={{0,24},{4,28},{8,16},{12,20},{16,8},{20,12},{24,0},{28,4},{1,25},{... | collective-permute-start | bytes 294920 | tf_op jit(solution)/shard_map/ppermute | solution.py:204
  12.7 5.4 %collective-permute-start.5 = (bf16[2,96,256]{2,1,0:T(8,128)(2,1)S(1)}, bf16[2,96,256]{2,1,0:T(8,128)(2,1)S(1)}, u32[]{:S(2)}, u32[]{:S(2)}) collective-permute-start(bf16[2,96,256]{2,1,0:T(8,128)(2,1)S(1)} %stack.6.refs_0_), channel_id=1, source_target_pairs={{0,8},{4,12},{8,0},{12,4},{16,24},{20,28},{24,16},{28,20},{1,9},{5... | collective-permute-start | bytes 294920 | tf_op jit(solution)/shard_map/ppermute | solution.py:204
  12.9 5.1 %collective-permute-start.4 = (bf16[2,96,256]{2,1,0:T(8,128)(2,1)S(1)}, bf16[2,96,256]{2,1,0:T(8,128)(2,1)S(1)}, u32[]{:S(2)}, u32[]{:S(2)}) collective-permute-start(bf16[2,96,256]{2,1,0:T(8,128)(2,1)S(1)} %stack.6.refs_0_), channel_id=1, source_target_pairs={{0,16},{4,20},{8,24},{12,28},{16,0},{20,4},{24,8},{28,12},{1,17},{... | collective-permute-start | bytes 294920 | tf_op jit(solution)/shard_map/ppermute | solution.py:204
  13.2 6.9 %collective-permute-start.9 = (bf16[4,96,256]{2,1,0:T(8,128)(2,1)S(1)}, bf16[4,96,256]{2,1,0:T(8,128)(2,1)S(1)}, u32[]{:S(2)}, u32[]{:S(2)}) collective-permute-start(bf16[4,96,256]{2,1,0:T(8,128)(2,1)S(1)} %stack.10.refs_1_), channel_id=1, source_target_pairs={{0,4},{4,0},{8,12},{12,8},{16,20},{20,16},{24,28},{28,24},{1,5},{5... | collective-permute-start | bytes 589832 | tf_op jit(solution)/shard_map/ppermute | solution.py:204
  16.0 4.1 %collective-permute-start.12 = (bf16[4,96,256]{2,1,0:T(8,128)(2,1)S(1)}, bf16[4,96,256]{2,1,0:T(8,128)(2,1)S(1)}, u32[]{:S(2)}, u32[]{:S(2)}) collective-permute-start(bf16[4,96,256]{2,1,0:T(8,128)(2,1)S(1)} %stack.11.refs_3_), channel_id=1, source_target_pairs={{0,4},{4,0},{8,12},{12,8},{16,20},{20,16},{24,28},{28,24},{1,5},{5... | collective-permute-start | bytes 589832 | tf_op jit(solution)/shard_map/ppermute | solution.py:204
  16.1 5.6 %collective-permute-start.3 = (bf16[4,96,256]{2,1,0:T(8,128)(2,1)S(1)}, bf16[4,96,256]{2,1,0:T(8,128)(2,1)S(1)}, u32[]{:S(2)}, u32[]{:S(2)}) collective-permute-start(bf16[4,96,256]{2,1,0:T(8,128)(2,1)S(1)} %stack.7.refs_1_), channel_id=1, source_target_pairs={{0,4},{4,0},{8,12},{12,8},{16,20},{20,16},{24,28},{28,24},{1,5},{5... | collective-permute-start | bytes 589832 | tf_op jit(solution)/shard_map/ppermute | solution.py:204
  18.1 3.6 %collective-permute-start.6 = (bf16[4,96,256]{2,1,0:T(8,128)(2,1)S(1)}, bf16[4,96,256]{2,1,0:T(8,128)(2,1)S(1)}, u32[]{:S(2)}, u32[]{:S(2)}) collective-permute-start(bf16[4,96,256]{2,1,0:T(8,128)(2,1)S(1)} %stack.8.refs_3_), channel_id=1, source_target_pairs={{0,4},{4,0},{8,12},{12,8},{16,20},{20,16},{24,28},{28,24},{1,5},{5... | collective-permute-start | bytes 589832 | tf_op jit(solution)/shard_map/ppermute | solution.py:204

commit v25 on v24

--- a/solution.py
+++ b/solution.py
@@ -227,7 +227,8 @@
 
 def halves(white, where):
     groups = lax.axis_size("tm")
-    blocks = [white[None]] + [swap(white[None], "tm", k) for k in range(1, groups)]
+    near_ks, far_ks = range(1, groups // 2), range(groups - 1, groups // 2 - 1, -1)
+    blocks = [white[None]] + [swap(white[None], "tm", k) for k in (*near_ks, *far_ks)]
     return stack(blocks[:groups // 2]), stack(blocks[groups // 2:], after=(where,), flops=10**9)
 
 

time: 24.5 us -> 25 us (1.020)
  starting transfers between devices: 16.7 us -> 17.1 us
    ppermute x13, starting transfers between devices: 16.7 us -> 17.1 us  [swap(): lax.ppermute(array, axis, [(i, i ^ k) for i in range(lax.axis_size(axis))])]
where the time goes in v25:
time: 25 us; the launch traced here: 24.9 us
  starting transfers between devices  17.1 us (68%)
  Pallas kernels  5.5 us (22%)
  waiting for transfers between devices  1.81 us (7%)
  local copies, waits for them, and re-layouts  0.26 us (1%)
    ppermute x13, starting transfers between devices, swap(): lax.ppermute(array, axis, [(i, i ^ k) for i in range(lax.axis_size(axis))])  17.1 us
    pallas_call x2, Pallas kernels, correlate(): pl.pallas_call(lambda *refs: correlate_kernel(norm, picked, adds, places,...  4.27 us
    ppermute x13, waiting for transfers between devices, swap(): lax.ppermute(array, axis, [(i, i ^ k) for i in range(lax.axis_size(axis))])  1.81 us
    pallas_call x1, Pallas kernels, whiten(): pl.pallas_call(whiten_kernel, out_shape=jax.ShapeDtypeStruct((chans, spec...  1.15 us
  transfers between devices with their start and end apart: 13, of which 1 were waited for; matrix products, arithmetic and copies ran while one was open for 1% of the time, Pallas kernels for 7%

profile of v25, /device:TPU:1, one launch (start us, length us, event | category | flops | bytes accessed | tf_op | source)
XLA Modules:
  0.0 24.9 jit_solution(6663311600040015565)
XLA Ops:
  0.0 0.0 copy-start
  0.0 1.2 %whiten.1 = bf16[96,256]{1,0:T(8,128)(2,1)S(1)} custom-call(bf16[256,96]{1,0:T(8,128)(2,1)} %bitcast.11, s32[1,96]{1,0:T(1,128)} %bitcast.12), custom_call_target="tpu_custom_call" | custom-call | tf_op jit(solution)/shard_map/whiten/pallas_call | solution.py:56
  1.2 2.2 %collective-permute-start.7 = (bf16[1,96,256]{2,1,0:T(8,128)(2,1)S(1)}, bf16[1,96,256]{2,1,0:T(8,128)(2,1)S(1)}, u32[]{:S(2)}, u32[]{:S(2)}) collective-permute-start(bf16[1,96,256]{2,1,0:T(8,128)(2,1)S(1)} %bitcast.7), channel_id=1, source_target_pairs={{0,1},{1,0},{2,3},{3,2},{4,5},{5,4},{6,7},{7,6},{8,9},{9,8},{10,11... | collective-permute-start | bytes 147464 | tf_op jit(solution)/shard_map/ppermute | solution.py:204
  3.4 2.3 %collective-permute-start.1 = (bf16[1,96,256]{2,1,0:T(8,128)(2,1)S(1)}, bf16[1,96,256]{2,1,0:T(8,128)(2,1)S(1)}, u32[]{:S(2)}, u32[]{:S(2)}) collective-permute-start(bf16[1,96,256]{2,1,0:T(8,128)(2,1)S(1)} %bitcast.8), channel_id=1, source_target_pairs={{0,2},{1,3},{2,0},{3,1},{4,6},{5,7},{6,4},{7,5},{8,10},{9,11},{10,... | collective-permute-start | bytes 147464 | tf_op jit(solution)/shard_map/ppermute | solution.py:204
  5.7 0.0 collective-permute-start
  5.7 0.0 copy-done
  5.7 0.1 constant_dynamic-slice_fusion
  5.7 0.1 copy.4
  5.8 0.1 reshape.19
  5.9 0.0 collective-permute-done.7.refs_1_
  5.9 2.2 %collective-permute-start.8 = (bf16[2,96,256]{2,1,0:T(8,128)(2,1)S(1)}, bf16[2,96,256]{2,1,0:T(8,128)(2,1)S(1)}, u32[]{:S(2)}, u32[]{:S(2)}) collective-permute-start(bf16[2,96,256]{2,1,0:T(8,128)(2,1)S(1)} %stack.9.refs_0_), channel_id=1, source_target_pairs={{0,24},{4,28},{8,16},{12,20},{16,8},{20,12},{24,0},{28,4},{1,25},{... | collective-permute-start | bytes 294920 | tf_op jit(solution)/shard_map/ppermute | solution.py:204
  8.2 0.1 add_bitcast_fusion.refs_2_.refs_0_
  8.2 0.3 %collective-permute-start.11 = (bf16[2,96,256]{2,1,0:T(8,128)(2,1)S(1)}, bf16[2,96,256]{2,1,0:T(8,128)(2,1)S(1)}, u32[]{:S(2)}, u32[]{:S(2)}) collective-permute-start(bf16[2,96,256]{2,1,0:T(8,128)(2,1)S(1)} %stack.9.refs_0_), channel_id=1, source_target_pairs={{0,8},{4,12},{8,0},{12,4},{16,24},{20,28},{24,16},{28,20},{1,9},{5... | collective-permute-start | bytes 294920 | tf_op jit(solution)/shard_map/ppermute | solution.py:204
  8.5 0.2 collective-permute-start.10
  8.7 0.0 collective-permute-done.1.refs_1_
  8.7 1.8 %collective-permute-done.refs_0_ = bf16[1,96,256]{2,1,0:T(8,128)(2,1)S(1)} collective-permute-done((bf16[1,96,256]{2,1,0:T(8,128)(2,1)S(1)}, bf16[1,96,256]{2,1,0:T(8,128)(2,1)S(1)}, u32[]{:S(2)}, u32[]{:S(2)}) %collective-permute-start) | collective-permute-done | bytes 49184 | tf_op jit(solution)/shard_map/ppermute | solution.py:204
  10.5 2.2 %collective-permute-start.2 = (bf16[2,96,256]{2,1,0:T(8,128)(2,1)S(1)}, bf16[2,96,256]{2,1,0:T(8,128)(2,1)S(1)}, u32[]{:S(2)}, u32[]{:S(2)}) collective-permute-start(bf16[2,96,256]{2,1,0:T(8,128)(2,1)S(1)} %stack.6.refs_0_), channel_id=1, source_target_pairs={{0,24},{4,28},{8,16},{12,20},{16,8},{20,12},{24,0},{28,4},{1,25},{... | collective-permute-start | bytes 294920 | tf_op jit(solution)/shard_map/ppermute | solution.py:204
  12.8 0.3 %collective-permute-start.5 = (bf16[2,96,256]{2,1,0:T(8,128)(2,1)S(1)}, bf16[2,96,256]{2,1,0:T(8,128)(2,1)S(1)}, u32[]{:S(2)}, u32[]{:S(2)}) collective-permute-start(bf16[2,96,256]{2,1,0:T(8,128)(2,1)S(1)} %stack.6.refs_0_), channel_id=1, source_target_pairs={{0,8},{4,12},{8,0},{12,4},{16,24},{20,28},{24,16},{28,20},{1,9},{5... | collective-permute-start | bytes 294920 | tf_op jit(solution)/shard_map/ppermute | solution.py:204
  13.0 0.0 collective-permute-done.8.refs_1_
  13.0 0.2 collective-permute-start.4
  13.3 0.0 collective-permute-done.11.refs_1_
  13.3 3.2 %collective-permute-start.9 = (bf16[4,96,256]{2,1,0:T(8,128)(2,1)S(1)}, bf16[4,96,256]{2,1,0:T(8,128)(2,1)S(1)}, u32[]{:S(2)}, u32[]{:S(2)}) collective-permute-start(bf16[4,96,256]{2,1,0:T(8,128)(2,1)S(1)} %stack.10.refs_1_), channel_id=1, source_target_pairs={{0,4},{4,0},{8,12},{12,8},{16,20},{20,16},{24,28},{28,24},{1,5},{5... | collective-permute-start | bytes 589832 | tf_op jit(solution)/shard_map/ppermute | solution.py:204
  16.5 0.0 collective-permute-done.10.refs_0_
  16.5 0.1 collective-permute-start.12
  16.6 0.0 collective-permute-done.2.refs_1_
  16.6 1.9 %collective-permute-start.3 = (bf16[4,96,256]{2,1,0:T(8,128)(2,1)S(1)}, bf16[4,96,256]{2,1,0:T(8,128)(2,1)S(1)}, u32[]{:S(2)}, u32[]{:S(2)}) collective-permute-start(bf16[4,96,256]{2,1,0:T(8,128)(2,1)S(1)} %stack.7.refs_1_), channel_id=1, source_target_pairs={{0,4},{4,0},{8,12},{12,8},{16,20},{20,16},{24,28},{28,24},{1,5},{5... | collective-permute-start | bytes 589832 | tf_op jit(solution)/shard_map/ppermute | solution.py:204
  18.5 0.0 collective-permute-done.5.refs_1_
  18.5 0.0 collective-permute-done.4.refs_0_
  18.5 2.1 %collective-permute-start.6 = (bf16[4,96,256]{2,1,0:T(8,128)(2,1)S(1)}, bf16[4,96,256]{2,1,0:T(8,128)(2,1)S(1)}, u32[]{:S(2)}, u32[]{:S(2)}) collective-permute-start(bf16[4,96,256]{2,1,0:T(8,128)(2,1)S(1)} %stack.8.refs_3_), channel_id=1, source_target_pairs={{0,4},{4,0},{8,12},{12,8},{16,20},{20,16},{24,28},{28,24},{1,5},{5... | collective-permute-start | bytes 589832 | tf_op jit(solution)/shard_map/ppermute | solution.py:204
  20.6 0.0 collective-permute-done.9.refs_2_
  20.6 0.0 collective-permute-done.12.refs_4_
  20.6 1.6 %correlate.1.refs_5_ = f32[2,4,8,128,128]{4,3,2,1,0:T(8,128)S(1)} custom-call(s32[1,5]{1,0:T(1,128)S(1)} %add_bitcast_fusion.refs_2_.refs_0_, bf16[4,96,256]{2,1,0:T(8,128)(2,1)S(1)} %stack.10.refs_1_, bf16[4,96,256]{2,1,0:T(8,128)(2,1)S(1)} %collective-permute-done.9.refs_2_, bf16[4,96,256]{2,1,0:T(8,128)(2,1)S(1)} %stack.11.refs_3_, ...), custom_call_target="tpu_custom_call" | custom-call | tf_op jit(solution)/shard_map/correlate/pallas_call | solution.py:186
  22.2 0.0 collective-permute-done.3.refs_2_
  22.2 0.0 collective-permute-done.6.refs_4_
  22.2 2.7 %correlate_add.1 = f32[2,4,8,128,128]{4,3,2,1,0:T(8,128)} custom-call(s32[1,5]{1,0:T(1,128)S(1)} %add_bitcast_fusion.refs_2_.refs_0_, bf16[4,96,256]{2,1,0:T(8,128)(2,1)S(1)} %stack.7.refs_1_, bf16[4,96,256]{2,1,0:T(8,128)(2,1)S(1)} %collective-permute-done.3.refs_2_, bf16[4,96,256]{2,1,0:T(8,128)(2,1)S(1)} %stack.8.refs_3_, ...), custom_call_target="tpu_custom_call" | custom-call | tf_op jit(solution)/shard_map/correlate_add/pallas_call | solution.py:186
  (6 shorter events, 0.1 us)
Async XLA Ops:
  0.0 5.7 %copy-start = (s32[8,2]{0,1:T(2,128)S(1)}, s32[8,2]{0,1:T(2,128)}, u32[]{:S(2)}) copy-start(s32[8,2]{0,1:T(2,128)} %param.5) | copy-start | bytes 196
  1.2 4.8 %collective-permute-start.7 = (bf16[1,96,256]{2,1,0:T(8,128)(2,1)S(1)}, bf16[1,96,256]{2,1,0:T(8,128)(2,1)S(1)}, u32[]{:S(2)}, u32[]{:S(2)}) collective-permute-start(bf16[1,96,256]{2,1,0:T(8,128)(2,1)S(1)} %bitcast.7), channel_id=1, source_target_pairs={{0,1},{1,0},{2,3},{3,2},{4,5},{5,4},{6,7},{7,6},{8,9},{9,8},{10,11... | collective-permute-start | bytes 147464 | tf_op jit(solution)/shard_map/ppermute | solution.py:204
  3.4 5.4 %collective-permute-start.1 = (bf16[1,96,256]{2,1,0:T(8,128)(2,1)S(1)}, bf16[1,96,256]{2,1,0:T(8,128)(2,1)S(1)}, u32[]{:S(2)}, u32[]{:S(2)}) collective-permute-start(bf16[1,96,256]{2,1,0:T(8,128)(2,1)S(1)} %bitcast.8), channel_id=1, source_target_pairs={{0,2},{1,3},{2,0},{3,1},{4,6},{5,7},{6,4},{7,5},{8,10},{9,11},{10,... | collective-permute-start | bytes 147464 | tf_op jit(solution)/shard_map/ppermute | solution.py:204
  5.7 4.8 %collective-permute-start = (bf16[1,96,256]{2,1,0:T(8,128)(2,1)S(1)}, bf16[1,96,256]{2,1,0:T(8,128)(2,1)S(1)}, u32[]{:S(2)}, u32[]{:S(2)}) collective-permute-start(bf16[1,96,256]{2,1,0:T(8,128)(2,1)S(1)} %bitcast.9), channel_id=1, source_target_pairs={{0,3},{1,2},{2,1},{3,0},{4,7},{5,6},{6,5},{7,4},{8,11},{9,10},{10,... | collective-permute-start | bytes 147464 | tf_op jit(solution)/shard_map/ppermute | solution.py:204
  5.9 7.1 %collective-permute-start.8 = (bf16[2,96,256]{2,1,0:T(8,128)(2,1)S(1)}, bf16[2,96,256]{2,1,0:T(8,128)(2,1)S(1)}, u32[]{:S(2)}, u32[]{:S(2)}) collective-permute-start(bf16[2,96,256]{2,1,0:T(8,128)(2,1)S(1)} %stack.9.refs_0_), channel_id=1, source_target_pairs={{0,24},{4,28},{8,16},{12,20},{16,8},{20,12},{24,0},{28,4},{1,25},{... | collective-permute-start | bytes 294920 | tf_op jit(solution)/shard_map/ppermute | solution.py:204
  8.2 5.0 %collective-permute-start.11 = (bf16[2,96,256]{2,1,0:T(8,128)(2,1)S(1)}, bf16[2,96,256]{2,1,0:T(8,128)(2,1)S(1)}, u32[]{:S(2)}, u32[]{:S(2)}) collective-permute-start(bf16[2,96,256]{2,1,0:T(8,128)(2,1)S(1)} %stack.9.refs_0_), channel_id=1, source_target_pairs={{0,8},{4,12},{8,0},{12,4},{16,24},{20,28},{24,16},{28,20},{1,9},{5... | collective-permute-start | bytes 294920 | tf_op jit(solution)/shard_map/ppermute | solution.py:204
  8.5 8.0 %collective-permute-start.10 = (bf16[2,96,256]{2,1,0:T(8,128)(2,1)S(1)}, bf16[2,96,256]{2,1,0:T(8,128)(2,1)S(1)}, u32[]{:S(2)}, u32[]{:S(2)}) collective-permute-start(bf16[2,96,256]{2,1,0:T(8,128)(2,1)S(1)} %stack.9.refs_0_), channel_id=1, source_target_pairs={{0,16},{4,20},{8,24},{12,28},{16,0},{20,4},{24,8},{28,12},{1,17},{... | collective-permute-start | bytes 294920 | tf_op jit(solution)/shard_map/ppermute | solution.py:204
  10.5 6.0 %collective-permute-start.2 = (bf16[2,96,256]{2,1,0:T(8,128)(2,1)S(1)}, bf16[2,96,256]{2,1,0:T(8,128)(2,1)S(1)}, u32[]{:S(2)}, u32[]{:S(2)}) collective-permute-start(bf16[2,96,256]{2,1,0:T(8,128)(2,1)S(1)} %stack.6.refs_0_), channel_id=1, source_target_pairs={{0,24},{4,28},{8,16},{12,20},{16,8},{20,12},{24,0},{28,4},{1,25},{... | collective-permute-start | bytes 294920 | tf_op jit(solution)/shard_map/ppermute | solution.py:204
  12.8 5.7 %collective-permute-start.5 = (bf16[2,96,256]{2,1,0:T(8,128)(2,1)S(1)}, bf16[2,96,256]{2,1,0:T(8,128)(2,1)S(1)}, u32[]{:S(2)}, u32[]{:S(2)}) collective-permute-start(bf16[2,96,256]{2,1,0:T(8,128)(2,1)S(1)} %stack.6.refs_0_), channel_id=1, source_target_pairs={{0,8},{4,12},{8,0},{12,4},{16,24},{20,28},{24,16},{28,20},{1,9},{5... | collective-permute-start | bytes 294920 | tf_op jit(solution)/shard_map/ppermute | solution.py:204
  13.0 5.5 %collective-permute-start.4 = (bf16[2,96,256]{2,1,0:T(8,128)(2,1)S(1)}, bf16[2,96,256]{2,1,0:T(8,128)(2,1)S(1)}, u32[]{:S(2)}, u32[]{:S(2)}) collective-permute-start(bf16[2,96,256]{2,1,0:T(8,128)(2,1)S(1)} %stack.6.refs_0_), channel_id=1, source_target_pairs={{0,16},{4,20},{8,24},{12,28},{16,0},{20,4},{24,8},{28,12},{1,17},{... | collective-permute-start | bytes 294920 | tf_op jit(solution)/shard_map/ppermute | solution.py:204
  13.3 7.3 %collective-permute-start.9 = (bf16[4,96,256]{2,1,0:T(8,128)(2,1)S(1)}, bf16[4,96,256]{2,1,0:T(8,128)(2,1)S(1)}, u32[]{:S(2)}, u32[]{:S(2)}) collective-permute-start(bf16[4,96,256]{2,1,0:T(8,128)(2,1)S(1)} %stack.10.refs_1_), channel_id=1, source_target_pairs={{0,4},{4,0},{8,12},{12,8},{16,20},{20,16},{24,28},{28,24},{1,5},{5... | collective-permute-start | bytes 589832 | tf_op jit(solution)/shard_map/ppermute | solution.py:204
  16.5 4.1 %collective-permute-start.12 = (bf16[4,96,256]{2,1,0:T(8,128)(2,1)S(1)}, bf16[4,96,256]{2,1,0:T(8,128)(2,1)S(1)}, u32[]{:S(2)}, u32[]{:S(2)}) collective-permute-start(bf16[4,96,256]{2,1,0:T(8,128)(2,1)S(1)} %stack.11.refs_3_), channel_id=1, source_target_pairs={{0,4},{4,0},{8,12},{12,8},{16,20},{20,16},{24,28},{28,24},{1,5},{5... | collective-permute-start | bytes 589832 | tf_op jit(solution)/shard_map/ppermute | solution.py:204
  16.6 5.6 %collective-permute-start.3 = (bf16[4,96,256]{2,1,0:T(8,128)(2,1)S(1)}, bf16[4,96,256]{2,1,0:T(8,128)(2,1)S(1)}, u32[]{:S(2)}, u32[]{:S(2)}) collective-permute-start(bf16[4,96,256]{2,1,0:T(8,128)(2,1)S(1)} %stack.7.refs_1_), channel_id=1, source_target_pairs={{0,4},{4,0},{8,12},{12,8},{16,20},{20,16},{24,28},{28,24},{1,5},{5... | collective-permute-start | bytes 589832 | tf_op jit(solution)/shard_map/ppermute | solution.py:204
  18.5 3.7 %collective-permute-start.6 = (bf16[4,96,256]{2,1,0:T(8,128)(2,1)S(1)}, bf16[4,96,256]{2,1,0:T(8,128)(2,1)S(1)}, u32[]{:S(2)}, u32[]{:S(2)}) collective-permute-start(bf16[4,96,256]{2,1,0:T(8,128)(2,1)S(1)} %stack.8.refs_3_), channel_id=1, source_target_pairs={{0,4},{4,0},{8,12},{12,8},{16,20},{20,16},{24,28},{28,24},{1,5},{5... | collective-permute-start | bytes 589832 | tf_op jit(solution)/shard_map/ppermute | solution.py:204

commit v26 on v24

--- a/solution.py
+++ b/solution.py
@@ -19,13 +19,13 @@
 
 
 def whiten_kernel(spectra_hbm, bad_hbm, out_ref, spectra_ref, bad_ref, sems):
-    copies = [
-        pltpu.make_async_copy(spectra_hbm, spectra_ref, sems.at[0]),
-        pltpu.make_async_copy(bad_hbm, bad_ref, sems.at[1]),
-    ]
+    rows, chans = spectra_ref.shape
+    parts = 4
+    slices = [pl.ds(i * rows // parts, rows // parts) for i in range(parts)]
+    copies = [pltpu.make_async_copy(spectra_hbm.at[at], spectra_ref.at[at], sems.at[i]) for i, at in enumerate(slices)]
+    copies.append(pltpu.make_async_copy(bad_hbm, bad_ref, sems.at[parts]))
     for copy in copies:
         copy.start()
-    rows, chans = spectra_ref.shape
     bins = F
     hours = rows // (2 * bins)
     row = lax.broadcasted_iota(jnp.int32, (rows, chans), 0)
@@ -61,7 +61,7 @@
         scratch_shapes=[
             pltpu.VMEM(spectra.shape, spectra.dtype),
             pltpu.VMEM((1, chans), bad_channels.dtype),
-            pltpu.SemaphoreType.DMA((2,)),
+            pltpu.SemaphoreType.DMA((5,)),
         ],
         compiler_params=pltpu.CompilerParams(vmem_limit_bytes=SMALL),
         name="whiten",

time: 24.5 us -> 24.5 us (level)
  no operation moved by 1% of the time
where the time goes in v26:
time: 24.5 us; the launch traced here: 24.3 us
  starting transfers between devices  16.7 us (68%)
  Pallas kernels  5.45 us (22%)
  waiting for transfers between devices  1.74 us (7%)
  local copies, waits for them, and re-layouts  0.26 us (1%)
    ppermute x13, starting transfers between devices, swap(): lax.ppermute(array, axis, [(i, i ^ k) for i in range(lax.axis_size(axis))])  16.7 us
    pallas_call x2, Pallas kernels, correlate(): pl.pallas_call(lambda *refs: correlate_kernel(norm, picked, adds, places,...  4.27 us
    ppermute x13, waiting for transfers between devices, swap(): lax.ppermute(array, axis, [(i, i ^ k) for i in range(lax.axis_size(axis))])  1.74 us
    pallas_call x1, Pallas kernels, whiten(): pl.pallas_call(whiten_kernel, out_shape=jax.ShapeDtypeStruct((chans, spec...  1.11 us
  transfers between devices with their start and end apart: 13, of which 1 were waited for; matrix products, arithmetic and copies ran while one was open for 1% of the time, Pallas kernels for 7%

profile of v26, /device:TPU:1, one launch (start us, length us, event | category | flops | bytes accessed | tf_op | source)
XLA Modules:
  0.0 24.3 jit_solution(125431811007212110)
XLA Ops:
  0.0 0.0 copy-start
  0.0 1.1 %whiten.1 = bf16[96,256]{1,0:T(8,128)(2,1)S(1)} custom-call(bf16[256,96]{1,0:T(8,128)(2,1)} %bitcast.11, s32[1,96]{1,0:T(1,128)} %bitcast.12), custom_call_target="tpu_custom_call" | custom-call | tf_op jit(solution)/shard_map/whiten/pallas_call | solution.py:56
  1.1 2.2 %collective-permute-start.7 = (bf16[1,96,256]{2,1,0:T(8,128)(2,1)S(1)}, bf16[1,96,256]{2,1,0:T(8,128)(2,1)S(1)}, u32[]{:S(2)}, u32[]{:S(2)}) collective-permute-start(bf16[1,96,256]{2,1,0:T(8,128)(2,1)S(1)} %bitcast.7), channel_id=1, source_target_pairs={{0,1},{1,0},{2,3},{3,2},{4,5},{5,4},{6,7},{7,6},{8,9},{9,8},{10,11... | collective-permute-start | bytes 147464 | tf_op jit(solution)/shard_map/ppermute | solution.py:204
  3.3 2.2 %collective-permute-start.1 = (bf16[1,96,256]{2,1,0:T(8,128)(2,1)S(1)}, bf16[1,96,256]{2,1,0:T(8,128)(2,1)S(1)}, u32[]{:S(2)}, u32[]{:S(2)}) collective-permute-start(bf16[1,96,256]{2,1,0:T(8,128)(2,1)S(1)} %bitcast.8), channel_id=1, source_target_pairs={{0,3},{1,2},{2,1},{3,0},{4,7},{5,6},{6,5},{7,4},{8,11},{9,10},{10,... | collective-permute-start | bytes 147464 | tf_op jit(solution)/shard_map/ppermute | solution.py:204
  5.5 0.1 collective-permute-start
  5.6 0.0 copy-done
  5.6 0.1 constant_dynamic-slice_fusion
  5.7 0.1 copy.4
  5.8 0.1 reshape.19
  5.9 0.0 collective-permute-done.7.refs_1_
  5.9 2.2 %collective-permute-start.8 = (bf16[2,96,256]{2,1,0:T(8,128)(2,1)S(1)}, bf16[2,96,256]{2,1,0:T(8,128)(2,1)S(1)}, u32[]{:S(2)}, u32[]{:S(2)}) collective-permute-start(bf16[2,96,256]{2,1,0:T(8,128)(2,1)S(1)} %stack.9.refs_0_), channel_id=1, source_target_pairs={{0,24},{4,28},{8,16},{12,20},{16,8},{20,12},{24,0},{28,4},{1,25},{... | collective-permute-start | bytes 294920 | tf_op jit(solution)/shard_map/ppermute | solution.py:204
  8.1 0.1 add_bitcast_fusion.refs_2_.refs_0_
  8.2 0.3 %collective-permute-start.11 = (bf16[2,96,256]{2,1,0:T(8,128)(2,1)S(1)}, bf16[2,96,256]{2,1,0:T(8,128)(2,1)S(1)}, u32[]{:S(2)}, u32[]{:S(2)}) collective-permute-start(bf16[2,96,256]{2,1,0:T(8,128)(2,1)S(1)} %stack.9.refs_0_), channel_id=1, source_target_pairs={{0,8},{4,12},{8,0},{12,4},{16,24},{20,28},{24,16},{28,20},{1,9},{5... | collective-permute-start | bytes 294920 | tf_op jit(solution)/shard_map/ppermute | solution.py:204
  8.5 0.2 collective-permute-start.10
  8.7 0.0 collective-permute-done.1.refs_1_
  8.7 1.7 %collective-permute-done.refs_0_ = bf16[1,96,256]{2,1,0:T(8,128)(2,1)S(1)} collective-permute-done((bf16[1,96,256]{2,1,0:T(8,128)(2,1)S(1)}, bf16[1,96,256]{2,1,0:T(8,128)(2,1)S(1)}, u32[]{:S(2)}, u32[]{:S(2)}) %collective-permute-start) | collective-permute-done | bytes 49184 | tf_op jit(solution)/shard_map/ppermute | solution.py:204
  10.4 2.2 %collective-permute-start.2 = (bf16[2,96,256]{2,1,0:T(8,128)(2,1)S(1)}, bf16[2,96,256]{2,1,0:T(8,128)(2,1)S(1)}, u32[]{:S(2)}, u32[]{:S(2)}) collective-permute-start(bf16[2,96,256]{2,1,0:T(8,128)(2,1)S(1)} %stack.6.refs_0_), channel_id=1, source_target_pairs={{0,24},{4,28},{8,16},{12,20},{16,8},{20,12},{24,0},{28,4},{1,25},{... | collective-permute-start | bytes 294920 | tf_op jit(solution)/shard_map/ppermute | solution.py:204
  12.6 0.3 %collective-permute-start.5 = (bf16[2,96,256]{2,1,0:T(8,128)(2,1)S(1)}, bf16[2,96,256]{2,1,0:T(8,128)(2,1)S(1)}, u32[]{:S(2)}, u32[]{:S(2)}) collective-permute-start(bf16[2,96,256]{2,1,0:T(8,128)(2,1)S(1)} %stack.6.refs_0_), channel_id=1, source_target_pairs={{0,8},{4,12},{8,0},{12,4},{16,24},{20,28},{24,16},{28,20},{1,9},{5... | collective-permute-start | bytes 294920 | tf_op jit(solution)/shard_map/ppermute | solution.py:204
  12.9 0.0 collective-permute-done.8.refs_1_
  12.9 0.2 collective-permute-start.4
  13.1 0.0 collective-permute-done.11.refs_1_
  13.2 2.8 %collective-permute-start.9 = (bf16[4,96,256]{2,1,0:T(8,128)(2,1)S(1)}, bf16[4,96,256]{2,1,0:T(8,128)(2,1)S(1)}, u32[]{:S(2)}, u32[]{:S(2)}) collective-permute-start(bf16[4,96,256]{2,1,0:T(8,128)(2,1)S(1)} %stack.10.refs_1_), channel_id=1, source_target_pairs={{0,4},{4,0},{8,12},{12,8},{16,20},{20,16},{24,28},{28,24},{1,5},{5... | collective-permute-start | bytes 589832 | tf_op jit(solution)/shard_map/ppermute | solution.py:204
  15.9 0.0 collective-permute-done.10.refs_0_
  15.9 0.1 collective-permute-start.12
  16.0 0.0 collective-permute-done.2.refs_1_
  16.1 2.0 %collective-permute-start.3 = (bf16[4,96,256]{2,1,0:T(8,128)(2,1)S(1)}, bf16[4,96,256]{2,1,0:T(8,128)(2,1)S(1)}, u32[]{:S(2)}, u32[]{:S(2)}) collective-permute-start(bf16[4,96,256]{2,1,0:T(8,128)(2,1)S(1)} %stack.7.refs_1_), channel_id=1, source_target_pairs={{0,4},{4,0},{8,12},{12,8},{16,20},{20,16},{24,28},{28,24},{1,5},{5... | collective-permute-start | bytes 589832 | tf_op jit(solution)/shard_map/ppermute | solution.py:204
  18.0 0.0 collective-permute-done.5.refs_1_
  18.0 0.0 collective-permute-done.4.refs_0_
  18.1 2.0 %collective-permute-start.6 = (bf16[4,96,256]{2,1,0:T(8,128)(2,1)S(1)}, bf16[4,96,256]{2,1,0:T(8,128)(2,1)S(1)}, u32[]{:S(2)}, u32[]{:S(2)}) collective-permute-start(bf16[4,96,256]{2,1,0:T(8,128)(2,1)S(1)} %stack.8.refs_3_), channel_id=1, source_target_pairs={{0,4},{4,0},{8,12},{12,8},{16,20},{20,16},{24,28},{28,24},{1,5},{5... | collective-permute-start | bytes 589832 | tf_op jit(solution)/shard_map/ppermute | solution.py:204
  20.0 0.0 collective-permute-done.9.refs_2_
  20.0 0.0 collective-permute-done.12.refs_4_
  20.0 1.6 %correlate.1.refs_5_ = f32[2,4,8,128,128]{4,3,2,1,0:T(8,128)S(1)} custom-call(s32[1,5]{1,0:T(1,128)S(1)} %add_bitcast_fusion.refs_2_.refs_0_, bf16[4,96,256]{2,1,0:T(8,128)(2,1)S(1)} %stack.10.refs_1_, bf16[4,96,256]{2,1,0:T(8,128)(2,1)S(1)} %collective-permute-done.9.refs_2_, bf16[4,96,256]{2,1,0:T(8,128)(2,1)S(1)} %stack.11.refs_3_, ...), custom_call_target="tpu_custom_call" | custom-call | tf_op jit(solution)/shard_map/correlate/pallas_call | solution.py:186
  21.6 0.0 collective-permute-done.3.refs_2_
  21.7 0.0 collective-permute-done.6.refs_4_
  21.7 2.7 %correlate_add.1 = f32[2,4,8,128,128]{4,3,2,1,0:T(8,128)} custom-call(s32[1,5]{1,0:T(1,128)S(1)} %add_bitcast_fusion.refs_2_.refs_0_, bf16[4,96,256]{2,1,0:T(8,128)(2,1)S(1)} %stack.7.refs_1_, bf16[4,96,256]{2,1,0:T(8,128)(2,1)S(1)} %collective-permute-done.3.refs_2_, bf16[4,96,256]{2,1,0:T(8,128)(2,1)S(1)} %stack.8.refs_3_, ...), custom_call_target="tpu_custom_call" | custom-call | tf_op jit(solution)/shard_map/correlate_add/pallas_call | solution.py:186
  (6 shorter events, 0.1 us)
Async XLA Ops:
  0.0 5.6 %copy-start = (s32[8,2]{0,1:T(2,128)S(1)}, s32[8,2]{0,1:T(2,128)}, u32[]{:S(2)}) copy-start(s32[8,2]{0,1:T(2,128)} %param.5) | copy-start | bytes 196
  1.1 4.8 %collective-permute-start.7 = (bf16[1,96,256]{2,1,0:T(8,128)(2,1)S(1)}, bf16[1,96,256]{2,1,0:T(8,128)(2,1)S(1)}, u32[]{:S(2)}, u32[]{:S(2)}) collective-permute-start(bf16[1,96,256]{2,1,0:T(8,128)(2,1)S(1)} %bitcast.7), channel_id=1, source_target_pairs={{0,1},{1,0},{2,3},{3,2},{4,5},{5,4},{6,7},{7,6},{8,9},{9,8},{10,11... | collective-permute-start | bytes 147464 | tf_op jit(solution)/shard_map/ppermute | solution.py:204
  3.3 5.4 %collective-permute-start.1 = (bf16[1,96,256]{2,1,0:T(8,128)(2,1)S(1)}, bf16[1,96,256]{2,1,0:T(8,128)(2,1)S(1)}, u32[]{:S(2)}, u32[]{:S(2)}) collective-permute-start(bf16[1,96,256]{2,1,0:T(8,128)(2,1)S(1)} %bitcast.8), channel_id=1, source_target_pairs={{0,3},{1,2},{2,1},{3,0},{4,7},{5,6},{6,5},{7,4},{8,11},{9,10},{10,... | collective-permute-start | bytes 147464 | tf_op jit(solution)/shard_map/ppermute | solution.py:204
  5.5 4.9 %collective-permute-start = (bf16[1,96,256]{2,1,0:T(8,128)(2,1)S(1)}, bf16[1,96,256]{2,1,0:T(8,128)(2,1)S(1)}, u32[]{:S(2)}, u32[]{:S(2)}) collective-permute-start(bf16[1,96,256]{2,1,0:T(8,128)(2,1)S(1)} %bitcast.9), channel_id=1, source_target_pairs={{0,2},{1,3},{2,0},{3,1},{4,6},{5,7},{6,4},{7,5},{8,10},{9,11},{10,... | collective-permute-start | bytes 147464 | tf_op jit(solution)/shard_map/ppermute | solution.py:204
  5.9 7.0 %collective-permute-start.8 = (bf16[2,96,256]{2,1,0:T(8,128)(2,1)S(1)}, bf16[2,96,256]{2,1,0:T(8,128)(2,1)S(1)}, u32[]{:S(2)}, u32[]{:S(2)}) collective-permute-start(bf16[2,96,256]{2,1,0:T(8,128)(2,1)S(1)} %stack.9.refs_0_), channel_id=1, source_target_pairs={{0,24},{4,28},{8,16},{12,20},{16,8},{20,12},{24,0},{28,4},{1,25},{... | collective-permute-start | bytes 294920 | tf_op jit(solution)/shard_map/ppermute | solution.py:204
  8.2 4.9 %collective-permute-start.11 = (bf16[2,96,256]{2,1,0:T(8,128)(2,1)S(1)}, bf16[2,96,256]{2,1,0:T(8,128)(2,1)S(1)}, u32[]{:S(2)}, u32[]{:S(2)}) collective-permute-start(bf16[2,96,256]{2,1,0:T(8,128)(2,1)S(1)} %stack.9.refs_0_), channel_id=1, source_target_pairs={{0,8},{4,12},{8,0},{12,4},{16,24},{20,28},{24,16},{28,20},{1,9},{5... | collective-permute-start | bytes 294920 | tf_op jit(solution)/shard_map/ppermute | solution.py:204
  8.5 7.5 %collective-permute-start.10 = (bf16[2,96,256]{2,1,0:T(8,128)(2,1)S(1)}, bf16[2,96,256]{2,1,0:T(8,128)(2,1)S(1)}, u32[]{:S(2)}, u32[]{:S(2)}) collective-permute-start(bf16[2,96,256]{2,1,0:T(8,128)(2,1)S(1)} %stack.9.refs_0_), channel_id=1, source_target_pairs={{0,16},{4,20},{8,24},{12,28},{16,0},{20,4},{24,8},{28,12},{1,17},{... | collective-permute-start | bytes 294920 | tf_op jit(solution)/shard_map/ppermute | solution.py:204
  10.4 5.6 %collective-permute-start.2 = (bf16[2,96,256]{2,1,0:T(8,128)(2,1)S(1)}, bf16[2,96,256]{2,1,0:T(8,128)(2,1)S(1)}, u32[]{:S(2)}, u32[]{:S(2)}) collective-permute-start(bf16[2,96,256]{2,1,0:T(8,128)(2,1)S(1)} %stack.6.refs_0_), channel_id=1, source_target_pairs={{0,24},{4,28},{8,16},{12,20},{16,8},{20,12},{24,0},{28,4},{1,25},{... | collective-permute-start | bytes 294920 | tf_op jit(solution)/shard_map/ppermute | solution.py:204
  12.6 5.4 %collective-permute-start.5 = (bf16[2,96,256]{2,1,0:T(8,128)(2,1)S(1)}, bf16[2,96,256]{2,1,0:T(8,128)(2,1)S(1)}, u32[]{:S(2)}, u32[]{:S(2)}) collective-permute-start(bf16[2,96,256]{2,1,0:T(8,128)(2,1)S(1)} %stack.6.refs_0_), channel_id=1, source_target_pairs={{0,8},{4,12},{8,0},{12,4},{16,24},{20,28},{24,16},{28,20},{1,9},{5... | collective-permute-start | bytes 294920 | tf_op jit(solution)/shard_map/ppermute | solution.py:204
  12.9 5.1 %collective-permute-start.4 = (bf16[2,96,256]{2,1,0:T(8,128)(2,1)S(1)}, bf16[2,96,256]{2,1,0:T(8,128)(2,1)S(1)}, u32[]{:S(2)}, u32[]{:S(2)}) collective-permute-start(bf16[2,96,256]{2,1,0:T(8,128)(2,1)S(1)} %stack.6.refs_0_), channel_id=1, source_target_pairs={{0,16},{4,20},{8,24},{12,28},{16,0},{20,4},{24,8},{28,12},{1,17},{... | collective-permute-start | bytes 294920 | tf_op jit(solution)/shard_map/ppermute | solution.py:204
  13.2 6.9 %collective-permute-start.9 = (bf16[4,96,256]{2,1,0:T(8,128)(2,1)S(1)}, bf16[4,96,256]{2,1,0:T(8,128)(2,1)S(1)}, u32[]{:S(2)}, u32[]{:S(2)}) collective-permute-start(bf16[4,96,256]{2,1,0:T(8,128)(2,1)S(1)} %stack.10.refs_1_), channel_id=1, source_target_pairs={{0,4},{4,0},{8,12},{12,8},{16,20},{20,16},{24,28},{28,24},{1,5},{5... | collective-permute-start | bytes 589832 | tf_op jit(solution)/shard_map/ppermute | solution.py:204
  15.9 4.1 %collective-permute-start.12 = (bf16[4,96,256]{2,1,0:T(8,128)(2,1)S(1)}, bf16[4,96,256]{2,1,0:T(8,128)(2,1)S(1)}, u32[]{:S(2)}, u32[]{:S(2)}) collective-permute-start(bf16[4,96,256]{2,1,0:T(8,128)(2,1)S(1)} %stack.11.refs_3_), channel_id=1, source_target_pairs={{0,4},{4,0},{8,12},{12,8},{16,20},{20,16},{24,28},{28,24},{1,5},{5... | collective-permute-start | bytes 589832 | tf_op jit(solution)/shard_map/ppermute | solution.py:204
  16.1 5.6 %collective-permute-start.3 = (bf16[4,96,256]{2,1,0:T(8,128)(2,1)S(1)}, bf16[4,96,256]{2,1,0:T(8,128)(2,1)S(1)}, u32[]{:S(2)}, u32[]{:S(2)}) collective-permute-start(bf16[4,96,256]{2,1,0:T(8,128)(2,1)S(1)} %stack.7.refs_1_), channel_id=1, source_target_pairs={{0,4},{4,0},{8,12},{12,8},{16,20},{20,16},{24,28},{28,24},{1,5},{5... | collective-permute-start | bytes 589832 | tf_op jit(solution)/shard_map/ppermute | solution.py:204
  18.1 3.6 %collective-permute-start.6 = (bf16[4,96,256]{2,1,0:T(8,128)(2,1)S(1)}, bf16[4,96,256]{2,1,0:T(8,128)(2,1)S(1)}, u32[]{:S(2)}, u32[]{:S(2)}) collective-permute-start(bf16[4,96,256]{2,1,0:T(8,128)(2,1)S(1)} %stack.8.refs_3_), channel_id=1, source_target_pairs={{0,4},{4,0},{8,12},{12,8},{16,20},{20,16},{24,28},{28,24},{1,5},{5... | collective-permute-start | bytes 589832 | tf_op jit(solution)/shard_map/ppermute | solution.py:204

commit v27 on v26

--- a/solution.py
+++ b/solution.py
@@ -159,11 +159,12 @@
                     more[0][i, u + v, fine] = partials[i // each][i % each, u + v, fine] + value
                 else:
                     out_ref[i, u + v, fine] = value
-        for s in range(2 if adds else 0):
-            done = (i, slice(None), FINE_PAIRS[j][s] + 4)
-            copy = pltpu.make_async_copy(more[0].at[done], out_ref.at[done], more[1])
-            copy.start(priority=s)
-            copies.append(copy)
+            ready = slice(u, u + 2) if not after else slice(None) if u else None
+            for s in range(2 if adds and ready else 0):
+                done = (i, ready, FINE_PAIRS[j][s] + 4)
+                copy = pltpu.make_async_copy(more[0].at[done], out_ref.at[done], more[1])
+                copy.start(priority=s)
+                copies.append(copy)
     for copy in copies:
         copy.wait()
 

time: 24.5 us -> 24.5 us (level)
  no operation moved by 1% of the time
where the time goes in v27:
time: 24.5 us; the launch traced here: 24.3 us
  starting transfers between devices  16.7 us (68%)
  Pallas kernels  5.47 us (22%)
  waiting for transfers between devices  1.74 us (7%)
  local copies, waits for them, and re-layouts  0.26 us (1%)
    ppermute x13, starting transfers between devices, swap(): lax.ppermute(array, axis, [(i, i ^ k) for i in range(lax.axis_size(axis))])  16.7 us
    pallas_call x2, Pallas kernels, correlate(): pl.pallas_call(lambda *refs: correlate_kernel(norm, picked, adds, places,...  4.29 us
    ppermute x13, waiting for transfers between devices, swap(): lax.ppermute(array, axis, [(i, i ^ k) for i in range(lax.axis_size(axis))])  1.74 us
    pallas_call x1, Pallas kernels, whiten(): pl.pallas_call(whiten_kernel, out_shape=jax.ShapeDtypeStruct((chans, spec...  1.11 us
  transfers between devices with their start and end apart: 13, of which 1 were waited for; matrix products, arithmetic and copies ran while one was open for 1% of the time, Pallas kernels for 7%

profile of v27, /device:TPU:1, one launch (start us, length us, event | category | flops | bytes accessed | tf_op | source)
XLA Modules:
  0.0 24.3 jit_solution(4391640417502973769)
XLA Ops:
  0.0 0.0 copy-start
  0.0 1.1 %whiten.1 = bf16[96,256]{1,0:T(8,128)(2,1)S(1)} custom-call(bf16[256,96]{1,0:T(8,128)(2,1)} %bitcast.11, s32[1,96]{1,0:T(1,128)} %bitcast.12), custom_call_target="tpu_custom_call" | custom-call | tf_op jit(solution)/shard_map/whiten/pallas_call | solution.py:56
  1.1 2.2 %collective-permute-start.7 = (bf16[1,96,256]{2,1,0:T(8,128)(2,1)S(1)}, bf16[1,96,256]{2,1,0:T(8,128)(2,1)S(1)}, u32[]{:S(2)}, u32[]{:S(2)}) collective-permute-start(bf16[1,96,256]{2,1,0:T(8,128)(2,1)S(1)} %bitcast.7), channel_id=1, source_target_pairs={{0,1},{1,0},{2,3},{3,2},{4,5},{5,4},{6,7},{7,6},{8,9},{9,8},{10,11... | collective-permute-start | bytes 147464 | tf_op jit(solution)/shard_map/ppermute | solution.py:205
  3.3 2.2 %collective-permute-start.1 = (bf16[1,96,256]{2,1,0:T(8,128)(2,1)S(1)}, bf16[1,96,256]{2,1,0:T(8,128)(2,1)S(1)}, u32[]{:S(2)}, u32[]{:S(2)}) collective-permute-start(bf16[1,96,256]{2,1,0:T(8,128)(2,1)S(1)} %bitcast.8), channel_id=1, source_target_pairs={{0,3},{1,2},{2,1},{3,0},{4,7},{5,6},{6,5},{7,4},{8,11},{9,10},{10,... | collective-permute-start | bytes 147464 | tf_op jit(solution)/shard_map/ppermute | solution.py:205
  5.5 0.1 collective-permute-start
  5.6 0.0 copy-done
  5.6 0.1 constant_dynamic-slice_fusion
  5.7 0.1 copy.4
  5.8 0.1 reshape.19
  5.9 0.0 collective-permute-done.7.refs_1_
  5.9 2.2 %collective-permute-start.8 = (bf16[2,96,256]{2,1,0:T(8,128)(2,1)S(1)}, bf16[2,96,256]{2,1,0:T(8,128)(2,1)S(1)}, u32[]{:S(2)}, u32[]{:S(2)}) collective-permute-start(bf16[2,96,256]{2,1,0:T(8,128)(2,1)S(1)} %stack.9.refs_0_), channel_id=1, source_target_pairs={{0,24},{4,28},{8,16},{12,20},{16,8},{20,12},{24,0},{28,4},{1,25},{... | collective-permute-start | bytes 294920 | tf_op jit(solution)/shard_map/ppermute | solution.py:205
  8.1 0.1 add_bitcast_fusion.refs_2_.refs_0_
  8.2 0.3 %collective-permute-start.11 = (bf16[2,96,256]{2,1,0:T(8,128)(2,1)S(1)}, bf16[2,96,256]{2,1,0:T(8,128)(2,1)S(1)}, u32[]{:S(2)}, u32[]{:S(2)}) collective-permute-start(bf16[2,96,256]{2,1,0:T(8,128)(2,1)S(1)} %stack.9.refs_0_), channel_id=1, source_target_pairs={{0,8},{4,12},{8,0},{12,4},{16,24},{20,28},{24,16},{28,20},{1,9},{5... | collective-permute-start | bytes 294920 | tf_op jit(solution)/shard_map/ppermute | solution.py:205
  8.5 0.2 collective-permute-start.10
  8.7 0.0 collective-permute-done.1.refs_1_
  8.7 1.7 %collective-permute-done.refs_0_ = bf16[1,96,256]{2,1,0:T(8,128)(2,1)S(1)} collective-permute-done((bf16[1,96,256]{2,1,0:T(8,128)(2,1)S(1)}, bf16[1,96,256]{2,1,0:T(8,128)(2,1)S(1)}, u32[]{:S(2)}, u32[]{:S(2)}) %collective-permute-start) | collective-permute-done | bytes 49184 | tf_op jit(solution)/shard_map/ppermute | solution.py:205
  10.4 2.2 %collective-permute-start.2 = (bf16[2,96,256]{2,1,0:T(8,128)(2,1)S(1)}, bf16[2,96,256]{2,1,0:T(8,128)(2,1)S(1)}, u32[]{:S(2)}, u32[]{:S(2)}) collective-permute-start(bf16[2,96,256]{2,1,0:T(8,128)(2,1)S(1)} %stack.6.refs_0_), channel_id=1, source_target_pairs={{0,24},{4,28},{8,16},{12,20},{16,8},{20,12},{24,0},{28,4},{1,25},{... | collective-permute-start | bytes 294920 | tf_op jit(solution)/shard_map/ppermute | solution.py:205
  12.6 0.3 %collective-permute-start.5 = (bf16[2,96,256]{2,1,0:T(8,128)(2,1)S(1)}, bf16[2,96,256]{2,1,0:T(8,128)(2,1)S(1)}, u32[]{:S(2)}, u32[]{:S(2)}) collective-permute-start(bf16[2,96,256]{2,1,0:T(8,128)(2,1)S(1)} %stack.6.refs_0_), channel_id=1, source_target_pairs={{0,8},{4,12},{8,0},{12,4},{16,24},{20,28},{24,16},{28,20},{1,9},{5... | collective-permute-start | bytes 294920 | tf_op jit(solution)/shard_map/ppermute | solution.py:205
  12.9 0.0 collective-permute-done.8.refs_1_
  12.9 0.2 collective-permute-start.4
  13.1 0.0 collective-permute-done.11.refs_1_
  13.2 2.8 %collective-permute-start.9 = (bf16[4,96,256]{2,1,0:T(8,128)(2,1)S(1)}, bf16[4,96,256]{2,1,0:T(8,128)(2,1)S(1)}, u32[]{:S(2)}, u32[]{:S(2)}) collective-permute-start(bf16[4,96,256]{2,1,0:T(8,128)(2,1)S(1)} %stack.10.refs_1_), channel_id=1, source_target_pairs={{0,4},{4,0},{8,12},{12,8},{16,20},{20,16},{24,28},{28,24},{1,5},{5... | collective-permute-start | bytes 589832 | tf_op jit(solution)/shard_map/ppermute | solution.py:205
  15.9 0.0 collective-permute-done.10.refs_0_
  15.9 0.1 collective-permute-start.12
  16.0 0.0 collective-permute-done.2.refs_1_
  16.1 2.0 %collective-permute-start.3 = (bf16[4,96,256]{2,1,0:T(8,128)(2,1)S(1)}, bf16[4,96,256]{2,1,0:T(8,128)(2,1)S(1)}, u32[]{:S(2)}, u32[]{:S(2)}) collective-permute-start(bf16[4,96,256]{2,1,0:T(8,128)(2,1)S(1)} %stack.7.refs_1_), channel_id=1, source_target_pairs={{0,4},{4,0},{8,12},{12,8},{16,20},{20,16},{24,28},{28,24},{1,5},{5... | collective-permute-start | bytes 589832 | tf_op jit(solution)/shard_map/ppermute | solution.py:205
  18.0 0.0 collective-permute-done.5.refs_1_
  18.0 0.0 collective-permute-done.4.refs_0_
  18.1 2.0 %collective-permute-start.6 = (bf16[4,96,256]{2,1,0:T(8,128)(2,1)S(1)}, bf16[4,96,256]{2,1,0:T(8,128)(2,1)S(1)}, u32[]{:S(2)}, u32[]{:S(2)}) collective-permute-start(bf16[4,96,256]{2,1,0:T(8,128)(2,1)S(1)} %stack.8.refs_3_), channel_id=1, source_target_pairs={{0,4},{4,0},{8,12},{12,8},{16,20},{20,16},{24,28},{28,24},{1,5},{5... | collective-permute-start | bytes 589832 | tf_op jit(solution)/shard_map/ppermute | solution.py:205
  20.0 0.0 collective-permute-done.9.refs_2_
  20.0 0.0 collective-permute-done.12.refs_4_
  20.0 1.6 %correlate.1.refs_5_ = f32[2,4,8,128,128]{4,3,2,1,0:T(8,128)S(1)} custom-call(s32[1,5]{1,0:T(1,128)S(1)} %add_bitcast_fusion.refs_2_.refs_0_, bf16[4,96,256]{2,1,0:T(8,128)(2,1)S(1)} %stack.10.refs_1_, bf16[4,96,256]{2,1,0:T(8,128)(2,1)S(1)} %collective-permute-done.9.refs_2_, bf16[4,96,256]{2,1,0:T(8,128)(2,1)S(1)} %stack.11.refs_3_, ...), custom_call_target="tpu_custom_call" | custom-call | tf_op jit(solution)/shard_map/correlate/pallas_call | solution.py:187
  21.6 0.0 collective-permute-done.3.refs_2_
  21.7 0.0 collective-permute-done.6.refs_4_
  21.7 2.7 %correlate_add.1 = f32[2,4,8,128,128]{4,3,2,1,0:T(8,128)} custom-call(s32[1,5]{1,0:T(1,128)S(1)} %add_bitcast_fusion.refs_2_.refs_0_, bf16[4,96,256]{2,1,0:T(8,128)(2,1)S(1)} %stack.7.refs_1_, bf16[4,96,256]{2,1,0:T(8,128)(2,1)S(1)} %collective-permute-done.3.refs_2_, bf16[4,96,256]{2,1,0:T(8,128)(2,1)S(1)} %stack.8.refs_3_, ...), custom_call_target="tpu_custom_call" | custom-call | tf_op jit(solution)/shard_map/correlate_add/pallas_call | solution.py:187
  (6 shorter events, 0.1 us)
Async XLA Ops:
  0.0 5.6 %copy-start = (s32[8,2]{0,1:T(2,128)S(1)}, s32[8,2]{0,1:T(2,128)}, u32[]{:S(2)}) copy-start(s32[8,2]{0,1:T(2,128)} %param.5) | copy-start | bytes 196
  1.1 4.8 %collective-permute-start.7 = (bf16[1,96,256]{2,1,0:T(8,128)(2,1)S(1)}, bf16[1,96,256]{2,1,0:T(8,128)(2,1)S(1)}, u32[]{:S(2)}, u32[]{:S(2)}) collective-permute-start(bf16[1,96,256]{2,1,0:T(8,128)(2,1)S(1)} %bitcast.7), channel_id=1, source_target_pairs={{0,1},{1,0},{2,3},{3,2},{4,5},{5,4},{6,7},{7,6},{8,9},{9,8},{10,11... | collective-permute-start | bytes 147464 | tf_op jit(solution)/shard_map/ppermute | solution.py:205
  3.3 5.4 %collective-permute-start.1 = (bf16[1,96,256]{2,1,0:T(8,128)(2,1)S(1)}, bf16[1,96,256]{2,1,0:T(8,128)(2,1)S(1)}, u32[]{:S(2)}, u32[]{:S(2)}) collective-permute-start(bf16[1,96,256]{2,1,0:T(8,128)(2,1)S(1)} %bitcast.8), channel_id=1, source_target_pairs={{0,3},{1,2},{2,1},{3,0},{4,7},{5,6},{6,5},{7,4},{8,11},{9,10},{10,... | collective-permute-start | bytes 147464 | tf_op jit(solution)/shard_map/ppermute | solution.py:205
  5.5 4.9 %collective-permute-start = (bf16[1,96,256]{2,1,0:T(8,128)(2,1)S(1)}, bf16[1,96,256]{2,1,0:T(8,128)(2,1)S(1)}, u32[]{:S(2)}, u32[]{:S(2)}) collective-permute-start(bf16[1,96,256]{2,1,0:T(8,128)(2,1)S(1)} %bitcast.9), channel_id=1, source_target_pairs={{0,2},{1,3},{2,0},{3,1},{4,6},{5,7},{6,4},{7,5},{8,10},{9,11},{10,... | collective-permute-start | bytes 147464 | tf_op jit(solution)/shard_map/ppermute | solution.py:205
  5.9 7.0 %collective-permute-start.8 = (bf16[2,96,256]{2,1,0:T(8,128)(2,1)S(1)}, bf16[2,96,256]{2,1,0:T(8,128)(2,1)S(1)}, u32[]{:S(2)}, u32[]{:S(2)}) collective-permute-start(bf16[2,96,256]{2,1,0:T(8,128)(2,1)S(1)} %stack.9.refs_0_), channel_id=1, source_target_pairs={{0,24},{4,28},{8,16},{12,20},{16,8},{20,12},{24,0},{28,4},{1,25},{... | collective-permute-start | bytes 294920 | tf_op jit(solution)/shard_map/ppermute | solution.py:205
  8.2 4.9 %collective-permute-start.11 = (bf16[2,96,256]{2,1,0:T(8,128)(2,1)S(1)}, bf16[2,96,256]{2,1,0:T(8,128)(2,1)S(1)}, u32[]{:S(2)}, u32[]{:S(2)}) collective-permute-start(bf16[2,96,256]{2,1,0:T(8,128)(2,1)S(1)} %stack.9.refs_0_), channel_id=1, source_target_pairs={{0,8},{4,12},{8,0},{12,4},{16,24},{20,28},{24,16},{28,20},{1,9},{5... | collective-permute-start | bytes 294920 | tf_op jit(solution)/shard_map/ppermute | solution.py:205
  8.5 7.5 %collective-permute-start.10 = (bf16[2,96,256]{2,1,0:T(8,128)(2,1)S(1)}, bf16[2,96,256]{2,1,0:T(8,128)(2,1)S(1)}, u32[]{:S(2)}, u32[]{:S(2)}) collective-permute-start(bf16[2,96,256]{2,1,0:T(8,128)(2,1)S(1)} %stack.9.refs_0_), channel_id=1, source_target_pairs={{0,16},{4,20},{8,24},{12,28},{16,0},{20,4},{24,8},{28,12},{1,17},{... | collective-permute-start | bytes 294920 | tf_op jit(solution)/shard_map/ppermute | solution.py:205
  10.4 5.6 %collective-permute-start.2 = (bf16[2,96,256]{2,1,0:T(8,128)(2,1)S(1)}, bf16[2,96,256]{2,1,0:T(8,128)(2,1)S(1)}, u32[]{:S(2)}, u32[]{:S(2)}) collective-permute-start(bf16[2,96,256]{2,1,0:T(8,128)(2,1)S(1)} %stack.6.refs_0_), channel_id=1, source_target_pairs={{0,24},{4,28},{8,16},{12,20},{16,8},{20,12},{24,0},{28,4},{1,25},{... | collective-permute-start | bytes 294920 | tf_op jit(solution)/shard_map/ppermute | solution.py:205
  12.6 5.4 %collective-permute-start.5 = (bf16[2,96,256]{2,1,0:T(8,128)(2,1)S(1)}, bf16[2,96,256]{2,1,0:T(8,128)(2,1)S(1)}, u32[]{:S(2)}, u32[]{:S(2)}) collective-permute-start(bf16[2,96,256]{2,1,0:T(8,128)(2,1)S(1)} %stack.6.refs_0_), channel_id=1, source_target_pairs={{0,8},{4,12},{8,0},{12,4},{16,24},{20,28},{24,16},{28,20},{1,9},{5... | collective-permute-start | bytes 294920 | tf_op jit(solution)/shard_map/ppermute | solution.py:205
  12.9 5.1 %collective-permute-start.4 = (bf16[2,96,256]{2,1,0:T(8,128)(2,1)S(1)}, bf16[2,96,256]{2,1,0:T(8,128)(2,1)S(1)}, u32[]{:S(2)}, u32[]{:S(2)}) collective-permute-start(bf16[2,96,256]{2,1,0:T(8,128)(2,1)S(1)} %stack.6.refs_0_), channel_id=1, source_target_pairs={{0,16},{4,20},{8,24},{12,28},{16,0},{20,4},{24,8},{28,12},{1,17},{... | collective-permute-start | bytes 294920 | tf_op jit(solution)/shard_map/ppermute | solution.py:205
  13.2 6.9 %collective-permute-start.9 = (bf16[4,96,256]{2,1,0:T(8,128)(2,1)S(1)}, bf16[4,96,256]{2,1,0:T(8,128)(2,1)S(1)}, u32[]{:S(2)}, u32[]{:S(2)}) collective-permute-start(bf16[4,96,256]{2,1,0:T(8,128)(2,1)S(1)} %stack.10.refs_1_), channel_id=1, source_target_pairs={{0,4},{4,0},{8,12},{12,8},{16,20},{20,16},{24,28},{28,24},{1,5},{5... | collective-permute-start | bytes 589832 | tf_op jit(solution)/shard_map/ppermute | solution.py:205
  15.9 4.1 %collective-permute-start.12 = (bf16[4,96,256]{2,1,0:T(8,128)(2,1)S(1)}, bf16[4,96,256]{2,1,0:T(8,128)(2,1)S(1)}, u32[]{:S(2)}, u32[]{:S(2)}) collective-permute-start(bf16[4,96,256]{2,1,0:T(8,128)(2,1)S(1)} %stack.11.refs_3_), channel_id=1, source_target_pairs={{0,4},{4,0},{8,12},{12,8},{16,20},{20,16},{24,28},{28,24},{1,5},{5... | collective-permute-start | bytes 589832 | tf_op jit(solution)/shard_map/ppermute | solution.py:205
  16.1 5.6 %collective-permute-start.3 = (bf16[4,96,256]{2,1,0:T(8,128)(2,1)S(1)}, bf16[4,96,256]{2,1,0:T(8,128)(2,1)S(1)}, u32[]{:S(2)}, u32[]{:S(2)}) collective-permute-start(bf16[4,96,256]{2,1,0:T(8,128)(2,1)S(1)} %stack.7.refs_1_), channel_id=1, source_target_pairs={{0,4},{4,0},{8,12},{12,8},{16,20},{20,16},{24,28},{28,24},{1,5},{5... | collective-permute-start | bytes 589832 | tf_op jit(solution)/shard_map/ppermute | solution.py:205
  18.1 3.6 %collective-permute-start.6 = (bf16[4,96,256]{2,1,0:T(8,128)(2,1)S(1)}, bf16[4,96,256]{2,1,0:T(8,128)(2,1)S(1)}, u32[]{:S(2)}, u32[]{:S(2)}) collective-permute-start(bf16[4,96,256]{2,1,0:T(8,128)(2,1)S(1)} %stack.8.refs_3_), channel_id=1, source_target_pairs={{0,4},{4,0},{8,12},{12,8},{16,20},{20,16},{24,28},{28,24},{1,5},{5... | collective-permute-start | bytes 589832 | tf_op jit(solution)/shard_map/ppermute | solution.py:205

commit v28 on v26

--- a/solution.py
+++ b/solution.py
@@ -249,8 +249,10 @@
     hours = spectra.shape[1] * groups
     tiles = tile_list.shape[0] // groups
     white = whiten(spectra, bad_channels)
-    pairs = lax.dynamic_slice_in_dim(tile_list, lax.axis_index("tm") * tiles, tiles, axis=0)
-    where = jnp.concatenate([lax.axis_index("chan").reshape(1), pairs.reshape(-1)]).astype(jnp.int32).reshape(1, -1)
+    at, row, side = (lax.broadcasted_iota(jnp.int32, (1 + 2 * tiles, *tile_list.shape), d) for d in range(3))
+    first = 2 * tiles * lax.axis_index("tm")
+    blocks = jnp.sum(jnp.where((at > 0) & (at - 1 + first == 2 * row + side), tile_list[None], 0), axis=(1, 2))
+    where = jnp.where(jnp.arange(1 + 2 * tiles) == 0, lax.axis_index("chan"), blocks).astype(jnp.int32).reshape(1, -1)
     near, far = halves(white, where)
     near, far = between_cores(between_chips(near, 2)), between_cores(between_chips(far, 2))
     partial = correlate(near, groups // 2, where, range(tiles), hours)

time: 24.5 us -> 24.6 us (level)
  other arithmetic: 0.07 us -> 0.96 us
  waiting for transfers between devices: 1.74 us -> 1.21 us
  local copies, waits for them, and re-layouts: 0.26 us -> 0 us
    reduce_sum x0 -> x1, other arithmetic: none -> 0.95 us  [per_device(): jnp.sum(jnp.where((at > 0) & (at - 1 + first == 2 * row + side), tile_lis...]
    ppermute x13, waiting for transfers between devices: 1.74 us -> 1.21 us  [swap(): lax.ppermute(array, axis, [(i, i ^ k) for i in range(lax.axis_size(axis))])]
  transfers between devices with their start and end apart: 13 -> 13, of which waited for: 1 -> 2; matrix products, arithmetic and copies ran while one was open for 1% -> 4% of each run, Pallas kernels for 7% -> 7%
where the time goes in v28:
time: 24.6 us; the launch traced here: 24.3 us
  starting transfers between devices  16.6 us (67%)
  Pallas kernels  5.44 us (22%)
  waiting for transfers between devices  1.21 us (5%)
  other arithmetic  0.96 us (4%)
    ppermute x13, starting transfers between devices, swap(): lax.ppermute(array, axis, [(i, i ^ k) for i in range(lax.axis_size(axis))])  16.6 us
    pallas_call x2, Pallas kernels, correlate(): pl.pallas_call(lambda *refs: correlate_kernel(norm, picked, adds, places,...  4.27 us
    ppermute x13, waiting for transfers between devices, swap(): lax.ppermute(array, axis, [(i, i ^ k) for i in range(lax.axis_size(axis))])  1.21 us
    pallas_call x1, Pallas kernels, whiten(): pl.pallas_call(whiten_kernel, out_shape=jax.ShapeDtypeStruct((chans, spec...  1.1 us
    reduce_sum x1, other arithmetic, per_device(): jnp.sum(jnp.where((at > 0) & (at - 1 + first == 2 * row + side), tile_lis...  0.95 us
  transfers between devices with their start and end apart: 13, of which 2 were waited for; matrix products, arithmetic and copies ran while one was open for 4% of the time, Pallas kernels for 7%

profile of v28, /device:TPU:1, one launch (start us, length us, event | category | flops | bytes accessed | tf_op | source)
XLA Modules:
  0.0 24.3 jit_solution(547731287462959719)
XLA Ops:
  0.0 1.1 %whiten.1 = bf16[96,256]{1,0:T(8,128)(2,1)S(1)} custom-call(bf16[256,96]{1,0:T(8,128)(2,1)} %bitcast.10, s32[1,96]{1,0:T(1,128)} %bitcast.11), custom_call_target="tpu_custom_call" | custom-call | tf_op jit(solution)/shard_map/whiten/pallas_call | solution.py:56
  1.1 2.2 %collective-permute-start.7 = (bf16[1,96,256]{2,1,0:T(8,128)(2,1)S(1)}, bf16[1,96,256]{2,1,0:T(8,128)(2,1)S(1)}, u32[]{:S(2)}, u32[]{:S(2)}) collective-permute-start(bf16[1,96,256]{2,1,0:T(8,128)(2,1)S(1)} %bitcast.6), channel_id=1, source_target_pairs={{0,1},{1,0},{2,3},{3,2},{4,5},{5,4},{6,7},{7,6},{8,9},{9,8},{10,11... | collective-permute-start | bytes 147464 | tf_op jit(solution)/shard_map/ppermute | solution.py:204
  3.3 2.2 %collective-permute-start.1 = (bf16[1,96,256]{2,1,0:T(8,128)(2,1)S(1)}, bf16[1,96,256]{2,1,0:T(8,128)(2,1)S(1)}, u32[]{:S(2)}, u32[]{:S(2)}) collective-permute-start(bf16[1,96,256]{2,1,0:T(8,128)(2,1)S(1)} %bitcast.7), channel_id=1, source_target_pairs={{0,3},{1,2},{2,1},{3,0},{4,7},{5,6},{6,5},{7,4},{8,11},{9,10},{10,... | collective-permute-start | bytes 147464 | tf_op jit(solution)/shard_map/ppermute | solution.py:204
  5.5 0.1 collective-permute-start
  5.6 0.9 %fusion = s32[5]{0:T(128)S(1)} fusion(pred[5]{0:T(512)(128)(4,1)S(1)} %iota_compare_fusion, s32[5]{0:T(128)S(1)} %add_add_fusion, s32[8,2]{0,1:T(2,128)} %param.5, s32[8]{0:T(128)S(1)} %iota_multiply_fusion), kind=kLoop, calls=%fused_computation.1 | loop fusion | flops 395 | bytes 141 | tf_op jit(solution)/shard_map/reduce_sum | solution.py:254
  6.6 0.0 collective-permute-done.7.refs_1_
  6.6 2.2 %collective-permute-start.8 = (bf16[2,96,256]{2,1,0:T(8,128)(2,1)S(1)}, bf16[2,96,256]{2,1,0:T(8,128)(2,1)S(1)}, u32[]{:S(2)}, u32[]{:S(2)}) collective-permute-start(bf16[2,96,256]{2,1,0:T(8,128)(2,1)S(1)} %stack.9.refs_0_), channel_id=1, source_target_pairs={{0,24},{4,28},{8,16},{12,20},{16,8},{20,12},{24,0},{28,4},{1,25},{... | collective-permute-start | bytes 294920 | tf_op jit(solution)/shard_map/ppermute | solution.py:204
  8.8 0.3 %collective-permute-start.11 = (bf16[2,96,256]{2,1,0:T(8,128)(2,1)S(1)}, bf16[2,96,256]{2,1,0:T(8,128)(2,1)S(1)}, u32[]{:S(2)}, u32[]{:S(2)}) collective-permute-start(bf16[2,96,256]{2,1,0:T(8,128)(2,1)S(1)} %stack.9.refs_0_), channel_id=1, source_target_pairs={{0,8},{4,12},{8,0},{12,4},{16,24},{20,28},{24,16},{28,20},{1,9},{5... | collective-permute-start | bytes 294920 | tf_op jit(solution)/shard_map/ppermute | solution.py:204
  9.1 0.2 collective-permute-start.10
  9.3 0.0 collective-permute-done.1.refs_1_
  9.3 1.1 %collective-permute-done.refs_0_ = bf16[1,96,256]{2,1,0:T(8,128)(2,1)S(1)} collective-permute-done((bf16[1,96,256]{2,1,0:T(8,128)(2,1)S(1)}, bf16[1,96,256]{2,1,0:T(8,128)(2,1)S(1)}, u32[]{:S(2)}, u32[]{:S(2)}) %collective-permute-start) | collective-permute-done | bytes 49184 | tf_op jit(solution)/shard_map/ppermute | solution.py:204
  10.4 2.2 %collective-permute-start.2 = (bf16[2,96,256]{2,1,0:T(8,128)(2,1)S(1)}, bf16[2,96,256]{2,1,0:T(8,128)(2,1)S(1)}, u32[]{:S(2)}, u32[]{:S(2)}) collective-permute-start(bf16[2,96,256]{2,1,0:T(8,128)(2,1)S(1)} %stack.6.refs_0_), channel_id=1, source_target_pairs={{0,24},{4,28},{8,16},{12,20},{16,8},{20,12},{24,0},{28,4},{1,25},{... | collective-permute-start | bytes 294920 | tf_op jit(solution)/shard_map/ppermute | solution.py:204
  12.6 0.3 %collective-permute-start.5 = (bf16[2,96,256]{2,1,0:T(8,128)(2,1)S(1)}, bf16[2,96,256]{2,1,0:T(8,128)(2,1)S(1)}, u32[]{:S(2)}, u32[]{:S(2)}) collective-permute-start(bf16[2,96,256]{2,1,0:T(8,128)(2,1)S(1)} %stack.6.refs_0_), channel_id=1, source_target_pairs={{0,8},{4,12},{8,0},{12,4},{16,24},{20,28},{24,16},{28,20},{1,9},{5... | collective-permute-start | bytes 294920 | tf_op jit(solution)/shard_map/ppermute | solution.py:204
  12.9 0.0 collective-permute-done.8.refs_1_
  12.9 0.2 collective-permute-start.4
  13.1 0.1 collective-permute-done.11.refs_1_
  13.2 2.7 %collective-permute-start.9 = (bf16[4,96,256]{2,1,0:T(8,128)(2,1)S(1)}, bf16[4,96,256]{2,1,0:T(8,128)(2,1)S(1)}, u32[]{:S(2)}, u32[]{:S(2)}) collective-permute-start(bf16[4,96,256]{2,1,0:T(8,128)(2,1)S(1)} %stack.10.refs_1_), channel_id=1, source_target_pairs={{0,4},{4,0},{8,12},{12,8},{16,20},{20,16},{24,28},{28,24},{1,5},{5... | collective-permute-start | bytes 589832 | tf_op jit(solution)/shard_map/ppermute | solution.py:204
  15.9 0.0 collective-permute-done.10.refs_0_
  15.9 1.0 %collective-permute-start.12 = (bf16[4,96,256]{2,1,0:T(8,128)(2,1)S(1)}, bf16[4,96,256]{2,1,0:T(8,128)(2,1)S(1)}, u32[]{:S(2)}, u32[]{:S(2)}) collective-permute-start(bf16[4,96,256]{2,1,0:T(8,128)(2,1)S(1)} %stack.11.refs_3_), channel_id=1, source_target_pairs={{0,4},{4,0},{8,12},{12,8},{16,20},{20,16},{24,28},{28,24},{1,5},{5... | collective-permute-start | bytes 589832 | tf_op jit(solution)/shard_map/ppermute | solution.py:204
  16.9 0.0 collective-permute-done.2.refs_1_
  17.0 1.4 %collective-permute-start.3 = (bf16[4,96,256]{2,1,0:T(8,128)(2,1)S(1)}, bf16[4,96,256]{2,1,0:T(8,128)(2,1)S(1)}, u32[]{:S(2)}, u32[]{:S(2)}) collective-permute-start(bf16[4,96,256]{2,1,0:T(8,128)(2,1)S(1)} %stack.7.refs_1_), channel_id=1, source_target_pairs={{0,4},{4,0},{8,12},{12,8},{16,20},{20,16},{24,28},{28,24},{1,5},{5... | collective-permute-start | bytes 589832 | tf_op jit(solution)/shard_map/ppermute | solution.py:204
  18.4 0.0 collective-permute-done.5.refs_1_
  18.4 0.0 collective-permute-done.4.refs_0_
  18.4 1.6 %collective-permute-start.6 = (bf16[4,96,256]{2,1,0:T(8,128)(2,1)S(1)}, bf16[4,96,256]{2,1,0:T(8,128)(2,1)S(1)}, u32[]{:S(2)}, u32[]{:S(2)}) collective-permute-start(bf16[4,96,256]{2,1,0:T(8,128)(2,1)S(1)} %stack.8.refs_3_), channel_id=1, source_target_pairs={{0,4},{4,0},{8,12},{12,8},{16,20},{20,16},{24,28},{28,24},{1,5},{5... | collective-permute-start | bytes 589832 | tf_op jit(solution)/shard_map/ppermute | solution.py:204
  20.0 0.0 collective-permute-done.9.refs_2_
  20.0 0.0 collective-permute-done.12.refs_4_
  20.0 1.6 %correlate.1.refs_5_ = f32[2,4,8,128,128]{4,3,2,1,0:T(8,128)S(1)} custom-call(s32[1,5]{1,0:T(1,128)S(1)} %compare_select_fusion.refs_2_.refs_0_, bf16[4,96,256]{2,1,0:T(8,128)(2,1)S(1)} %stack.10.refs_1_, bf16[4,96,256]{2,1,0:T(8,128)(2,1)S(1)} %collective-permute-done.9.refs_2_, bf16[4,96,256]{2,1,0:T(8,128)(2,1)S(1)} %stack.11.refs_3_, ...), custom_call_target="tpu_custom_call" | custom-call | tf_op jit(solution)/shard_map/correlate/pallas_call | solution.py:186
  21.6 0.0 collective-permute-done.3.refs_2_
  21.6 0.0 collective-permute-done.6.refs_4_
  21.7 2.7 %correlate_add.1 = f32[2,4,8,128,128]{4,3,2,1,0:T(8,128)} custom-call(s32[1,5]{1,0:T(1,128)S(1)} %compare_select_fusion.refs_2_.refs_0_, bf16[4,96,256]{2,1,0:T(8,128)(2,1)S(1)} %stack.7.refs_1_, bf16[4,96,256]{2,1,0:T(8,128)(2,1)S(1)} %collective-permute-done.3.refs_2_, bf16[4,96,256]{2,1,0:T(8,128)(2,1)S(1)} %stack.8.refs_3_, ...), custom_call_target="tpu_custom_call" | custom-call | tf_op jit(solution)/shard_map/correlate_add/pallas_call | solution.py:186
  (10 shorter events, 0.1 us)
Async XLA Ops:
  1.1 5.5 %collective-permute-start.7 = (bf16[1,96,256]{2,1,0:T(8,128)(2,1)S(1)}, bf16[1,96,256]{2,1,0:T(8,128)(2,1)S(1)}, u32[]{:S(2)}, u32[]{:S(2)}) collective-permute-start(bf16[1,96,256]{2,1,0:T(8,128)(2,1)S(1)} %bitcast.6), channel_id=1, source_target_pairs={{0,1},{1,0},{2,3},{3,2},{4,5},{5,4},{6,7},{7,6},{8,9},{9,8},{10,11... | collective-permute-start | bytes 147464 | tf_op jit(solution)/shard_map/ppermute | solution.py:204
  3.3 6.0 %collective-permute-start.1 = (bf16[1,96,256]{2,1,0:T(8,128)(2,1)S(1)}, bf16[1,96,256]{2,1,0:T(8,128)(2,1)S(1)}, u32[]{:S(2)}, u32[]{:S(2)}) collective-permute-start(bf16[1,96,256]{2,1,0:T(8,128)(2,1)S(1)} %bitcast.7), channel_id=1, source_target_pairs={{0,3},{1,2},{2,1},{3,0},{4,7},{5,6},{6,5},{7,4},{8,11},{9,10},{10,... | collective-permute-start | bytes 147464 | tf_op jit(solution)/shard_map/ppermute | solution.py:204
  5.5 4.9 %collective-permute-start = (bf16[1,96,256]{2,1,0:T(8,128)(2,1)S(1)}, bf16[1,96,256]{2,1,0:T(8,128)(2,1)S(1)}, u32[]{:S(2)}, u32[]{:S(2)}) collective-permute-start(bf16[1,96,256]{2,1,0:T(8,128)(2,1)S(1)} %bitcast.8), channel_id=1, source_target_pairs={{0,2},{1,3},{2,0},{3,1},{4,6},{5,7},{6,4},{7,5},{8,10},{9,11},{10,... | collective-permute-start | bytes 147464 | tf_op jit(solution)/shard_map/ppermute | solution.py:204
  6.6 6.3 %collective-permute-start.8 = (bf16[2,96,256]{2,1,0:T(8,128)(2,1)S(1)}, bf16[2,96,256]{2,1,0:T(8,128)(2,1)S(1)}, u32[]{:S(2)}, u32[]{:S(2)}) collective-permute-start(bf16[2,96,256]{2,1,0:T(8,128)(2,1)S(1)} %stack.9.refs_0_), channel_id=1, source_target_pairs={{0,24},{4,28},{8,16},{12,20},{16,8},{20,12},{24,0},{28,4},{1,25},{... | collective-permute-start | bytes 294920 | tf_op jit(solution)/shard_map/ppermute | solution.py:204
  8.8 4.4 %collective-permute-start.11 = (bf16[2,96,256]{2,1,0:T(8,128)(2,1)S(1)}, bf16[2,96,256]{2,1,0:T(8,128)(2,1)S(1)}, u32[]{:S(2)}, u32[]{:S(2)}) collective-permute-start(bf16[2,96,256]{2,1,0:T(8,128)(2,1)S(1)} %stack.9.refs_0_), channel_id=1, source_target_pairs={{0,8},{4,12},{8,0},{12,4},{16,24},{20,28},{24,16},{28,20},{1,9},{5... | collective-permute-start | bytes 294920 | tf_op jit(solution)/shard_map/ppermute | solution.py:204
  9.1 6.8 %collective-permute-start.10 = (bf16[2,96,256]{2,1,0:T(8,128)(2,1)S(1)}, bf16[2,96,256]{2,1,0:T(8,128)(2,1)S(1)}, u32[]{:S(2)}, u32[]{:S(2)}) collective-permute-start(bf16[2,96,256]{2,1,0:T(8,128)(2,1)S(1)} %stack.9.refs_0_), channel_id=1, source_target_pairs={{0,16},{4,20},{8,24},{12,28},{16,0},{20,4},{24,8},{28,12},{1,17},{... | collective-permute-start | bytes 294920 | tf_op jit(solution)/shard_map/ppermute | solution.py:204
  10.4 6.5 %collective-permute-start.2 = (bf16[2,96,256]{2,1,0:T(8,128)(2,1)S(1)}, bf16[2,96,256]{2,1,0:T(8,128)(2,1)S(1)}, u32[]{:S(2)}, u32[]{:S(2)}) collective-permute-start(bf16[2,96,256]{2,1,0:T(8,128)(2,1)S(1)} %stack.6.refs_0_), channel_id=1, source_target_pairs={{0,24},{4,28},{8,16},{12,20},{16,8},{20,12},{24,0},{28,4},{1,25},{... | collective-permute-start | bytes 294920 | tf_op jit(solution)/shard_map/ppermute | solution.py:204
  12.6 5.8 %collective-permute-start.5 = (bf16[2,96,256]{2,1,0:T(8,128)(2,1)S(1)}, bf16[2,96,256]{2,1,0:T(8,128)(2,1)S(1)}, u32[]{:S(2)}, u32[]{:S(2)}) collective-permute-start(bf16[2,96,256]{2,1,0:T(8,128)(2,1)S(1)} %stack.6.refs_0_), channel_id=1, source_target_pairs={{0,8},{4,12},{8,0},{12,4},{16,24},{20,28},{24,16},{28,20},{1,9},{5... | collective-permute-start | bytes 294920 | tf_op jit(solution)/shard_map/ppermute | solution.py:204
  12.9 5.5 %collective-permute-start.4 = (bf16[2,96,256]{2,1,0:T(8,128)(2,1)S(1)}, bf16[2,96,256]{2,1,0:T(8,128)(2,1)S(1)}, u32[]{:S(2)}, u32[]{:S(2)}) collective-permute-start(bf16[2,96,256]{2,1,0:T(8,128)(2,1)S(1)} %stack.6.refs_0_), channel_id=1, source_target_pairs={{0,16},{4,20},{8,24},{12,28},{16,0},{20,4},{24,8},{28,12},{1,17},{... | collective-permute-start | bytes 294920 | tf_op jit(solution)/shard_map/ppermute | solution.py:204
  13.2 6.8 %collective-permute-start.9 = (bf16[4,96,256]{2,1,0:T(8,128)(2,1)S(1)}, bf16[4,96,256]{2,1,0:T(8,128)(2,1)S(1)}, u32[]{:S(2)}, u32[]{:S(2)}) collective-permute-start(bf16[4,96,256]{2,1,0:T(8,128)(2,1)S(1)} %stack.10.refs_1_), channel_id=1, source_target_pairs={{0,4},{4,0},{8,12},{12,8},{16,20},{20,16},{24,28},{28,24},{1,5},{5... | collective-permute-start | bytes 589832 | tf_op jit(solution)/shard_map/ppermute | solution.py:204
  15.9 4.1 %collective-permute-start.12 = (bf16[4,96,256]{2,1,0:T(8,128)(2,1)S(1)}, bf16[4,96,256]{2,1,0:T(8,128)(2,1)S(1)}, u32[]{:S(2)}, u32[]{:S(2)}) collective-permute-start(bf16[4,96,256]{2,1,0:T(8,128)(2,1)S(1)} %stack.11.refs_3_), channel_id=1, source_target_pairs={{0,4},{4,0},{8,12},{12,8},{16,20},{20,16},{24,28},{28,24},{1,5},{5... | collective-permute-start | bytes 589832 | tf_op jit(solution)/shard_map/ppermute | solution.py:204
  17.0 4.7 %collective-permute-start.3 = (bf16[4,96,256]{2,1,0:T(8,128)(2,1)S(1)}, bf16[4,96,256]{2,1,0:T(8,128)(2,1)S(1)}, u32[]{:S(2)}, u32[]{:S(2)}) collective-permute-start(bf16[4,96,256]{2,1,0:T(8,128)(2,1)S(1)} %stack.7.refs_1_), channel_id=1, source_target_pairs={{0,4},{4,0},{8,12},{12,8},{16,20},{20,16},{24,28},{28,24},{1,5},{5... | collective-permute-start | bytes 589832 | tf_op jit(solution)/shard_map/ppermute | solution.py:204
  18.4 3.2 %collective-permute-start.6 = (bf16[4,96,256]{2,1,0:T(8,128)(2,1)S(1)}, bf16[4,96,256]{2,1,0:T(8,128)(2,1)S(1)}, u32[]{:S(2)}, u32[]{:S(2)}) collective-permute-start(bf16[4,96,256]{2,1,0:T(8,128)(2,1)S(1)} %stack.8.refs_3_), channel_id=1, source_target_pairs={{0,4},{4,0},{8,12},{12,8},{16,20},{20,16},{24,28},{28,24},{1,5},{5... | collective-permute-start | bytes 589832 | tf_op jit(solution)/shard_map/ppermute | solution.py:204

commit v29 on v26

--- a/solution.py
+++ b/solution.py
@@ -118,7 +118,7 @@
 
     def turn_left(i):
         for g in range(groups):
-            re, im = load(where_ref[0, 1 + 2 * picked[i]], g)
+            re, im = load(where_ref[0, 1 + picked[i]], g)
             for k in (4, 12):
                 forward, backward = turn_by(re, im, *(norm * part for part in table[k]), True)
                 store(left_turned, i % slots, COARSE.index(k), g, forward)
@@ -126,7 +126,7 @@
 
     def turn_right(i, j):
         for g in range(groups):
-            re, im = load(where_ref[0, 2 + 2 * picked[i]], g)
+            re, im = load(where_ref[0, (where_ref.shape[1] + 1) // 2 + picked[i]], g)
             if j == 0:
                 turns = (turn_by(re, im, *table[4], False)[0], (re, im))
             else:
@@ -249,7 +249,7 @@
     hours = spectra.shape[1] * groups
     tiles = tile_list.shape[0] // groups
     white = whiten(spectra, bad_channels)
-    pairs = lax.dynamic_slice_in_dim(tile_list, lax.axis_index("tm") * tiles, tiles, axis=0)
+    pairs = lax.dynamic_slice_in_dim(tile_list.T, lax.axis_index("tm") * tiles, tiles, axis=1)
     where = jnp.concatenate([lax.axis_index("chan").reshape(1), pairs.reshape(-1)]).astype(jnp.int32).reshape(1, -1)
     near, far = halves(white, where)
     near, far = between_cores(between_chips(near, 2)), between_cores(between_chips(far, 2))

time: 24.5 us -> 24.5 us (level)
  no operation moved by 1% of the time
where the time goes in v29:
time: 24.5 us; the launch traced here: 24.3 us
  starting transfers between devices  16.7 us (68%)
  Pallas kernels  5.45 us (22%)
  waiting for transfers between devices  1.84 us (8%)
    ppermute x13, starting transfers between devices, swap(): lax.ppermute(array, axis, [(i, i ^ k) for i in range(lax.axis_size(axis))])  16.7 us
    pallas_call x2, Pallas kernels, correlate(): pl.pallas_call(lambda *refs: correlate_kernel(norm, picked, adds, places,...  4.27 us
    ppermute x13, waiting for transfers between devices, swap(): lax.ppermute(array, axis, [(i, i ^ k) for i in range(lax.axis_size(axis))])  1.84 us
    pallas_call x1, Pallas kernels, whiten(): pl.pallas_call(whiten_kernel, out_shape=jax.ShapeDtypeStruct((chans, spec...  1.11 us
  transfers between devices with their start and end apart: 13, of which 1 were waited for; matrix products, arithmetic and copies ran while one was open for 1% of the time, Pallas kernels for 7%

profile of v29, /device:TPU:1, one launch (start us, length us, event | category | flops | bytes accessed | tf_op | source)
XLA Modules:
  0.0 24.3 jit_solution(8766705977887612284)
XLA Ops:
  0.0 0.0 copy-start
  0.0 1.1 %whiten.1 = bf16[96,256]{1,0:T(8,128)(2,1)S(1)} custom-call(bf16[256,96]{1,0:T(8,128)(2,1)} %bitcast.13, s32[1,96]{1,0:T(1,128)} %bitcast.14), custom_call_target="tpu_custom_call" | custom-call | tf_op jit(solution)/shard_map/whiten/pallas_call | solution.py:56
  1.1 2.2 %collective-permute-start.7 = (bf16[1,96,256]{2,1,0:T(8,128)(2,1)S(1)}, bf16[1,96,256]{2,1,0:T(8,128)(2,1)S(1)}, u32[]{:S(2)}, u32[]{:S(2)}) collective-permute-start(bf16[1,96,256]{2,1,0:T(8,128)(2,1)S(1)} %bitcast.9), channel_id=1, source_target_pairs={{0,1},{1,0},{2,3},{3,2},{4,5},{5,4},{6,7},{7,6},{8,9},{9,8},{10,11... | collective-permute-start | bytes 147464 | tf_op jit(solution)/shard_map/ppermute | solution.py:204
  3.3 2.2 %collective-permute-start.1 = (bf16[1,96,256]{2,1,0:T(8,128)(2,1)S(1)}, bf16[1,96,256]{2,1,0:T(8,128)(2,1)S(1)}, u32[]{:S(2)}, u32[]{:S(2)}) collective-permute-start(bf16[1,96,256]{2,1,0:T(8,128)(2,1)S(1)} %bitcast.10), channel_id=1, source_target_pairs={{0,3},{1,2},{2,1},{3,0},{4,7},{5,6},{6,5},{7,4},{8,11},{9,10},{10,... | collective-permute-start | bytes 147464 | tf_op jit(solution)/shard_map/ppermute | solution.py:204
  5.5 0.1 collective-permute-start
  5.6 0.0 copy-done
  5.6 0.1 dynamic-slice_bitcast_fusion
  5.7 0.1 reshape.19
  5.8 0.0 collective-permute-done.7.refs_1_
  5.8 2.2 %collective-permute-start.8 = (bf16[2,96,256]{2,1,0:T(8,128)(2,1)S(1)}, bf16[2,96,256]{2,1,0:T(8,128)(2,1)S(1)}, u32[]{:S(2)}, u32[]{:S(2)}) collective-permute-start(bf16[2,96,256]{2,1,0:T(8,128)(2,1)S(1)} %stack.9.refs_0_), channel_id=1, source_target_pairs={{0,24},{4,28},{8,16},{12,20},{16,8},{20,12},{24,0},{28,4},{1,25},{... | collective-permute-start | bytes 294920 | tf_op jit(solution)/shard_map/ppermute | solution.py:204
  8.0 0.1 add_bitcast_fusion.refs_2_.refs_0_
  8.1 0.3 %collective-permute-start.11 = (bf16[2,96,256]{2,1,0:T(8,128)(2,1)S(1)}, bf16[2,96,256]{2,1,0:T(8,128)(2,1)S(1)}, u32[]{:S(2)}, u32[]{:S(2)}) collective-permute-start(bf16[2,96,256]{2,1,0:T(8,128)(2,1)S(1)} %stack.9.refs_0_), channel_id=1, source_target_pairs={{0,8},{4,12},{8,0},{12,4},{16,24},{20,28},{24,16},{28,20},{1,9},{5... | collective-permute-start | bytes 294920 | tf_op jit(solution)/shard_map/ppermute | solution.py:204
  8.4 0.2 collective-permute-start.10
  8.6 0.0 collective-permute-done.1.refs_1_
  8.6 1.8 %collective-permute-done.refs_0_ = bf16[1,96,256]{2,1,0:T(8,128)(2,1)S(1)} collective-permute-done((bf16[1,96,256]{2,1,0:T(8,128)(2,1)S(1)}, bf16[1,96,256]{2,1,0:T(8,128)(2,1)S(1)}, u32[]{:S(2)}, u32[]{:S(2)}) %collective-permute-start) | collective-permute-done | bytes 49184 | tf_op jit(solution)/shard_map/ppermute | solution.py:204
  10.4 2.2 %collective-permute-start.2 = (bf16[2,96,256]{2,1,0:T(8,128)(2,1)S(1)}, bf16[2,96,256]{2,1,0:T(8,128)(2,1)S(1)}, u32[]{:S(2)}, u32[]{:S(2)}) collective-permute-start(bf16[2,96,256]{2,1,0:T(8,128)(2,1)S(1)} %stack.6.refs_0_), channel_id=1, source_target_pairs={{0,24},{4,28},{8,16},{12,20},{16,8},{20,12},{24,0},{28,4},{1,25},{... | collective-permute-start | bytes 294920 | tf_op jit(solution)/shard_map/ppermute | solution.py:204
  12.6 0.3 %collective-permute-start.5 = (bf16[2,96,256]{2,1,0:T(8,128)(2,1)S(1)}, bf16[2,96,256]{2,1,0:T(8,128)(2,1)S(1)}, u32[]{:S(2)}, u32[]{:S(2)}) collective-permute-start(bf16[2,96,256]{2,1,0:T(8,128)(2,1)S(1)} %stack.6.refs_0_), channel_id=1, source_target_pairs={{0,8},{4,12},{8,0},{12,4},{16,24},{20,28},{24,16},{28,20},{1,9},{5... | collective-permute-start | bytes 294920 | tf_op jit(solution)/shard_map/ppermute | solution.py:204
  12.9 0.0 collective-permute-done.8.refs_1_
  12.9 0.2 collective-permute-start.4
  13.1 0.0 collective-permute-done.11.refs_1_
  13.2 2.8 %collective-permute-start.9 = (bf16[4,96,256]{2,1,0:T(8,128)(2,1)S(1)}, bf16[4,96,256]{2,1,0:T(8,128)(2,1)S(1)}, u32[]{:S(2)}, u32[]{:S(2)}) collective-permute-start(bf16[4,96,256]{2,1,0:T(8,128)(2,1)S(1)} %stack.10.refs_1_), channel_id=1, source_target_pairs={{0,4},{4,0},{8,12},{12,8},{16,20},{20,16},{24,28},{28,24},{1,5},{5... | collective-permute-start | bytes 589832 | tf_op jit(solution)/shard_map/ppermute | solution.py:204
  15.9 0.0 collective-permute-done.10.refs_0_
  15.9 0.1 collective-permute-start.12
  16.0 0.0 collective-permute-done.2.refs_1_
  16.1 2.0 %collective-permute-start.3 = (bf16[4,96,256]{2,1,0:T(8,128)(2,1)S(1)}, bf16[4,96,256]{2,1,0:T(8,128)(2,1)S(1)}, u32[]{:S(2)}, u32[]{:S(2)}) collective-permute-start(bf16[4,96,256]{2,1,0:T(8,128)(2,1)S(1)} %stack.7.refs_1_), channel_id=1, source_target_pairs={{0,4},{4,0},{8,12},{12,8},{16,20},{20,16},{24,28},{28,24},{1,5},{5... | collective-permute-start | bytes 589832 | tf_op jit(solution)/shard_map/ppermute | solution.py:204
  18.0 0.0 collective-permute-done.5.refs_1_
  18.0 0.0 collective-permute-done.4.refs_0_
  18.1 2.0 %collective-permute-start.6 = (bf16[4,96,256]{2,1,0:T(8,128)(2,1)S(1)}, bf16[4,96,256]{2,1,0:T(8,128)(2,1)S(1)}, u32[]{:S(2)}, u32[]{:S(2)}) collective-permute-start(bf16[4,96,256]{2,1,0:T(8,128)(2,1)S(1)} %stack.8.refs_3_), channel_id=1, source_target_pairs={{0,4},{4,0},{8,12},{12,8},{16,20},{20,16},{24,28},{28,24},{1,5},{5... | collective-permute-start | bytes 589832 | tf_op jit(solution)/shard_map/ppermute | solution.py:204
  20.0 0.0 collective-permute-done.9.refs_2_
  20.0 0.0 collective-permute-done.12.refs_4_
  20.0 1.6 %correlate.1.refs_5_ = f32[2,4,8,128,128]{4,3,2,1,0:T(8,128)S(1)} custom-call(s32[1,5]{1,0:T(1,128)S(1)} %add_bitcast_fusion.refs_2_.refs_0_, bf16[4,96,256]{2,1,0:T(8,128)(2,1)S(1)} %stack.10.refs_1_, bf16[4,96,256]{2,1,0:T(8,128)(2,1)S(1)} %collective-permute-done.9.refs_2_, bf16[4,96,256]{2,1,0:T(8,128)(2,1)S(1)} %stack.11.refs_3_, ...), custom_call_target="tpu_custom_call" | custom-call | tf_op jit(solution)/shard_map/correlate/pallas_call | solution.py:186
  21.6 0.0 collective-permute-done.3.refs_2_
  21.7 0.0 collective-permute-done.6.refs_4_
  21.7 2.7 %correlate_add.1 = f32[2,4,8,128,128]{4,3,2,1,0:T(8,128)} custom-call(s32[1,5]{1,0:T(1,128)S(1)} %add_bitcast_fusion.refs_2_.refs_0_, bf16[4,96,256]{2,1,0:T(8,128)(2,1)S(1)} %stack.7.refs_1_, bf16[4,96,256]{2,1,0:T(8,128)(2,1)S(1)} %collective-permute-done.3.refs_2_, bf16[4,96,256]{2,1,0:T(8,128)(2,1)S(1)} %stack.8.refs_3_, ...), custom_call_target="tpu_custom_call" | custom-call | tf_op jit(solution)/shard_map/correlate_add/pallas_call | solution.py:186
  (6 shorter events, 0.1 us)
Async XLA Ops:
  0.0 5.6 %copy-start = (s32[8,2]{0,1:T(2,128)S(1)}, s32[8,2]{0,1:T(2,128)}, u32[]{:S(2)}) copy-start(s32[8,2]{0,1:T(2,128)} %param.5) | copy-start | bytes 196
  1.1 4.7 %collective-permute-start.7 = (bf16[1,96,256]{2,1,0:T(8,128)(2,1)S(1)}, bf16[1,96,256]{2,1,0:T(8,128)(2,1)S(1)}, u32[]{:S(2)}, u32[]{:S(2)}) collective-permute-start(bf16[1,96,256]{2,1,0:T(8,128)(2,1)S(1)} %bitcast.9), channel_id=1, source_target_pairs={{0,1},{1,0},{2,3},{3,2},{4,5},{5,4},{6,7},{7,6},{8,9},{9,8},{10,11... | collective-permute-start | bytes 147464 | tf_op jit(solution)/shard_map/ppermute | solution.py:204
  3.3 5.3 %collective-permute-start.1 = (bf16[1,96,256]{2,1,0:T(8,128)(2,1)S(1)}, bf16[1,96,256]{2,1,0:T(8,128)(2,1)S(1)}, u32[]{:S(2)}, u32[]{:S(2)}) collective-permute-start(bf16[1,96,256]{2,1,0:T(8,128)(2,1)S(1)} %bitcast.10), channel_id=1, source_target_pairs={{0,3},{1,2},{2,1},{3,0},{4,7},{5,6},{6,5},{7,4},{8,11},{9,10},{10,... | collective-permute-start | bytes 147464 | tf_op jit(solution)/shard_map/ppermute | solution.py:204
  5.5 4.9 %collective-permute-start = (bf16[1,96,256]{2,1,0:T(8,128)(2,1)S(1)}, bf16[1,96,256]{2,1,0:T(8,128)(2,1)S(1)}, u32[]{:S(2)}, u32[]{:S(2)}) collective-permute-start(bf16[1,96,256]{2,1,0:T(8,128)(2,1)S(1)} %bitcast.11), channel_id=1, source_target_pairs={{0,2},{1,3},{2,0},{3,1},{4,6},{5,7},{6,4},{7,5},{8,10},{9,11},{10,... | collective-permute-start | bytes 147464 | tf_op jit(solution)/shard_map/ppermute | solution.py:204
  5.8 7.1 %collective-permute-start.8 = (bf16[2,96,256]{2,1,0:T(8,128)(2,1)S(1)}, bf16[2,96,256]{2,1,0:T(8,128)(2,1)S(1)}, u32[]{:S(2)}, u32[]{:S(2)}) collective-permute-start(bf16[2,96,256]{2,1,0:T(8,128)(2,1)S(1)} %stack.9.refs_0_), channel_id=1, source_target_pairs={{0,24},{4,28},{8,16},{12,20},{16,8},{20,12},{24,0},{28,4},{1,25},{... | collective-permute-start | bytes 294920 | tf_op jit(solution)/shard_map/ppermute | solution.py:204
  8.1 5.0 %collective-permute-start.11 = (bf16[2,96,256]{2,1,0:T(8,128)(2,1)S(1)}, bf16[2,96,256]{2,1,0:T(8,128)(2,1)S(1)}, u32[]{:S(2)}, u32[]{:S(2)}) collective-permute-start(bf16[2,96,256]{2,1,0:T(8,128)(2,1)S(1)} %stack.9.refs_0_), channel_id=1, source_target_pairs={{0,8},{4,12},{8,0},{12,4},{16,24},{20,28},{24,16},{28,20},{1,9},{5... | collective-permute-start | bytes 294920 | tf_op jit(solution)/shard_map/ppermute | solution.py:204
  8.4 7.6 %collective-permute-start.10 = (bf16[2,96,256]{2,1,0:T(8,128)(2,1)S(1)}, bf16[2,96,256]{2,1,0:T(8,128)(2,1)S(1)}, u32[]{:S(2)}, u32[]{:S(2)}) collective-permute-start(bf16[2,96,256]{2,1,0:T(8,128)(2,1)S(1)} %stack.9.refs_0_), channel_id=1, source_target_pairs={{0,16},{4,20},{8,24},{12,28},{16,0},{20,4},{24,8},{28,12},{1,17},{... | collective-permute-start | bytes 294920 | tf_op jit(solution)/shard_map/ppermute | solution.py:204
  10.4 5.6 %collective-permute-start.2 = (bf16[2,96,256]{2,1,0:T(8,128)(2,1)S(1)}, bf16[2,96,256]{2,1,0:T(8,128)(2,1)S(1)}, u32[]{:S(2)}, u32[]{:S(2)}) collective-permute-start(bf16[2,96,256]{2,1,0:T(8,128)(2,1)S(1)} %stack.6.refs_0_), channel_id=1, source_target_pairs={{0,24},{4,28},{8,16},{12,20},{16,8},{20,12},{24,0},{28,4},{1,25},{... | collective-permute-start | bytes 294920 | tf_op jit(solution)/shard_map/ppermute | solution.py:204
  12.6 5.4 %collective-permute-start.5 = (bf16[2,96,256]{2,1,0:T(8,128)(2,1)S(1)}, bf16[2,96,256]{2,1,0:T(8,128)(2,1)S(1)}, u32[]{:S(2)}, u32[]{:S(2)}) collective-permute-start(bf16[2,96,256]{2,1,0:T(8,128)(2,1)S(1)} %stack.6.refs_0_), channel_id=1, source_target_pairs={{0,8},{4,12},{8,0},{12,4},{16,24},{20,28},{24,16},{28,20},{1,9},{5... | collective-permute-start | bytes 294920 | tf_op jit(solution)/shard_map/ppermute | solution.py:204
  12.9 5.1 %collective-permute-start.4 = (bf16[2,96,256]{2,1,0:T(8,128)(2,1)S(1)}, bf16[2,96,256]{2,1,0:T(8,128)(2,1)S(1)}, u32[]{:S(2)}, u32[]{:S(2)}) collective-permute-start(bf16[2,96,256]{2,1,0:T(8,128)(2,1)S(1)} %stack.6.refs_0_), channel_id=1, source_target_pairs={{0,16},{4,20},{8,24},{12,28},{16,0},{20,4},{24,8},{28,12},{1,17},{... | collective-permute-start | bytes 294920 | tf_op jit(solution)/shard_map/ppermute | solution.py:204
  13.2 6.9 %collective-permute-start.9 = (bf16[4,96,256]{2,1,0:T(8,128)(2,1)S(1)}, bf16[4,96,256]{2,1,0:T(8,128)(2,1)S(1)}, u32[]{:S(2)}, u32[]{:S(2)}) collective-permute-start(bf16[4,96,256]{2,1,0:T(8,128)(2,1)S(1)} %stack.10.refs_1_), channel_id=1, source_target_pairs={{0,4},{4,0},{8,12},{12,8},{16,20},{20,16},{24,28},{28,24},{1,5},{5... | collective-permute-start | bytes 589832 | tf_op jit(solution)/shard_map/ppermute | solution.py:204
  15.9 4.1 %collective-permute-start.12 = (bf16[4,96,256]{2,1,0:T(8,128)(2,1)S(1)}, bf16[4,96,256]{2,1,0:T(8,128)(2,1)S(1)}, u32[]{:S(2)}, u32[]{:S(2)}) collective-permute-start(bf16[4,96,256]{2,1,0:T(8,128)(2,1)S(1)} %stack.11.refs_3_), channel_id=1, source_target_pairs={{0,4},{4,0},{8,12},{12,8},{16,20},{20,16},{24,28},{28,24},{1,5},{5... | collective-permute-start | bytes 589832 | tf_op jit(solution)/shard_map/ppermute | solution.py:204
  16.1 5.6 %collective-permute-start.3 = (bf16[4,96,256]{2,1,0:T(8,128)(2,1)S(1)}, bf16[4,96,256]{2,1,0:T(8,128)(2,1)S(1)}, u32[]{:S(2)}, u32[]{:S(2)}) collective-permute-start(bf16[4,96,256]{2,1,0:T(8,128)(2,1)S(1)} %stack.7.refs_1_), channel_id=1, source_target_pairs={{0,4},{4,0},{8,12},{12,8},{16,20},{20,16},{24,28},{28,24},{1,5},{5... | collective-permute-start | bytes 589832 | tf_op jit(solution)/shard_map/ppermute | solution.py:204
  18.1 3.6 %collective-permute-start.6 = (bf16[4,96,256]{2,1,0:T(8,128)(2,1)S(1)}, bf16[4,96,256]{2,1,0:T(8,128)(2,1)S(1)}, u32[]{:S(2)}, u32[]{:S(2)}) collective-permute-start(bf16[4,96,256]{2,1,0:T(8,128)(2,1)S(1)} %stack.8.refs_3_), channel_id=1, source_target_pairs={{0,4},{4,0},{8,12},{12,8},{16,20},{20,16},{24,28},{28,24},{1,5},{5... | collective-permute-start | bytes 589832 | tf_op jit(solution)/shard_map/ppermute | solution.py:204

commit v30 on v29

--- a/solution.py
+++ b/solution.py
@@ -250,7 +250,7 @@
     tiles = tile_list.shape[0] // groups
     white = whiten(spectra, bad_channels)
     pairs = lax.dynamic_slice_in_dim(tile_list.T, lax.axis_index("tm") * tiles, tiles, axis=1)
-    where = jnp.concatenate([lax.axis_index("chan").reshape(1), pairs.reshape(-1)]).astype(jnp.int32).reshape(1, -1)
+    where = jnp.concatenate([lax.axis_index("chan").reshape(1), pairs[0], pairs[1]]).astype(jnp.int32).reshape(1, -1)
     near, far = halves(white, where)
     near, far = between_cores(between_chips(near, 2)), between_cores(between_chips(far, 2))
     partial = correlate(near, groups // 2, where, range(tiles), hours)

time: 24.5 us -> 24.5 us (level)
  no operation moved by 1% of the time
where the time goes in v30:
time: 24.5 us; the launch traced here: 24.3 us
  starting transfers between devices  16.7 us (68%)
  Pallas kernels  5.45 us (22%)
  waiting for transfers between devices  1.91 us (8%)
    ppermute x13, starting transfers between devices, swap(): lax.ppermute(array, axis, [(i, i ^ k) for i in range(lax.axis_size(axis))])  16.7 us
    pallas_call x2, Pallas kernels, correlate(): pl.pallas_call(lambda *refs: correlate_kernel(norm, picked, adds, places,...  4.27 us
    ppermute x13, waiting for transfers between devices, swap(): lax.ppermute(array, axis, [(i, i ^ k) for i in range(lax.axis_size(axis))])  1.91 us
    pallas_call x1, Pallas kernels, whiten(): pl.pallas_call(whiten_kernel, out_shape=jax.ShapeDtypeStruct((chans, spec...  1.11 us
  transfers between devices with their start and end apart: 13, of which 1 were waited for; matrix products, arithmetic and copies ran while one was open for 1% of the time, Pallas kernels for 7%

profile of v30, /device:TPU:1, one launch (start us, length us, event | category | flops | bytes accessed | tf_op | source)
XLA Modules:
  0.0 24.3 jit_solution(16402801519115127008)
XLA Ops:
  0.0 0.0 copy-start
  0.0 1.1 %whiten.1 = bf16[96,256]{1,0:T(8,128)(2,1)S(1)} custom-call(bf16[256,96]{1,0:T(8,128)(2,1)} %bitcast.17, s32[1,96]{1,0:T(1,128)} %bitcast.18), custom_call_target="tpu_custom_call" | custom-call | tf_op jit(solution)/shard_map/whiten/pallas_call | solution.py:56
  1.1 2.2 %collective-permute-start.7 = (bf16[1,96,256]{2,1,0:T(8,128)(2,1)S(1)}, bf16[1,96,256]{2,1,0:T(8,128)(2,1)S(1)}, u32[]{:S(2)}, u32[]{:S(2)}) collective-permute-start(bf16[1,96,256]{2,1,0:T(8,128)(2,1)S(1)} %bitcast.13), channel_id=1, source_target_pairs={{0,1},{1,0},{2,3},{3,2},{4,5},{5,4},{6,7},{7,6},{8,9},{9,8},{10,11... | collective-permute-start | bytes 147464 | tf_op jit(solution)/shard_map/ppermute | solution.py:204
  3.3 2.2 %collective-permute-start.1 = (bf16[1,96,256]{2,1,0:T(8,128)(2,1)S(1)}, bf16[1,96,256]{2,1,0:T(8,128)(2,1)S(1)}, u32[]{:S(2)}, u32[]{:S(2)}) collective-permute-start(bf16[1,96,256]{2,1,0:T(8,128)(2,1)S(1)} %bitcast.14), channel_id=1, source_target_pairs={{0,3},{1,2},{2,1},{3,0},{4,7},{5,6},{6,5},{7,4},{8,11},{9,10},{10,... | collective-permute-start | bytes 147464 | tf_op jit(solution)/shard_map/ppermute | solution.py:204
  5.5 0.1 collective-permute-start
  5.6 0.0 copy-done
  5.6 0.1 dynamic-slice_bitcast_fusion
  5.7 0.0 collective-permute-done.7.refs_1_
  5.7 2.2 %collective-permute-start.8 = (bf16[2,96,256]{2,1,0:T(8,128)(2,1)S(1)}, bf16[2,96,256]{2,1,0:T(8,128)(2,1)S(1)}, u32[]{:S(2)}, u32[]{:S(2)}) collective-permute-start(bf16[2,96,256]{2,1,0:T(8,128)(2,1)S(1)} %stack.9.refs_0_), channel_id=1, source_target_pairs={{0,24},{4,28},{8,16},{12,20},{16,8},{20,12},{24,0},{28,4},{1,25},{... | collective-permute-start | bytes 294920 | tf_op jit(solution)/shard_map/ppermute | solution.py:204
  8.0 0.1 add_bitcast_fusion.refs_2_.refs_0_
  8.0 0.3 %collective-permute-start.11 = (bf16[2,96,256]{2,1,0:T(8,128)(2,1)S(1)}, bf16[2,96,256]{2,1,0:T(8,128)(2,1)S(1)}, u32[]{:S(2)}, u32[]{:S(2)}) collective-permute-start(bf16[2,96,256]{2,1,0:T(8,128)(2,1)S(1)} %stack.9.refs_0_), channel_id=1, source_target_pairs={{0,8},{4,12},{8,0},{12,4},{16,24},{20,28},{24,16},{28,20},{1,9},{5... | collective-permute-start | bytes 294920 | tf_op jit(solution)/shard_map/ppermute | solution.py:204
  8.3 0.2 collective-permute-start.10
  8.5 0.0 collective-permute-done.1.refs_1_
  8.5 1.9 %collective-permute-done.refs_0_ = bf16[1,96,256]{2,1,0:T(8,128)(2,1)S(1)} collective-permute-done((bf16[1,96,256]{2,1,0:T(8,128)(2,1)S(1)}, bf16[1,96,256]{2,1,0:T(8,128)(2,1)S(1)}, u32[]{:S(2)}, u32[]{:S(2)}) %collective-permute-start) | collective-permute-done | bytes 49184 | tf_op jit(solution)/shard_map/ppermute | solution.py:204
  10.4 2.2 %collective-permute-start.2 = (bf16[2,96,256]{2,1,0:T(8,128)(2,1)S(1)}, bf16[2,96,256]{2,1,0:T(8,128)(2,1)S(1)}, u32[]{:S(2)}, u32[]{:S(2)}) collective-permute-start(bf16[2,96,256]{2,1,0:T(8,128)(2,1)S(1)} %stack.6.refs_0_), channel_id=1, source_target_pairs={{0,24},{4,28},{8,16},{12,20},{16,8},{20,12},{24,0},{28,4},{1,25},{... | collective-permute-start | bytes 294920 | tf_op jit(solution)/shard_map/ppermute | solution.py:204
  12.6 0.3 %collective-permute-start.5 = (bf16[2,96,256]{2,1,0:T(8,128)(2,1)S(1)}, bf16[2,96,256]{2,1,0:T(8,128)(2,1)S(1)}, u32[]{:S(2)}, u32[]{:S(2)}) collective-permute-start(bf16[2,96,256]{2,1,0:T(8,128)(2,1)S(1)} %stack.6.refs_0_), channel_id=1, source_target_pairs={{0,8},{4,12},{8,0},{12,4},{16,24},{20,28},{24,16},{28,20},{1,9},{5... | collective-permute-start | bytes 294920 | tf_op jit(solution)/shard_map/ppermute | solution.py:204
  12.9 0.0 collective-permute-done.8.refs_1_
  12.9 0.2 collective-permute-start.4
  13.1 0.0 collective-permute-done.11.refs_1_
  13.2 2.8 %collective-permute-start.9 = (bf16[4,96,256]{2,1,0:T(8,128)(2,1)S(1)}, bf16[4,96,256]{2,1,0:T(8,128)(2,1)S(1)}, u32[]{:S(2)}, u32[]{:S(2)}) collective-permute-start(bf16[4,96,256]{2,1,0:T(8,128)(2,1)S(1)} %stack.10.refs_1_), channel_id=1, source_target_pairs={{0,4},{4,0},{8,12},{12,8},{16,20},{20,16},{24,28},{28,24},{1,5},{5... | collective-permute-start | bytes 589832 | tf_op jit(solution)/shard_map/ppermute | solution.py:204
  15.9 0.0 collective-permute-done.10.refs_0_
  15.9 0.1 collective-permute-start.12
  16.0 0.0 collective-permute-done.2.refs_1_
  16.1 2.0 %collective-permute-start.3 = (bf16[4,96,256]{2,1,0:T(8,128)(2,1)S(1)}, bf16[4,96,256]{2,1,0:T(8,128)(2,1)S(1)}, u32[]{:S(2)}, u32[]{:S(2)}) collective-permute-start(bf16[4,96,256]{2,1,0:T(8,128)(2,1)S(1)} %stack.7.refs_1_), channel_id=1, source_target_pairs={{0,4},{4,0},{8,12},{12,8},{16,20},{20,16},{24,28},{28,24},{1,5},{5... | collective-permute-start | bytes 589832 | tf_op jit(solution)/shard_map/ppermute | solution.py:204
  18.0 0.0 collective-permute-done.5.refs_1_
  18.0 0.0 collective-permute-done.4.refs_0_
  18.1 2.0 %collective-permute-start.6 = (bf16[4,96,256]{2,1,0:T(8,128)(2,1)S(1)}, bf16[4,96,256]{2,1,0:T(8,128)(2,1)S(1)}, u32[]{:S(2)}, u32[]{:S(2)}) collective-permute-start(bf16[4,96,256]{2,1,0:T(8,128)(2,1)S(1)} %stack.8.refs_3_), channel_id=1, source_target_pairs={{0,4},{4,0},{8,12},{12,8},{16,20},{20,16},{24,28},{28,24},{1,5},{5... | collective-permute-start | bytes 589832 | tf_op jit(solution)/shard_map/ppermute | solution.py:204
  20.0 0.0 collective-permute-done.9.refs_2_
  20.0 0.0 collective-permute-done.12.refs_4_
  20.0 1.6 %correlate.1.refs_5_ = f32[2,4,8,128,128]{4,3,2,1,0:T(8,128)S(1)} custom-call(s32[1,5]{1,0:T(1,128)S(1)} %add_bitcast_fusion.refs_2_.refs_0_, bf16[4,96,256]{2,1,0:T(8,128)(2,1)S(1)} %stack.10.refs_1_, bf16[4,96,256]{2,1,0:T(8,128)(2,1)S(1)} %collective-permute-done.9.refs_2_, bf16[4,96,256]{2,1,0:T(8,128)(2,1)S(1)} %stack.11.refs_3_, ...), custom_call_target="tpu_custom_call" | custom-call | tf_op jit(solution)/shard_map/correlate/pallas_call | solution.py:186
  21.6 0.0 collective-permute-done.3.refs_2_
  21.7 0.0 collective-permute-done.6.refs_4_
  21.7 2.7 %correlate_add.1 = f32[2,4,8,128,128]{4,3,2,1,0:T(8,128)} custom-call(s32[1,5]{1,0:T(1,128)S(1)} %add_bitcast_fusion.refs_2_.refs_0_, bf16[4,96,256]{2,1,0:T(8,128)(2,1)S(1)} %stack.7.refs_1_, bf16[4,96,256]{2,1,0:T(8,128)(2,1)S(1)} %collective-permute-done.3.refs_2_, bf16[4,96,256]{2,1,0:T(8,128)(2,1)S(1)} %stack.8.refs_3_, ...), custom_call_target="tpu_custom_call" | custom-call | tf_op jit(solution)/shard_map/correlate_add/pallas_call | solution.py:186
  (7 shorter events, 0.1 us)
Async XLA Ops:
  0.0 5.6 %copy-start = (s32[8,2]{0,1:T(2,128)S(1)}, s32[8,2]{0,1:T(2,128)}, u32[]{:S(2)}) copy-start(s32[8,2]{0,1:T(2,128)} %param.5) | copy-start | bytes 196
  1.1 4.6 %collective-permute-start.7 = (bf16[1,96,256]{2,1,0:T(8,128)(2,1)S(1)}, bf16[1,96,256]{2,1,0:T(8,128)(2,1)S(1)}, u32[]{:S(2)}, u32[]{:S(2)}) collective-permute-start(bf16[1,96,256]{2,1,0:T(8,128)(2,1)S(1)} %bitcast.13), channel_id=1, source_target_pairs={{0,1},{1,0},{2,3},{3,2},{4,5},{5,4},{6,7},{7,6},{8,9},{9,8},{10,11... | collective-permute-start | bytes 147464 | tf_op jit(solution)/shard_map/ppermute | solution.py:204
  3.3 5.2 %collective-permute-start.1 = (bf16[1,96,256]{2,1,0:T(8,128)(2,1)S(1)}, bf16[1,96,256]{2,1,0:T(8,128)(2,1)S(1)}, u32[]{:S(2)}, u32[]{:S(2)}) collective-permute-start(bf16[1,96,256]{2,1,0:T(8,128)(2,1)S(1)} %bitcast.14), channel_id=1, source_target_pairs={{0,3},{1,2},{2,1},{3,0},{4,7},{5,6},{6,5},{7,4},{8,11},{9,10},{10,... | collective-permute-start | bytes 147464 | tf_op jit(solution)/shard_map/ppermute | solution.py:204
  5.5 4.9 %collective-permute-start = (bf16[1,96,256]{2,1,0:T(8,128)(2,1)S(1)}, bf16[1,96,256]{2,1,0:T(8,128)(2,1)S(1)}, u32[]{:S(2)}, u32[]{:S(2)}) collective-permute-start(bf16[1,96,256]{2,1,0:T(8,128)(2,1)S(1)} %bitcast.15), channel_id=1, source_target_pairs={{0,2},{1,3},{2,0},{3,1},{4,6},{5,7},{6,4},{7,5},{8,10},{9,11},{10,... | collective-permute-start | bytes 147464 | tf_op jit(solution)/shard_map/ppermute | solution.py:204
  5.7 7.2 %collective-permute-start.8 = (bf16[2,96,256]{2,1,0:T(8,128)(2,1)S(1)}, bf16[2,96,256]{2,1,0:T(8,128)(2,1)S(1)}, u32[]{:S(2)}, u32[]{:S(2)}) collective-permute-start(bf16[2,96,256]{2,1,0:T(8,128)(2,1)S(1)} %stack.9.refs_0_), channel_id=1, source_target_pairs={{0,24},{4,28},{8,16},{12,20},{16,8},{20,12},{24,0},{28,4},{1,25},{... | collective-permute-start | bytes 294920 | tf_op jit(solution)/shard_map/ppermute | solution.py:204
  8.0 5.1 %collective-permute-start.11 = (bf16[2,96,256]{2,1,0:T(8,128)(2,1)S(1)}, bf16[2,96,256]{2,1,0:T(8,128)(2,1)S(1)}, u32[]{:S(2)}, u32[]{:S(2)}) collective-permute-start(bf16[2,96,256]{2,1,0:T(8,128)(2,1)S(1)} %stack.9.refs_0_), channel_id=1, source_target_pairs={{0,8},{4,12},{8,0},{12,4},{16,24},{20,28},{24,16},{28,20},{1,9},{5... | collective-permute-start | bytes 294920 | tf_op jit(solution)/shard_map/ppermute | solution.py:204
  8.3 7.6 %collective-permute-start.10 = (bf16[2,96,256]{2,1,0:T(8,128)(2,1)S(1)}, bf16[2,96,256]{2,1,0:T(8,128)(2,1)S(1)}, u32[]{:S(2)}, u32[]{:S(2)}) collective-permute-start(bf16[2,96,256]{2,1,0:T(8,128)(2,1)S(1)} %stack.9.refs_0_), channel_id=1, source_target_pairs={{0,16},{4,20},{8,24},{12,28},{16,0},{20,4},{24,8},{28,12},{1,17},{... | collective-permute-start | bytes 294920 | tf_op jit(solution)/shard_map/ppermute | solution.py:204
  10.4 5.6 %collective-permute-start.2 = (bf16[2,96,256]{2,1,0:T(8,128)(2,1)S(1)}, bf16[2,96,256]{2,1,0:T(8,128)(2,1)S(1)}, u32[]{:S(2)}, u32[]{:S(2)}) collective-permute-start(bf16[2,96,256]{2,1,0:T(8,128)(2,1)S(1)} %stack.6.refs_0_), channel_id=1, source_target_pairs={{0,24},{4,28},{8,16},{12,20},{16,8},{20,12},{24,0},{28,4},{1,25},{... | collective-permute-start | bytes 294920 | tf_op jit(solution)/shard_map/ppermute | solution.py:204
  12.6 5.4 %collective-permute-start.5 = (bf16[2,96,256]{2,1,0:T(8,128)(2,1)S(1)}, bf16[2,96,256]{2,1,0:T(8,128)(2,1)S(1)}, u32[]{:S(2)}, u32[]{:S(2)}) collective-permute-start(bf16[2,96,256]{2,1,0:T(8,128)(2,1)S(1)} %stack.6.refs_0_), channel_id=1, source_target_pairs={{0,8},{4,12},{8,0},{12,4},{16,24},{20,28},{24,16},{28,20},{1,9},{5... | collective-permute-start | bytes 294920 | tf_op jit(solution)/shard_map/ppermute | solution.py:204
  12.9 5.1 %collective-permute-start.4 = (bf16[2,96,256]{2,1,0:T(8,128)(2,1)S(1)}, bf16[2,96,256]{2,1,0:T(8,128)(2,1)S(1)}, u32[]{:S(2)}, u32[]{:S(2)}) collective-permute-start(bf16[2,96,256]{2,1,0:T(8,128)(2,1)S(1)} %stack.6.refs_0_), channel_id=1, source_target_pairs={{0,16},{4,20},{8,24},{12,28},{16,0},{20,4},{24,8},{28,12},{1,17},{... | collective-permute-start | bytes 294920 | tf_op jit(solution)/shard_map/ppermute | solution.py:204
  13.2 6.9 %collective-permute-start.9 = (bf16[4,96,256]{2,1,0:T(8,128)(2,1)S(1)}, bf16[4,96,256]{2,1,0:T(8,128)(2,1)S(1)}, u32[]{:S(2)}, u32[]{:S(2)}) collective-permute-start(bf16[4,96,256]{2,1,0:T(8,128)(2,1)S(1)} %stack.10.refs_1_), channel_id=1, source_target_pairs={{0,4},{4,0},{8,12},{12,8},{16,20},{20,16},{24,28},{28,24},{1,5},{5... | collective-permute-start | bytes 589832 | tf_op jit(solution)/shard_map/ppermute | solution.py:204
  15.9 4.1 %collective-permute-start.12 = (bf16[4,96,256]{2,1,0:T(8,128)(2,1)S(1)}, bf16[4,96,256]{2,1,0:T(8,128)(2,1)S(1)}, u32[]{:S(2)}, u32[]{:S(2)}) collective-permute-start(bf16[4,96,256]{2,1,0:T(8,128)(2,1)S(1)} %stack.11.refs_3_), channel_id=1, source_target_pairs={{0,4},{4,0},{8,12},{12,8},{16,20},{20,16},{24,28},{28,24},{1,5},{5... | collective-permute-start | bytes 589832 | tf_op jit(solution)/shard_map/ppermute | solution.py:204
  16.1 5.6 %collective-permute-start.3 = (bf16[4,96,256]{2,1,0:T(8,128)(2,1)S(1)}, bf16[4,96,256]{2,1,0:T(8,128)(2,1)S(1)}, u32[]{:S(2)}, u32[]{:S(2)}) collective-permute-start(bf16[4,96,256]{2,1,0:T(8,128)(2,1)S(1)} %stack.7.refs_1_), channel_id=1, source_target_pairs={{0,4},{4,0},{8,12},{12,8},{16,20},{20,16},{24,28},{28,24},{1,5},{5... | collective-permute-start | bytes 589832 | tf_op jit(solution)/shard_map/ppermute | solution.py:204
  18.1 3.6 %collective-permute-start.6 = (bf16[4,96,256]{2,1,0:T(8,128)(2,1)S(1)}, bf16[4,96,256]{2,1,0:T(8,128)(2,1)S(1)}, u32[]{:S(2)}, u32[]{:S(2)}) collective-permute-start(bf16[4,96,256]{2,1,0:T(8,128)(2,1)S(1)} %stack.8.refs_3_), channel_id=1, source_target_pairs={{0,4},{4,0},{8,12},{12,8},{16,20},{20,16},{24,28},{28,24},{1,5},{5... | collective-permute-start | bytes 589832 | tf_op jit(solution)/shard_map/ppermute | solution.py:204
